TPU v7x, 32 devices: a whole 2x2x4 slice. The times are simulated.
32 devices in a mesh: seq: 4 (over y, core), ctx: 8 (over z, x).
Axes of the slice: x: 2, y: 2, z: 4, core: 2. Of those that a mesh axis runs over, the one named last changes fastest.
Arguments:
- tokens: bfloat16 [4, 2048, 1152], P('seq', 'ctx'), may hold values from -6 to 6
- cotangent: bfloat16 [4, 2048, 1152], P('seq', 'ctx'), may hold values from -6 to 6
- segments: int32 [4, 2048], P('seq'), may hold values from 0 to 256, as said below
- positions: int32 [4, 2048], P('seq', 'ctx'), may hold values from 0 to 4094, as said below
- attn_w: float32 [2949120], P(('seq', 'ctx'))
- attn_m: float32 [2949120], P(('seq', 'ctx')), may hold values from -256 to 256
- attn_v: float32 [2949120], P(('seq', 'ctx')), may hold values from 1024 to 16384
- mlp_w: float32 [6912, 3456], P('ctx', 'seq')
- mlp_m: float32 [6912, 3456], P('ctx', 'seq'), may hold values from -256 to 256
- mlp_v: float32 [6912, 3456], P('ctx', 'seq'), may hold values from 1024 to 16384
- gains: float32 [5120], P(('seq', 'ctx')), may hold values from 0.6 to 2
- gain_m: float32 [5120], P(('seq', 'ctx')), may hold values from -512 to 512
- gain_v: float32 [5120], P(('seq', 'ctx')), may hold values from 4096 to 65536
Outputs:
- mixed: bfloat16 [4, 2048, 1152], P('seq', 'ctx')
- input_grad: bfloat16 [4, 2048, 1152], P('seq', 'ctx')
- attn_grad: float32 [2949120], P(('seq', 'ctx'))
- attn_m_new: float32 [2949120], P(('seq', 'ctx'))
- attn_v_new: float32 [2949120], P(('seq', 'ctx'))
- attn_new: float32 [2949120], P(('seq', 'ctx'))
- mlp_grad: float32 [6912, 3456], P('ctx', 'seq')
- mlp_m_new: float32 [6912, 3456], P('ctx', 'seq')
- mlp_v_new: float32 [6912, 3456], P('ctx', 'seq')
- mlp_new: float32 [6912, 3456], P('ctx', 'seq')
- gain_grad: float32 [5120], P(('seq', 'ctx'))
- gain_m_new: float32 [5120], P(('seq', 'ctx'))
- gain_v_new: float32 [5120], P(('seq', 'ctx'))
- gain_new: float32 [5120], P(('seq', 'ctx'))
Inputs may be any that keep to these rules, and one draw needn't show every extreme that they name: `segments`: in each sequence document numbers start at 0 and never fall; one document covers at least the positions 128 to 1919. Within a document positions start at 0 and rise by 1 or 2 from one token to the next.
All inputs are finite; a program needn't handle non-finite values.
Results may differ from a plain program's by a relative error of at most 0.03.
The roundings to bfloat16 on the way count: a program that leaves them out, or rounds other values in their place, can miss the bound.
Values may be sent and summed in bfloat16 or wider, within the bound.
No kernel may reach another device: no remote copies, remote signals or barrier semaphores. Data moves between devices by JAX's collectives and lax.ppermute only.
A program may use at most 320 MiB of HBM per device.

v0:
```python
import jax
import jax.numpy as jnp
from jax import lax
from jax.sharding import PartitionSpec as P

D = 1152
H = 4
HD = 256
STEP = 5


NORM_EPS = 1e-06
SCORE_FLOOR = -1e30
ROPE_BASE = 1000000.0
BETA_MOMENT = 0.5
ADAM_EPS = 1e-08
RATE_MATRIX = 0.03
RATE_GAIN = 0.5
DECAY_MATRIX = 0.1


def normed(value):
    factor = lax.rsqrt(jnp.mean(value * value, axis=-1, keepdims=True) + NORM_EPS)
    return (value * factor, factor)


def norm_back(unit, factor, d_unit):
    return factor * (d_unit - unit * jnp.mean(d_unit * unit, axis=-1, keepdims=True))


def angles(position):
    half_index = jnp.arange(HD // 2, dtype=jnp.float32)
    frequency = jnp.exp(half_index * (-2.0 * jnp.log(ROPE_BASE) / HD))
    angle = position.astype(jnp.float32)[:, None] * frequency[None, :]
    return (jnp.cos(angle), jnp.sin(angle))


def rotate(value, cosine, sine):
    half_width = value.shape[-1] // 2
    first_half = value[..., :half_width]
    second_half = value[..., half_width:]
    return jnp.concatenate(
        [first_half * cosine - second_half * sine, second_half * cosine + first_half * sine],
        axis=-1,
    )


def contract(left, right, left_dim, right_dim):
    return lax.dot_general(
        left, right, (((left_dim,), (right_dim,)), ((), ())), preferred_element_type=jnp.float32
    )


def gelu_gate(gate_part, up_part):
    return jax.nn.gelu(gate_part, approximate=True) * up_part


def adam_update(weight, moment_one, second, gradient, learn_rate, decay_rate):
    moment_new = BETA_MOMENT * moment_one + (1.0 - BETA_MOMENT) * gradient
    second_new = BETA_MOMENT * second + (1.0 - BETA_MOMENT) * gradient * gradient
    correction = 1.0 - BETA_MOMENT**STEP
    update = moment_new / correction / (jnp.sqrt(second_new / correction) + ADAM_EPS)
    return (moment_new, second_new, weight - learn_rate * (update + decay_rate * weight))


def shards(
    tokens,
    cotangent,
    segments,
    positions,
    attn_w,
    attn_m,
    attn_v,
    mlp_w,
    mlp_m,
    mlp_v,
    gains,
    gain_m,
    gain_v,
):
    score_scale = HD ** (-0.5)
    whole_attn, whole_gain = (
        lax.all_gather(attn_w.astype(jnp.bfloat16), ("seq", "ctx"), axis=0, tiled=True),
        lax.all_gather(gains.astype(jnp.bfloat16), ("seq", "ctx"), axis=0, tiled=True),
    )
    qkv_width = (H + 2) * HD
    w_qkv = whole_attn[: D * qkv_width].reshape(D, qkv_width)
    w_out = whole_attn[D * qkv_width :].reshape(H * HD, D)
    mlp_local = lax.all_gather(mlp_w.astype(jnp.bfloat16), "seq", axis=1, tiled=True)
    gain_all = whole_gain.astype(jnp.float32)
    gain_pre = gain_all[:D]
    gain_q = gain_all[D : D + HD]
    gain_k = gain_all[D + HD : D + 2 * HD]
    gain_post = gain_all[D + 2 * HD : 2 * D + 2 * HD]
    gain_fpre = gain_all[2 * D + 2 * HD : 3 * D + 2 * HD]
    gain_fpost = gain_all[3 * D + 2 * HD :]
    tok_rows = tokens.shape[1]
    ctx_place = lax.axis_index("ctx")
    length = tok_rows * lax.axis_size("ctx")
    head_rows = tok_rows * H
    key_span = min(512, length)
    block_count = length // key_span
    hidden_in = tokens[0].astype(jnp.float32)
    unit_in, scale_in = normed(hidden_in)
    normed_in = (unit_in * gain_pre).astype(jnp.bfloat16)
    qkv = jnp.dot(normed_in, w_qkv, preferred_element_type=jnp.float32)
    unit_q, scale_q = normed(qkv[:, : H * HD].reshape(tok_rows, H, HD))
    unit_k, scale_k = normed(qkv[:, H * HD : (H + 1) * HD])
    cosine, sine = angles(positions[0])
    query_flat = (
        rotate(unit_q * gain_q, cosine[:, None, :], sine[:, None, :])
        .astype(jnp.bfloat16)
        .reshape(head_rows, HD)
    )
    key_local = rotate(unit_k * gain_k, cosine, sine).astype(jnp.bfloat16)
    value_local = qkv[:, (H + 1) * HD :].astype(jnp.bfloat16)
    key_all, value_all = (
        lax.all_gather(key_local, "ctx", axis=0, tiled=True),
        lax.all_gather(value_local, "ctx", axis=0, tiled=True),
    )
    doc_all = segments[0]
    query_doc = lax.dynamic_slice_in_dim(doc_all, ctx_place * tok_rows, tok_rows)
    query_docs = jnp.repeat(query_doc, H)
    query_pos = ctx_place * tok_rows + jnp.repeat(jnp.arange(tok_rows, dtype=jnp.int32), H)
    first_doc = query_doc[0]
    last_query = ctx_place * tok_rows + tok_rows - 1

    def block_live(start):
        last_doc = lax.dynamic_index_in_dim(doc_all, start + key_span - 1, keepdims=False)
        return (start <= last_query) & (last_doc >= first_doc)

    def scores_of(key_rows, start):
        raw = contract(query_flat, key_rows, 1, 1) * score_scale
        key_pos = start + jnp.arange(key_span, dtype=jnp.int32)
        key_docs = lax.dynamic_slice_in_dim(doc_all, start, key_span)
        allowed = (query_docs[:, None] == key_docs[None, :]) & (
            query_pos[:, None] >= key_pos[None, :]
        )
        return (raw, allowed)

    def forward_block(state, block_index):
        start = block_index * key_span
        key_rows = lax.dynamic_slice_in_dim(key_all, start, key_span)
        value_rows = lax.dynamic_slice_in_dim(value_all, start, key_span)

        def forward_visit(current):
            row_max, row_sum, weighted = current
            raw, allowed = scores_of(key_rows, start)
            new_max = jnp.maximum(row_max, jnp.max(jnp.where(allowed, raw, SCORE_FLOOR), axis=1))
            exponent = jnp.where(allowed, jnp.exp(raw - new_max[:, None]), 0.0)
            shrink = jnp.exp(row_max - new_max)
            summed = row_sum * shrink + jnp.sum(exponent, axis=1)
            mixed_rows = weighted * shrink[:, None] + jnp.dot(
                exponent.astype(jnp.bfloat16), value_rows, preferred_element_type=jnp.float32
            )
            return (new_max, summed, mixed_rows)

        def forward_skip_block(current):
            return current

        return (lax.cond(block_live(start), forward_visit, forward_skip_block, state), None)

    start_state = (
        jnp.full((head_rows,), SCORE_FLOOR, jnp.float32),
        jnp.zeros((head_rows,), jnp.float32),
        jnp.zeros((head_rows, HD), jnp.float32),
    )
    (row_max, row_sum, weighted), unused_out = lax.scan(
        forward_block, start_state, jnp.arange(block_count, dtype=jnp.int32)
    )
    attn_rows = weighted / row_sum[:, None]
    log_total = row_max + jnp.log(row_sum)
    heads_low = attn_rows.astype(jnp.bfloat16)
    heads_flat = heads_low.reshape(tok_rows, H * HD)
    attn_out = jnp.dot(heads_flat, w_out, preferred_element_type=jnp.float32)
    unit_post, scale_post = normed(attn_out)
    middle = hidden_in + unit_post * gain_post
    unit_mid, scale_mid = normed(middle)
    ffn_in = (unit_mid * gain_fpre).astype(jnp.bfloat16)
    weight_rows = lax.all_gather(mlp_local, "ctx", axis=0, tiled=True)
    gate = contract(ffn_in, weight_rows[:, :D], 1, 1)
    up_part = contract(ffn_in, weight_rows[:, D : 2 * D], 1, 1)
    activated, gelu_pull = jax.vjp(gelu_gate, gate, up_part)
    act_low = activated.astype(jnp.bfloat16)
    out_rows = contract(act_low, weight_rows[:, 2 * D :], 1, 0)
    unit_out, scale_out = normed(out_rows)
    mixed = (middle + unit_out * gain_fpost).astype(jnp.bfloat16)[None]
    upstream = cotangent[0].astype(jnp.float32)
    d_gfpost = jnp.sum(upstream * unit_out, axis=0)
    d_mlp_out = norm_back(unit_out, scale_out, upstream * gain_fpost).astype(jnp.bfloat16)
    d_act = contract(d_mlp_out, weight_rows[:, 2 * D :], 1, 1)
    d_gate, d_up = gelu_pull(d_act)
    d_gate_low = d_gate.astype(jnp.bfloat16)
    d_up_low = d_up.astype(jnp.bfloat16)
    grad_gate = contract(d_gate_low, ffn_in, 0, 0)
    grad_up = contract(d_up_low, ffn_in, 0, 0)
    grad_down = contract(act_low, d_mlp_out, 0, 0)
    d_rows_in = contract(d_gate_low, weight_rows[:, :D], 1, 0) + contract(
        d_up_low, weight_rows[:, D : 2 * D], 1, 0
    )
    owned_gate, owned_up, owned_down = (
        lax.psum_scatter(
            grad_gate.astype(jnp.bfloat16), "ctx", scatter_dimension=0, tiled=True
        ).astype(jnp.float32),
        lax.psum_scatter(
            grad_up.astype(jnp.bfloat16), "ctx", scatter_dimension=0, tiled=True
        ).astype(jnp.float32),
        lax.psum_scatter(
            grad_down.astype(jnp.bfloat16), "ctx", scatter_dimension=0, tiled=True
        ).astype(jnp.float32),
    )
    grad_local = jnp.concatenate([owned_gate, owned_up, owned_down], axis=1)
    mlp_red = lax.psum_scatter(
        grad_local.astype(jnp.bfloat16), "seq", scatter_dimension=1, tiled=True
    ).astype(jnp.float32)
    d_gfpre = jnp.sum(d_rows_in * unit_mid, axis=0)
    d_middle = upstream + norm_back(unit_mid, scale_mid, d_rows_in * gain_fpre)
    d_gpost = jnp.sum(d_middle * unit_post, axis=0)
    d_attn_out = norm_back(unit_post, scale_post, d_middle * gain_post).astype(jnp.bfloat16)
    d_wout = contract(heads_flat, d_attn_out, 0, 0)
    d_heads = contract(d_attn_out, w_out, 1, 1).astype(jnp.bfloat16).reshape(head_rows, HD)
    delta_rows = jnp.sum(d_heads.astype(jnp.float32) * attn_rows, axis=1)

    def backward_block(grad_query, block_index):
        start = block_index * key_span
        key_rows = lax.dynamic_slice_in_dim(key_all, start, key_span)
        value_rows = lax.dynamic_slice_in_dim(value_all, start, key_span)

        def backward_visit(current):
            raw, allowed = scores_of(key_rows, start)
            probs = jnp.where(allowed, jnp.exp(raw - log_total[:, None]), 0.0)
            d_value = contract(probs.astype(jnp.bfloat16), d_heads, 0, 0)
            d_probs = contract(d_heads, value_rows, 1, 1)
            d_scores = (probs * (d_probs - delta_rows[:, None])).astype(jnp.bfloat16)
            grown = (
                current
                + jnp.dot(d_scores, key_rows, preferred_element_type=jnp.float32) * score_scale
            )
            d_key = contract(d_scores, query_flat, 0, 0) * score_scale
            return (grown, jnp.concatenate([d_key, d_value], axis=1))

        def backward_skip_block(current):
            return (current, jnp.zeros((key_span, 2 * HD), jnp.float32))

        return lax.cond(block_live(start), backward_visit, backward_skip_block, grad_query)

    grad_query, kv_blocks = lax.scan(
        backward_block,
        jnp.zeros((head_rows, HD), jnp.float32),
        jnp.arange(block_count, dtype=jnp.int32),
    )
    kv_mine = lax.psum_scatter(
        kv_blocks.reshape(length, 2 * HD).astype(jnp.bfloat16),
        "ctx",
        scatter_dimension=0,
        tiled=True,
    ).astype(jnp.float32)
    rotated_q = rotate(grad_query.reshape(tok_rows, H, HD), cosine[:, None, :], -sine[:, None, :])
    d_gq = jnp.sum(rotated_q * unit_q, axis=(0, 1))
    d_qraw = norm_back(unit_q, scale_q, rotated_q * gain_q)
    rotated_k = rotate(kv_mine[:, :HD], cosine, -sine)
    d_gk = jnp.sum(rotated_k * unit_k, axis=0)
    d_kraw = norm_back(unit_k, scale_k, rotated_k * gain_k)
    d_qkv = jnp.concatenate(
        [d_qraw.reshape(tok_rows, H * HD), d_kraw, kv_mine[:, HD:]], axis=1
    ).astype(jnp.bfloat16)
    d_wqkv = contract(normed_in, d_qkv, 0, 0)
    d_normed_in = contract(d_qkv, w_qkv, 1, 1)
    d_gpre = jnp.sum(d_normed_in * unit_in, axis=0)
    input_grad = (d_middle + norm_back(unit_in, scale_in, d_normed_in * gain_pre)).astype(
        jnp.bfloat16
    )[None]
    attn_grad = jnp.concatenate([d_wqkv.reshape(-1), d_wout.reshape(-1)])
    gain_grad = jnp.concatenate([d_gpre, d_gq, d_gk, d_gpost, d_gfpre, d_gfpost])
    attn_red, gain_red = (
        lax.psum_scatter(attn_grad, ("seq", "ctx"), scatter_dimension=0, tiled=True),
        lax.psum_scatter(gain_grad, ("seq", "ctx"), scatter_dimension=0, tiled=True),
    )
    attn_m_new, attn_v_new, attn_new = adam_update(
        attn_w, attn_m, attn_v, attn_red, RATE_MATRIX, DECAY_MATRIX
    )
    mlp_m_new, mlp_v_new, mlp_new = adam_update(
        mlp_w, mlp_m, mlp_v, mlp_red, RATE_MATRIX, DECAY_MATRIX
    )
    gain_m_new, gain_v_new, gain_new = adam_update(gains, gain_m, gain_v, gain_red, RATE_GAIN, 0.0)
    return (
        mixed,
        input_grad,
        attn_red,
        attn_m_new,
        attn_v_new,
        attn_new,
        mlp_red,
        mlp_m_new,
        mlp_v_new,
        mlp_new,
        gain_red,
        gain_m_new,
        gain_v_new,
        gain_new,
    )


def solution(mesh):
    in_specs = (
        P("seq", "ctx", None),
        P("seq", "ctx", None),
        P("seq", None),
        P("seq", "ctx"),
        P(("seq", "ctx")),
        P(("seq", "ctx")),
        P(("seq", "ctx")),
        P("ctx", "seq"),
        P("ctx", "seq"),
        P("ctx", "seq"),
        P(("seq", "ctx")),
        P(("seq", "ctx")),
        P(("seq", "ctx")),
    )
    out_specs = (
        P("seq", "ctx", None),
        P("seq", "ctx", None),
        P(("seq", "ctx")),
        P(("seq", "ctx")),
        P(("seq", "ctx")),
        P(("seq", "ctx")),
        P("ctx", "seq"),
        P("ctx", "seq"),
        P("ctx", "seq"),
        P("ctx", "seq"),
        P(("seq", "ctx")),
        P(("seq", "ctx")),
        P(("seq", "ctx")),
        P(("seq", "ctx")),
    )
    return jax.shard_map(shards, mesh=mesh, in_specs=in_specs, out_specs=out_specs, check_vma=False)
```

profile of v0, /device:TPU:0, one launch (start us, length us, event | category | flops | bytes accessed | tf_op | source)
XLA Modules:
  0.0 2436.7 jit_solution(3799737499820166787)
XLA Ops:
  9.0 3.9 copy.34
  13.8 42.2 %all-reduce = bf16[5120]{0:T(1024)(128)(2,1)S(1)} all-reduce(bf16[5120]{0:T(1024)(128)(2,1)S(1)} %dynamic-update-slice), channel_id=1, replica_groups=mesh['seq'=4,'ctx'=8] {'seq','ctx'}, use_global_device_ids=true, to_apply=%add | all-reduce | flops 5120 | bytes 20480
  58.5 23.6 all-gather.6.cloned.1.call-done
  82.1 2.0 slice-done
  84.1 5.2 slice.104
  89.2 4.0 fusion.91
  96.9 32.2 %all-gather.12.cloned.1.call-done = bf16[864,3456]{0,1:T(8,128)(2,1)} async-done(((bf16[864,864]{0,1:T(8,128)(2,1)}), bf16[864,3456]{0,1:T(8,128)(2,1)}) %all-gather.12.cloned.1.call-update) | async-done | bytes 5971984 | tf_op jit(solution)/shard_map/all_gather | solution.py:89
  129.0 9.2 copy.35
  141.4 2.0 slice-done.1
  143.5 3.7 slice.115
  148.5 23.5 all-gather.8.cloned.1.call-done
  171.9 41.5 %all-gather.10.cloned.1.call-done = bf16[2048,256]{1,0:T(8,128)(2,1)} async-done(((bf16[256,256]{1,0:T(8,128)(2,1)}), bf16[2048,256]{1,0:T(8,128)(2,1)}) %all-gather.10.cloned.1.call-update) | async-done | bytes 1048592 | tf_op jit(solution)/shard_map/all_gather | solution.py:119
  213.5 17.9 while.39
  216.7 4.9 conditional.6
  219.5 2.1 convolution_add_fusion
  232.8 2.8 multiply_reduce_fusion.6
  237.2 880.8 %all-gather.14.cloned.1.call-done = bf16[6912,3456]{1,0:T(8,128)(2,1)} async-done(((bf16[864,3456]{1,0:T(8,128)(2,1)}), bf16[6912,3456]{1,0:T(8,128)(2,1)}) %all-gather.14.cloned.1.call-update) | async-done | bytes 47775760 | tf_op jit(solution)/shard_map/all_gather | solution.py:180
  1118.0 13.3 fusion.48
  1131.3 12.8 multiply_convert_fusion.1
  1144.0 10.4 multiply_reduce_fusion.4
  1157.2 17.1 fusion.56
  1174.3 10.4 fusion.42
  1184.7 9.6 multiply_reduce_fusion
  1200.9 22.6 while.40
  1204.2 6.3 conditional.7
  1223.6 4.1 copy.36
  1228.8 10.8 convolution_convert_fusion
  1239.6 10.9 convolution_convert_fusion.1
  1259.4 3.0 fusion.110
  1262.4 5.7 reshape.278
  1268.1 10.9 convolution_convert_fusion.2
  1280.8 2.9 multiply_reduce_fusion.7
  1283.6 30.7 %reduce-scatter.8.cloned.1.call-done = bf16[256,512]{1,0:T(8,128)(2,1)} async-done(((bf16[2048,512]{1,0:T(8,128)(2,1)}), bf16[256,512]{1,0:T(8,128)(2,1)}) %reduce-scatter.8.cloned.1.call-update) | async-done | bytes 262160 | tf_op jit(solution)/shard_map/reduce_scatter | solution.py:252
  1316.4 4.2 fusion.82
  1320.6 8.1 reshape.277
  1328.7 10.8 pad_maximum_fusion
  1339.6 246.8 %reduce-scatter.14.cloned.1.call-done = bf16[864,1152]{1,0:T(8,128)(2,1)} async-done(((bf16[6912,1152]{1,0:T(8,128)(2,1)}), bf16[864,1152]{1,0:T(8,128)(2,1)}) %reduce-scatter.14.cloned.1.call-update) | async-done | bytes 1990672 | tf_op jit(solution)/shard_map/reduce_scatter | solution.py:208
  1586.4 272.2 %reduce-scatter.12.cloned.1.call-done = bf16[864,1152]{1,0:T(8,128)(2,1)} async-done(((bf16[6912,1152]{1,0:T(8,128)(2,1)}), bf16[864,1152]{1,0:T(8,128)(2,1)}) %reduce-scatter.12.cloned.1.call-update) | async-done | bytes 1990672 | tf_op jit(solution)/shard_map/reduce_scatter | solution.py:205
  1858.7 272.4 %reduce-scatter.10.cloned.1.call-done = bf16[864,1152]{1,0:T(8,128)(2,1)} async-done(((bf16[6912,1152]{1,0:T(8,128)(2,1)}), bf16[864,1152]{1,0:T(8,128)(2,1)}) %reduce-scatter.10.cloned.1.call-update) | async-done | bytes 1990672 | tf_op jit(solution)/shard_map/reduce_scatter | solution.py:202
  2131.0 6.1 pad_maximum_fusion.1
  2137.2 9.2 copy.37
  2147.5 3.7 fusion.76
  2151.3 40.7 %all-reduce.2 = f32[5120]{0:T(1024)S(1)} all-reduce(f32[5120]{0:T(1024)S(1)} %constant_dynamic-update-slice_fusion.1), channel_id=8, replica_groups=mesh['seq'=4,'ctx'=8] {'seq','ctx'}, use_global_device_ids=true, to_apply=%region_36.37.clone | all-reduce | flops 5120 | bytes 40960
  2193.8 166.1 %all-reduce.5.cloned.1.call-done = f32[2949120]{0:T(1024)} async-done(((f32[2949120]{0:T(1024)}), f32[2949120]{0:T(1024)}) %all-reduce.5.cloned.1.call-update) | async-done | bytes 11796496
  2359.9 2.4 multiply_subtract_fusion.2
  2362.3 56.7 %reduce-scatter.16.cloned.1.call-done = bf16[864,864]{1,0:T(8,128)(2,1)} async-done(((bf16[3456,864]{1,0:T(8,128)(2,1)}), bf16[864,864]{1,0:T(8,128)(2,1)}) %reduce-scatter.16.cloned.1.call-update) | async-done | bytes 1493008
  2419.0 3.5 copy.38
  2422.5 7.5 multiply_subtract_fusion
  (277 shorter events, 63.9 us)
Async XLA Ops:
  7.2 74.9 %all-gather.6.cloned.1.call-start = ((), (), s32[]{:S(2)}) async-start(), calls=%async_computation.5 | async-start | bytes 6082560 | tf_op jit(solution)/shard_map/all_gather | solution.py:83
  8.9 4.1 copy-start.52
  8.9 4.1 copy-start.56
  9.0 47.6 %copy-start.8 = (bf16[1,256,1152]{2,1,0:T(8,128)(2,1)S(1)}, bf16[1,256,1152]{2,1,0:T(8,128)(2,1)}, u32[]{:S(2)}) copy-start(bf16[1,256,1152]{2,1,0:T(8,128)(2,1)} %param.21) | copy-start | bytes 1769476
  9.0 120.1 %all-gather.12.cloned.1.call-start = ((), (), s32[]{:S(2)}) async-start(), calls=%async_computation.8 | async-start | bytes 7741440 | tf_op jit(solution)/shard_map/all_gather | solution.py:89
  12.9 159.0 %all-gather.8.cloned.1.call-start = ((), (), s32[]{:S(2)}) async-start(), calls=%async_computation.6 | async-start | bytes 1179648 | tf_op jit(solution)/shard_map/all_gather | solution.py:118
  58.5 30.8 %copy-start.35 = (f32[1152]{0:T(1024)}, f32[1152]{0:T(1024)S(1)}, u32[]{:S(2)}) copy-start(f32[1152]{0:T(1024)S(1)} %get-tuple-element.1042) | copy-start | bytes 13828
  89.2 4.2 copy-start.46
  89.2 4.8 copy-start.48
  89.2 4.8 copy-start.50
  93.2 47.6 %copy-start.14 = (f32[256,1536]{1,0:T(8,128)}, f32[256,1536]{1,0:T(8,128)S(1)}, u32[]{:S(2)}) copy-start(f32[256,1536]{1,0:T(8,128)S(1)} %fusion.91) | copy-start | bytes 4718596
  95.4 52.6 %copy-start.29 = (f32[256,128]{1,0:T(8,128)}, f32[256,128]{1,0:T(8,128)S(1)}, u32[]{:S(2)}) copy-start(f32[256,128]{1,0:T(8,128)S(1)} %get-tuple-element.1049) | copy-start | bytes 393220
  96.1 117.4 %all-gather.10.cloned.1.call-start = ((), (), s32[]{:S(2)}) async-start(), calls=%async_computation.7 | async-start | bytes 1179648 | tf_op jit(solution)/shard_map/all_gather | solution.py:119
  96.8 1021.2 %all-gather.14.cloned.1.call-start = ((), (), s32[]{:S(2)}) async-start(), calls=%async_computation.9 | async-start | bytes 53747712 | tf_op jit(solution)/shard_map/all_gather | solution.py:180
  138.2 1176.1 %reduce-scatter.8.cloned.1.call-start = ((), (), s32[]{:S(2)}) async-start(), calls=%async_computation.10 | async-start | bytes 2359296 | tf_op jit(solution)/shard_map/reduce_scatter | solution.py:252
  141.4 6.2 copy-start.3
  143.5 4.1 copy-start.41
  147.9 65.6 %copy-start.39 = (s32[1,2048]{1,0:T(1,128)S(1)}, s32[1,2048]{1,0:T(1,128)}, u32[]{:S(2)}) copy-start(s32[1,2048]{1,0:T(1,128)} %param.23) | copy-start | bytes 24580
  232.7 3.2 copy-start.16
  232.8 2.8 copy-start.9
  1144.0 10.4 copy-start.18
  1144.0 10.4 copy-start.38
  1174.2 10.4 copy-start.2
  1174.3 10.4 copy-start.19
  1197.4 3.0 copy-start.13
  1227.7 358.7 %reduce-scatter.14.cloned.1.call-start = ((), (), s32[]{:S(2)}) async-start(), calls=%async_computation.13 | async-start | bytes 17915904 | tf_op jit(solution)/shard_map/reduce_scatter | solution.py:208
  1239.6 619.1 %reduce-scatter.12.cloned.1.call-start = ((), (), s32[]{:S(2)}) async-start(), calls=%async_computation.12 | async-start | bytes 17915904 | tf_op jit(solution)/shard_map/reduce_scatter | solution.py:205
  1250.6 880.4 %reduce-scatter.10.cloned.1.call-start = ((), (), s32[]{:S(2)}) async-start(), calls=%async_computation.11 | async-start | bytes 17915904 | tf_op jit(solution)/shard_map/reduce_scatter | solution.py:202
  1253.0 2.8 copy-start.4
  1279.0 1080.8 %all-reduce.5.cloned.1.call-start = ((), (), s32[]{:S(2)}) async-start(), calls=%async_computation.15 | async-start | bytes 23592960
  1280.8 34.6 %copy-start.49 = (f32[1,256]{1,0:T(1,128)S(1)}, f32[1,256]{1,0:T(1,128)}, u32[]{:S(2)}) copy-start(f32[1,256]{1,0:T(1,128)} %convert_element_type.142) | copy-start | bytes 3076
  1280.8 34.6 %copy-start.51 = (f32[128]{0:T(128)S(1)}, f32[128]{0:T(128)}, u32[]{:S(2)}) copy-start(f32[128]{0:T(128)} %multiply_exponential_fusion) | copy-start | bytes 1540
  1280.8 35.2 %copy-start.45 = (f32[256]{0:T(256)S(1)}, f32[256]{0:T(256)}, u32[]{:S(2)}) copy-start(f32[256]{0:T(256)} %copy-done.44) | copy-start | bytes 3076
  1280.8 35.2 %copy-start.47 = (f32[256]{0:T(256)S(1)}, f32[256]{0:T(256)}, u32[]{:S(2)}) copy-start(f32[256]{0:T(256)} %get-tuple-element.1044) | copy-start | bytes 3076
  1283.6 32.8 %copy-start.10 = (bf16[1,256,1152]{2,1,0:T(8,128)(2,1)S(1)}, bf16[1,256,1152]{2,1,0:T(8,128)(2,1)}, u32[]{:S(2)}) copy-start(bf16[1,256,1152]{2,1,0:T(8,128)(2,1)} %param.21) | copy-start | bytes 1769476
  1283.6 32.8 %copy-start.24 = (bf16[256,1024]{1,0:T(8,128)(2,1)S(1)}, bf16[256,1024]{1,0:T(8,128)(2,1)}, u32[]{:S(2)}) copy-start(bf16[256,1024]{1,0:T(8,128)(2,1)} %get-tuple-element.1026) | copy-start | bytes 1572868
  1283.6 32.8 %copy-start.36 = (f32[1152]{0:T(1024)S(1)}, f32[1152]{0:T(1024)}, u32[]{:S(2)}) copy-start(f32[1152]{0:T(1024)} %copy-done.35) | copy-start | bytes 13828
  1283.6 32.8 %copy-start.43 = (f32[256]{0:T(256)S(1)}, f32[256]{0:T(256)}, u32[]{:S(2)}) copy-start(f32[256]{0:T(256)} %add_rsqrt_fusion.5) | copy-start | bytes 3076
  1316.4 4.2 copy-start.32
  1316.4 4.2 copy-start.33
  1339.5 1079.5 %reduce-scatter.16.cloned.1.call-start = ((), (), s32[]{:S(2)}) async-start(), calls=%async_computation.14 | async-start | bytes 7741440
  2147.5 3.8 copy-start.40
  2147.5 44.5 %copy-start.53 = (f32[160]{0:T(256)S(1)}, f32[160]{0:T(256)}, u32[]{:S(2)}) copy-start(f32[160]{0:T(256)} %param.31) | copy-start | bytes 1924
  2147.5 44.5 %copy-start.54 = (f32[160]{0:T(256)S(1)}, f32[160]{0:T(256)}, u32[]{:S(2)}) copy-start(f32[160]{0:T(256)} %param.33) | copy-start | bytes 1924
  2147.5 44.5 %copy-start.55 = (f32[160]{0:T(256)S(1)}, f32[160]{0:T(256)}, u32[]{:S(2)}) copy-start(f32[160]{0:T(256)} %param.32) | copy-start | bytes 1924
  2147.5 45.2 %copy-start.7 = (f32[256,1152]{1,0:T(8,128)S(1)}, f32[256,1152]{1,0:T(8,128)}, u32[]{:S(2)}) copy-start(f32[256,1152]{1,0:T(8,128)} %copy-done.6) | copy-start | bytes 3538948
  2151.2 208.7 %copy-start.28 = (f32[92160]{0:T(1024)S(1)}, f32[92160]{0:T(1024)}, u32[]{:S(2)}) copy-start(f32[92160]{0:T(1024)} %param.25) | copy-start | bytes 1105924
  2362.3 60.3 %copy-start.5 = (f32[864,864]{1,0:T(8,128)S(1)}, f32[864,864]{1,0:T(8,128)}, u32[]{:S(2)}) copy-start(f32[864,864]{1,0:T(8,128)} %param.28) | copy-start | bytes 8957956
  (22 other events, 30.0 us)
Sparse Core Ops, SparseCore 0:
  11.6 70.4 all-gather.5
  84.2 44.8 all-gather.11
  131.7 40.1 all-gather.7
  174.5 38.8 all-gather.9
  214.8 903.1 all-gather.13
  1227.9 86.3 reduce-scatter.7
  1318.2 268.1 reduce-scatter.13
  1590.3 268.2 reduce-scatter.11
  1862.5 268.4 reduce-scatter.9
  2137.2 222.6 all-reduce.4
  2362.5 56.5 reduce-scatter.15
where the time goes:
time: 2440 us
  waiting for transfers between devices  2050 us (84%)
  matrix products  135 us (6%)
  local copies, waits for them, and re-layouts  91.3 us (4%)
  blocking collectives  82.9 us (3%)
  other arithmetic  48 us (2%)
    all_gather x1, waiting for transfers between devices, shards(): weight_rows = lax.all_gather(mlp_local, 'ctx', axis=0, tiled=True)  881 us
    reduce_scatter x1, waiting for transfers between devices, shards(): lax.psum_scatter(grad_gate.astype(jnp.bfloat16), 'ctx', scatter_dimension...  272 us
    reduce_scatter x1, waiting for transfers between devices, shards(): lax.psum_scatter(grad_up.astype(jnp.bfloat16), 'ctx', scatter_dimension=0...  272 us
    reduce_scatter x1, waiting for transfers between devices, shards(): lax.psum_scatter(grad_down.astype(jnp.bfloat16), 'ctx', scatter_dimension...  247 us
    unnamed x13, waiting for transfers between devices  223 us
    dot_general x18, matrix products, contract(): lax.dot_general(left, right, (((left_dim,), (right_dim,)), ((), ())), pre...  124 us
    unnamed x2, blocking collectives  82.9 us
  transfers between devices with their start and end apart: 11, of which 11 were waited for; matrix products, arithmetic and copies ran while one was open for 6% of the time, Pallas kernels for 0%

commit v1 on v0

v1 whole, which is shorter than its diff:
```python
import jax
import jax.numpy as jnp
import numpy as np
from jax import lax
from jax.experimental import pallas as pl
from jax.experimental.pallas import tpu as pltpu
from jax.sharding import Mesh, PartitionSpec as P

D = 1152
H = 4
HD = 256
STEP = 5

NORM_EPS = 1e-06
SCORE_FLOOR = -1e30
ROPE_BASE = 1000000.0
BETA_MOMENT = 0.5
ADAM_EPS = 1e-08
RATE_MATRIX = 0.03
RATE_GAIN = 0.5
DECAY_MATRIX = 0.1

bf16 = jnp.bfloat16
f32 = jnp.float32
LANES = 128


def normed(value):
    factor = lax.rsqrt(jnp.mean(value * value, axis=-1, keepdims=True) + NORM_EPS)
    return (value * factor, factor)


def norm_back(unit, factor, d_unit):
    return factor * (d_unit - unit * jnp.mean(d_unit * unit, axis=-1, keepdims=True))


def angles(position):
    half_index = jnp.arange(HD // 2, dtype=f32)
    frequency = jnp.exp(half_index * (-2.0 * jnp.log(ROPE_BASE) / HD))
    angle = position.astype(f32)[:, None] * frequency[None, :]
    return (jnp.cos(angle), jnp.sin(angle))


def rotate(value, cosine, sine):
    half_width = value.shape[-1] // 2
    first_half = value[..., :half_width]
    second_half = value[..., half_width:]
    return jnp.concatenate(
        [first_half * cosine - second_half * sine, second_half * cosine + first_half * sine],
        axis=-1,
    )


def contract(left, right, left_dim, right_dim):
    return lax.dot_general(
        left, right, (((left_dim,), (right_dim,)), ((), ())), preferred_element_type=f32
    )


def adam_update(weight, moment_one, second, gradient, learn_rate, decay_rate):
    moment_new = BETA_MOMENT * moment_one + (1.0 - BETA_MOMENT) * gradient
    second_new = BETA_MOMENT * second + (1.0 - BETA_MOMENT) * gradient * gradient
    correction = 1.0 - BETA_MOMENT**STEP
    update = moment_new / correction / (jnp.sqrt(second_new / correction) + ADAM_EPS)
    return (moment_new, second_new, weight - learn_rate * (update + decay_rate * weight))


def add_low(*parts):
    total = parts[0].astype(f32)
    for part in parts[1:]:
        total = total + part.astype(f32)
    return total.astype(bf16)


def after(value, *earlier):
    return lax.optimization_barrier((value,) + earlier)[0]


def halfway(rows):
    return rows // 32 * 16 if rows >= 32 else rows // 2


VMEM_LIMIT = 56 * 1024 * 1024


def spread_rows(parts, order, lines, q_rows, q_width, o_rows, o_width):
    count = sum(part.shape[0] for part in parts)
    padded = parts[0].shape[1]
    gain_at = -(-lines // 16) * 16
    q_across, o_across = q_width // LANES, o_width // LANES
    total = count * lines

    def body(order_ref, *refs):
        sources = refs[: len(parts)]
        q_ref, o_ref, gain_ref, held, flat, sems = refs[len(parts) :]
        copies = []
        for part, source in zip(parts, sources):
            for i in range(part.shape[0]):
                k = len(copies)
                copies.append(
                    pltpu.make_async_copy(source.at[i], held.at[order_ref[k]], sems.at[k])
                )
        for copy in copies:
            copy.start()
        for copy in copies:
            copy.wait()
        for i in range(count):
            flat[i * lines : (i + 1) * lines, :] = held[i, :gain_at, :].astype(f32)[:lines]
            gain_ref[i] = held[i, gain_at:, :].astype(f32)
        for j in range(q_across):
            q_ref[:, j * LANES : (j + 1) * LANES] = flat[
                pl.ds(j, q_rows, stride=q_across), :
            ].astype(bf16)
        for j in range(o_across):
            o_ref[:, j * LANES : (j + 1) * LANES] = flat[
                pl.ds(q_rows * q_across + j, o_rows, stride=o_across), :
            ].astype(bf16)

    return pl.pallas_call(
        body,
        out_shape=(
            jax.ShapeDtypeStruct((q_rows, q_width), bf16),
            jax.ShapeDtypeStruct((o_rows, o_width), bf16),
            jax.ShapeDtypeStruct((count, padded - gain_at, LANES), f32),
        ),
        in_specs=[pl.BlockSpec(memory_space=pltpu.SMEM)]
        + [pl.BlockSpec(memory_space=pl.ANY)] * len(parts),
        out_specs=[pl.BlockSpec(memory_space=pltpu.VMEM)] * 3,
        scratch_shapes=[
            pltpu.VMEM((count, padded, LANES), bf16),
            pltpu.VMEM((total, LANES), f32),
            pltpu.SemaphoreType.DMA((count,)),
        ],
        compiler_params=pltpu.CompilerParams(vmem_limit_bytes=VMEM_LIMIT),
        cost_estimate=pl.CostEstimate(flops=0, bytes_accessed=24 * total * LANES, transcendentals=0),
        name="spread_rows",
    )(order, *parts)


def pack_rows(d_wqkv, d_wout, gain_lines, place, lines):
    count, gain_rows, _ = gain_lines.shape
    q_rows, q_width = d_wqkv.shape
    o_rows, o_width = d_wout.shape
    gain_at = -(-lines // 16) * 16
    q_across, o_across = q_width // LANES, o_width // LANES
    total = count * lines

    def body(place_ref, q_ref, o_ref, gain_ref, out_ref, flat):
        flat[total:, :] = jnp.zeros((flat.shape[0] - total, LANES), f32)
        for j in range(q_across):
            flat[pl.ds(j, q_rows, stride=q_across), :] = q_ref[:, j * LANES : (j + 1) * LANES]
        for j in range(o_across):
            flat[pl.ds(q_rows * q_across + j, o_rows, stride=o_across), :] = o_ref[
                :, j * LANES : (j + 1) * LANES
            ]
        for i in range(count):
            out_ref[place_ref[i], :gain_at, :] = flat[i * lines : i * lines + gain_at, :].astype(bf16)
            out_ref[place_ref[i], gain_at:, :] = gain_ref[i].astype(bf16)

    return pl.pallas_call(
        body,
        out_shape=jax.ShapeDtypeStruct((count, gain_at + gain_rows, LANES), bf16),
        in_specs=[pl.BlockSpec(memory_space=pltpu.SMEM)]
        + [pl.BlockSpec(memory_space=pltpu.VMEM)] * 3,
        out_specs=pl.BlockSpec(memory_space=pltpu.VMEM),
        scratch_shapes=[pltpu.VMEM((total + 16, LANES), f32)],
        compiler_params=pltpu.CompilerParams(vmem_limit_bytes=VMEM_LIMIT),
        cost_estimate=pl.CostEstimate(flops=0, bytes_accessed=24 * total * LANES, transcendentals=0),
        name="pack_rows",
    )(place, d_wqkv, d_wout, gain_lines)


DEAD, WHOLE, MASKED = 0, 1, 2


def allowed_of(kdoc_ref, qdoc_ref, shift):
    keys, queries = kdoc_ref.shape[0], qdoc_ref.shape[1]
    key_at = lax.broadcasted_iota(jnp.int32, (keys, queries), 0) + shift
    query_at = lax.broadcasted_iota(jnp.int32, (keys, queries), 1)
    return (kdoc_ref[...] == qdoc_ref[...]) & (key_at <= query_at)


def attend(info, query, kv, key_docs, query_docs):
    blocks, rows, _ = kv.shape

    def body(info_ref, q_ref, kv_ref, kdoc_ref, qdoc_ref, o_ref, lse_ref, peak, total, acc):
        step = pl.program_id(0)

        @pl.when(step == 0)
        def _():
            peak[...] = jnp.full_like(peak, SCORE_FLOOR)
            total[...] = jnp.zeros_like(total)
            acc[...] = jnp.zeros_like(acc)

        def visit(masked):
            key = kv_ref[0, :, :HD]
            value_t = kv_ref[0, :, HD:].T
            if masked:
                allowed = allowed_of(
                    kdoc_ref, qdoc_ref, (info_ref[0, step] - info_ref[0, 0]) * rows
                )
            for h in range(H):
                score = contract(key, q_ref[:, h * HD : (h + 1) * HD], 1, 1)
                if masked:
                    score = jnp.where(allowed, score, SCORE_FLOOR)
                old = peak[h : h + 1, :]
                new = jnp.maximum(old, jnp.max(score, axis=0, keepdims=True))
                weight = jnp.exp(score - new)
                shrink = jnp.exp(old - new)
                peak[h : h + 1, :] = new
                total[h : h + 1, :] = total[h : h + 1, :] * shrink + jnp.sum(
                    weight, axis=0, keepdims=True
                )
                acc[h] = acc[h] * shrink + contract(value_t, weight.astype(bf16), 1, 0)

        pl.when(info_ref[1, step] == WHOLE)(lambda: visit(False))
        pl.when(info_ref[1, step] == MASKED)(lambda: visit(True))

        @pl.when(step == blocks - 1)
        def _():
            lse_ref[...] = jnp.zeros_like(lse_ref)
            for h in range(H):
                lse_ref[h : h + 1, :] = peak[h : h + 1, :] + jnp.log(total[h : h + 1, :])
                o_ref[:, h * HD : (h + 1) * HD] = (acc[h] / total[h : h + 1, :]).T.astype(bf16)

    return pl.pallas_call(
        body,
        grid_spec=pltpu.PrefetchScalarGridSpec(
            num_scalar_prefetch=1,
            grid=(blocks,),
            in_specs=[
                pl.BlockSpec((rows, H * HD), lambda i, info: (0, 0)),
                pl.BlockSpec((1, rows, 2 * HD), lambda i, info: (i, 0, 0)),
                pl.BlockSpec((rows, 1), lambda i, info: (info[0, i], 0)),
                pl.BlockSpec((1, rows), lambda i, info: (0, 0)),
            ],
            out_specs=[
                pl.BlockSpec((rows, H * HD), lambda i, info: (0, 0)),
                pl.BlockSpec((8, rows), lambda i, info: (0, 0)),
            ],
            scratch_shapes=[
                pltpu.VMEM((8, rows), f32),
                pltpu.VMEM((8, rows), f32),
                pltpu.VMEM((H, HD, rows), f32),
            ],
        ),
        out_shape=(
            jax.ShapeDtypeStruct((rows, H * HD), bf16),
            jax.ShapeDtypeStruct((8, rows), f32),
        ),
        compiler_params=pltpu.CompilerParams(vmem_limit_bytes=VMEM_LIMIT),
        cost_estimate=pl.CostEstimate(
            flops=4 * blocks * rows * rows * H * HD,
            bytes_accessed=2 * kv.size,
            transcendentals=blocks * rows * rows * H,
        ),
        name="attend",
    )(info, query, kv, key_docs, query_docs)


def attend_back(info, query, kv, key_docs, query_docs, d_heads, log_total, delta):
    blocks, rows, _ = kv.shape

    def body(
        info_ref, q_ref, kv_ref, kdoc_ref, qdoc_ref, do_ref, lse_ref, delta_ref, dq_ref, dkv_ref
    ):
        step = pl.program_id(0)

        @pl.when(step == 0)
        def _():
            dq_ref[...] = jnp.zeros_like(dq_ref)

        def visit(masked):
            key, value = kv_ref[0, :, :HD], kv_ref[0, :, HD:]
            if masked:
                allowed = allowed_of(
                    kdoc_ref, qdoc_ref, (info_ref[0, step] - info_ref[0, 0]) * rows
                )
            d_key = jnp.zeros((rows, HD), f32)
            d_value = jnp.zeros((rows, HD), f32)
            for h in range(H):
                cols = slice(h * HD, (h + 1) * HD)
                q, d_o = q_ref[:, cols], do_ref[:, cols]
                prob = jnp.exp(contract(key, q, 1, 1) - lse_ref[h : h + 1, :])
                if masked:
                    prob = jnp.where(allowed, prob, 0.0)
                d_value = d_value + contract(prob.astype(bf16), d_o, 1, 0)
                d_prob = contract(value, d_o, 1, 1)
                d_score = (prob * (d_prob - delta_ref[h : h + 1, :])).astype(bf16)
                d_key = d_key + contract(d_score, q, 1, 0)
                dq_ref[:, cols] = dq_ref[:, cols] + contract(d_score, key, 0, 0)
            dkv_ref[0, :, :HD] = d_key.astype(bf16)
            dkv_ref[0, :, HD:] = d_value.astype(bf16)

        pl.when(info_ref[1, step] == WHOLE)(lambda: visit(False))
        pl.when(info_ref[1, step] == MASKED)(lambda: visit(True))

        @pl.when(info_ref[1, step] == DEAD)
        def _():
            dkv_ref[...] = jnp.zeros_like(dkv_ref)

        @pl.when(step == blocks - 1)
        def _():
            dq_ref[...] = dq_ref[...] * HD ** (-0.5)

    whole = pl.BlockSpec((rows, H * HD), lambda i, info: (0, 0))
    stats = pl.BlockSpec((8, rows), lambda i, info: (0, 0))
    block = pl.BlockSpec((1, rows, 2 * HD), lambda i, info: (i, 0, 0))
    return pl.pallas_call(
        body,
        grid_spec=pltpu.PrefetchScalarGridSpec(
            num_scalar_prefetch=1,
            grid=(blocks,),
            in_specs=[
                whole,
                block,
                pl.BlockSpec((rows, 1), lambda i, info: (info[0, i], 0)),
                pl.BlockSpec((1, rows), lambda i, info: (0, 0)),
                whole,
                stats,
                stats,
            ],
            out_specs=[whole, block],
        ),
        out_shape=(
            jax.ShapeDtypeStruct((rows, H * HD), f32),
            jax.ShapeDtypeStruct(kv.shape, bf16),
        ),
        compiler_params=pltpu.CompilerParams(vmem_limit_bytes=VMEM_LIMIT),
        cost_estimate=pl.CostEstimate(
            flops=10 * blocks * rows * rows * H * HD,
            bytes_accessed=4 * kv.size,
            transcendentals=blocks * rows * rows * H,
        ),
        name="attend_back",
    )(info, query, kv, key_docs, query_docs, d_heads, log_total, delta)


class Ways:
    def __init__(self, sizes):
        self.sizes = sizes

    def size(self, axis):
        if isinstance(axis, str):
            return self.sizes[axis]
        n = 1
        for a in axis:
            n *= self.sizes[a]
        return n

    def fro(self, value, axis, offset):
        n = self.size(axis)
        if offset % n == 0:
            return value
        return lax.ppermute(value, axis, [((i + offset) % n, i) for i in range(n)])

    def places(self):
        nx, ny = self.sizes["x"], self.sizes["y"]
        return [(ox, oy) for ox in range(nx) for oy in range(ny)]

    def outers(self):
        return [(ou, ov) for ou in range(self.sizes["u"]) for ov in range(self.sizes["v"])]

    def plane_gather(self, value):
        nx, ny = self.sizes["x"], self.sizes["y"]
        half = halfway(value.shape[0])
        found = {(0, 0): value}
        for ox in range(1, nx):
            found[ox, 0] = self.fro(value, "x", ox)
        for oy in range(1, ny):
            found[0, oy] = self.fro(value, "y", oy)
        for ox in range(1, nx):
            for oy in range(1, ny):
                first = self.fro(found[ox, 0][:half], "y", oy)
                second = self.fro(found[0, oy][half:], "x", ox)
                found[ox, oy] = jnp.concatenate([first, second], axis=0)
        return {at: [block, self.fro(block, "c", 1)] for at, block in found.items()}

    def plane_scatter(self, parts):
        nx, ny = self.sizes["x"], self.sizes["y"]
        low = {
            at: add_low(parts[at][0], self.fro(parts[at][1], "c", 1))
            for at in sorted(parts, reverse=True)
        }
        half = halfway(low[0, 0].shape[0])
        along_x = {ox: [low[ox, 0][:half]] for ox in range(1, nx)}
        along_y = {oy: [low[0, oy][half:]] for oy in range(1, ny)}
        for ox in range(1, nx):
            for oy in range(1, ny):
                along_x[ox].append(self.fro(low[ox, oy][:half], "y", -oy))
                along_y[oy].append(self.fro(low[ox, oy][half:], "x", -ox))
        total = low[0, 0].astype(f32)
        for ox in range(1, nx):
            whole = jnp.concatenate([add_low(*along_x[ox]), low[ox, 0][half:]], axis=0)
            total = total + self.fro(whole, "x", -ox).astype(f32)
        for oy in range(1, ny):
            whole = jnp.concatenate([low[0, oy][:half], add_low(*along_y[oy])], axis=0)
            total = total + self.fro(whole, "y", -oy).astype(f32)
        return total

    def z_gather(self, value, cut=None, later=()):
        n = self.sizes["z"]
        if n != 4:
            return [self.fro(value, "z", oz) for oz in range(n)]
        above, below = self.fro(value, "z", 1), self.fro(value, "z", -1)
        if cut is None:
            half = halfway(value.shape[0])
            near = above[:half], below[half:]
        else:
            near = above[:, :cut], below[:, cut:]
        if later:
            near = lax.optimization_barrier(near + tuple(later))[:2]
        first, second = self.fro(near[0], "z", 1), self.fro(near[1], "z", -1)
        return [value, above, jnp.concatenate([first, second], axis=0 if cut is None else 1), below]

    def z_scatter_begin(self, parts):
        if self.sizes["z"] != 4:
            return ()
        half = halfway(parts[0].shape[0])
        return self.fro(parts[2][:half], "z", -1), self.fro(parts[2][half:], "z", 1)

    def z_scatter_go(self, parts, begun):
        n = self.sizes["z"]
        if n != 4:
            return [self.fro(parts[oz], "z", -oz) for oz in range(1, n)]
        half = halfway(parts[0].shape[0])
        above = jnp.concatenate([add_low(parts[1][:half], begun[0]), parts[1][half:]], axis=0)
        below = jnp.concatenate([parts[3][:half], add_low(parts[3][half:], begun[1])], axis=0)
        return [self.fro(above, "z", -1), self.fro(below, "z", 1)]

    def z_scatter(self, parts):
        total = parts[0].astype(f32)
        for heard in self.z_scatter_go(parts, self.z_scatter_begin(parts)):
            total = total + heard.astype(f32)
        return total


def gelu_parts(gate):
    scale = 0.7978845608028654
    square = gate * gate
    inner = jnp.tanh(scale * gate * (1.0 + 0.044715 * square))
    half_up = 0.5 * (1.0 + inner)
    slope = half_up + 0.5 * gate * (1.0 - inner * inner) * scale * (1.0 + 3 * 0.044715 * square)
    return gate * half_up, slope


SEQ = ("u", "y", "c")
CTX = ("z", "v", "x")
ACROSS = ("v", "x")


def make_shards(sizes):
    ways = Ways(sizes)
    ns, nctx, nx = ways.size(SEQ), ways.size(CTX), ways.size(ACROSS)
    nz = sizes["z"]
    devices = ns * nctx
    places, outers = ways.places(), ways.outers()

    def shards(
        tokens, cotangent, segments, positions, attn_w, attn_m, attn_v,
        mlp_w, mlp_m, mlp_v, gains, gain_m, gain_v,
    ):
        at = {a: lax.axis_index(a) for a in sizes}
        seq_place = lax.axis_index(SEQ)
        across_place = lax.axis_index(ACROSS)
        ctx_place = at["z"] * nx + across_place
        piece, gain_piece = attn_w.shape[0], gains.shape[0]
        lines = piece // LANES
        gain_at = -(-lines // 16) * 16
        gain_rows = -(-gain_piece // (16 * LANES)) * 16
        qkv_width = (H + 2) * HD

        sides = [sizes[a] for a in ("x", "y", "c", "u", "v", "z")]
        here = [at[a] for a in ("x", "y", "c", "u", "v", "z")]
        ox, oy, oc, ou, ov, oz = (
            (jnp.asarray(o, jnp.int32) + h) % n
            for o, h, n in zip(np.unravel_index(np.arange(devices), sides), here, sides)
        )
        order = ((ou * sizes["y"] + oy) * sizes["c"] + oc) * nz + oz
        order = (order * sizes["v"] + ov) * sizes["x"] + ox
        by_axis = dict(zip(SEQ + CTX, np.unravel_index(np.arange(devices), [sizes[a] for a in SEQ + CTX])))
        place_of = jnp.zeros((devices,), jnp.int32)
        for a, h, n in zip(("x", "y", "c", "u", "v", "z"), here, sides):
            place_of = place_of * n + (jnp.asarray(by_axis[a], jnp.int32) + (n - h)) % n

        def gain_lines_of(value):
            value = value.reshape(-1, gain_piece)
            value = jnp.pad(value, ((0, 0), (0, gain_rows * LANES - gain_piece)))
            return value.reshape(-1, gain_rows, LANES)

        low_piece = jnp.concatenate(
            [
                jnp.pad(attn_w.reshape(lines, LANES), ((0, gain_at - lines), (0, 0))),
                gain_lines_of(gains)[0],
            ],
            axis=0,
        ).astype(bf16)
        line_z = jnp.concatenate(ways.z_gather(low_piece), axis=0)
        line_z = jnp.concatenate(
            [ways.fro(ways.fro(line_z, "u", ou), "v", ov) for ou, ov in outers], axis=0
        )
        gathered = ways.plane_gather(line_z)
        line_parts = [part for p in places for part in gathered[p]]
        w_qkv, w_out, gain_lines = spread_rows(
            [part.reshape(-1, gain_at + gain_rows, LANES) for part in line_parts],
            order, lines, D, qkv_width, H * HD, D,
        )
        gain_all = gain_lines.reshape(devices, -1)[:, :gain_piece].reshape(-1)
        gain_pre = gain_all[:D]
        gain_q = gain_all[D : D + HD]
        gain_k = gain_all[D + HD : D + 2 * HD]
        gain_post = gain_all[D + 2 * HD : 2 * D + 2 * HD]
        gain_fpre = gain_all[2 * D + 2 * HD : 3 * D + 2 * HD]
        gain_fpost = gain_all[3 * D + 2 * HD :]

        units, width = mlp_w.shape
        share = units // ns
        held = -(-share // 32) * 32

        def seq_exchange(by_place):
            kept = jnp.zeros_like(by_place)
            for offset in range(ns):
                sent = lax.dynamic_index_in_dim(by_place, (seq_place - offset) % ns, 0, keepdims=False)
                heard = ways.fro(sent, SEQ, offset)
                kept = lax.dynamic_update_index_in_dim(kept, heard, (seq_place + offset) % ns, 0)
            return kept

        by_cols = seq_exchange(mlp_w.astype(bf16).reshape(ns, share, width))
        rows_own = jnp.concatenate([by_cols[i] for i in range(ns)], axis=1)
        rows_own = jnp.pad(rows_own, ((0, held - share), (0, 0)))

        tok_rows = tokens.shape[1]
        hidden_in = tokens[0].astype(f32)
        unit_in, scale_in = normed(hidden_in)
        normed_in = (unit_in * gain_pre).astype(bf16)
        qkv = jnp.dot(normed_in, w_qkv, preferred_element_type=f32)
        head_cols = [slice(h * HD, (h + 1) * HD) for h in range(H)]
        normed_q = [normed(qkv[:, cols]) for cols in head_cols]
        unit_k, scale_k = normed(qkv[:, H * HD : (H + 1) * HD])
        cosine, sine = angles(positions[0])
        query = jnp.concatenate(
            [rotate(unit * gain_q, cosine, sine).astype(bf16) for unit, _ in normed_q], axis=1
        ) * jnp.asarray(HD ** (-0.5), bf16)
        key_local = rotate(unit_k * gain_k, cosine, sine).astype(bf16)
        value_local = qkv[:, (H + 1) * HD :].astype(bf16)
        kv_local = jnp.concatenate([key_local, value_local], axis=1)
        kv_all = jnp.stack(
            [ways.fro(block, ACROSS, oa) for block in ways.z_gather(kv_local) for oa in range(nx)]
        )

        def all_units(blocks):
            whole = jnp.concatenate(blocks, axis=0)
            return jnp.concatenate(
                [ways.fro(ways.fro(whole, "u", ou), "v", ov) for ou, ov in outers], axis=0
            )

        gate_up = ways.z_gather(rows_own[:, : 2 * D], cut=D, later=(kv_all,))
        w_gate = all_units([block[:, :D] for block in gate_up])
        w_up = all_units([block[:, D:] for block in gate_up])

        doc_all = segments[0]
        first_docs, last_docs = doc_all[::tok_rows], doc_all[tok_rows - 1 :: tok_rows]
        key_at = np.arange(nctx)
        key_place = (at["z"] + jnp.asarray(key_at // nx, jnp.int32)) % nz * nx
        key_place = key_place + (across_place + jnp.asarray(key_at % nx, jnp.int32)) % nx
        is_place = key_place[:, None] == jnp.arange(nctx, dtype=jnp.int32)[None, :]
        key_first = jnp.sum(jnp.where(is_place, first_docs[None, :], 0), axis=1)
        key_last = jnp.sum(jnp.where(is_place, last_docs[None, :], 0), axis=1)
        live = (key_place < ctx_place) & (key_last >= key_first[0])
        same = key_first == key_last[0]
        task = jnp.where(live, jnp.where(same, WHOLE, MASKED), DEAD)
        task = jnp.where(key_place == ctx_place, MASKED, task)
        info = jnp.stack([key_place, task]).astype(jnp.int32)
        key_docs = doc_all[:, None]
        query_docs = lax.dynamic_slice_in_dim(doc_all, ctx_place * tok_rows, tok_rows)[None]

        heads_flat, log_total = attend(info, query, kv_all, key_docs, query_docs)
        w_down = all_units(ways.z_gather(after(rows_own[:, 2 * D :], heads_flat)))
        attn_out = jnp.dot(heads_flat, w_out, preferred_element_type=f32)
        unit_post, scale_post = normed(attn_out)
        middle = hidden_in + unit_post * gain_post
        unit_mid, scale_mid = normed(middle)
        ffn_in = (unit_mid * gain_fpre).astype(bf16)

        ffn_rows = {p: jnp.concatenate(b, axis=0) for p, b in ways.plane_gather(ffn_in).items()}
        act_low, gelu_low, slope_low, partial = {}, {}, {}, {}
        for p in places:
            gate = contract(ffn_rows[p], w_gate, 1, 1)
            up_part = contract(ffn_rows[p], w_up, 1, 1)
            gelu, slope = gelu_parts(gate)
            act_low[p] = (gelu * up_part).astype(bf16)
            gelu_low[p] = gelu.astype(bf16)
            slope_low[p] = (slope * up_part).astype(bf16)
            low = contract(act_low[p], w_down, 1, 0).astype(bf16)
            partial[p] = [low[:tok_rows], low[tok_rows:]]
        out_rows = ways.plane_scatter(partial)
        unit_out, scale_out = normed(out_rows)
        mixed = (middle + unit_out * gain_fpost).astype(bf16)[None]

        upstream = cotangent[0].astype(f32)
        d_gfpost = jnp.sum(upstream * unit_out, axis=0)
        d_mlp_out = norm_back(unit_out, scale_out, upstream * gain_fpost).astype(bf16)
        d_out_rows = {p: jnp.concatenate(b, axis=0) for p, b in ways.plane_gather(d_mlp_out).items()}
        d_gate_low, d_up_low, partial = {}, {}, {}
        for p in places:
            d_act = contract(d_out_rows[p], w_down, 1, 1)
            d_gate_low[p] = (d_act * slope_low[p].astype(f32)).astype(bf16)
            d_up_low[p] = (d_act * gelu_low[p].astype(f32)).astype(bf16)
            low = (
                contract(d_gate_low[p], w_gate, 1, 0) + contract(d_up_low[p], w_up, 1, 0)
            ).astype(bf16)
            partial[p] = [low[:tok_rows], low[tok_rows:]]
        d_rows_in = ways.plane_scatter(partial)

        def together(by_place):
            return jnp.concatenate([by_place[p] for p in places], axis=0)

        ffn_all = after(together(ffn_rows), *[partial[p][0] for p in places])
        grads = [
            contract(together(act_low), after(together(d_out_rows), ffn_all), 0, 0).astype(bf16),
            contract(together(d_gate_low), ffn_all, 0, 0).astype(bf16),
            contract(together(d_up_low), ffn_all, 0, 0).astype(bf16),
        ]

        def own_plane(grad):
            per = nz * held
            total = add_low(
                *[
                    ways.fro(ways.fro(grad[i * per : (i + 1) * per], "u", -ou), "v", -ov)
                    for i, (ou, ov) in enumerate(outers)
                ]
            )
            return [total[oz * held : (oz + 1) * held] for oz in range(nz)]

        grad_parts = [own_plane(g) for g in grads]
        begun = [ways.z_scatter_begin(parts) for parts in grad_parts]

        d_gfpre = jnp.sum(d_rows_in * unit_mid, axis=0)
        d_middle = upstream + norm_back(unit_mid, scale_mid, d_rows_in * gain_fpre)
        d_gpost = jnp.sum(d_middle * unit_post, axis=0)
        d_attn_out = norm_back(unit_post, scale_post, d_middle * gain_post).astype(bf16)
        d_wout = contract(heads_flat, d_attn_out, 0, 0)
        d_heads = contract(d_attn_out, w_out, 1, 1).astype(bf16)
        going = []
        for parts, sent in zip(grad_parts, begun):
            sent = tuple(after(s, d_heads) for s in sent)
            going.append(ways.z_scatter_go(parts, sent))
        delta = jnp.stack(
            [
                jnp.sum(d_heads[:, cols].astype(f32) * heads_flat[:, cols].astype(f32), axis=1)
                for cols in head_cols
            ]
        )
        delta = jnp.pad(delta, ((0, 8 - H), (0, 0)))
        d_query, d_kv = attend_back(
            info, query, kv_all, key_docs, query_docs, d_heads, log_total, delta
        )
        d_kv = d_kv.reshape(nz, nx, tok_rows, 2 * HD)
        kv_parts = {}
        for oz in sorted(range(nz), key=lambda o: abs(o - nz // 2)):
            kv_parts[oz] = add_low(*[ways.fro(d_kv[oz, oa], ACROSS, -oa) for oa in range(nx)])
        kv_mine = ways.z_scatter([kv_parts[oz] for oz in range(nz)])

        d_gq = jnp.zeros((HD,), f32)
        d_raw = []
        for (unit, scale), cols in zip(normed_q, head_cols):
            rotated = rotate(d_query[:, cols], cosine, -sine)
            d_gq = d_gq + jnp.sum(rotated * unit, axis=0)
            d_raw.append(norm_back(unit, scale, rotated * gain_q).astype(bf16))
        rotated_k = rotate(kv_mine[:, :HD], cosine, -sine)
        d_gk = jnp.sum(rotated_k * unit_k, axis=0)
        d_raw.append(norm_back(unit_k, scale_k, rotated_k * gain_k).astype(bf16))
        d_raw.append(kv_mine[:, HD:].astype(bf16))
        d_qkv = jnp.concatenate(d_raw, axis=1)
        d_wqkv = contract(normed_in, d_qkv, 0, 0)
        d_normed_in = contract(d_qkv, w_qkv, 1, 1)
        d_gpre = jnp.sum(d_normed_in * unit_in, axis=0)
        input_grad = (d_middle + norm_back(unit_in, scale_in, d_normed_in * gain_pre)).astype(bf16)[None]

        gain_grad = jnp.concatenate([d_gpre, d_gq, d_gk, d_gpost, d_gfpre, d_gfpost])
        packed = pack_rows(d_wqkv, d_wout, gain_lines_of(gain_grad), place_of, lines)
        rows = gain_at + gain_rows
        packed = packed.reshape(len(places), sizes["c"], len(outers) * nz * rows, LANES)
        plane_sum = ways.plane_scatter(
            {p: [packed[i, oc] for oc in range(sizes["c"])] for i, p in enumerate(places)}
        ).astype(bf16)
        plane_sum = plane_sum.reshape(len(outers), nz * rows, LANES)
        plane_sum = add_low(
            *[
                ways.fro(ways.fro(plane_sum[i], "u", -ou), "v", -ov)
                for i, (ou, ov) in enumerate(outers)
            ]
        )
        red = ways.z_scatter([plane_sum[oz * rows : (oz + 1) * rows] for oz in range(nz)])
        attn_red = red[:lines].reshape(-1)
        gain_red = red[gain_at:].reshape(-1)[:gain_piece]

        owned = []
        for parts, heard in zip(grad_parts, going):
            total = after(parts[0], d_kv).astype(f32)
            for value in heard:
                total = total + value.astype(f32)
            owned.append(total.astype(bf16)[:share])
        own_rows = jnp.concatenate([owned[1], owned[2], owned[0]], axis=1)
        by_cols = jnp.stack([own_rows[:, i * width : (i + 1) * width] for i in range(ns)])
        mlp_red = seq_exchange(by_cols).astype(f32).reshape(units, width)

        attn_m_new, attn_v_new, attn_new = adam_update(
            attn_w, attn_m, attn_v, attn_red, RATE_MATRIX, DECAY_MATRIX
        )
        mlp_m_new, mlp_v_new, mlp_new = adam_update(
            mlp_w, mlp_m, mlp_v, mlp_red, RATE_MATRIX, DECAY_MATRIX
        )
        gain_m_new, gain_v_new, gain_new = adam_update(
            gains, gain_m, gain_v, gain_red, RATE_GAIN, 0.0
        )
        return (
            mixed, input_grad,
            attn_red, attn_m_new, attn_v_new, attn_new,
            mlp_red, mlp_m_new, mlp_v_new, mlp_new,
            gain_red, gain_m_new, gain_v_new, gain_new,
        )

    return shards


def solution(mesh):
    seq, ctx = mesh.shape["seq"], mesh.shape["ctx"]
    nz = 4 if ctx % 4 == 0 else 1
    chips_y, chips_x = seq // 2, ctx // nz
    y, x = 2 - chips_y % 2, 2 - chips_x % 2
    sizes = {"u": chips_y // y, "y": y, "c": 2, "z": nz, "v": chips_x // x, "x": x}
    fine = Mesh(mesh.devices.reshape(*sizes.values()), tuple(sizes))
    s, x = SEQ, CTX
    both = s + x
    in_specs = (
        P(s, x, None), P(s, x, None), P(s, None), P(s, x),
        P(both), P(both), P(both),
        P(x, s), P(x, s), P(x, s),
        P(both), P(both), P(both),
    )
    out_specs = (
        P(s, x, None), P(s, x, None),
        P(both), P(both), P(both), P(both),
        P(x, s), P(x, s), P(x, s), P(x, s),
        P(both), P(both), P(both), P(both),
    )
    return jax.shard_map(
        make_shards(sizes), mesh=fine, in_specs=in_specs, out_specs=out_specs, check_vma=False
    )
```

time: 2440 us -> 559 us (0.23)
  waiting for transfers between devices: 2050 us -> 231 us
  starting transfers between devices: 1.39 us -> 111 us
  blocking collectives: 82.9 us -> 0 us
  matrix products: 135 us -> 84 us
  local copies, waits for them, and re-layouts: 91.3 us -> 46.4 us
  Pallas kernels: 0 us -> 32.2 us
    all_gather x5 -> x0, waiting for transfers between devices: 1000 us -> none  [the longest x1 881 us: shards(): weight_rows = lax.all_gather(mlp_local, 'ctx', axis=0, tiled=True)]
    reduce_scatter x4 -> x0, waiting for transfers between devices: 822 us -> none  [the longest x1 272 us: shards(): lax.psum_scatter(grad_gate.astype(jnp.bfloat16), 'ctx', scatter_dimension...]
    ppermute x0 -> x98, waiting for transfers between devices: none -> 231 us  [fro(): return lax.ppermute(value, axis, [((i + offset) % n, i) for i in range(n)])]
    unnamed x13 -> x0, waiting for transfers between devices: 223 us -> none
    ppermute x0 -> x98, starting transfers between devices: none -> 111 us  [fro(): return lax.ppermute(value, axis, [((i + offset) % n, i) for i in range(n)])]
    unnamed x2 -> x0, blocking collectives: 82.9 us -> none
    dot_general x18 -> x31, matrix products: 124 us -> 78.8 us  [contract(): lax.dot_general(left, right, (((left_dim,), (right_dim,)), ((), ())), pre...]
    pallas_call x0 -> x4, Pallas kernels: none -> 32.2 us  [the longest x1 9.06 us: attend_back(): pl.pallas_call(body, grid_spec=pltpu.PrefetchScalarGridSpec(num_scalar_pr...]
  transfers between devices with their start and end apart: 11 -> 98, of which waited for: 11 -> 44; matrix products, arithmetic and copies ran while one was open for 6% -> 28% of each run, Pallas kernels for 0% -> 6%
where the time goes in v1:
time: 559 us; the launch traced here: 551 us
  waiting for transfers between devices  231 us (41%)
  starting transfers between devices  111 us (20%)
  matrix products  84 us (15%)
  local copies, waits for them, and re-layouts  46.4 us (8%)
  other arithmetic  42.4 us (8%)
  Pallas kernels  32.2 us (6%)
    ppermute x98, waiting for transfers between devices, fro(): return lax.ppermute(value, axis, [((i + offset) % n, i) for i in range(n)])  231 us
    ppermute x98, starting transfers between devices, fro(): return lax.ppermute(value, axis, [((i + offset) % n, i) for i in range(n)])  111 us
    dot_general x31, matrix products, contract(): lax.dot_general(left, right, (((left_dim,), (right_dim,)), ((), ())), pre...  78.8 us
    unnamed x309, local copies, waits for them, and re-layouts  19.1 us
  transfers between devices with their start and end apart: 98, of which 44 were waited for; matrix products, arithmetic and copies ran while one was open for 28% of the time, Pallas kernels for 6%

profile of v1, /device:TPU:0, one launch (start us, length us, event | category | flops | bytes accessed | tf_op | source)
XLA Modules:
  0.0 551.5 jit_solution(705860501135710472)
XLA Ops:
  3.1 5.1 collective-permute-start
  16.4 3.9 collective-permute-start.1
  24.0 3.3 collective-permute-done.3
  38.4 8.9 %collective-permute-done.7 = bf16[2944,128]{1,0:T(8,128)(2,1)S(1)} collective-permute-done((bf16[2944,128]{1,0:T(8,128)(2,1)}, bf16[2944,128]{1,0:T(8,128)(2,1)S(1)}, u32[]{:S(2)}, u32[]{:S(2)}) %collective-permute-start.7) | collective-permute-done | bytes 753696 | tf_op jit(solution)/shard_map/ppermute | solution.py:355
  58.1 5.4 collective-permute-done.10
  65.8 10.8 %collective-permute-done.25 = bf16[224,2304]{1,0:T(8,128)(2,1)} collective-permute-done((bf16[224,2304]{1,0:T(8,128)(2,1)}, bf16[224,2304]{1,0:T(8,128)(2,1)}, u32[]{:S(2)}, u32[]{:S(2)}) %collective-permute-start.25) | collective-permute-done | bytes 1032224 | tf_op jit(solution)/shard_map/ppermute | solution.py:355
  80.5 7.4 %spread_rows.1 = (bf16[1152,1536]{1,0:T(8,128)(2,1)}, bf16[1024,1152]{1,0:T(8,128)(2,1)}, f32[32,16,128]{2,1,0:T(8,128)}) custom-call(s32[32]{0:T(128)} %get-tuple-element.230.order_ref, bf16[4,736,128]{2,1,0:T(8,128)(2,1)} %bitcast.8.refs_0_, bf16[4,736,128]{2,1,0:T(8,128)(2,1)} %bitcast.232, bf16[4,736,128]{2,1,0:T(8,128)(2,1)} %bitcast.10.refs_2_, ...), custom_call_target="tpu_custom_call" | custom-call | bytes 70778880 | tf_op jit(solution)/shard_map/spread_rows/pallas_call | solution.py:119
  89.1 3.2 fusion.141
  103.8 8.5 %collective-permute-done.13 = bf16[256,512]{1,0:T(8,128)(2,1)S(1)} collective-permute-done((bf16[256,512]{1,0:T(8,128)(2,1)S(1)}, bf16[256,512]{1,0:T(8,128)(2,1)S(1)}, u32[]{:S(2)}, u32[]{:S(2)}) %collective-permute-start.13) | collective-permute-done | bytes 262176 | tf_op jit(solution)/shard_map/ppermute | solution.py:355
  116.5 3.0 collective-permute-done.15
  123.7 7.1 %collective-permute-done.18 = bf16[256,512]{1,0:T(8,128)(2,1)S(1)} collective-permute-done((bf16[256,512]{1,0:T(8,128)(2,1)S(1)}, bf16[256,512]{1,0:T(8,128)(2,1)S(1)}, u32[]{:S(2)}, u32[]{:S(2)}) %collective-permute-start.18) | collective-permute-done | bytes 262176 | tf_op jit(solution)/shard_map/ppermute | solution.py:355
  132.2 7.3 %attend.1 = (bf16[256,1024]{1,0:T(8,128)(2,1)}, f32[8,256]{1,0:T(8,128)}) custom-call(s32[2,8]{1,0:T(2,128)} %pad_add_fusion.info_ref, bf16[256,1024]{1,0:T(8,128)(2,1)} %broadcast_multiply_fusion.q_ref, bf16[8,256,512]{2,1,0:T(8,128)(2,1)} %copy-done.69, s32[2048,1]{1,0:T(8,128)} %copy.39.kdoc_ref, s32[1,256]{1,0:T(1,128)} %constant_dynamic-slice_fusion.qdoc_ref), custom_call_target="tpu_custom_call" | custom-call | flops 2147483648 | bytes 2097152 | tf_op jit(solution)/shard_map/attend/pallas_call | solution.py:226
  139.4 7.0 %collective-permute-start.28 = (bf16[224,1152]{1,0:T(8,128)(2,1)S(1)}, bf16[224,1152]{1,0:T(8,128)(2,1)S(1)}, u32[]{:S(2)}, u32[]{:S(2)}) collective-permute-start(bf16[224,1152]{1,0:T(8,128)(2,1)S(1)} %get-tuple-element.41), channel_id=1, source_target_pairs={{2,0},{4,2},{6,4},{0,6},{3,1},{5,3},{7,5},{1,7},{10,8},{12,10},{14... | collective-permute-start | bytes 1548296 | tf_op jit(solution)/shard_map/ppermute | solution.py:355
  152.1 6.5 %collective-permute-done.28 = bf16[224,1152]{1,0:T(8,128)(2,1)S(1)} collective-permute-done((bf16[224,1152]{1,0:T(8,128)(2,1)S(1)}, bf16[224,1152]{1,0:T(8,128)(2,1)S(1)}, u32[]{:S(2)}, u32[]{:S(2)}) %collective-permute-start.28) | collective-permute-done | bytes 516128 | tf_op jit(solution)/shard_map/ppermute | solution.py:355
  158.6 4.3 collective-permute-start.26
  163.0 7.8 %collective-permute-done.30 = bf16[224,1152]{1,0:T(8,128)(2,1)S(1)} collective-permute-done((bf16[224,1152]{1,0:T(8,128)(2,1)S(1)}, bf16[224,1152]{1,0:T(8,128)(2,1)S(1)}, u32[]{:S(2)}, u32[]{:S(2)}) %collective-permute-start.30) | collective-permute-done | bytes 516128 | tf_op jit(solution)/shard_map/ppermute | solution.py:355
  175.5 13.2 %collective-permute-done.26 = bf16[224,1152]{1,0:T(8,128)(2,1)S(1)} collective-permute-done((bf16[224,1152]{1,0:T(8,128)(2,1)S(1)}, bf16[224,1152]{1,0:T(8,128)(2,1)S(1)}, u32[]{:S(2)}, u32[]{:S(2)}) %collective-permute-start.26) | collective-permute-done | bytes 516128 | tf_op jit(solution)/shard_map/ppermute | solution.py:355
  196.5 5.3 collective-permute-done.31
  206.1 2.9 multiply_convert_fusion.14
  229.0 6.0 %collective-permute-done.41 = bf16[128,1152]{1,0:T(8,128)(2,1)S(1)} collective-permute-done((bf16[128,1152]{1,0:T(8,128)(2,1)S(1)}, bf16[128,1152]{1,0:T(8,128)(2,1)S(1)}, u32[]{:S(2)}, u32[]{:S(2)}) %collective-permute-start.41) | collective-permute-done | bytes 294944 | tf_op jit(solution)/shard_map/ppermute | solution.py:355
  237.4 12.8 %collective-permute-done.42 = bf16[256,1152]{1,0:T(8,128)(2,1)S(1)} collective-permute-done((bf16[256,1152]{1,0:T(8,128)(2,1)S(1)}, bf16[256,1152]{1,0:T(8,128)(2,1)S(1)}, u32[]{:S(2)}, u32[]{:S(2)}) %collective-permute-start.42) | collective-permute-done | bytes 589856 | tf_op jit(solution)/shard_map/ppermute | solution.py:355
  257.2 12.2 %collective-permute-done.49 = bf16[256,1152]{1,0:T(8,128)(2,1)S(1)} collective-permute-done((bf16[256,1152]{1,0:T(8,128)(2,1)}, bf16[256,1152]{1,0:T(8,128)(2,1)S(1)}, u32[]{:S(2)}, u32[]{:S(2)}) %collective-permute-start.49) | collective-permute-done | bytes 589856 | tf_op jit(solution)/shard_map/ppermute | solution.py:355
  271.8 5.4 multiply_convert_fusion.10
  297.4 4.1 multiply_convert_fusion.4
  301.6 5.0 fusion.30
  309.0 6.4 %fusion.27 = bf16[896,1152]{1,0:T(8,128)(2,1)S(1)} fusion(bf16[2048,1152]{1,0:T(8,128)(2,1)S(1)} %bitcast.252, bf16[512,896]{1,0:T(8,128)(2,1)} %get-tuple-element.126, bf16[512,896]{1,0:T(8,128)(2,1)S(1)} %copy-done.127, bf16[512,896]{1,0:T(8,128)(2,1)} %copy-done.128, bf16[512,896]{1,0:T(8,128)(2,1)S(1)} %copy-done.125), kind=kOutput, calls=%fused_computation.27 | convolution fusion | flops 4243570688 | bytes 10452992 | tf_op jit(solution)/shard_map/dot_general | solution.py:55
  315.4 3.4 fusion.218
  326.8 6.4 %collective-permute-done.57 = bf16[128,1152]{1,0:T(8,128)(2,1)S(1)} collective-permute-done((bf16[128,1152]{1,0:T(8,128)(2,1)S(1)}, bf16[128,1152]{1,0:T(8,128)(2,1)S(1)}, u32[]{:S(2)}, u32[]{:S(2)}) %collective-permute-start.57) | collective-permute-done | bytes 294944 | tf_op jit(solution)/shard_map/ppermute | solution.py:355
  335.5 5.0 fusion.24
  341.5 3.6 collective-permute-start.89
  348.1 3.5 collective-permute-start.93
  355.3 3.0 fusion.240.o_ref
  360.3 9.1 %attend_back.1 = (f32[256,1024]{1,0:T(8,128)}, bf16[8,256,512]{2,1,0:T(8,128)(2,1)}) custom-call(s32[2,8]{1,0:T(2,128)} %pad_add_fusion.info_ref, bf16[256,1024]{1,0:T(8,128)(2,1)} %broadcast_multiply_fusion.q_ref, bf16[8,256,512]{2,1,0:T(8,128)(2,1)} %copy-done.69, s32[2048,1]{1,0:T(8,128)} %copy.39.kdoc_ref, s32[1,256]{1,0:T(1,128)} %constant_dynamic-slice_fusion.qdoc_ref, ...), custom_call_target="tpu_custom_call" | custom-call | flops 5368709120 | bytes 4194304 | tf_op jit(solution)/shard_map/attend_back/pallas_call | solution.py:309
  372.3 7.3 %collective-permute-start.86 = (bf16[224,1152]{1,0:T(8,128)(2,1)S(1)}, bf16[224,1152]{1,0:T(8,128)(2,1)S(1)}, u32[]{:S(2)}, u32[]{:S(2)}) collective-permute-start(bf16[224,1152]{1,0:T(8,128)(2,1)S(1)} %pad_maximum_fusion.15), channel_id=1, source_target_pairs={{2,0},{4,2},{6,4},{0,6},{3,1},{5,3},{7,5},{1,7},{10,8},{12,10},{14... | collective-permute-start | bytes 1548296 | tf_op jit(solution)/shard_map/ppermute | solution.py:355
  389.9 3.7 collective-permute-done.65
  397.0 27.4 %collective-permute-done.66 = bf16[128,512]{1,0:T(8,128)(2,1)S(1)} collective-permute-done((bf16[128,512]{1,0:T(8,128)(2,1)S(1)}, bf16[128,512]{1,0:T(8,128)(2,1)S(1)}, u32[]{:S(2)}, u32[]{:S(2)}) %collective-permute-start.66) | collective-permute-done | bytes 131104 | tf_op jit(solution)/shard_map/ppermute | solution.py:355
  425.4 10.8 %collective-permute-done.69 = bf16[128,512]{1,0:T(8,128)(2,1)S(1)} collective-permute-done((bf16[128,512]{1,0:T(8,128)(2,1)S(1)}, bf16[128,512]{1,0:T(8,128)(2,1)S(1)}, u32[]{:S(2)}, u32[]{:S(2)}) %collective-permute-start.69) | collective-permute-done | bytes 131104 | tf_op jit(solution)/shard_map/ppermute | solution.py:355
  436.3 3.9 collective-permute-start.94
  442.0 8.2 %collective-permute-done.92 = bf16[224,1152]{1,0:T(8,128)(2,1)S(1)} collective-permute-done((bf16[224,1152]{1,0:T(8,128)(2,1)S(1)}, bf16[224,1152]{1,0:T(8,128)(2,1)S(1)}, u32[]{:S(2)}, u32[]{:S(2)}) %collective-permute-start.92) | collective-permute-done | bytes 516128 | tf_op jit(solution)/shard_map/ppermute | solution.py:355
  450.9 6.0 %collective-permute-done.94 = bf16[224,1152]{1,0:T(8,128)(2,1)S(1)} collective-permute-done((bf16[224,1152]{1,0:T(8,128)(2,1)S(1)}, bf16[224,1152]{1,0:T(8,128)(2,1)S(1)}, u32[]{:S(2)}, u32[]{:S(2)}) %collective-permute-start.94) | collective-permute-done | bytes 516128 | tf_op jit(solution)/shard_map/ppermute | solution.py:355
  467.4 4.1 fusion.139.q_ref
  472.5 8.4 %pack_rows.1 = bf16[32,736,128]{2,1,0:T(8,128)(2,1)} custom-call(s32[32]{0:T(128)} %get-tuple-element.229.place_ref, f32[1152,1536]{1,0:T(8,128)} %fusion.139.q_ref, f32[1024,1152]{1,0:T(8,128)} %fusion.240.o_ref, f32[32,16,128]{2,1,0:T(8,128)} %bitcast.231), custom_call_target="tpu_custom_call" | custom-call | bytes 70778880 | tf_op jit(solution)/shard_map/pack_rows/pallas_call | solution.py:160
  493.0 6.8 %collective-permute-done.74 = bf16[1472,128]{1,0:T(8,128)(2,1)S(1)} collective-permute-done((bf16[1472,128]{1,0:T(8,128)(2,1)S(1)}, bf16[1472,128]{1,0:T(8,128)(2,1)S(1)}, u32[]{:S(2)}, u32[]{:S(2)}) %collective-permute-start.74) | collective-permute-done | bytes 376864 | tf_op jit(solution)/shard_map/ppermute | solution.py:355
  508.3 8.1 %collective-permute-done.96 = bf16[216,864]{1,0:T(8,128)(2,1)S(1)} collective-permute-done((bf16[216,864]{1,0:T(8,128)(2,1)S(1)}, bf16[216,864]{1,0:T(8,128)(2,1)S(1)}, u32[]{:S(2)}, u32[]{:S(2)}) %collective-permute-start.96) | collective-permute-done | bytes 373280 | tf_op jit(solution)/shard_map/ppermute | solution.py:355
  518.8 12.9 %collective-permute-done.78 = bf16[2944,128]{1,0:T(8,128)(2,1)S(1)} collective-permute-done((bf16[2944,128]{1,0:T(8,128)(2,1)S(1)}, bf16[2944,128]{1,0:T(8,128)(2,1)S(1)}, u32[]{:S(2)}, u32[]{:S(2)}) %collective-permute-start.78) | collective-permute-done | bytes 753696 | tf_op jit(solution)/shard_map/ppermute | solution.py:355
  532.8 3.3 collective-permute-start.81
  536.1 3.4 collective-permute-done.79
  543.6 5.5 multiply_subtract_fusion
  (695 shorter events, 220.9 us)
Async XLA Ops:
  12.7 18.6 %collective-permute-start.21 = (bf16[216,864]{1,0:T(8,128)(2,1)}, bf16[216,864]{1,0:T(8,128)(2,1)}, u32[]{:S(2)}, u32[]{:S(2)}) collective-permute-start(bf16[216,864]{1,0:T(8,128)(2,1)} %get-tuple-element.171), channel_id=1, source_target_pairs={{8,0},{16,8},{24,16},{0,24},{9,1},{17,9},{25,17},{1,25},{10,2},{18... | collective-permute-start | bytes 1119752 | tf_op jit(solution)/shard_map/ppermute | solution.py:355
  13.4 19.2 %collective-permute-start.22 = (bf16[216,864]{1,0:T(8,128)(2,1)}, bf16[216,864]{1,0:T(8,128)(2,1)}, u32[]{:S(2)}, u32[]{:S(2)}) collective-permute-start(bf16[216,864]{1,0:T(8,128)(2,1)} %get-tuple-element.170), channel_id=1, source_target_pairs={{16,0},{24,8},{0,16},{8,24},{17,1},{25,9},{1,17},{9,25},{18,2},{26... | collective-permute-start | bytes 1119752 | tf_op jit(solution)/shard_map/ppermute | solution.py:355
  14.2 19.4 %collective-permute-start.23 = (bf16[216,864]{1,0:T(8,128)(2,1)S(1)}, bf16[216,864]{1,0:T(8,128)(2,1)}, u32[]{:S(2)}, u32[]{:S(2)}) collective-permute-start(bf16[216,864]{1,0:T(8,128)(2,1)S(1)} %get-tuple-element.169), channel_id=1, source_target_pairs={{24,0},{0,8},{8,16},{16,24},{25,1},{1,9},{9,17},{17,25},{26,2},{2,... | collective-permute-start | bytes 1119752 | tf_op jit(solution)/shard_map/ppermute | solution.py:355
  28.6 18.7 %collective-permute-start.7 = (bf16[2944,128]{1,0:T(8,128)(2,1)}, bf16[2944,128]{1,0:T(8,128)(2,1)S(1)}, u32[]{:S(2)}, u32[]{:S(2)}) collective-permute-start(bf16[2944,128]{1,0:T(8,128)(2,1)} %constant_dynamic-update-slice_fusion), channel_id=1, source_target_pairs={{1,0},{0,1},{3,2},{2,3},{5,4},{4,5},{7,6},{6,7},{9,8},{8,9},{11,10... | collective-permute-start | bytes 2261000 | tf_op jit(solution)/shard_map/ppermute | solution.py:355
  30.1 21.4 %collective-permute-start.5 = (bf16[2944,128]{1,0:T(8,128)(2,1)}, bf16[2944,128]{1,0:T(8,128)(2,1)}, u32[]{:S(2)}, u32[]{:S(2)}) collective-permute-start(bf16[2944,128]{1,0:T(8,128)(2,1)} %constant_dynamic-update-slice_fusion), channel_id=1, source_target_pairs={{16,0},{0,16},{17,1},{1,17},{18,2},{2,18},{19,3},{3,19},{20,4},{4,... | collective-permute-start | bytes 2261000 | tf_op jit(solution)/shard_map/ppermute | solution.py:355
  50.6 25.9 %collective-permute-start.25 = (bf16[224,2304]{1,0:T(8,128)(2,1)}, bf16[224,2304]{1,0:T(8,128)(2,1)}, u32[]{:S(2)}, u32[]{:S(2)}) collective-permute-start(bf16[224,2304]{1,0:T(8,128)(2,1)} %pad_slice_fusion.2), channel_id=1, source_target_pairs={{6,0},{0,2},{2,4},{4,6},{7,1},{1,3},{3,5},{5,7},{14,8},{8,10},{10,... | collective-permute-start | bytes 3096584 | tf_op jit(solution)/shard_map/ppermute | solution.py:355
  56.7 22.1 %collective-permute-start.4 = (bf16[2944,128]{1,0:T(8,128)(2,1)}, bf16[2944,128]{1,0:T(8,128)(2,1)S(1)}, u32[]{:S(2)}, u32[]{:S(2)}) collective-permute-start(bf16[2944,128]{1,0:T(8,128)(2,1)} %constant_dynamic-update-slice_fusion), channel_id=1, source_target_pairs={{8,0},{0,8},{9,1},{1,9},{10,2},{2,10},{11,3},{3,11},{12,4},{4,12},... | collective-permute-start | bytes 2261000 | tf_op jit(solution)/shard_map/ppermute | solution.py:355
  56.7 22.1 %collective-permute-start.6 = (bf16[2944,128]{1,0:T(8,128)(2,1)}, bf16[2944,128]{1,0:T(8,128)(2,1)S(1)}, u32[]{:S(2)}, u32[]{:S(2)}) collective-permute-start(bf16[2944,128]{1,0:T(8,128)(2,1)} %collective-permute-done.5), channel_id=1, source_target_pairs={{8,0},{0,8},{9,1},{1,9},{10,2},{2,10},{11,3},{3,11},{12,4},{4,12},... | collective-permute-start | bytes 2261000 | tf_op jit(solution)/shard_map/ppermute | solution.py:355
  58.1 20.7 %collective-permute-start.8 = (bf16[2944,128]{1,0:T(8,128)(2,1)S(1)}, bf16[2944,128]{1,0:T(8,128)(2,1)S(1)}, u32[]{:S(2)}, u32[]{:S(2)}) collective-permute-start(bf16[2944,128]{1,0:T(8,128)(2,1)S(1)} %collective-permute-done.7), channel_id=1, source_target_pairs={{8,0},{0,8},{9,1},{1,9},{10,2},{2,10},{11,3},{3,11},{12,4},{4,12},... | collective-permute-start | bytes 2261000 | tf_op jit(solution)/shard_map/ppermute | solution.py:355
  76.5 72.6 %collective-permute-start.24 = (bf16[224,2304]{1,0:T(8,128)(2,1)}, bf16[224,2304]{1,0:T(8,128)(2,1)}, u32[]{:S(2)}, u32[]{:S(2)}) collective-permute-start(bf16[224,2304]{1,0:T(8,128)(2,1)} %pad_slice_fusion.2), channel_id=1, source_target_pairs={{2,0},{4,2},{6,4},{0,6},{3,1},{5,3},{7,5},{1,7},{10,8},{12,10},{14... | collective-permute-start | bytes 3096584 | tf_op jit(solution)/shard_map/ppermute | solution.py:355
  94.1 18.1 %collective-permute-start.13 = (bf16[256,512]{1,0:T(8,128)(2,1)S(1)}, bf16[256,512]{1,0:T(8,128)(2,1)S(1)}, u32[]{:S(2)}, u32[]{:S(2)}) collective-permute-start(bf16[256,512]{1,0:T(8,128)(2,1)S(1)} %pad_maximum_fusion.22), channel_id=1, source_target_pairs={{2,0},{4,2},{6,4},{0,6},{3,1},{5,3},{7,5},{1,7},{10,8},{12,10},{14... | collective-permute-start | bytes 786440 | tf_op jit(solution)/shard_map/ppermute | solution.py:355
  94.3 18.0 %collective-permute-start.16 = (bf16[256,512]{1,0:T(8,128)(2,1)S(1)}, bf16[256,512]{1,0:T(8,128)(2,1)S(1)}, u32[]{:S(2)}, u32[]{:S(2)}) collective-permute-start(bf16[256,512]{1,0:T(8,128)(2,1)S(1)} %pad_maximum_fusion.22), channel_id=1, source_target_pairs={{6,0},{0,2},{2,4},{4,6},{7,1},{1,3},{3,5},{5,7},{14,8},{8,10},{10,... | collective-permute-start | bytes 786440 | tf_op jit(solution)/shard_map/ppermute | solution.py:355
  96.5 19.4 %collective-permute-start.12 = (bf16[256,512]{1,0:T(8,128)(2,1)S(1)}, bf16[256,512]{1,0:T(8,128)(2,1)S(1)}, u32[]{:S(2)}, u32[]{:S(2)}) collective-permute-start(bf16[256,512]{1,0:T(8,128)(2,1)S(1)} %pad_maximum_fusion.22), channel_id=1, source_target_pairs={{1,0},{0,1},{3,2},{2,3},{5,4},{4,5},{7,6},{6,7},{9,8},{8,9},{11,10... | collective-permute-start | bytes 786440 | tf_op jit(solution)/shard_map/ppermute | solution.py:355
  115.9 14.9 %collective-permute-start.19 = (bf16[256,512]{1,0:T(8,128)(2,1)S(1)}, bf16[256,512]{1,0:T(8,128)(2,1)S(1)}, u32[]{:S(2)}, u32[]{:S(2)}) collective-permute-start(bf16[256,512]{1,0:T(8,128)(2,1)S(1)} %collective-permute-done.16), channel_id=1, source_target_pairs={{1,0},{0,1},{3,2},{2,3},{5,4},{4,5},{7,6},{6,7},{9,8},{8,9},{11,10... | collective-permute-start | bytes 786440 | tf_op jit(solution)/shard_map/ppermute | solution.py:355
  139.4 19.2 %collective-permute-start.28 = (bf16[224,1152]{1,0:T(8,128)(2,1)S(1)}, bf16[224,1152]{1,0:T(8,128)(2,1)S(1)}, u32[]{:S(2)}, u32[]{:S(2)}) collective-permute-start(bf16[224,1152]{1,0:T(8,128)(2,1)S(1)} %get-tuple-element.41), channel_id=1, source_target_pairs={{2,0},{4,2},{6,4},{0,6},{3,1},{5,3},{7,5},{1,7},{10,8},{12,10},{14... | collective-permute-start | bytes 1548296 | tf_op jit(solution)/shard_map/ppermute | solution.py:355
  146.4 24.4 %collective-permute-start.30 = (bf16[224,1152]{1,0:T(8,128)(2,1)S(1)}, bf16[224,1152]{1,0:T(8,128)(2,1)S(1)}, u32[]{:S(2)}, u32[]{:S(2)}) collective-permute-start(bf16[224,1152]{1,0:T(8,128)(2,1)S(1)} %get-tuple-element.41), channel_id=1, source_target_pairs={{6,0},{0,2},{2,4},{4,6},{7,1},{1,3},{3,5},{5,7},{14,8},{8,10},{10,... | collective-permute-start | bytes 1548296 | tf_op jit(solution)/shard_map/ppermute | solution.py:355
  149.0 26.3 %collective-permute-start.20 = (bf16[256,1152]{1,0:T(8,128)(2,1)S(1)}, bf16[256,1152]{1,0:T(8,128)(2,1)S(1)}, u32[]{:S(2)}, u32[]{:S(2)}) collective-permute-start(bf16[256,1152]{1,0:T(8,128)(2,1)S(1)} %get-tuple-element.98), channel_id=1, source_target_pairs={{8,0},{0,8},{9,1},{1,9},{10,2},{2,10},{11,3},{3,11},{12,4},{4,12},... | collective-permute-start | bytes 1769480 | tf_op jit(solution)/shard_map/ppermute | solution.py:355
  149.1 25.7 %collective-permute-start.37 = (bf16[256,1152]{1,0:T(8,128)(2,1)S(1)}, bf16[256,1152]{1,0:T(8,128)(2,1)S(1)}, u32[]{:S(2)}, u32[]{:S(2)}) collective-permute-start(bf16[256,1152]{1,0:T(8,128)(2,1)S(1)} %get-tuple-element.98), channel_id=1, source_target_pairs={{16,0},{0,16},{17,1},{1,17},{18,2},{2,18},{19,3},{3,19},{20,4},{4,... | collective-permute-start | bytes 1769480 | tf_op jit(solution)/shard_map/ppermute | solution.py:355
  149.2 23.1 %collective-permute-start.33 = (bf16[256,1152]{1,0:T(8,128)(2,1)S(1)}, bf16[256,1152]{1,0:T(8,128)(2,1)S(1)}, u32[]{:S(2)}, u32[]{:S(2)}) collective-permute-start(bf16[256,1152]{1,0:T(8,128)(2,1)S(1)} %get-tuple-element.98), channel_id=1, source_target_pairs={{1,0},{0,1},{3,2},{2,3},{5,4},{4,5},{7,6},{6,7},{9,8},{8,9},{11,10... | collective-permute-start | bytes 1769480 | tf_op jit(solution)/shard_map/ppermute | solution.py:355
  158.6 30.1 %collective-permute-start.26 = (bf16[224,1152]{1,0:T(8,128)(2,1)S(1)}, bf16[224,1152]{1,0:T(8,128)(2,1)S(1)}, u32[]{:S(2)}, u32[]{:S(2)}) collective-permute-start(bf16[224,1152]{1,0:T(8,128)(2,1)S(1)} %get-tuple-element.39), channel_id=1, source_target_pairs={{2,0},{4,2},{6,4},{0,6},{3,1},{5,3},{7,5},{1,7},{10,8},{12,10},{14... | collective-permute-start | bytes 1548296 | tf_op jit(solution)/shard_map/ppermute | solution.py:355
  170.8 22.2 %collective-permute-start.27 = (bf16[224,1152]{1,0:T(8,128)(2,1)S(1)}, bf16[224,1152]{1,0:T(8,128)(2,1)S(1)}, u32[]{:S(2)}, u32[]{:S(2)}) collective-permute-start(bf16[224,1152]{1,0:T(8,128)(2,1)S(1)} %copy-done.37), channel_id=1, source_target_pairs={{6,0},{0,2},{2,4},{4,6},{7,1},{1,3},{3,5},{5,7},{14,8},{8,10},{10,... | collective-permute-start | bytes 1548296 | tf_op jit(solution)/shard_map/ppermute | solution.py:355
  172.2 24.2 %collective-permute-start.29 = (bf16[112,1152]{1,0:T(8,128)(2,1)S(1)}, bf16[112,1152]{1,0:T(8,128)(2,1)S(1)}, u32[]{:S(2)}, u32[]{:S(2)}) collective-permute-start(bf16[112,1152]{1,0:T(8,128)(2,1)S(1)} %slice.753), channel_id=1, source_target_pairs={{2,0},{4,2},{6,4},{0,6},{3,1},{5,3},{7,5},{1,7},{10,8},{12,10},{14... | collective-permute-start | bytes 774152 | tf_op jit(solution)/shard_map/ppermute | solution.py:355
  174.8 27.0 %collective-permute-start.31 = (bf16[112,1152]{1,0:T(8,128)(2,1)S(1)}, bf16[112,1152]{1,0:T(8,128)(2,1)S(1)}, u32[]{:S(2)}, u32[]{:S(2)}) collective-permute-start(bf16[112,1152]{1,0:T(8,128)(2,1)S(1)} %slice.754), channel_id=1, source_target_pairs={{6,0},{0,2},{2,4},{4,6},{7,1},{1,3},{3,5},{5,7},{14,8},{8,10},{10,... | collective-permute-start | bytes 774152 | tf_op jit(solution)/shard_map/ppermute | solution.py:355
  175.3 28.2 %collective-permute-start.36 = (bf16[128,1152]{1,0:T(8,128)(2,1)S(1)}, bf16[128,1152]{1,0:T(8,128)(2,1)S(1)}, u32[]{:S(2)}, u32[]{:S(2)}) collective-permute-start(bf16[128,1152]{1,0:T(8,128)(2,1)S(1)} %slice.760), channel_id=1, source_target_pairs={{16,0},{0,16},{17,1},{1,17},{18,2},{2,18},{19,3},{3,19},{20,4},{4,... | collective-permute-start | bytes 884744 | tf_op jit(solution)/shard_map/ppermute | solution.py:355
  203.5 33.9 %collective-permute-start.32 = (bf16[256,1152]{1,0:T(8,128)(2,1)S(1)}, bf16[256,1152]{1,0:T(8,128)(2,1)S(1)}, u32[]{:S(2)}, u32[]{:S(2)}) collective-permute-start(bf16[256,1152]{1,0:T(8,128)(2,1)S(1)} %slice.756), channel_id=1, source_target_pairs={{8,0},{0,8},{9,1},{1,9},{10,2},{2,10},{11,3},{3,11},{12,4},{4,12},... | collective-permute-start | bytes 1769480 | tf_op jit(solution)/shard_map/ppermute | solution.py:355
  235.1 15.0 %collective-permute-start.42 = (bf16[256,1152]{1,0:T(8,128)(2,1)S(1)}, bf16[256,1152]{1,0:T(8,128)(2,1)S(1)}, u32[]{:S(2)}, u32[]{:S(2)}) collective-permute-start(bf16[256,1152]{1,0:T(8,128)(2,1)S(1)} %pad_maximum_fusion.9), channel_id=1, source_target_pairs={{1,0},{0,1},{3,2},{2,3},{5,4},{4,5},{7,6},{6,7},{9,8},{8,9},{11,10... | collective-permute-start | bytes 1769480 | tf_op jit(solution)/shard_map/ppermute | solution.py:355
  280.7 60.8 %collective-permute-start.48 = (bf16[256,1152]{1,0:T(8,128)(2,1)S(1)}, bf16[256,1152]{1,0:T(8,128)(2,1)S(1)}, u32[]{:S(2)}, u32[]{:S(2)}) collective-permute-start(bf16[256,1152]{1,0:T(8,128)(2,1)S(1)} %slice.773), channel_id=1, source_target_pairs={{8,0},{0,8},{9,1},{1,9},{10,2},{2,10},{11,3},{3,11},{12,4},{4,12},... | collective-permute-start | bytes 1769480 | tf_op jit(solution)/shard_map/ppermute | solution.py:355
  289.3 34.6 %collective-permute-start.51 = (bf16[256,1152]{1,0:T(8,128)(2,1)S(1)}, bf16[256,1152]{1,0:T(8,128)(2,1)S(1)}, u32[]{:S(2)}, u32[]{:S(2)}) collective-permute-start(bf16[256,1152]{1,0:T(8,128)(2,1)S(1)} %slice.775), channel_id=1, source_target_pairs={{8,0},{0,8},{9,1},{1,9},{10,2},{2,10},{11,3},{3,11},{12,4},{4,12},... | collective-permute-start | bytes 1769480 | tf_op jit(solution)/shard_map/ppermute | solution.py:355
  295.1 30.4 %collective-permute-start.60 = (bf16[256,1152]{1,0:T(8,128)(2,1)S(1)}, bf16[256,1152]{1,0:T(8,128)(2,1)S(1)}, u32[]{:S(2)}, u32[]{:S(2)}) collective-permute-start(bf16[256,1152]{1,0:T(8,128)(2,1)S(1)} %slice.784), channel_id=1, source_target_pairs={{8,0},{0,8},{9,1},{1,9},{10,2},{2,10},{11,3},{3,11},{12,4},{4,12},... | collective-permute-start | bytes 1769480 | tf_op jit(solution)/shard_map/ppermute | solution.py:355
  321.0 38.2 %collective-permute-start.85 = (bf16[112,1152]{1,0:T(8,128)(2,1)S(1)}, bf16[112,1152]{1,0:T(8,128)(2,1)S(1)}, u32[]{:S(2)}, u32[]{:S(2)}) collective-permute-start(bf16[112,1152]{1,0:T(8,128)(2,1)S(1)} %get-tuple-element.137), channel_id=1, source_target_pairs={{2,0},{4,2},{6,4},{0,6},{3,1},{5,3},{7,5},{1,7},{10,8},{12,10},{14... | collective-permute-start | bytes 774152 | tf_op jit(solution)/shard_map/ppermute | solution.py:355
  323.9 35.7 %collective-permute-start.83 = (bf16[112,1152]{1,0:T(8,128)(2,1)S(1)}, bf16[112,1152]{1,0:T(8,128)(2,1)S(1)}, u32[]{:S(2)}, u32[]{:S(2)}) collective-permute-start(bf16[112,1152]{1,0:T(8,128)(2,1)S(1)} %get-tuple-element.136), channel_id=1, source_target_pairs={{6,0},{0,2},{2,4},{4,6},{7,1},{1,3},{3,5},{5,7},{14,8},{8,10},{10,... | collective-permute-start | bytes 774152 | tf_op jit(solution)/shard_map/ppermute | solution.py:355
  341.5 30.7 %collective-permute-start.89 = (bf16[112,1152]{1,0:T(8,128)(2,1)}, bf16[112,1152]{1,0:T(8,128)(2,1)}, u32[]{:S(2)}, u32[]{:S(2)}) collective-permute-start(bf16[112,1152]{1,0:T(8,128)(2,1)} %get-tuple-element.143), channel_id=1, source_target_pairs={{2,0},{4,2},{6,4},{0,6},{3,1},{5,3},{7,5},{1,7},{10,8},{12,10},{14... | collective-permute-start | bytes 774152 | tf_op jit(solution)/shard_map/ppermute | solution.py:355
  347.4 32.2 %collective-permute-start.87 = (bf16[112,1152]{1,0:T(8,128)(2,1)}, bf16[112,1152]{1,0:T(8,128)(2,1)}, u32[]{:S(2)}, u32[]{:S(2)}) collective-permute-start(bf16[112,1152]{1,0:T(8,128)(2,1)} %get-tuple-element.142), channel_id=1, source_target_pairs={{6,0},{0,2},{2,4},{4,6},{7,1},{1,3},{3,5},{5,7},{14,8},{8,10},{10,... | collective-permute-start | bytes 774152 | tf_op jit(solution)/shard_map/ppermute | solution.py:355
  348.1 31.5 %collective-permute-start.93 = (bf16[112,1152]{1,0:T(8,128)(2,1)}, bf16[112,1152]{1,0:T(8,128)(2,1)}, u32[]{:S(2)}, u32[]{:S(2)}) collective-permute-start(bf16[112,1152]{1,0:T(8,128)(2,1)} %get-tuple-element.149), channel_id=1, source_target_pairs={{2,0},{4,2},{6,4},{0,6},{3,1},{5,3},{7,5},{1,7},{10,8},{12,10},{14... | collective-permute-start | bytes 774152 | tf_op jit(solution)/shard_map/ppermute | solution.py:355
  359.2 20.4 %collective-permute-start.91 = (bf16[112,1152]{1,0:T(8,128)(2,1)}, bf16[112,1152]{1,0:T(8,128)(2,1)S(1)}, u32[]{:S(2)}, u32[]{:S(2)}) collective-permute-start(bf16[112,1152]{1,0:T(8,128)(2,1)} %get-tuple-element.148), channel_id=1, source_target_pairs={{6,0},{0,2},{2,4},{4,6},{7,1},{1,3},{3,5},{5,7},{14,8},{8,10},{10,... | collective-permute-start | bytes 774152 | tf_op jit(solution)/shard_map/ppermute | solution.py:355
  369.6 66.7 %collective-permute-start.84 = (bf16[224,1152]{1,0:T(8,128)(2,1)S(1)}, bf16[224,1152]{1,0:T(8,128)(2,1)S(1)}, u32[]{:S(2)}, u32[]{:S(2)}) collective-permute-start(bf16[224,1152]{1,0:T(8,128)(2,1)S(1)} %pad_maximum_fusion.14), channel_id=1, source_target_pairs={{6,0},{0,2},{2,4},{4,6},{7,1},{1,3},{3,5},{5,7},{14,8},{8,10},{10,... | collective-permute-start | bytes 1548296 | tf_op jit(solution)/shard_map/ppermute | solution.py:355
  372.3 67.9 %collective-permute-start.86 = (bf16[224,1152]{1,0:T(8,128)(2,1)S(1)}, bf16[224,1152]{1,0:T(8,128)(2,1)S(1)}, u32[]{:S(2)}, u32[]{:S(2)}) collective-permute-start(bf16[224,1152]{1,0:T(8,128)(2,1)S(1)} %pad_maximum_fusion.15), channel_id=1, source_target_pairs={{2,0},{4,2},{6,4},{0,6},{3,1},{5,3},{7,5},{1,7},{10,8},{12,10},{14... | collective-permute-start | bytes 1548296 | tf_op jit(solution)/shard_map/ppermute | solution.py:355
  389.9 93.8 %collective-permute-start.88 = (bf16[224,1152]{1,0:T(8,128)(2,1)}, bf16[224,1152]{1,0:T(8,128)(2,1)}, u32[]{:S(2)}, u32[]{:S(2)}) collective-permute-start(bf16[224,1152]{1,0:T(8,128)(2,1)} %pad_maximum_fusion.16), channel_id=1, source_target_pairs={{6,0},{0,2},{2,4},{4,6},{7,1},{1,3},{3,5},{5,7},{14,8},{8,10},{10,... | collective-permute-start | bytes 1548296 | tf_op jit(solution)/shard_map/ppermute | solution.py:355
  393.7 90.0 %collective-permute-start.90 = (bf16[224,1152]{1,0:T(8,128)(2,1)}, bf16[224,1152]{1,0:T(8,128)(2,1)}, u32[]{:S(2)}, u32[]{:S(2)}) collective-permute-start(bf16[224,1152]{1,0:T(8,128)(2,1)} %pad_maximum_fusion.17), channel_id=1, source_target_pairs={{2,0},{4,2},{6,4},{0,6},{3,1},{5,3},{7,5},{1,7},{10,8},{12,10},{14... | collective-permute-start | bytes 1548296 | tf_op jit(solution)/shard_map/ppermute | solution.py:355
  396.7 27.6 %collective-permute-start.66 = (bf16[128,512]{1,0:T(8,128)(2,1)S(1)}, bf16[128,512]{1,0:T(8,128)(2,1)S(1)}, u32[]{:S(2)}, u32[]{:S(2)}) collective-permute-start(bf16[128,512]{1,0:T(8,128)(2,1)S(1)} %get-tuple-element.221), channel_id=1, source_target_pairs={{6,0},{0,2},{2,4},{4,6},{7,1},{1,3},{3,5},{5,7},{14,8},{8,10},{10,... | collective-permute-start | bytes 393224 | tf_op jit(solution)/shard_map/ppermute | solution.py:355
  436.3 20.7 %collective-permute-start.94 = (bf16[224,1152]{1,0:T(8,128)(2,1)S(1)}, bf16[224,1152]{1,0:T(8,128)(2,1)S(1)}, u32[]{:S(2)}, u32[]{:S(2)}) collective-permute-start(bf16[224,1152]{1,0:T(8,128)(2,1)S(1)} %pad_maximum_fusion.19), channel_id=1, source_target_pairs={{2,0},{4,2},{6,4},{0,6},{3,1},{5,3},{7,5},{1,7},{10,8},{12,10},{14... | collective-permute-start | bytes 1548296 | tf_op jit(solution)/shard_map/ppermute | solution.py:355
  440.2 19.5 %collective-permute-start.63 = (bf16[256,512]{1,0:T(8,128)(2,1)S(1)}, bf16[256,512]{1,0:T(8,128)(2,1)S(1)}, u32[]{:S(2)}, u32[]{:S(2)}) collective-permute-start(bf16[256,512]{1,0:T(8,128)(2,1)S(1)} %get-tuple-element.127), channel_id=1, source_target_pairs={{1,0},{0,1},{3,2},{2,3},{5,4},{4,5},{7,6},{6,7},{9,8},{8,9},{11,10... | collective-permute-start | bytes 786440 | tf_op jit(solution)/shard_map/ppermute | solution.py:355
  489.9 16.8 %collective-permute-start.95 = (bf16[216,864]{1,0:T(8,128)(2,1)S(1)}, bf16[216,864]{1,0:T(8,128)(2,1)S(1)}, u32[]{:S(2)}, u32[]{:S(2)}) collective-permute-start(bf16[216,864]{1,0:T(8,128)(2,1)S(1)} %get-tuple-element.163), channel_id=1, source_target_pairs={{8,0},{16,8},{24,16},{0,24},{9,1},{17,9},{25,17},{1,25},{10,2},{18... | collective-permute-start | bytes 1119752 | tf_op jit(solution)/shard_map/ppermute | solution.py:355
  490.4 26.0 %collective-permute-start.96 = (bf16[216,864]{1,0:T(8,128)(2,1)S(1)}, bf16[216,864]{1,0:T(8,128)(2,1)S(1)}, u32[]{:S(2)}, u32[]{:S(2)}) collective-permute-start(bf16[216,864]{1,0:T(8,128)(2,1)S(1)} %get-tuple-element.162), channel_id=1, source_target_pairs={{16,0},{24,8},{0,16},{8,24},{17,1},{25,9},{1,17},{9,25},{18,2},{26... | collective-permute-start | bytes 1119752 | tf_op jit(solution)/shard_map/ppermute | solution.py:355
  491.4 25.1 %collective-permute-start.71 = (bf16[2944,128]{1,0:T(8,128)(2,1)S(1)}, bf16[2944,128]{1,0:T(8,128)(2,1)S(1)}, u32[]{:S(2)}, u32[]{:S(2)}) collective-permute-start(bf16[2944,128]{1,0:T(8,128)(2,1)S(1)} %get-tuple-element.112), channel_id=1, source_target_pairs={{8,0},{0,8},{9,1},{1,9},{10,2},{2,10},{11,3},{3,11},{12,4},{4,12},... | collective-permute-start | bytes 2261000 | tf_op jit(solution)/shard_map/ppermute | solution.py:355
  500.0 18.8 %collective-permute-start.75 = (bf16[2944,128]{1,0:T(8,128)(2,1)S(1)}, bf16[2944,128]{1,0:T(8,128)(2,1)S(1)}, u32[]{:S(2)}, u32[]{:S(2)}) collective-permute-start(bf16[2944,128]{1,0:T(8,128)(2,1)S(1)} %pad_maximum_fusion.6), channel_id=1, source_target_pairs={{1,0},{0,1},{3,2},{2,3},{5,4},{4,5},{7,6},{6,7},{9,8},{8,9},{11,10... | collective-permute-start | bytes 2261000 | tf_op jit(solution)/shard_map/ppermute | solution.py:355
  503.2 28.5 %collective-permute-start.78 = (bf16[2944,128]{1,0:T(8,128)(2,1)S(1)}, bf16[2944,128]{1,0:T(8,128)(2,1)S(1)}, u32[]{:S(2)}, u32[]{:S(2)}) collective-permute-start(bf16[2944,128]{1,0:T(8,128)(2,1)S(1)} %pad_maximum_fusion.7), channel_id=1, source_target_pairs={{16,0},{0,16},{17,1},{1,17},{18,2},{2,18},{19,3},{3,19},{20,4},{4,... | collective-permute-start | bytes 2261000 | tf_op jit(solution)/shard_map/ppermute | solution.py:355
  506.7 29.4 %collective-permute-start.97 = (bf16[216,864]{1,0:T(8,128)(2,1)S(1)}, bf16[216,864]{1,0:T(8,128)(2,1)S(1)}, u32[]{:S(2)}, u32[]{:S(2)}) collective-permute-start(bf16[216,864]{1,0:T(8,128)(2,1)S(1)} %get-tuple-element.161), channel_id=1, source_target_pairs={{24,0},{0,8},{8,16},{16,24},{25,1},{1,9},{9,17},{17,25},{26,2},{2,... | collective-permute-start | bytes 1119752 | tf_op jit(solution)/shard_map/ppermute | solution.py:355
  (189 other events, 1879.3 us)

commit v2 on v1

v2 whole, which is shorter than its diff:
```python
import jax
import jax.numpy as jnp
import numpy as np
from jax import lax
from jax.experimental import pallas as pl
from jax.experimental.pallas import tpu as pltpu
from jax.sharding import Mesh, PartitionSpec as P

D = 1152
H = 4
HD = 256
STEP = 5

NORM_EPS = 1e-06
SCORE_FLOOR = -1e30
ROPE_BASE = 1000000.0
BETA_MOMENT = 0.5
ADAM_EPS = 1e-08
RATE_MATRIX = 0.03
RATE_GAIN = 0.5
DECAY_MATRIX = 0.1

bf16 = jnp.bfloat16
f32 = jnp.float32
LANES = 128


def normed(value):
    factor = lax.rsqrt(jnp.mean(value * value, axis=-1, keepdims=True) + NORM_EPS)
    return (value * factor, factor)


def norm_back(unit, factor, d_unit):
    return factor * (d_unit - unit * jnp.mean(d_unit * unit, axis=-1, keepdims=True))


def angles(position):
    half_index = jnp.arange(HD // 2, dtype=f32)
    frequency = jnp.exp(half_index * (-2.0 * jnp.log(ROPE_BASE) / HD))
    angle = position.astype(f32)[:, None] * frequency[None, :]
    return (jnp.cos(angle), jnp.sin(angle))


def rotate(value, cosine, sine):
    half_width = value.shape[-1] // 2
    first_half = value[..., :half_width]
    second_half = value[..., half_width:]
    return jnp.concatenate(
        [first_half * cosine - second_half * sine, second_half * cosine + first_half * sine],
        axis=-1,
    )


def contract(left, right, left_dim, right_dim):
    return lax.dot_general(
        left, right, (((left_dim,), (right_dim,)), ((), ())), preferred_element_type=f32
    )


def adam_update(weight, moment_one, second, gradient, learn_rate, decay_rate):
    moment_new = BETA_MOMENT * moment_one + (1.0 - BETA_MOMENT) * gradient
    second_new = BETA_MOMENT * second + (1.0 - BETA_MOMENT) * gradient * gradient
    correction = 1.0 - BETA_MOMENT**STEP
    update = moment_new / correction / (jnp.sqrt(second_new / correction) + ADAM_EPS)
    return (moment_new, second_new, weight - learn_rate * (update + decay_rate * weight))


def add_low(*parts):
    total = parts[0].astype(f32)
    for part in parts[1:]:
        total = total + part.astype(f32)
    return total.astype(bf16)


def after(value, *earlier):
    return lax.optimization_barrier((value,) + earlier)[0]


def halfway(rows):
    return rows // 32 * 16 if rows >= 32 else rows // 2


VMEM_LIMIT = 56 * 1024 * 1024
SCORE_SCALE = HD ** (-0.5)
SPACES = {"v": pltpu.VMEM, "h": pl.ANY, "s": pltpu.SMEM}


def run(name, body, operands, spaces, out_shape, scratch=(), out_spaces=None):
    return pl.pallas_call(
        body,
        out_shape=tuple(jax.ShapeDtypeStruct(s, d) for s, d in out_shape),
        in_specs=[pl.BlockSpec(memory_space=SPACES[s]) for s in spaces],
        out_specs=tuple(
            pl.BlockSpec(memory_space=SPACES[s]) for s in out_spaces or "v" * len(out_shape)
        ),
        scratch_shapes=list(scratch),
        compiler_params=pltpu.CompilerParams(vmem_limit_bytes=VMEM_LIMIT),
        cost_estimate=pl.CostEstimate(flops=0, bytes_accessed=0, transcendentals=0),
        name=name,
    )(*operands)


class Flat:
    def __init__(self, piece, gain_piece, devices):
        self.devices = devices
        self.lines = piece // LANES
        self.gain_at = -(-self.lines // 16) * 16
        self.gain_piece = gain_piece
        self.rows = self.gain_at + 16
        self.q_across, self.o_across = (H + 2) * HD // LANES, D // LANES
        self.q_lines, self.o_lines = D * self.q_across, H * HD * self.o_across
        widths = [D, HD, HD, D, D, D]
        self.gain_rows = [w // LANES for w in widths]
        self.gain_lines = sum(self.gain_rows)

    def gain_line(self, device):
        return self.gain_piece * device // LANES


def fetch(order_ref, sources, held, sems):
    copies = []
    for source in sources:
        for i in range(source.shape[0]):
            k = len(copies)
            copies.append(pltpu.make_async_copy(source.at[i], held.at[order_ref[k]], sems.at[k]))
    for copy in copies:
        copy.start()
    return copies


def first_part(flat, parts, order, tokens, cosine, sine):
    tok_rows = tokens.shape[0]
    wide = (H + 2) * HD
    blocks = -(-flat.q_lines // flat.lines)

    def body(order_ref, *refs):
        sources = refs[: len(parts)]
        (
            tok_ref, cos_ref, sin_ref, w_ref, g_pre, g_q, g_k, g_post, g_fpre, g_fpost,
            a_ref, q_ref, kv_ref, raw_ref, held, lines, gains, sems,
        ) = refs[len(parts) :]
        copies = fetch(order_ref, sources, held, sems)
        unit, _ = normed(tok_ref[...].astype(f32))
        gains[...] = jnp.zeros_like(gains)
        for copy in copies:
            copy.wait()
        for i in range(flat.devices):
            at = flat.gain_line(i)
            gains[at : at + 3, :] += held[i, flat.gain_at :, :].astype(f32)[:3]
        at = 0
        for ref, rows in zip((g_pre, g_q, g_k, g_post, g_fpre, g_fpost), flat.gain_rows):
            for i in range(rows):
                ref[:, i * LANES : (i + 1) * LANES] = gains[at + i : at + i + 1, :]
            at += rows
        a_ref[...] = (unit * g_pre[...]).astype(bf16)
        for i in range(blocks):
            lines[i * flat.lines : (i + 1) * flat.lines, :] = held[i, : flat.gain_at, :].astype(f32)[
                : flat.lines
            ]
        for j in range(flat.q_across):
            w_ref[:, j * LANES : (j + 1) * LANES] = lines[
                pl.ds(j, D, stride=flat.q_across), :
            ].astype(bf16)
        qkv = contract(a_ref[...], w_ref[...], 1, 0)
        raw_ref[...] = qkv[:, : (H + 1) * HD]
        cos, sin = cos_ref[...], sin_ref[...]
        for h in range(H):
            head = normed(qkv[:, h * HD : (h + 1) * HD])[0] * g_q[...]
            low = rotate(head, cos, sin).astype(bf16)
            q_ref[:, h * HD : (h + 1) * HD] = (low.astype(f32) * SCORE_SCALE).astype(bf16)
        key = normed(qkv[:, H * HD : (H + 1) * HD])[0] * g_k[...]
        kv_ref[:, :HD] = rotate(key, cos, sin).astype(bf16)
        kv_ref[:, HD:] = qkv[:, (H + 1) * HD :].astype(bf16)

    row = [((1, w * LANES), f32) for w in flat.gain_rows]
    return run(
        "first_part",
        body,
        [order, *parts, tokens, cosine, sine],
        "s" + "h" * len(parts) + "vvv",
        [((D, wide), bf16), *row]
        + [((tok_rows, D), bf16), ((tok_rows, H * HD), bf16), ((tok_rows, 2 * HD), bf16)]
        + [((tok_rows, (H + 1) * HD), f32)],
        [
            pltpu.VMEM((flat.devices, flat.rows, LANES), bf16),
            pltpu.VMEM((blocks * flat.lines, LANES), f32),
            pltpu.VMEM((-(-(flat.gain_lines + 3) // 8) * 8, LANES), f32),
            pltpu.SemaphoreType.DMA((flat.devices,)),
        ],
    )


def spread_out(flat, parts, order):
    start = flat.q_lines // flat.lines

    def body(order_ref, *refs):
        sources = refs[: len(parts)]
        w_ref, held, lines, sems = refs[len(parts) :]
        for copy in fetch(order_ref, sources, held, sems):
            copy.wait()
        for i in range(start, flat.devices):
            at = (i - start) * flat.lines
            lines[at : at + flat.lines, :] = held[i, : flat.gain_at, :].astype(f32)[: flat.lines]
        for j in range(flat.o_across):
            w_ref[:, j * LANES : (j + 1) * LANES] = lines[
                pl.ds(flat.q_lines - start * flat.lines + j, H * HD, stride=flat.o_across), :
            ].astype(bf16)

    return run(
        "spread_out",
        body,
        [order, *parts],
        "s" + "h" * len(parts),
        [((H * HD, D), bf16)],
        [
            pltpu.VMEM((flat.devices, flat.rows, LANES), bf16),
            pltpu.VMEM(((flat.devices - start) * flat.lines, LANES), f32),
            pltpu.SemaphoreType.DMA((flat.devices,)),
        ],
    )[0]


DEAD, WHOLE, MASKED = 0, 1, 2


def allowed_of(kdoc_ref, qdoc_ref, shift):
    keys, queries = kdoc_ref.shape[0], qdoc_ref.shape[1]
    key_at = lax.broadcasted_iota(jnp.int32, (keys, queries), 0) + shift
    query_at = lax.broadcasted_iota(jnp.int32, (keys, queries), 1)
    return (kdoc_ref[...] == qdoc_ref[...]) & (key_at <= query_at)


def same(shape):
    return pl.BlockSpec(shape, lambda i, info: (0,) * len(shape))


def attend(info, query, kv, key_docs, query_docs, w_out, tokens, g_post, g_fpre):
    blocks, rows, _ = kv.shape

    def body(
        info_ref, q_ref, kv_ref, kdoc_ref, qdoc_ref, w_ref, tok_ref, g_post_ref, g_fpre_ref,
        o_ref, lse_ref, out_ref, mid_ref, in_ref, peak, total, acc,
    ):
        step = pl.program_id(0)

        @pl.when(step == 0)
        def _():
            peak[...] = jnp.full_like(peak, SCORE_FLOOR)
            total[...] = jnp.zeros_like(total)
            acc[...] = jnp.zeros_like(acc)

        def visit(masked):
            key = kv_ref[0, :, :HD]
            value_t = kv_ref[0, :, HD:].T
            if masked:
                allowed = allowed_of(
                    kdoc_ref, qdoc_ref, (info_ref[0, step] - info_ref[0, 0]) * rows
                )
            for h in range(H):
                score = contract(key, q_ref[:, h * HD : (h + 1) * HD], 1, 1)
                if masked:
                    score = jnp.where(allowed, score, SCORE_FLOOR)
                old = peak[h : h + 1, :]
                new = jnp.maximum(old, jnp.max(score, axis=0, keepdims=True))
                weight = jnp.exp(score - new)
                shrink = jnp.exp(old - new)
                peak[h : h + 1, :] = new
                total[h : h + 1, :] = total[h : h + 1, :] * shrink + jnp.sum(
                    weight, axis=0, keepdims=True
                )
                acc[h] = acc[h] * shrink + contract(value_t, weight.astype(bf16), 1, 0)

        pl.when(info_ref[1, step] == WHOLE)(lambda: visit(False))
        pl.when(info_ref[1, step] == MASKED)(lambda: visit(True))

        @pl.when(step == blocks - 1)
        def _():
            lse_ref[...] = jnp.zeros_like(lse_ref)
            for h in range(H):
                lse_ref[h : h + 1, :] = peak[h : h + 1, :] + jnp.log(total[h : h + 1, :])
                o_ref[:, h * HD : (h + 1) * HD] = (acc[h] / total[h : h + 1, :]).T.astype(bf16)
            attn_out = contract(o_ref[...], w_ref[...], 1, 0)
            out_ref[...] = attn_out
            middle = tok_ref[...].astype(f32) + normed(attn_out)[0] * g_post_ref[...]
            mid_ref[...] = middle
            in_ref[...] = (normed(middle)[0] * g_fpre_ref[...]).astype(bf16)

    return pl.pallas_call(
        body,
        grid_spec=pltpu.PrefetchScalarGridSpec(
            num_scalar_prefetch=1,
            grid=(blocks,),
            in_specs=[
                same((rows, H * HD)),
                pl.BlockSpec((1, rows, 2 * HD), lambda i, info: (i, 0, 0)),
                pl.BlockSpec((rows, 1), lambda i, info: (info[0, i], 0)),
                same((1, rows)),
                same((H * HD, D)),
                same((rows, D)),
                same((1, D)),
                same((1, D)),
            ],
            out_specs=[
                same((rows, H * HD)),
                same((8, rows)),
                same((rows, D)),
                same((rows, D)),
                same((rows, D)),
            ],
            scratch_shapes=[
                pltpu.VMEM((8, rows), f32),
                pltpu.VMEM((8, rows), f32),
                pltpu.VMEM((H, HD, rows), f32),
            ],
        ),
        out_shape=(
            jax.ShapeDtypeStruct((rows, H * HD), bf16),
            jax.ShapeDtypeStruct((8, rows), f32),
            jax.ShapeDtypeStruct((rows, D), f32),
            jax.ShapeDtypeStruct((rows, D), f32),
            jax.ShapeDtypeStruct((rows, D), bf16),
        ),
        compiler_params=pltpu.CompilerParams(vmem_limit_bytes=VMEM_LIMIT),
        cost_estimate=pl.CostEstimate(flops=0, bytes_accessed=0, transcendentals=0),
        name="attend",
    )(info, query, kv, key_docs, query_docs, w_out, tokens, g_post, g_fpre)


def attend_back(
    info, query, kv, key_docs, query_docs, heads, log_total, d_in, middle, attn_out, cotangent,
    w_out, g_post, g_fpre,
):
    blocks, rows, _ = kv.shape
    terms = len(d_in)

    def body(info_ref, q_ref, kv_ref, kdoc_ref, qdoc_ref, o_ref, lse_ref, *refs):
        terms_ref = refs[:terms]
        (
            mid_ref, out_ref, cot_ref, w_ref, g_post_ref, g_fpre_ref,
            dq_ref, dkv_ref, dout_ref, dmid_ref, dg_fpre_ref, dg_post_ref, do_ref, delta_ref,
        ) = refs[terms:]
        step = pl.program_id(0)

        @pl.when(step == 0)
        def _():
            d_rows = sum(ref[...].astype(f32) for ref in terms_ref)
            unit, scale = normed(mid_ref[...])
            dg_fpre_ref[...] = jnp.sum(d_rows * unit, axis=0, keepdims=True)
            d_middle = cot_ref[...].astype(f32) + norm_back(unit, scale, d_rows * g_fpre_ref[...])
            dmid_ref[...] = d_middle
            unit, scale = normed(out_ref[...])
            dg_post_ref[...] = jnp.sum(d_middle * unit, axis=0, keepdims=True)
            d_out = norm_back(unit, scale, d_middle * g_post_ref[...]).astype(bf16)
            dout_ref[...] = d_out
            delta_ref[...] = jnp.zeros_like(delta_ref)
            for h in range(H):
                cols = slice(h * HD, (h + 1) * HD)
                d_o = contract(d_out, w_ref[cols, :], 1, 1).astype(bf16)
                do_ref[:, cols] = d_o
                each = (d_o.astype(f32) * o_ref[:, cols].astype(f32)).T
                delta_ref[h : h + 1, :] = jnp.sum(each, axis=0, keepdims=True)
            dq_ref[...] = jnp.zeros_like(dq_ref)

        def visit(masked):
            key, value = kv_ref[0, :, :HD], kv_ref[0, :, HD:]
            if masked:
                allowed = allowed_of(
                    kdoc_ref, qdoc_ref, (info_ref[0, step] - info_ref[0, 0]) * rows
                )
            d_key = jnp.zeros((rows, HD), f32)
            d_value = jnp.zeros((rows, HD), f32)
            for h in range(H):
                cols = slice(h * HD, (h + 1) * HD)
                q, d_o = q_ref[:, cols], do_ref[:, cols]
                prob = jnp.exp(contract(key, q, 1, 1) - lse_ref[h : h + 1, :])
                if masked:
                    prob = jnp.where(allowed, prob, 0.0)
                d_value = d_value + contract(prob.astype(bf16), d_o, 1, 0)
                d_prob = contract(value, d_o, 1, 1)
                d_score = (prob * (d_prob - delta_ref[h : h + 1, :])).astype(bf16)
                d_key = d_key + contract(d_score, q, 1, 0)
                dq_ref[:, cols] = dq_ref[:, cols] + contract(d_score, key, 0, 0)
            dkv_ref[0, :, :HD] = d_key.astype(bf16)
            dkv_ref[0, :, HD:] = d_value.astype(bf16)

        pl.when(info_ref[1, step] == WHOLE)(lambda: visit(False))
        pl.when(info_ref[1, step] == MASKED)(lambda: visit(True))

        @pl.when(info_ref[1, step] == DEAD)
        def _():
            dkv_ref[...] = jnp.zeros_like(dkv_ref)

        @pl.when(step == blocks - 1)
        def _():
            dq_ref[...] = dq_ref[...] * SCORE_SCALE

    block = pl.BlockSpec((1, rows, 2 * HD), lambda i, info: (i, 0, 0))
    return pl.pallas_call(
        body,
        grid_spec=pltpu.PrefetchScalarGridSpec(
            num_scalar_prefetch=1,
            grid=(blocks,),
            in_specs=[
                same((rows, H * HD)),
                block,
                pl.BlockSpec((rows, 1), lambda i, info: (info[0, i], 0)),
                same((1, rows)),
                same((rows, H * HD)),
                same((8, rows)),
                *[same((rows, D))] * (terms + 3),
                same((H * HD, D)),
                same((1, D)),
                same((1, D)),
            ],
            out_specs=[
                same((rows, H * HD)),
                block,
                same((rows, D)),
                same((rows, D)),
                same((1, D)),
                same((1, D)),
            ],
            scratch_shapes=[pltpu.VMEM((rows, H * HD), bf16), pltpu.VMEM((8, rows), f32)],
        ),
        out_shape=(
            jax.ShapeDtypeStruct((rows, H * HD), f32),
            jax.ShapeDtypeStruct(kv.shape, bf16),
            jax.ShapeDtypeStruct((rows, D), bf16),
            jax.ShapeDtypeStruct((rows, D), f32),
            jax.ShapeDtypeStruct((1, D), f32),
            jax.ShapeDtypeStruct((1, D), f32),
        ),
        compiler_params=pltpu.CompilerParams(vmem_limit_bytes=VMEM_LIMIT),
        cost_estimate=pl.CostEstimate(flops=0, bytes_accessed=0, transcendentals=0),
        name="attend_back",
    )(
        info, query, kv, key_docs, query_docs, heads, log_total, *d_in, middle, attn_out, cotangent,
        w_out, g_post, g_fpre,
    )


def gelu_parts(gate):
    scale = 0.7978845608028654
    square = gate * gate
    inner = jnp.tanh(scale * gate * (1.0 + 0.044715 * square))
    half_up = 0.5 * (1.0 + inner)
    slope = half_up + 0.5 * gate * (1.0 - inner * inner) * scale * (1.0 + 3 * 0.044715 * square)
    return gate * half_up, slope


def gather_rows(refs, held, sems):
    tok = refs[0].shape[0]
    return [
        pltpu.make_async_copy(ref, held.at[k * tok : (k + 1) * tok], sems.at[k])
        for k, ref in enumerate(refs)
    ]


def scatter_rows(held, refs, sems):
    tok = refs[0].shape[0]
    return [
        pltpu.make_async_copy(held.at[k * tok : (k + 1) * tok], ref, sems.at[k])
        for k, ref in enumerate(refs)
    ]


def by_chunk(step, chunks, copies, do):
    per = len(copies) // chunks
    for k in range(chunks):

        @pl.when(step == k)
        def _(k=k):
            for copy in copies[k * per : (k + 1) * per]:
                do(copy)


def ffn_call(name, body, rows, streams, weights, outs):
    count, (tok, wide) = len(rows), rows[0].shape
    chunks = -(-count * tok // 512)
    both = count * tok // chunks
    per = weights.shape[0]

    def kernel(*refs):
        row_refs, refs = refs[:count], refs[count:]
        stream_refs, refs = refs[: len(streams)], refs[len(streams) :]
        w_refs, refs = refs[:3], refs[3:]
        out_refs, refs = refs[: len(outs)], refs[len(outs) :]
        sum_refs, (held, given, sems_in, sems_out) = refs[:count], refs[count:]
        step = pl.program_id(0)
        coming = gather_rows(row_refs, held, sems_in)
        going = scatter_rows(given, sum_refs, sems_out)

        @pl.when(step == 0)
        def _():
            for copy in coming:
                copy.start()

        by_chunk(step, chunks, coming, lambda copy: copy.wait())
        here = pl.ds(pl.multiple_of(step * both, both), both)
        given[here, :] = body(held[here, :], stream_refs, w_refs, out_refs)
        by_chunk(step, chunks, going, lambda copy: copy.start())

        @pl.when(step == chunks - 1)
        def _():
            for copy in going:
                copy.wait()

    def chunk(width):
        return pl.BlockSpec((both, width), lambda i: (i, 0))

    anywhere = pl.BlockSpec(memory_space=pl.ANY)
    return pl.pallas_call(
        kernel,
        grid=(chunks,),
        in_specs=[anywhere] * count
        + [chunk(s.shape[1]) for s in streams]
        + [pl.BlockSpec((per, D), lambda i, k=k: (0, k)) for k in range(3)],
        out_specs=tuple([chunk(w) for w in outs] + [anywhere] * count),
        out_shape=tuple(
            [jax.ShapeDtypeStruct((count * tok, w), bf16) for w in outs]
            + [jax.ShapeDtypeStruct((tok, wide), bf16)] * count
        ),
        scratch_shapes=[
            pltpu.VMEM((count * tok, wide), bf16),
            pltpu.VMEM((count * tok, wide), bf16),
            pltpu.SemaphoreType.DMA((count,)),
            pltpu.SemaphoreType.DMA((count,)),
        ],
        compiler_params=pltpu.CompilerParams(vmem_limit_bytes=VMEM_LIMIT),
        cost_estimate=pl.CostEstimate(
            flops=6 * count * tok * per * D, bytes_accessed=0, transcendentals=0
        ),
        name=name,
    )(*rows, *streams, weights, weights, weights)


def ffn_forward(rows, weights):
    def body(x, _, w_refs, out_refs):
        act_ref, gelu_ref, slope_ref = out_refs
        gate = contract(x, w_refs[0][...], 1, 1)
        up = contract(x, w_refs[1][...], 1, 1)
        gelu, slope = gelu_parts(gate)
        act = (gelu * up).astype(bf16)
        act_ref[...] = act
        gelu_ref[...] = gelu.astype(bf16)
        slope_ref[...] = (slope * up).astype(bf16)
        return contract(act, w_refs[2][...], 1, 0).astype(bf16)

    per = weights.shape[0]
    act, gelu, slope, *parts = ffn_call("ffn_forward", body, rows, [], weights, [per] * 3)
    return act, gelu, slope, parts


def ffn_backward(rows, gelu, slope, weights):
    per = weights.shape[0]

    def body(x, stream_refs, w_refs, out_refs):
        gelu_ref, slope_ref = stream_refs
        d_act = contract(x, w_refs[2][...], 1, 1)
        d_gate = (d_act * slope_ref[...].astype(f32)).astype(bf16)
        d_up = (d_act * gelu_ref[...].astype(f32)).astype(bf16)
        out_refs[0][:, :per] = d_gate
        out_refs[0][:, per:] = d_up
        return (contract(d_gate, w_refs[0][...], 1, 0) + contract(d_up, w_refs[1][...], 1, 0)).astype(bf16)

    d_both, *parts = ffn_call("ffn_backward", body, rows, [gelu, slope], weights, [2 * per])
    return d_both, parts


def unit_grads(units, per, rows):
    parts, count = len(units), len(rows)
    tokens, wide = sum(u.shape[0] for u in units), units[0].shape[1]
    n = wide // per

    def body(*refs):
        unit_refs, row_refs = refs[:parts], refs[parts : parts + count]
        out_ref, held, sems = refs[parts + count :]
        copies = gather_rows(row_refs, held, sems)

        @pl.when(pl.program_id(0) == 0)
        def _():
            for copy in copies:
                copy.start()
            for copy in copies:
                copy.wait()

        total, at = None, 0
        for ref in unit_refs:
            part = contract(ref[...], held[at : at + ref.shape[0], :], 0, 0)
            total = part if total is None else total + part
            at += ref.shape[0]
        out_ref[...] = total.astype(bf16)

    return pl.pallas_call(
        body,
        grid=(n,),
        in_specs=[pl.BlockSpec((u.shape[0], per), lambda i: (0, i)) for u in units]
        + [pl.BlockSpec(memory_space=pl.ANY)] * count,
        out_specs=pl.BlockSpec((per, D), lambda i: (0, i)),
        out_shape=jax.ShapeDtypeStruct((per, n * D), bf16),
        scratch_shapes=[pltpu.VMEM((tokens, D), bf16), pltpu.SemaphoreType.DMA((count,))],
        compiler_params=pltpu.CompilerParams(vmem_limit_bytes=VMEM_LIMIT),
        cost_estimate=pl.CostEstimate(
            flops=2 * tokens * wide * D, bytes_accessed=0, transcendentals=0
        ),
        name="unit_grads",
    )(*units, *rows)


def after_ffn(out_parts, middle, cotangent, g_fpost):
    terms = len(out_parts)

    def body(*refs):
        mid_ref, cot_ref, g_ref, mixed_ref, d_ref, dg_ref = refs[terms:]
        total = refs[0][...].astype(f32)
        for ref in refs[1:terms]:
            total = total + ref[...].astype(f32)
        unit, scale = normed(total)
        mixed_ref[...] = (mid_ref[...] + unit * g_ref[...]).astype(bf16)
        upstream = cot_ref[...].astype(f32)
        dg_ref[...] = jnp.sum(upstream * unit, axis=0, keepdims=True)
        d_ref[...] = norm_back(unit, scale, upstream * g_ref[...]).astype(bf16)

    shape = out_parts[0].shape
    return run(
        "after_ffn",
        body,
        [*out_parts, middle, cotangent, g_fpost],
        "v" * (terms + 3),
        [(shape, bf16), (shape, bf16), ((1, D), f32)],
    )


def query_side(flat, d_query, raw, cosine, sine, g_q, a, w_qkv, heads, d_attn_out):
    tok = a.shape[0]
    wide = H * HD

    def body(
        dq_ref, raw_ref, cos_ref, sin_ref, g_ref, a_ref, w_ref, o_ref, dout_ref,
        lines, da_ref, dg_ref, low, grad, grad_o,
    ):
        cos, sin = cos_ref[...], sin_ref[...]
        dg = jnp.zeros((1, HD), f32)
        for h in range(H):
            cols = slice(h * HD, (h + 1) * HD)
            unit, scale = normed(raw_ref[:, cols])
            turned = rotate(dq_ref[:, cols], cos, -sin)
            dg = dg + jnp.sum(turned * unit, axis=0, keepdims=True)
            low[:, cols] = norm_back(unit, scale, turned * g_ref[...]).astype(bf16)
        dg_ref[...] = dg
        da_ref[...] = contract(low[...], w_ref[:, :wide], 1, 1)
        grad[...] = contract(a_ref[...], low[...], 0, 0)
        for j in range(wide // LANES):
            lines[pl.ds(j, D, stride=flat.q_across), :] = grad[:, j * LANES : (j + 1) * LANES]
        grad_o[...] = contract(o_ref[...], dout_ref[...], 0, 0)
        for j in range(flat.o_across):
            lines[pl.ds(flat.q_lines + j, wide, stride=flat.o_across), :] = grad_o[
                :, j * LANES : (j + 1) * LANES
            ]
        lines[flat.q_lines + flat.o_lines :, :] = jnp.zeros((16, LANES), f32)

    return run(
        "query_side",
        body,
        [d_query, raw, cosine, sine, g_q, a, w_qkv, heads, d_attn_out],
        "v" * 9,
        [((flat.q_lines + flat.o_lines + 16, LANES), f32), ((tok, D), f32), ((1, HD), f32)],
        [pltpu.VMEM((tok, wide), bf16), pltpu.VMEM((D, wide), f32), pltpu.VMEM((wide, D), f32)],
    )


def last_part(
    flat, order, groups, lines, kv_parts, raw, cosine, sine, g_k, a, w_qkv, tokens, g_pre, d_middle,
    da_query, gain_grads,
):
    tok = a.shape[0]
    terms = len(kv_parts)
    wide = H * HD
    each = flat.devices // groups

    def body(order_ref, lines_ref, *refs):
        kv_refs = refs[:terms]
        (
            raw_ref, cos_ref, sin_ref, gk_ref, a_ref, w_ref, tok_ref, gpre_ref, dmid_ref, da_ref,
            dgq, dgpost, dgfpre, dgfpost, in_ref, *outs, held, grad, gains, blocks, sems,
        ) = refs[terms:]
        q_copy = pltpu.make_async_copy(
            lines_ref.at[: flat.q_lines], held.at[: flat.q_lines], sems.at[0]
        )
        o_copy = pltpu.make_async_copy(
            lines_ref.at[flat.q_lines :], held.at[flat.q_lines :], sems.at[1]
        )
        q_copy.start()
        o_copy.start()
        d_kv = kv_refs[0][...].astype(f32)
        for ref in kv_refs[1:]:
            d_kv = d_kv + ref[...].astype(f32)
        unit, scale = normed(raw_ref[:, wide:])
        turned = rotate(d_kv[:, :HD], cos_ref[...], -sin_ref[...])
        dgk = jnp.sum(turned * unit, axis=0, keepdims=True)
        low = jnp.concatenate(
            [norm_back(unit, scale, turned * gk_ref[...]).astype(bf16), d_kv[:, HD:].astype(bf16)],
            axis=1,
        )
        grad[...] = contract(a_ref[...], low, 0, 0)
        d_a = da_ref[...] + contract(low, w_ref[:, wide:], 1, 1)
        unit, scale = normed(tok_ref[...].astype(f32))
        dgpre = jnp.sum(d_a * unit, axis=0, keepdims=True)
        in_ref[...] = (dmid_ref[...] + norm_back(unit, scale, d_a * gpre_ref[...])).astype(bf16)
        gains[...] = jnp.zeros_like(gains)
        at = 0
        for value in (dgpre, dgq[...], dgk, dgpost[...], dgfpre[...], dgfpost[...]):
            for i in range(value.shape[1] // LANES):
                gains[at : at + 1, :] = value[:, i * LANES : (i + 1) * LANES]
                at += 1
        q_copy.wait()
        for j in range(2 * HD // LANES):
            held[pl.ds(wide // LANES + j, D, stride=flat.q_across), :] = grad[
                :, j * LANES : (j + 1) * LANES
            ]
        o_copy.wait()
        for i in range(flat.devices):
            at = i * flat.lines
            blocks[i, : flat.gain_at, :] = held[at : at + flat.gain_at, :].astype(bf16)
            at = flat.gain_line(i)
            blocks[i, flat.gain_at :, :] = gains[at : at + 16, :].astype(bf16)
        copies = [
            pltpu.make_async_copy(
                blocks.at[order_ref[k]], outs[k // each].at[k % each], sems.at[2 + k]
            )
            for k in range(flat.devices)
        ]
        for copy in copies:
            copy.start()
        for copy in copies:
            copy.wait()

    return run(
        "last_part",
        body,
        [order, lines, *kv_parts, raw, cosine, sine, g_k, a, w_qkv, tokens, g_pre, d_middle]
        + [da_query, *gain_grads],
        "sh" + "v" * (terms + 14),
        [((tok, D), bf16)] + [((each, flat.rows, LANES), bf16)] * groups,
        [
            pltpu.VMEM(lines.shape, f32),
            pltpu.VMEM((D, 2 * HD), f32),
            pltpu.VMEM((-(-(flat.gain_lines + 16) // 8) * 8, LANES), f32),
            pltpu.VMEM((flat.devices, flat.rows, LANES), bf16),
            pltpu.SemaphoreType.DMA((2 + flat.devices,)),
        ],
        "v" + "h" * groups,
    )


class Ways:
    def __init__(self, sizes):
        self.sizes = sizes
        self.what = ""

    def size(self, axis):
        if isinstance(axis, str):
            return self.sizes[axis]
        n = 1
        for a in axis:
            n *= self.sizes[a]
        return n

    def fro(self, value, axis, offset):
        n = self.size(axis)
        if offset % n == 0:
            return value
        with jax.named_scope(self.what + "_" + "".join(axis) + str(offset)):
            return lax.ppermute(value, axis, [((i + offset) % n, i) for i in range(n)])

    def places(self):
        nx, ny = self.sizes["x"], self.sizes["y"]
        return [(ox, oy) for ox in range(nx) for oy in range(ny)]

    def outers(self):
        return [(ou, ov) for ou in range(self.sizes["u"]) for ov in range(self.sizes["v"])]

    def plane_gather(self, value, beside=None):
        nx, ny = self.sizes["x"], self.sizes["y"]
        half = halfway(value.shape[0])
        found = {(0, 0): value}
        for ox in range(1, nx):
            found[ox, 0] = self.fro(value, "x", ox)
        for oy in range(1, ny):
            found[0, oy] = self.fro(value, "y", oy)
        if beside is not None:
            found, beside = lax.optimization_barrier((found, beside))
        for ox in range(1, nx):
            for oy in range(1, ny):
                first = self.fro(found[ox, 0][:half], "y", oy)
                second = self.fro(found[0, oy][half:], "x", ox)
                found[ox, oy] = jnp.concatenate([first, second], axis=0)
        found = {at: [block, self.fro(block, "c", 1)] for at, block in found.items()}
        return found if beside is None else (found, beside)

    def plane_scatter(self, parts, beside=None):
        nx, ny = self.sizes["x"], self.sizes["y"]
        low = {
            at: add_low(parts[at][0], self.fro(parts[at][1], "c", 1))
            for at in sorted(parts, reverse=True)
        }
        half = halfway(low[0, 0].shape[0])
        along_x = {ox: [low[ox, 0][:half]] for ox in range(1, nx)}
        along_y = {oy: [low[0, oy][half:]] for oy in range(1, ny)}
        for ox in range(1, nx):
            for oy in range(1, ny):
                along_x[ox].append(self.fro(low[ox, oy][:half], "y", -oy))
                along_y[oy].append(self.fro(low[ox, oy][half:], "x", -ox))
        if beside is not None:
            along_x, along_y, beside = lax.optimization_barrier((along_x, along_y, beside))
        terms = [low[0, 0]]
        for ox in range(1, nx):
            whole = jnp.concatenate([add_low(*along_x[ox]), low[ox, 0][half:]], axis=0)
            terms.append(self.fro(whole, "x", -ox))
        for oy in range(1, ny):
            whole = jnp.concatenate([low[0, oy][:half], add_low(*along_y[oy])], axis=0)
            terms.append(self.fro(whole, "y", -oy))
        return terms if beside is None else (terms, beside)

    def z_begin(self, value):
        n = self.sizes["z"]
        if n != 4:
            return ()
        return self.fro(value, "z", 1), self.fro(value, "z", -1)

    def z_end(self, value, begun, halves=None):
        n = self.sizes["z"]
        if n != 4:
            return [self.fro(value, "z", oz) for oz in range(n)]
        above, below = begun
        half = halfway(value.shape[0])
        first, second = self.fro(above[:half], "z", 1), self.fro(below[half:], "z", -1)
        return [value, above, jnp.concatenate([first, second], axis=0), below]

    def z_gather(self, value):
        return self.z_end(value, self.z_begin(value))

    def z_pair(self, one, other, begun_one, begun_other):
        if self.sizes["z"] != 4:
            return self.z_end(one, ()), self.z_end(other, ())
        far_one = self.fro(begun_one[0], "z", 1)
        far_other = self.fro(begun_other[1], "z", -1)
        return [one, begun_one[0], far_one, begun_one[1]], [
            other, begun_other[0], far_other, begun_other[1]
        ]

    def z_scatter_begin(self, parts):
        if self.sizes["z"] != 4:
            return ()
        half = halfway(parts[0].shape[0])
        return self.fro(parts[2][:half], "z", -1), self.fro(parts[2][half:], "z", 1)

    def z_scatter_go(self, parts, begun):
        n = self.sizes["z"]
        if n != 4:
            return [self.fro(parts[oz], "z", -oz) for oz in range(1, n)]
        half = halfway(parts[0].shape[0])
        above = jnp.concatenate([add_low(parts[1][:half], begun[0]), parts[1][half:]], axis=0)
        below = jnp.concatenate([parts[3][:half], add_low(parts[3][half:], begun[1])], axis=0)
        return [self.fro(above, "z", -1), self.fro(below, "z", 1)]

    def z_scatter(self, parts):
        return [parts[0], *self.z_scatter_go(parts, self.z_scatter_begin(parts))]


SEQ = ("u", "y", "c")
CTX = ("z", "v", "x")
ACROSS = ("v", "x")


def make_shards(sizes):
    ways = Ways(sizes)
    ns, nctx, nx = ways.size(SEQ), ways.size(CTX), ways.size(ACROSS)
    nz, nc = sizes["z"], sizes["c"]
    devices = ns * nctx
    places, outers = ways.places(), ways.outers()

    def from_outers(value):
        if len(outers) == 1:
            return value
        return jnp.concatenate(
            [ways.fro(ways.fro(value, "u", ou), "v", ov) for ou, ov in outers], axis=0
        )

    def to_outers(value):
        if len(outers) == 1:
            return value
        rows = value.shape[0] // len(outers)
        return add_low(
            *[
                ways.fro(ways.fro(value[i * rows : (i + 1) * rows], "u", -ou), "v", -ov)
                for i, (ou, ov) in enumerate(outers)
            ]
        )

    def plane_rows(value):
        found = ways.plane_gather(value)
        return [block for p in places for block in found[p]]

    def by_device(parts):
        return {p: parts[i * nc : (i + 1) * nc] for i, p in enumerate(places)}

    def own_units(grad):
        return lax.psum_scatter(to_outers(grad), "z", scatter_dimension=0, tiled=True)

    def shards(
        tokens, cotangent, segments, positions, attn_w, attn_m, attn_v,
        mlp_w, mlp_m, mlp_v, gains, gain_m, gain_v,
    ):
        at = {a: lax.axis_index(a) for a in sizes}
        seq_place = lax.axis_index(SEQ)
        across_place = lax.axis_index(ACROSS)
        ctx_place = at["z"] * nx + across_place
        device = seq_place * nctx + ctx_place
        piece, gain_piece = attn_w.shape[0], gains.shape[0]
        flat = Flat(piece, gain_piece, devices)

        sides = [sizes[a] for a in ("x", "y", "c", "u", "v", "z")]
        here = [at[a] for a in ("x", "y", "c", "u", "v", "z")]
        ox, oy, oc, ou, ov, oz = (
            (jnp.asarray(o, jnp.int32) + h) % n
            for o, h, n in zip(np.unravel_index(np.arange(devices), sides), here, sides)
        )
        order = ((ou * sizes["y"] + oy) * sizes["c"] + oc) * nz + oz
        order = (order * sizes["v"] + ov) * sizes["x"] + ox

        ways.what = "attn_gather"
        gain_offset = gain_piece * device % LANES
        gain_window = lax.dynamic_update_slice(
            jnp.zeros((16 * LANES,), bf16), gains.astype(bf16), (gain_offset,)
        )
        low_piece = jnp.concatenate(
            [
                jnp.pad(
                    attn_w.astype(bf16).reshape(flat.lines, LANES),
                    ((0, flat.gain_at - flat.lines), (0, 0)),
                ),
                gain_window.reshape(16, LANES),
            ],
            axis=0,
        )
        line_blocks = ways.z_gather(low_piece)

        ways.what = "unit_exchange"
        units, width = mlp_w.shape
        share = units // ns
        held = -(-share // 32) * 32

        def seq_send(by_place):
            return [
                ways.fro(
                    lax.dynamic_index_in_dim(by_place, (seq_place - offset) % ns, 0, keepdims=False),
                    SEQ,
                    offset,
                )
                for offset in range(ns)
            ]

        def seq_place_all(heard):
            kept = jnp.zeros((ns,) + heard[0].shape, heard[0].dtype)
            for offset, value in enumerate(heard):
                kept = lax.dynamic_update_index_in_dim(kept, value, (seq_place + offset) % ns, 0)
            return kept

        heard = seq_send(mlp_w.astype(bf16).reshape(ns, share, width))
        line_blocks, heard = lax.optimization_barrier((line_blocks, heard))
        by_cols = seq_place_all(heard)
        rows_own = jnp.concatenate([by_cols[i] for i in range(ns)], axis=1)
        rows_own = jnp.pad(rows_own, ((0, held - share), (0, 0)))
        ways.what = "attn_gather"
        line_z = from_outers(jnp.concatenate(line_blocks, axis=0))
        gathered = ways.plane_gather(line_z)
        line_parts = [part.reshape(-1, flat.rows, LANES) for p in places for part in gathered[p]]
        units_here = from_outers(lax.all_gather(rows_own, "z", axis=0, tiled=True))

        tok_rows = tokens.shape[1]
        cosine, sine = angles(positions[0])
        (
            w_qkv, g_pre, g_q, g_k, g_post, g_fpre, g_fpost, normed_in, query, kv_local, raw,
        ) = first_part(flat, line_parts, order, tokens[0], cosine, sine)
        w_out = spread_out(flat, [after(part, kv_local) for part in line_parts], order)
        ways.what = "kv_gather"
        kv_all = jnp.stack(
            [ways.fro(block, ACROSS, oa) for block in ways.z_gather(kv_local) for oa in range(nx)]
        )

        doc_all = segments[0]
        first_docs, last_docs = doc_all[::tok_rows], doc_all[tok_rows - 1 :: tok_rows]
        key_at = np.arange(nctx)
        key_place = (at["z"] + jnp.asarray(key_at // nx, jnp.int32)) % nz * nx
        key_place = key_place + (across_place + jnp.asarray(key_at % nx, jnp.int32)) % nx
        is_place = key_place[:, None] == jnp.arange(nctx, dtype=jnp.int32)[None, :]
        key_first = jnp.sum(jnp.where(is_place, first_docs[None, :], 0), axis=1)
        key_last = jnp.sum(jnp.where(is_place, last_docs[None, :], 0), axis=1)
        live = (key_place < ctx_place) & (key_last >= key_first[0])
        one_doc = key_first == key_last[0]
        task = jnp.where(live, jnp.where(one_doc, WHOLE, MASKED), DEAD)
        task = jnp.where(key_place == ctx_place, MASKED, task)
        info = jnp.stack([key_place, task]).astype(jnp.int32)
        key_docs = doc_all[:, None]
        query_docs = lax.dynamic_slice_in_dim(doc_all, ctx_place * tok_rows, tok_rows)[None]

        heads, log_total, attn_out, middle, ffn_in = attend(
            info, query, kv_all, key_docs, query_docs, w_out, tokens[0], g_post, g_fpre
        )

        ways.what = "ffn_in_gather"
        ffn_rows = plane_rows(ffn_in)
        act, gelu, slope, parts = ffn_forward(ffn_rows, units_here)
        ways.what = "ffn_out_sum"
        out_parts = ways.plane_scatter(by_device(parts))
        mixed, d_mlp_out, d_gfpost = after_ffn(out_parts, middle, cotangent[0], g_fpost)

        ways.what = "d_out_gather"
        d_out_rows = plane_rows(d_mlp_out)
        held_here = units_here.shape[0]
        d_w_down = unit_grads([act], held_here, d_out_rows)
        ways.what = "ffn_grad_sum"
        owned_down = own_units(d_w_down)
        d_out_rows[0] = after(d_out_rows[0], d_w_down)
        d_both, parts = ffn_backward(d_out_rows, gelu, slope, units_here)
        ways.what = "d_in_sum"
        d_in_parts, d_both = ways.plane_scatter(by_device(parts), d_both)

        d_w_gate_up = unit_grads([d_both], held_here, ffn_rows)
        owned_gate_up = own_units(d_w_gate_up)
        d_in_parts = lax.optimization_barrier((d_in_parts, d_w_gate_up))[0]

        d_query, d_kv, d_attn_out, d_middle, d_gfpre, d_gpost = attend_back(
            info, query, kv_all, key_docs, query_docs, heads, log_total, d_in_parts, middle, attn_out,
            cotangent[0], w_out, g_post, g_fpre,
        )
        ways.what = "kv_sum"
        d_kv = d_kv.reshape(nz, nx, tok_rows, 2 * HD)
        kv_parts = {}
        for oz in sorted(range(nz), key=lambda o: abs(o - nz // 2)):
            kv_parts[oz] = add_low(*[ways.fro(d_kv[oz, oa], ACROSS, -oa) for oa in range(nx)])
        kv_parts[0], owned_down = lax.optimization_barrier((kv_parts[0], owned_down))
        kv_parts = ways.z_scatter([kv_parts[oz] for oz in range(nz)])
        lines, da_query, d_gq = query_side(
            flat, d_query, raw, cosine, sine, g_q, normed_in, w_qkv, heads, d_attn_out
        )
        input_grad, *packed = last_part(
            flat, order, len(places) * nc, lines, kv_parts, raw, cosine, sine, g_k, normed_in, w_qkv, tokens[0],
            g_pre, d_middle, da_query, [d_gq, d_gpost, d_gfpre, d_gfpost],
        )

        ways.what = "attn_grad_sum"
        packed[0], owned_gate_up = lax.optimization_barrier((packed[0], owned_gate_up))
        packed = [part.reshape(-1, LANES) for part in packed]
        plane_sum = add_low(
            *ways.plane_scatter(
                {p: packed[i * nc : (i + 1) * nc] for i, p in enumerate(places)}
            )
        )
        plane_sum = to_outers(plane_sum)
        red = sum(
            part.astype(f32)
            for part in ways.z_scatter(
                [plane_sum[oz * flat.rows : (oz + 1) * flat.rows] for oz in range(nz)]
            )
        )
        attn_red = red[: flat.lines].reshape(-1)
        gain_red = lax.dynamic_slice(red[flat.gain_at :].reshape(-1), (gain_offset,), (gain_piece,))

        ways.what = "grad_exchange"
        own_rows = jnp.concatenate([owned_gate_up[:share], owned_down[:share]], axis=1)
        by_cols = jnp.stack([own_rows[:, i * width : (i + 1) * width] for i in range(ns)])
        mlp_red = seq_place_all(seq_send(by_cols)).astype(f32).reshape(units, width)

        attn_m_new, attn_v_new, attn_new = adam_update(
            attn_w, attn_m, attn_v, attn_red, RATE_MATRIX, DECAY_MATRIX
        )
        mlp_m_new, mlp_v_new, mlp_new = adam_update(
            mlp_w, mlp_m, mlp_v, mlp_red, RATE_MATRIX, DECAY_MATRIX
        )
        gain_m_new, gain_v_new, gain_new = adam_update(
            gains, gain_m, gain_v, gain_red, RATE_GAIN, 0.0
        )
        return (
            mixed[None], input_grad[None],
            attn_red, attn_m_new, attn_v_new, attn_new,
            mlp_red, mlp_m_new, mlp_v_new, mlp_new,
            gain_red, gain_m_new, gain_v_new, gain_new,
        )

    return shards


def solution(mesh):
    seq, ctx = mesh.shape["seq"], mesh.shape["ctx"]
    nz = 4 if ctx % 4 == 0 else 1
    chips_y, chips_x = seq // 2, ctx // nz
    y, x = 2 - chips_y % 2, 2 - chips_x % 2
    sizes = {"u": chips_y // y, "y": y, "c": 2, "z": nz, "v": chips_x // x, "x": x}
    fine = Mesh(mesh.devices.reshape(*sizes.values()), tuple(sizes))
    s, x = SEQ, CTX
    both = s + x
    in_specs = (
        P(s, x, None), P(s, x, None), P(s, None), P(s, x),
        P(both), P(both), P(both),
        P(x, s), P(x, s), P(x, s),
        P(both), P(both), P(both),
    )
    out_specs = (
        P(s, x, None), P(s, x, None),
        P(both), P(both), P(both), P(both),
        P(x, s), P(x, s), P(x, s), P(x, s),
        P(both), P(both), P(both), P(both),
    )
    return jax.shard_map(
        make_shards(sizes), mesh=fine, in_specs=in_specs, out_specs=out_specs, check_vma=False
    )
```

time: 559 us -> 509 us (0.911)
  Pallas kernels: 32.2 us -> 141 us
  matrix products: 84 us -> 0 us
  local copies, waits for them, and re-layouts: 46.4 us -> 20.6 us
  starting transfers between devices: 111 us -> 87 us
  other arithmetic: 42.4 us -> 23.5 us
  waiting for transfers between devices: 231 us -> 214 us
  between operations: 4.13 us -> 15.6 us
    pallas_call x2 -> x9, Pallas kernels: 15.8 us -> 117 us  [the longest x2 49.1 us: ffn_call(): pl.pallas_call(kernel, grid=(chunks,), in_specs=[anywhere] * count + [chu...]
    dot_general x33 -> x0, matrix products: 84 us -> none  [the longest x31 78.8 us: contract(): lax.dot_general(left, right, (((left_dim,), (right_dim,)), ((), ())), pre...]
    ppermute x98 -> x78, starting transfers between devices: 111 us -> 86.9 us  [fro(): return lax.ppermute(value, axis, [((i + offset) % n, i) for i in range(n)])]
    ppermute x98 -> x78, waiting for transfers between devices: 231 us -> 213 us  [fro(): return lax.ppermute(value, axis, [((i + offset) % n, i) for i in range(n)])]
    unnamed x309 -> x142, local copies, waits for them, and re-layouts: 19.1 us -> 9.85 us
    unnamed x21 -> x0, other arithmetic: 8.21 us -> none
    reduce_sum x10 -> x0, other arithmetic: 6.79 us -> none  [the longest x1 1.91 us: shards(): d_gfpost = jnp.sum(upstream * unit_out, axis=0)]
    slice x29 -> x12, local copies, waits for them, and re-layouts: 6.28 us -> 0.2 us  [the longest x2 0.09 us: plane_scatter(): along_y[oy].append(self.fro(low[ox, oy][half:], 'x', -ox))]
  transfers between devices with their start and end apart: 98 -> 81, of which waited for: 44 -> 51; matrix products, arithmetic and copies ran while one was open for 28% -> 5% of each run, Pallas kernels for 6% -> 15%
where the time goes in v2:
time: 509 us; the launch traced here: 502 us
  waiting for transfers between devices  214 us (42%)
  Pallas kernels  141 us (28%)
  starting transfers between devices  87 us (17%)
  other arithmetic  23.5 us (5%)
  local copies, waits for them, and re-layouts  20.6 us (4%)
  between operations  15.6 us (3%)
    ppermute x78, waiting for transfers between devices, fro(): return lax.ppermute(value, axis, [((i + offset) % n, i) for i in range(n)])  213 us
    ppermute x78, starting transfers between devices, fro(): return lax.ppermute(value, axis, [((i + offset) % n, i) for i in range(n)])  86.9 us
    pallas_call x2, Pallas kernels, ffn_call(): pl.pallas_call(kernel, grid=(chunks,), in_specs=[anywhere] * count + [chu...  49.1 us
    pallas_call x5, Pallas kernels, run(): pl.pallas_call(body, out_shape=tuple((jax.ShapeDtypeStruct(s, d) for s, d...  41.3 us
    pallas_call x2, Pallas kernels, unit_grads(): pl.pallas_call(body, grid=(n,), in_specs=[pl.BlockSpec((u.shape[0], per),...  26.8 us
    pallas_call x1, Pallas kernels, attend_back(): pl.pallas_call(body, grid_spec=pltpu.PrefetchScalarGridSpec(num_scalar_pr...  13.8 us
    pallas_call x1, Pallas kernels, attend(): pl.pallas_call(body, grid_spec=pltpu.PrefetchScalarGridSpec(num_scalar_pr...  10.2 us
  transfers between devices with their start and end apart: 81, of which 51 were waited for; matrix products, arithmetic and copies ran while one was open for 5% of the time, Pallas kernels for 15%

profile of v2, /device:TPU:0, one launch (start us, length us, event | category | flops | bytes accessed | tf_op | source)
XLA Modules:
  0.0 502.3 jit_solution(12910175108867068675)
XLA Ops:
  9.2 5.1 %collective-permute-start = (bf16[736,128]{1,0:T(8,128)(2,1)S(1)}, bf16[736,128]{1,0:T(8,128)(2,1)S(1)}, u32[]{:S(2)}, u32[]{:S(2)}) collective-permute-start(bf16[736,128]{1,0:T(8,128)(2,1)S(1)} %pad_maximum_fusion.10), channel_id=1, source_target_pairs={{2,0},{4,2},{6,4},{0,6},{3,1},{5,3},{7,5},{1,7},{10,8},{12,10},{14... | collective-permute-start | bytes 565256 | tf_op jit(solution)/shard_map/attn_gather_z1/ppermute | solution.py:774
  19.5 4.3 collective-permute-start.1
  26.9 3.4 collective-permute-done.3
  30.3 7.0 %collective-permute-done.5 = bf16[216,864]{1,0:T(8,128)(2,1)S(1)} collective-permute-done((bf16[216,864]{1,0:T(8,128)(2,1)}, bf16[216,864]{1,0:T(8,128)(2,1)S(1)}, u32[]{:S(2)}, u32[]{:S(2)}) %collective-permute-start.5) | collective-permute-done | bytes 373280 | tf_op jit(solution)/shard_map/unit_exchange_uyc2/ppermute | solution.py:774
  44.0 14.9 %collective-permute-done.10 = bf16[2944,128]{1,0:T(8,128)(2,1)S(1)} collective-permute-done((bf16[2944,128]{1,0:T(8,128)(2,1)S(1)}, bf16[2944,128]{1,0:T(8,128)(2,1)S(1)}, u32[]{:S(2)}, u32[]{:S(2)}) %collective-permute-start.10) | collective-permute-done | bytes 753696 | tf_op jit(solution)/shard_map/attn_gather_x1/ppermute | solution.py:774
  63.8 4.3 collective-permute-done.12
  74.3 8.9 %first_part.1 = (bf16[1152,1536]{1,0:T(8,128)(2,1)}, f32[1,1152]{1,0:T(1,128)}, f32[1,256]{1,0:T(1,128)}, f32[1,256]{1,0:T(1,128)}, f32[1,1152]{1,0:T(1,128)}, /...) custom-call(s32[32]{0:T(128)} %fusion.15.order_ref, ...), custom_call_target="tpu_custom_call" | custom-call | tf_op jit(solution)/shard_map/first_part/pallas_call | solution.py:89
  83.3 3.6 collective-permute-start.16
  90.3 6.0 %spread_out.1.w_ref.refs_6_ = bf16[1024,1152]{1,0:T(8,128)(2,1)} custom-call(s32[32]{0:T(128)} %fusion.15.order_ref, bf16[4,736,128]{2,1,0:T(8,128)(2,1)} %bitcast.151, bf16[4,736,128]{2,1,0:T(8,128)(2,1)} %bitcast.153, bf16[4,736,128]{2,1,0:T(8,128)(2,1)} %bitcast.147, bf16[4,736,128]{2,1,0:T(8,128)(2,1)} %bitcast.155, bf16[4,736,128]{2,1,0:T(8,128)(2,1)} %bitcast.145, ...), custom_call_target="tpu_custom_call" | custom-call | tf_op jit(solution)/shard_map/spread_out/pallas_call | solution.py:89
  96.4 11.5 %collective-permute-done.16 = bf16[256,512]{1,0:T(8,128)(2,1)S(1)} collective-permute-done((bf16[256,512]{1,0:T(8,128)(2,1)}, bf16[256,512]{1,0:T(8,128)(2,1)S(1)}, u32[]{:S(2)}, u32[]{:S(2)}) %collective-permute-start.16) | collective-permute-done | bytes 262176 | tf_op jit(solution)/shard_map/kv_gather_z1/ppermute | solution.py:774
  107.9 3.1 collective-permute-done.19
  111.1 2.5 collective-permute-start.20
  115.7 7.9 %collective-permute-done.18 = bf16[128,512]{1,0:T(8,128)(2,1)S(1)} collective-permute-done((bf16[128,512]{1,0:T(8,128)(2,1)S(1)}, bf16[128,512]{1,0:T(8,128)(2,1)S(1)}, u32[]{:S(2)}, u32[]{:S(2)}) %collective-permute-start.18) | collective-permute-done | bytes 131104 | tf_op jit(solution)/shard_map/kv_gather_z1/ppermute | solution.py:774
  125.0 7.4 %collective-permute-done.21 = bf16[256,512]{1,0:T(8,128)(2,1)S(1)} collective-permute-done((bf16[256,512]{1,0:T(8,128)(2,1)S(1)}, bf16[256,512]{1,0:T(8,128)(2,1)S(1)}, u32[]{:S(2)}, u32[]{:S(2)}) %collective-permute-start.21) | collective-permute-done | bytes 262176 | tf_op jit(solution)/shard_map/kv_gather_vx1/ppermute | solution.py:774
  133.8 10.2 %attend.1 = (bf16[256,1024]{1,0:T(8,128)(2,1)}, f32[8,256]{1,0:T(8,128)}, f32[256,1152]{1,0:T(8,128)}, f32[256,1152]{1,0:T(8,128)}, bf16[256,1152]{1,0:T(8,128)(2,1)}) custom-call(s32[2,8]{1,0:T(2,128)} %pad_add_fusion.info_ref, bf16[256,1024]{1,0:T(8,128)(2,1)} %get-tuple-element.104.q_ref, bf16[8,256,512]{2,1,0:T(8,128)(2,1)} %copy-done.1, ...), custom_call_target="tpu_custom_call" | custom-call | tf_op jit(solution)/shard_map/attend/pallas_call | solution.py:288
  144.0 2.4 collective-permute-start.26
  147.2 12.0 %collective-permute-done.26.refs_4_.refs_5_ = bf16[256,1152]{1,0:T(8,128)(2,1)S(1)} collective-permute-done((bf16[256,1152]{1,0:T(8,128)(2,1)}, bf16[256,1152]{1,0:T(8,128)(2,1)S(1)}, u32[]{:S(2)}, u32[]{:S(2)}) %collective-permute-start.26) | collective-permute-done | bytes 589856 | tf_op jit(solution)/shard_map/ffn_in_gather_x1/ppermute | solution.py:774
  161.9 5.1 %collective-permute-done.28 = bf16[128,1152]{1,0:T(8,128)(2,1)S(1)} collective-permute-done((bf16[128,1152]{1,0:T(8,128)(2,1)S(1)}, bf16[128,1152]{1,0:T(8,128)(2,1)S(1)}, u32[]{:S(2)}, u32[]{:S(2)}) %collective-permute-start.28) | collective-permute-done | bytes 294944 | tf_op jit(solution)/shard_map/ffn_in_gather_y1/ppermute | solution.py:774
  171.7 24.9 %ffn_forward.1 = (bf16[2048,896]{1,0:T(8,128)(2,1)}, bf16[2048,896]{1,0:T(8,128)(2,1)}, bf16[2048,896]{1,0:T(8,128)(2,1)}, bf16[256,1152]{1,0:T(8,128)(2,1)}, bf...) custom-call(bf16[256,1152]{1,0:T(8,128)(2,1)} %get-tuple-element.116, ...), custom_call_target="tpu_custom_call" | custom-call | flops 12683575296 | tf_op jit(solution)/shard_map/ffn_forward/pallas_call | solution.py:512
  203.6 5.7 %collective-permute-done.37 = bf16[128,1152]{1,0:T(8,128)(2,1)S(1)} collective-permute-done((bf16[128,1152]{1,0:T(8,128)(2,1)S(1)}, bf16[128,1152]{1,0:T(8,128)(2,1)S(1)}, u32[]{:S(2)}, u32[]{:S(2)}) %collective-permute-start.37) | collective-permute-done | bytes 294944 | tf_op jit(solution)/shard_map/ffn_out_sum_x-1/ppermute | solution.py:774
  213.6 10.5 %collective-permute-done.38.refs_2_ = bf16[256,1152]{1,0:T(8,128)(2,1)S(1)} collective-permute-done((bf16[256,1152]{1,0:T(8,128)(2,1)S(1)}, bf16[256,1152]{1,0:T(8,128)(2,1)S(1)}, u32[]{:S(2)}, u32[]{:S(2)}) %collective-permute-start.38) | collective-permute-done | bytes 589856 | tf_op jit(solution)/shard_map/ffn_out_sum_y-1/ppermute | solution.py:774
  226.3 3.7 after_ffn.1
  232.0 11.5 %collective-permute-done.42.refs_5_.refs_4_ = bf16[256,1152]{1,0:T(8,128)(2,1)S(1)} collective-permute-done((bf16[256,1152]{1,0:T(8,128)(2,1)}, bf16[256,1152]{1,0:T(8,128)(2,1)S(1)}, u32[]{:S(2)}, u32[]{:S(2)}) %collective-permute-start.42) | collective-permute-done | bytes 589856 | tf_op jit(solution)/shard_map/d_out_gather_x1/ppermute | solution.py:774
  246.6 4.3 collective-permute-done.44
  255.7 10.6 %unit_grads.2 = bf16[896,1152]{1,0:T(8,128)(2,1)} custom-call(bf16[2048,896]{1,0:T(8,128)(2,1)} %get-tuple-element.135.refs_0_, bf16[256,1152]{1,0:T(8,128)(2,1)} %get-tuple-element.136.refs_1_.refs_0_, bf16[256,1152]{1,0:T(8,128)(2,1)} %copy-done.60, bf16[256,1152]{1,0:T(8,128)(2,1)} %copy-done.42, bf16[256,1152]{1,0:T(8,128)(2,1)} %copy-done.61, ...), custom_call_target="tpu_custom_call" | custom-call | flops 4227858432 | tf_op jit(solution)/shard_map/unit_grads/pallas_call | solution.py:594
  266.3 24.3 %ffn_backward.1 = (bf16[2048,1792]{1,0:T(8,128)(2,1)}, bf16[256,1152]{1,0:T(8,128)(2,1)}, bf16[256,1152]{1,0:T(8,128)(2,1)}, bf16[256,1152]{1,0:T(8,128)(2,1)}, ...) custom-call(bf16[256,1152]{1,0:T(8,128)(2,1)} %get-tuple-element.136, ...), custom_call_target="tpu_custom_call" | custom-call | flops 12683575296 | tf_op jit(solution)/shard_map/ffn_backward/pallas_call | solution.py:512
  295.4 6.8 %collective-permute-done.50 = bf16[128,1152]{1,0:T(8,128)(2,1)S(1)} collective-permute-done((bf16[128,1152]{1,0:T(8,128)(2,1)S(1)}, bf16[128,1152]{1,0:T(8,128)(2,1)S(1)}, u32[]{:S(2)}, u32[]{:S(2)}) %collective-permute-start.50) | collective-permute-done | bytes 294944 | tf_op jit(solution)/shard_map/d_in_sum_y-1/ppermute | solution.py:774
  304.6 16.2 %unit_grads.3 = bf16[896,2304]{1,0:T(8,128)(2,1)} custom-call(bf16[2048,1792]{1,0:T(8,128)(2,1)} %get-tuple-element.152.refs_0_, bf16[256,1152]{1,0:T(8,128)(2,1)} %get-tuple-element.116.refs_0_.refs_1_, bf16[256,1152]{1,0:T(8,128)(2,1)} %copy-done.56, bf16[256,1152]{1,0:T(8,128)(2,1)} %copy-done.40, bf16[256,1152]{1,0:T(8,128)(2,1)} %copy-done.57, ...), custom_call_target="tpu_custom_call" | custom-call | flops 8455716864 | tf_op jit(solution)/shard_map/unit_grads/pallas_call | solution.py:594
  323.9 13.8 %attend_back.1 = (f32[256,1024]{1,0:T(8,128)}, bf16[8,256,512]{2,1,0:T(8,128)(2,1)}, bf16[256,1152]{1,0:T(8,128)(2,1)}, f32[256,1152]{1,0:T(8,128)}, f32[1,1152]{1,0:T(1,128)}, /*index=5*/f32[1,1152]{1,0:T(1,128)}) custom-call(s32[2,8]{1,0:T(2,128)} %pad_add_fusion.info_ref, bf16[256,1024]{1,0:T(8,128)(2,1)} %get-tuple-element.104.q_ref, ...), custom_call_target="tpu_custom_call" | custom-call | tf_op jit(solution)/shard_map/attend_back/pallas_call | solution.py:398
  339.1 2.7 collective-permute-start.55
  343.9 5.1 %collective-permute-done.55 = bf16[256,512]{1,0:T(8,128)(2,1)S(1)} collective-permute-done((bf16[256,512]{1,0:T(8,128)(2,1)S(1)}, bf16[256,512]{1,0:T(8,128)(2,1)S(1)}, u32[]{:S(2)}, u32[]{:S(2)}) %collective-permute-start.55) | collective-permute-done | bytes 262176 | tf_op jit(solution)/shard_map/kv_sum_vx-1/ppermute | solution.py:774
  349.0 5.6 %collective-permute-done.56 = bf16[256,512]{1,0:T(8,128)(2,1)S(1)} collective-permute-done((bf16[256,512]{1,0:T(8,128)(2,1)S(1)}, bf16[256,512]{1,0:T(8,128)(2,1)S(1)}, u32[]{:S(2)}, u32[]{:S(2)}) %collective-permute-start.56) | collective-permute-done | bytes 262176 | tf_op jit(solution)/shard_map/kv_sum_vx-1/ppermute | solution.py:774
  354.6 5.6 %collective-permute-done.57 = bf16[256,512]{1,0:T(8,128)(2,1)S(1)} collective-permute-done((bf16[256,512]{1,0:T(8,128)(2,1)S(1)}, bf16[256,512]{1,0:T(8,128)(2,1)S(1)}, u32[]{:S(2)}, u32[]{:S(2)}) %collective-permute-start.57) | collective-permute-done | bytes 262176 | tf_op jit(solution)/shard_map/kv_sum_vx-1/ppermute | solution.py:774
  360.2 3.4 collective-permute-done.60
  364.7 9.2 %collective-permute-start.61 = (bf16[128,512]{1,0:T(8,128)(2,1)S(1)}, bf16[128,512]{1,0:T(8,128)(2,1)S(1)}, u32[]{:S(2)}, u32[]{:S(2)}) collective-permute-start(bf16[128,512]{1,0:T(8,128)(2,1)S(1)} %get-tuple-element.238), channel_id=1, source_target_pairs={{2,0},{4,2},{6,4},{0,6},{3,1},{5,3},{7,5},{1,7},{10,8},{12,10},{14... | collective-permute-start | bytes 393224 | tf_op jit(solution)/shard_map/kv_sum_z1/ppermute | solution.py:774
  374.0 6.8 %collective-permute-done.61 = bf16[128,512]{1,0:T(8,128)(2,1)S(1)} collective-permute-done((bf16[128,512]{1,0:T(8,128)(2,1)S(1)}, bf16[128,512]{1,0:T(8,128)(2,1)S(1)}, u32[]{:S(2)}, u32[]{:S(2)}) %collective-permute-start.61) | collective-permute-done | bytes 131104 | tf_op jit(solution)/shard_map/kv_sum_z1/ppermute | solution.py:774
  380.8 4.3 collective-permute-start.62
  386.9 2.3 collective-permute-start.59
  389.2 10.2 %query_side.1 = (f32[23056,128]{1,0:T(8,128)}, f32[256,1152]{1,0:T(8,128)}, f32[1,256]{1,0:T(1,128)}) custom-call(f32[256,1024]{1,0:T(8,128)} %get-tuple-element.157.dq_ref, f32[256,1280]{1,0:T(8,128)} %get-tuple-element.158.raw_ref.refs_3_, f32[256,128]{1,0:T(8,128)} %get-tuple-element.241.refs_9_.cos_ref.refs_4_, ...), custom_call_target="tpu_custom_call" | custom-call | tf_op jit(solution)/shard_map/query_side/pallas_call | solution.py:89
  399.4 7.0 %collective-permute-done.62.refs_2_ = bf16[256,512]{1,0:T(8,128)(2,1)S(1)} collective-permute-done((bf16[256,512]{1,0:T(8,128)(2,1)S(1)}, bf16[256,512]{1,0:T(8,128)(2,1)S(1)}, u32[]{:S(2)}, u32[]{:S(2)}) %collective-permute-start.62) | collective-permute-done | bytes 262176 | tf_op jit(solution)/shard_map/kv_sum_z1/ppermute | solution.py:774
  406.4 2.2 collective-permute-done.59.refs_1_
  409.3 12.5 %last_part.1 = (bf16[256,1152]{1,0:T(8,128)(2,1)}, bf16[4,736,128]{2,1,0:T(8,128)(2,1)}, bf16[4,736,128]{2,1,0:T(8,128)(2,1)}, bf16[4,736,128]{2,1,0:T(8,128)(2,...) custom-call(s32[32]{0:T(128)} %fusion.15.order_ref, ...), custom_call_target="tpu_custom_call" | custom-call | tf_op jit(solution)/shard_map/last_part/pallas_call | solution.py:89
  429.6 7.0 %collective-permute-done.66 = bf16[1472,128]{1,0:T(8,128)(2,1)S(1)} collective-permute-done((bf16[1472,128]{1,0:T(8,128)(2,1)S(1)}, bf16[1472,128]{1,0:T(8,128)(2,1)S(1)}, u32[]{:S(2)}, u32[]{:S(2)}) %collective-permute-start.66) | collective-permute-done | bytes 376864 | tf_op jit(solution)/shard_map/attn_grad_sum_y-1/ppermute | solution.py:774
  442.5 12.5 %collective-permute-done.67 = bf16[2944,128]{1,0:T(8,128)(2,1)S(1)} collective-permute-done((bf16[2944,128]{1,0:T(8,128)(2,1)S(1)}, bf16[2944,128]{1,0:T(8,128)(2,1)S(1)}, u32[]{:S(2)}, u32[]{:S(2)}) %collective-permute-start.67) | collective-permute-done | bytes 753696 | tf_op jit(solution)/shard_map/attn_grad_sum_x-1/ppermute | solution.py:774
  454.9 2.7 collective-permute-done.70
  467.1 2.5 collective-permute-start.74
  479.0 10.6 %collective-permute-done.76 = bf16[216,864]{1,0:T(8,128)(2,1)S(1)} collective-permute-done((bf16[216,864]{1,0:T(8,128)(2,1)S(1)}, bf16[216,864]{1,0:T(8,128)(2,1)S(1)}, u32[]{:S(2)}, u32[]{:S(2)}) %collective-permute-start.76) | collective-permute-done | bytes 373280 | tf_op jit(solution)/shard_map/grad_exchange_uyc2/ppermute | solution.py:774
  489.9 5.5 %multiply_subtract_fusion = (f32[864,864]{1,0:T(8,128)}, f32[864,864]{1,0:T(8,128)}, f32[864,864]{1,0:T(8,128)}, f32[864,864]{1,0:T(8,128)}) fusion(f32[864,864]{1,0:T(8,128)S(1)} %copy-done, f32[864,864]{1,0:T(8,128)S(1)} %copy-done.7, f32[864,864]{1,0:T(8,128)S(1)} %copy-done.8, bf16[4,216,864]{2,1,0:T(8,128)(2,1)S(1)} %bitcast_dynamic-update-slice_fusion), kind=kLoop, calls=%fused_computation.3 | loop fusion | flops 11197440 | bytes 22394880 | tf_op jit(solution)/shard_map/sub | solution.py:65
  (377 shorter events, 117.0 us)
Async XLA Ops:
  7.2 164.5 %all-gather.2.cloned.1.call-start = ((), (), s32[]{:S(2)}) async-start(), calls=%async_computation.2 | async-start | bytes 7741440 | tf_op jit(solution)/shard_map/all_gather | solution.py:979
  9.2 10.2 %collective-permute-start = (bf16[736,128]{1,0:T(8,128)(2,1)S(1)}, bf16[736,128]{1,0:T(8,128)(2,1)S(1)}, u32[]{:S(2)}, u32[]{:S(2)}) collective-permute-start(bf16[736,128]{1,0:T(8,128)(2,1)S(1)} %pad_maximum_fusion.10), channel_id=1, source_target_pairs={{2,0},{4,2},{6,4},{0,6},{3,1},{5,3},{7,5},{1,7},{10,8},{12,10},{14... | collective-permute-start | bytes 565256 | tf_op jit(solution)/shard_map/attn_gather_z1/ppermute | solution.py:774
  14.3 9.5 %collective-permute-start.2 = (bf16[736,128]{1,0:T(8,128)(2,1)S(1)}, bf16[736,128]{1,0:T(8,128)(2,1)S(1)}, u32[]{:S(2)}, u32[]{:S(2)}) collective-permute-start(bf16[736,128]{1,0:T(8,128)(2,1)S(1)} %pad_maximum_fusion.10), channel_id=1, source_target_pairs={{6,0},{0,2},{2,4},{4,6},{7,1},{1,3},{3,5},{5,7},{14,8},{8,10},{10,... | collective-permute-start | bytes 565256 | tf_op jit(solution)/shard_map/attn_gather_z-1/ppermute | solution.py:774
  17.4 12.8 %collective-permute-start.4 = (bf16[216,864]{1,0:T(8,128)(2,1)}, bf16[216,864]{1,0:T(8,128)(2,1)S(1)}, u32[]{:S(2)}, u32[]{:S(2)}) collective-permute-start(bf16[216,864]{1,0:T(8,128)(2,1)} %get-tuple-element.218), channel_id=1, source_target_pairs={{8,0},{16,8},{24,16},{0,24},{9,1},{17,9},{25,17},{1,25},{10,2},{18... | collective-permute-start | bytes 1119752 | tf_op jit(solution)/shard_map/unit_exchange_uyc1/ppermute | solution.py:774
  18.1 19.1 %collective-permute-start.5 = (bf16[216,864]{1,0:T(8,128)(2,1)}, bf16[216,864]{1,0:T(8,128)(2,1)S(1)}, u32[]{:S(2)}, u32[]{:S(2)}) collective-permute-start(bf16[216,864]{1,0:T(8,128)(2,1)} %get-tuple-element.217), channel_id=1, source_target_pairs={{16,0},{24,8},{0,16},{8,24},{17,1},{25,9},{1,17},{9,25},{18,2},{26... | collective-permute-start | bytes 1119752 | tf_op jit(solution)/shard_map/unit_exchange_uyc2/ppermute | solution.py:774
  19.0 18.3 %collective-permute-start.6 = (bf16[216,864]{1,0:T(8,128)(2,1)S(1)}, bf16[216,864]{1,0:T(8,128)(2,1)S(1)}, u32[]{:S(2)}, u32[]{:S(2)}) collective-permute-start(bf16[216,864]{1,0:T(8,128)(2,1)S(1)} %get-tuple-element.216), channel_id=1, source_target_pairs={{24,0},{0,8},{8,16},{16,24},{25,1},{1,9},{9,17},{17,25},{26,2},{2,... | collective-permute-start | bytes 1119752 | tf_op jit(solution)/shard_map/unit_exchange_uyc3/ppermute | solution.py:774
  40.2 359.2 %reduce-scatter.3.cloned.1.call-start = ((), (), s32[]{:S(2)}) async-start(), calls=%async_computation.3 | async-start | bytes 2580480 | tf_op jit(solution)/shard_map/reduce_scatter | solution.py:909
  41.3 17.6 %collective-permute-start.10 = (bf16[2944,128]{1,0:T(8,128)(2,1)S(1)}, bf16[2944,128]{1,0:T(8,128)(2,1)S(1)}, u32[]{:S(2)}, u32[]{:S(2)}) collective-permute-start(bf16[2944,128]{1,0:T(8,128)(2,1)S(1)} %constant_dynamic-update-slice_fusion), channel_id=1, source_target_pairs={{1,0},{0,1},{3,2},{2,3},{5,4},{4,5},{7,6},{6,7},{9,8},{8,9},{11,10... | collective-permute-start | bytes 2261000 | tf_op jit(solution)/shard_map/attn_gather_x1/ppermute | solution.py:774
  42.8 17.7 %collective-permute-start.8 = (bf16[2944,128]{1,0:T(8,128)(2,1)S(1)}, bf16[2944,128]{1,0:T(8,128)(2,1)S(1)}, u32[]{:S(2)}, u32[]{:S(2)}) collective-permute-start(bf16[2944,128]{1,0:T(8,128)(2,1)S(1)} %constant_dynamic-update-slice_fusion), channel_id=1, source_target_pairs={{16,0},{0,16},{17,1},{1,17},{18,2},{2,18},{19,3},{3,19},{20,4},{4,... | collective-permute-start | bytes 2261000 | tf_op jit(solution)/shard_map/attn_gather_y1/ppermute | solution.py:774
  58.9 9.3 %collective-permute-start.12 = (bf16[1472,128]{1,0:T(8,128)(2,1)S(1)}, bf16[1472,128]{1,0:T(8,128)(2,1)S(1)}, u32[]{:S(2)}, u32[]{:S(2)}) collective-permute-start(bf16[1472,128]{1,0:T(8,128)(2,1)S(1)} %slice.274), channel_id=1, source_target_pairs={{16,0},{0,16},{17,1},{1,17},{18,2},{2,18},{19,3},{3,19},{20,4},{4,... | collective-permute-start | bytes 1130504 | tf_op jit(solution)/shard_map/attn_gather_y1/ppermute | solution.py:774
  63.2 9.5 %collective-permute-start.7 = (bf16[2944,128]{1,0:T(8,128)(2,1)S(1)}, bf16[2944,128]{1,0:T(8,128)(2,1)S(1)}, u32[]{:S(2)}, u32[]{:S(2)}) collective-permute-start(bf16[2944,128]{1,0:T(8,128)(2,1)S(1)} %constant_dynamic-update-slice_fusion), channel_id=1, source_target_pairs={{8,0},{0,8},{9,1},{1,9},{10,2},{2,10},{11,3},{3,11},{12,4},{4,12},... | collective-permute-start | bytes 2261000 | tf_op jit(solution)/shard_map/attn_gather_c1/ppermute | solution.py:774
  63.3 9.5 %collective-permute-start.9 = (bf16[2944,128]{1,0:T(8,128)(2,1)S(1)}, bf16[2944,128]{1,0:T(8,128)(2,1)S(1)}, u32[]{:S(2)}, u32[]{:S(2)}) collective-permute-start(bf16[2944,128]{1,0:T(8,128)(2,1)S(1)} %collective-permute-done.8), channel_id=1, source_target_pairs={{8,0},{0,8},{9,1},{1,9},{10,2},{2,10},{11,3},{3,11},{12,4},{4,12},... | collective-permute-start | bytes 2261000 | tf_op jit(solution)/shard_map/attn_gather_c1/ppermute | solution.py:774
  83.3 24.6 %collective-permute-start.16 = (bf16[256,512]{1,0:T(8,128)(2,1)}, bf16[256,512]{1,0:T(8,128)(2,1)S(1)}, u32[]{:S(2)}, u32[]{:S(2)}) collective-permute-start(bf16[256,512]{1,0:T(8,128)(2,1)} %get-tuple-element.105), channel_id=1, source_target_pairs={{2,0},{4,2},{6,4},{0,6},{3,1},{5,3},{7,5},{1,7},{10,8},{12,10},{14... | collective-permute-start | bytes 786440 | tf_op jit(solution)/shard_map/kv_gather_z1/ppermute | solution.py:774
  86.9 24.2 %collective-permute-start.19 = (bf16[256,512]{1,0:T(8,128)(2,1)}, bf16[256,512]{1,0:T(8,128)(2,1)S(1)}, u32[]{:S(2)}, u32[]{:S(2)}) collective-permute-start(bf16[256,512]{1,0:T(8,128)(2,1)} %get-tuple-element.105), channel_id=1, source_target_pairs={{6,0},{0,2},{2,4},{4,6},{7,1},{1,3},{3,5},{5,7},{14,8},{8,10},{10,... | collective-permute-start | bytes 786440 | tf_op jit(solution)/shard_map/kv_gather_z-1/ppermute | solution.py:774
  86.9 28.8 %collective-permute-start.15 = (bf16[256,512]{1,0:T(8,128)(2,1)}, bf16[256,512]{1,0:T(8,128)(2,1)S(1)}, u32[]{:S(2)}, u32[]{:S(2)}) collective-permute-start(bf16[256,512]{1,0:T(8,128)(2,1)} %get-tuple-element.105), channel_id=1, source_target_pairs={{1,0},{0,1},{3,2},{2,3},{5,4},{4,5},{7,6},{6,7},{9,8},{8,9},{11,10... | collective-permute-start | bytes 786440 | tf_op jit(solution)/shard_map/kv_gather_vx1/ppermute | solution.py:774
  107.9 15.8 %collective-permute-start.18 = (bf16[128,512]{1,0:T(8,128)(2,1)S(1)}, bf16[128,512]{1,0:T(8,128)(2,1)S(1)}, u32[]{:S(2)}, u32[]{:S(2)}) collective-permute-start(bf16[128,512]{1,0:T(8,128)(2,1)S(1)} %slice.276), channel_id=1, source_target_pairs={{2,0},{4,2},{6,4},{0,6},{3,1},{5,3},{7,5},{1,7},{10,8},{12,10},{14... | collective-permute-start | bytes 393224 | tf_op jit(solution)/shard_map/kv_gather_z1/ppermute | solution.py:774
  111.1 12.6 %collective-permute-start.20 = (bf16[128,512]{1,0:T(8,128)(2,1)S(1)}, bf16[128,512]{1,0:T(8,128)(2,1)S(1)}, u32[]{:S(2)}, u32[]{:S(2)}) collective-permute-start(bf16[128,512]{1,0:T(8,128)(2,1)S(1)} %slice.277), channel_id=1, source_target_pairs={{6,0},{0,2},{2,4},{4,6},{7,1},{1,3},{3,5},{5,7},{14,8},{8,10},{10,... | collective-permute-start | bytes 393224 | tf_op jit(solution)/shard_map/kv_gather_z-1/ppermute | solution.py:774
  113.6 11.3 %collective-permute-start.17 = (bf16[256,512]{1,0:T(8,128)(2,1)S(1)}, bf16[256,512]{1,0:T(8,128)(2,1)S(1)}, u32[]{:S(2)}, u32[]{:S(2)}) collective-permute-start(bf16[256,512]{1,0:T(8,128)(2,1)S(1)} %collective-permute-done.16), channel_id=1, source_target_pairs={{1,0},{0,1},{3,2},{2,3},{5,4},{4,5},{7,6},{6,7},{9,8},{8,9},{11,10... | collective-permute-start | bytes 786440 | tf_op jit(solution)/shard_map/kv_gather_vx1/ppermute | solution.py:774
  115.1 17.3 %collective-permute-start.22 = (bf16[256,512]{1,0:T(8,128)(2,1)S(1)}, bf16[256,512]{1,0:T(8,128)(2,1)S(1)}, u32[]{:S(2)}, u32[]{:S(2)}) collective-permute-start(bf16[256,512]{1,0:T(8,128)(2,1)S(1)} %collective-permute-done.19), channel_id=1, source_target_pairs={{1,0},{0,1},{3,2},{2,3},{5,4},{4,5},{7,6},{6,7},{9,8},{8,9},{11,10... | collective-permute-start | bytes 786440 | tf_op jit(solution)/shard_map/kv_gather_vx1/ppermute | solution.py:774
  144.0 15.2 %collective-permute-start.26 = (bf16[256,1152]{1,0:T(8,128)(2,1)}, bf16[256,1152]{1,0:T(8,128)(2,1)S(1)}, u32[]{:S(2)}, u32[]{:S(2)}) collective-permute-start(bf16[256,1152]{1,0:T(8,128)(2,1)} %get-tuple-element.116.refs_0_.refs_1_), channel_id=1, source_target_pairs={{1,0},{0,1},{3,2},{2,3},{5,4},{4,5},{7,6},{6,7},{9,8},{8,9},{11,10... | collective-permute-start | bytes 1769480 | tf_op jit(solution)/shard_map/ffn_in_gather_x1/ppermute | solution.py:774
  146.4 14.4 %collective-permute-start.24 = (bf16[256,1152]{1,0:T(8,128)(2,1)}, bf16[256,1152]{1,0:T(8,128)(2,1)S(1)}, u32[]{:S(2)}, u32[]{:S(2)}) collective-permute-start(bf16[256,1152]{1,0:T(8,128)(2,1)} %get-tuple-element.116.refs_0_.refs_1_), channel_id=1, source_target_pairs={{16,0},{0,16},{17,1},{1,17},{18,2},{2,18},{19,3},{3,19},{20,4},{4,... | collective-permute-start | bytes 1769480 | tf_op jit(solution)/shard_map/ffn_in_gather_y1/ppermute | solution.py:774
  197.3 15.3 %collective-permute-start.31 = (bf16[256,1152]{1,0:T(8,128)(2,1)}, bf16[256,1152]{1,0:T(8,128)(2,1)S(1)}, u32[]{:S(2)}, u32[]{:S(2)}) collective-permute-start(bf16[256,1152]{1,0:T(8,128)(2,1)} %get-tuple-element.122), channel_id=1, source_target_pairs={{8,0},{0,8},{9,1},{1,9},{10,2},{2,10},{11,3},{3,11},{12,4},{4,12},... | collective-permute-start | bytes 1769480 | tf_op jit(solution)/shard_map/ffn_out_sum_c1/ppermute | solution.py:774
  200.2 9.1 %collective-permute-start.37 = (bf16[128,1152]{1,0:T(8,128)(2,1)S(1)}, bf16[128,1152]{1,0:T(8,128)(2,1)S(1)}, u32[]{:S(2)}, u32[]{:S(2)}) collective-permute-start(bf16[128,1152]{1,0:T(8,128)(2,1)S(1)} %get-tuple-element.236), channel_id=1, source_target_pairs={{1,0},{0,1},{3,2},{2,3},{5,4},{4,5},{7,6},{6,7},{9,8},{8,9},{11,10... | collective-permute-start | bytes 884744 | tf_op jit(solution)/shard_map/ffn_out_sum_x-1/ppermute | solution.py:774
  201.9 9.1 %collective-permute-start.34 = (bf16[128,1152]{1,0:T(8,128)(2,1)S(1)}, bf16[128,1152]{1,0:T(8,128)(2,1)S(1)}, u32[]{:S(2)}, u32[]{:S(2)}) collective-permute-start(bf16[128,1152]{1,0:T(8,128)(2,1)S(1)} %get-tuple-element.237), channel_id=1, source_target_pairs={{16,0},{0,16},{17,1},{1,17},{18,2},{2,18},{19,3},{3,19},{20,4},{4,... | collective-permute-start | bytes 884744 | tf_op jit(solution)/shard_map/ffn_out_sum_y-1/ppermute | solution.py:774
  209.5 14.6 %collective-permute-start.38 = (bf16[256,1152]{1,0:T(8,128)(2,1)S(1)}, bf16[256,1152]{1,0:T(8,128)(2,1)S(1)}, u32[]{:S(2)}, u32[]{:S(2)}) collective-permute-start(bf16[256,1152]{1,0:T(8,128)(2,1)S(1)} %pad_maximum_fusion.4), channel_id=1, source_target_pairs={{16,0},{0,16},{17,1},{1,17},{18,2},{2,18},{19,3},{3,19},{20,4},{4,... | collective-permute-start | bytes 1769480 | tf_op jit(solution)/shard_map/ffn_out_sum_y-1/ppermute | solution.py:774
  211.1 14.3 %collective-permute-start.35 = (bf16[256,1152]{1,0:T(8,128)(2,1)S(1)}, bf16[256,1152]{1,0:T(8,128)(2,1)S(1)}, u32[]{:S(2)}, u32[]{:S(2)}) collective-permute-start(bf16[256,1152]{1,0:T(8,128)(2,1)S(1)} %pad_maximum_fusion.3), channel_id=1, source_target_pairs={{1,0},{0,1},{3,2},{2,3},{5,4},{4,5},{7,6},{6,7},{9,8},{8,9},{11,10... | collective-permute-start | bytes 1769480 | tf_op jit(solution)/shard_map/ffn_out_sum_x-1/ppermute | solution.py:774
  229.9 13.6 %collective-permute-start.42 = (bf16[256,1152]{1,0:T(8,128)(2,1)}, bf16[256,1152]{1,0:T(8,128)(2,1)S(1)}, u32[]{:S(2)}, u32[]{:S(2)}) collective-permute-start(bf16[256,1152]{1,0:T(8,128)(2,1)} %get-tuple-element.136.refs_1_.refs_0_), channel_id=1, source_target_pairs={{1,0},{0,1},{3,2},{2,3},{5,4},{4,5},{7,6},{6,7},{9,8},{8,9},{11,10... | collective-permute-start | bytes 1769480 | tf_op jit(solution)/shard_map/d_out_gather_x1/ppermute | solution.py:774
  231.4 14.5 %collective-permute-start.40 = (bf16[256,1152]{1,0:T(8,128)(2,1)}, bf16[256,1152]{1,0:T(8,128)(2,1)S(1)}, u32[]{:S(2)}, u32[]{:S(2)}) collective-permute-start(bf16[256,1152]{1,0:T(8,128)(2,1)} %get-tuple-element.136.refs_1_.refs_0_), channel_id=1, source_target_pairs={{16,0},{0,16},{17,1},{1,17},{18,2},{2,18},{19,3},{3,19},{20,4},{4,... | collective-permute-start | bytes 1769480 | tf_op jit(solution)/shard_map/d_out_gather_y1/ppermute | solution.py:774
  290.8 150.2 %reduce-scatter.5.cloned.1.call-start = ((), (), s32[]{:S(2)}) async-start(), calls=%async_computation.4 | async-start | bytes 5160960 | tf_op jit(solution)/shard_map/reduce_scatter | solution.py:909
  291.8 29.1 %collective-permute-start.47 = (bf16[256,1152]{1,0:T(8,128)(2,1)}, bf16[256,1152]{1,0:T(8,128)(2,1)S(1)}, u32[]{:S(2)}, u32[]{:S(2)}) collective-permute-start(bf16[256,1152]{1,0:T(8,128)(2,1)} %get-tuple-element.140), channel_id=1, source_target_pairs={{8,0},{0,8},{9,1},{1,9},{10,2},{2,10},{11,3},{3,11},{12,4},{4,12},... | collective-permute-start | bytes 1769480 | tf_op jit(solution)/shard_map/d_in_sum_c1/ppermute | solution.py:774
  293.1 9.1 %collective-permute-start.50 = (bf16[128,1152]{1,0:T(8,128)(2,1)S(1)}, bf16[128,1152]{1,0:T(8,128)(2,1)S(1)}, u32[]{:S(2)}, u32[]{:S(2)}) collective-permute-start(bf16[128,1152]{1,0:T(8,128)(2,1)S(1)} %get-tuple-element.233), channel_id=1, source_target_pairs={{16,0},{0,16},{17,1},{1,17},{18,2},{2,18},{19,3},{3,19},{20,4},{4,... | collective-permute-start | bytes 884744 | tf_op jit(solution)/shard_map/d_in_sum_y-1/ppermute | solution.py:774
  302.4 20.4 %collective-permute-start.54 = (bf16[256,1152]{1,0:T(8,128)(2,1)S(1)}, bf16[256,1152]{1,0:T(8,128)(2,1)S(1)}, u32[]{:S(2)}, u32[]{:S(2)}) collective-permute-start(bf16[256,1152]{1,0:T(8,128)(2,1)S(1)} %pad_maximum_fusion.6), channel_id=1, source_target_pairs={{16,0},{0,16},{17,1},{1,17},{18,2},{2,18},{19,3},{3,19},{20,4},{4,... | collective-permute-start | bytes 1769480 | tf_op jit(solution)/shard_map/d_in_sum_y-1/ppermute | solution.py:774
  304.3 18.6 %collective-permute-start.53 = (bf16[256,1152]{1,0:T(8,128)(2,1)S(1)}, bf16[256,1152]{1,0:T(8,128)(2,1)S(1)}, u32[]{:S(2)}, u32[]{:S(2)}) collective-permute-start(bf16[256,1152]{1,0:T(8,128)(2,1)S(1)} %pad_maximum_fusion.5), channel_id=1, source_target_pairs={{1,0},{0,1},{3,2},{2,3},{5,4},{4,5},{7,6},{6,7},{9,8},{8,9},{11,10... | collective-permute-start | bytes 1769480 | tf_op jit(solution)/shard_map/d_in_sum_x-1/ppermute | solution.py:774
  339.1 9.9 %collective-permute-start.55 = (bf16[256,512]{1,0:T(8,128)(2,1)S(1)}, bf16[256,512]{1,0:T(8,128)(2,1)S(1)}, u32[]{:S(2)}, u32[]{:S(2)}) collective-permute-start(bf16[256,512]{1,0:T(8,128)(2,1)S(1)} %get-tuple-element.207), channel_id=1, source_target_pairs={{1,0},{0,1},{3,2},{2,3},{5,4},{4,5},{7,6},{6,7},{9,8},{8,9},{11,10... | collective-permute-start | bytes 786440 | tf_op jit(solution)/shard_map/kv_sum_vx-1/ppermute | solution.py:774
  341.7 12.8 %collective-permute-start.56 = (bf16[256,512]{1,0:T(8,128)(2,1)S(1)}, bf16[256,512]{1,0:T(8,128)(2,1)S(1)}, u32[]{:S(2)}, u32[]{:S(2)}) collective-permute-start(bf16[256,512]{1,0:T(8,128)(2,1)S(1)} %get-tuple-element.206), channel_id=1, source_target_pairs={{1,0},{0,1},{3,2},{2,3},{5,4},{4,5},{7,6},{6,7},{9,8},{8,9},{11,10... | collective-permute-start | bytes 786440 | tf_op jit(solution)/shard_map/kv_sum_vx-1/ppermute | solution.py:774
  341.8 18.4 %collective-permute-start.57 = (bf16[256,512]{1,0:T(8,128)(2,1)S(1)}, bf16[256,512]{1,0:T(8,128)(2,1)S(1)}, u32[]{:S(2)}, u32[]{:S(2)}) collective-permute-start(bf16[256,512]{1,0:T(8,128)(2,1)S(1)} %get-tuple-element.205), channel_id=1, source_target_pairs={{1,0},{0,1},{3,2},{2,3},{5,4},{4,5},{7,6},{6,7},{9,8},{8,9},{11,10... | collective-permute-start | bytes 786440 | tf_op jit(solution)/shard_map/kv_sum_vx-1/ppermute | solution.py:774
  343.8 19.9 %collective-permute-start.60 = (bf16[256,512]{1,0:T(8,128)(2,1)S(1)}, bf16[256,512]{1,0:T(8,128)(2,1)S(1)}, u32[]{:S(2)}, u32[]{:S(2)}) collective-permute-start(bf16[256,512]{1,0:T(8,128)(2,1)S(1)} %get-tuple-element.204), channel_id=1, source_target_pairs={{1,0},{0,1},{3,2},{2,3},{5,4},{4,5},{7,6},{6,7},{9,8},{8,9},{11,10... | collective-permute-start | bytes 786440 | tf_op jit(solution)/shard_map/kv_sum_vx-1/ppermute | solution.py:774
  364.7 16.0 %collective-permute-start.61 = (bf16[128,512]{1,0:T(8,128)(2,1)S(1)}, bf16[128,512]{1,0:T(8,128)(2,1)S(1)}, u32[]{:S(2)}, u32[]{:S(2)}) collective-permute-start(bf16[128,512]{1,0:T(8,128)(2,1)S(1)} %get-tuple-element.238), channel_id=1, source_target_pairs={{2,0},{4,2},{6,4},{0,6},{3,1},{5,3},{7,5},{1,7},{10,8},{12,10},{14... | collective-permute-start | bytes 393224 | tf_op jit(solution)/shard_map/kv_sum_z1/ppermute | solution.py:774
  373.9 13.0 %collective-permute-start.58 = (bf16[128,512]{1,0:T(8,128)(2,1)S(1)}, bf16[128,512]{1,0:T(8,128)(2,1)S(1)}, u32[]{:S(2)}, u32[]{:S(2)}) collective-permute-start(bf16[128,512]{1,0:T(8,128)(2,1)S(1)} %get-tuple-element.239), channel_id=1, source_target_pairs={{6,0},{0,2},{2,4},{4,6},{7,1},{1,3},{3,5},{5,7},{14,8},{8,10},{10,... | collective-permute-start | bytes 393224 | tf_op jit(solution)/shard_map/kv_sum_z-1/ppermute | solution.py:774
  380.8 25.6 %collective-permute-start.62 = (bf16[256,512]{1,0:T(8,128)(2,1)S(1)}, bf16[256,512]{1,0:T(8,128)(2,1)S(1)}, u32[]{:S(2)}, u32[]{:S(2)}) collective-permute-start(bf16[256,512]{1,0:T(8,128)(2,1)S(1)} %pad_maximum_fusion.9), channel_id=1, source_target_pairs={{2,0},{4,2},{6,4},{0,6},{3,1},{5,3},{7,5},{1,7},{10,8},{12,10},{14... | collective-permute-start | bytes 786440 | tf_op jit(solution)/shard_map/kv_sum_z1/ppermute | solution.py:774
  386.9 21.7 %collective-permute-start.59 = (bf16[256,512]{1,0:T(8,128)(2,1)S(1)}, bf16[256,512]{1,0:T(8,128)(2,1)S(1)}, u32[]{:S(2)}, u32[]{:S(2)}) collective-permute-start(bf16[256,512]{1,0:T(8,128)(2,1)S(1)} %pad_maximum_fusion.8), channel_id=1, source_target_pairs={{6,0},{0,2},{2,4},{4,6},{7,1},{1,3},{3,5},{5,7},{14,8},{8,10},{10,... | collective-permute-start | bytes 786440 | tf_op jit(solution)/shard_map/kv_sum_z-1/ppermute | solution.py:774
  422.5 20.0 %collective-permute-start.63 = (bf16[2944,128]{1,0:T(8,128)(2,1)}, bf16[2944,128]{1,0:T(8,128)(2,1)S(1)}, u32[]{:S(2)}, u32[]{:S(2)}) collective-permute-start(bf16[2944,128]{1,0:T(8,128)(2,1)} %bitcast.172), channel_id=1, source_target_pairs={{8,0},{0,8},{9,1},{1,9},{10,2},{2,10},{11,3},{3,11},{12,4},{4,12},... | collective-permute-start | bytes 2261000 | tf_op jit(solution)/shard_map/attn_grad_sum_c1/ppermute | solution.py:774
  425.8 10.9 %collective-permute-start.66 = (bf16[1472,128]{1,0:T(8,128)(2,1)S(1)}, bf16[1472,128]{1,0:T(8,128)(2,1)S(1)}, u32[]{:S(2)}, u32[]{:S(2)}) collective-permute-start(bf16[1472,128]{1,0:T(8,128)(2,1)S(1)} %get-tuple-element.228), channel_id=1, source_target_pairs={{16,0},{0,16},{17,1},{1,17},{18,2},{2,18},{19,3},{3,19},{20,4},{4,... | collective-permute-start | bytes 1130504 | tf_op jit(solution)/shard_map/attn_grad_sum_y-1/ppermute | solution.py:774
  427.6 11.0 %collective-permute-start.69 = (bf16[1472,128]{1,0:T(8,128)(2,1)S(1)}, bf16[1472,128]{1,0:T(8,128)(2,1)S(1)}, u32[]{:S(2)}, u32[]{:S(2)}) collective-permute-start(bf16[1472,128]{1,0:T(8,128)(2,1)S(1)} %get-tuple-element.229), channel_id=1, source_target_pairs={{1,0},{0,1},{3,2},{2,3},{5,4},{4,5},{7,6},{6,7},{9,8},{8,9},{11,10... | collective-permute-start | bytes 1130504 | tf_op jit(solution)/shard_map/attn_grad_sum_x-1/ppermute | solution.py:774
  436.8 18.1 %collective-permute-start.67 = (bf16[2944,128]{1,0:T(8,128)(2,1)S(1)}, bf16[2944,128]{1,0:T(8,128)(2,1)S(1)}, u32[]{:S(2)}, u32[]{:S(2)}) collective-permute-start(bf16[2944,128]{1,0:T(8,128)(2,1)S(1)} %pad_maximum_fusion.1), channel_id=1, source_target_pairs={{1,0},{0,1},{3,2},{2,3},{5,4},{4,5},{7,6},{6,7},{9,8},{8,9},{11,10... | collective-permute-start | bytes 2261000 | tf_op jit(solution)/shard_map/attn_grad_sum_x-1/ppermute | solution.py:774
  439.6 18.0 %collective-permute-start.70 = (bf16[2944,128]{1,0:T(8,128)(2,1)}, bf16[2944,128]{1,0:T(8,128)(2,1)S(1)}, u32[]{:S(2)}, u32[]{:S(2)}) collective-permute-start(bf16[2944,128]{1,0:T(8,128)(2,1)} %pad_maximum_fusion.2), channel_id=1, source_target_pairs={{16,0},{0,16},{17,1},{1,17},{18,2},{2,18},{19,3},{3,19},{20,4},{4,... | collective-permute-start | bytes 2261000 | tf_op jit(solution)/shard_map/attn_grad_sum_y-1/ppermute | solution.py:774
  470.4 19.1 %collective-permute-start.76 = (bf16[216,864]{1,0:T(8,128)(2,1)S(1)}, bf16[216,864]{1,0:T(8,128)(2,1)S(1)}, u32[]{:S(2)}, u32[]{:S(2)}) collective-permute-start(bf16[216,864]{1,0:T(8,128)(2,1)S(1)} %get-tuple-element.209), channel_id=1, source_target_pairs={{16,0},{24,8},{0,16},{8,24},{17,1},{25,9},{1,17},{9,25},{18,2},{26... | collective-permute-start | bytes 1119752 | tf_op jit(solution)/shard_map/grad_exchange_uyc2/ppermute | solution.py:774
  471.8 18.1 %collective-permute-start.77 = (bf16[216,864]{1,0:T(8,128)(2,1)S(1)}, bf16[216,864]{1,0:T(8,128)(2,1)S(1)}, u32[]{:S(2)}, u32[]{:S(2)}) collective-permute-start(bf16[216,864]{1,0:T(8,128)(2,1)S(1)} %get-tuple-element.208), channel_id=1, source_target_pairs={{24,0},{0,8},{8,16},{16,24},{25,1},{1,9},{9,17},{17,25},{26,2},{2,... | collective-permute-start | bytes 1119752 | tf_op jit(solution)/shard_map/grad_exchange_uyc3/ppermute | solution.py:774
  (99 other events, 795.3 us)
Sparse Core Ops, SparseCore 0:
  40.3 131.3 all-gather.1
  290.9 43.6 reduce-scatter.2
  337.0 91.8 reduce-scatter.4

commit v3 on v2

--- a/solution.py
+++ b/solution.py
@@ -811,15 +811,17 @@
             for oy in range(1, ny):
                 along_x[ox].append(self.fro(low[ox, oy][:half], "y", -oy))
                 along_y[oy].append(self.fro(low[ox, oy][half:], "x", -ox))
+        by_x = {
+            ox: jnp.concatenate([add_low(*v), low[ox, 0][half:]], axis=0) for ox, v in along_x.items()
+        }
+        by_y = {
+            oy: jnp.concatenate([low[0, oy][:half], add_low(*v)], axis=0) for oy, v in along_y.items()
+        }
         if beside is not None:
-            along_x, along_y, beside = lax.optimization_barrier((along_x, along_y, beside))
+            by_x, by_y, beside = lax.optimization_barrier((by_x, by_y, beside))
         terms = [low[0, 0]]
-        for ox in range(1, nx):
-            whole = jnp.concatenate([add_low(*along_x[ox]), low[ox, 0][half:]], axis=0)
-            terms.append(self.fro(whole, "x", -ox))
-        for oy in range(1, ny):
-            whole = jnp.concatenate([low[0, oy][:half], add_low(*along_y[oy])], axis=0)
-            terms.append(self.fro(whole, "y", -oy))
+        terms += [self.fro(v, "x", -ox) for ox, v in by_x.items()]
+        terms += [self.fro(v, "y", -oy) for oy, v in by_y.items()]
         return terms if beside is None else (terms, beside)
 
     def z_begin(self, value):
@@ -849,11 +851,11 @@
             other, begun_other[0], far_other, begun_other[1]
         ]
 
-    def z_scatter_begin(self, parts):
+    def z_scatter_begin(self, far):
         if self.sizes["z"] != 4:
             return ()
-        half = halfway(parts[0].shape[0])
-        return self.fro(parts[2][:half], "z", -1), self.fro(parts[2][half:], "z", 1)
+        half = halfway(far.shape[0])
+        return self.fro(far[:half], "z", -1), self.fro(far[half:], "z", 1)
 
     def z_scatter_go(self, parts, begun):
         n = self.sizes["z"]
@@ -865,7 +867,7 @@
         return [self.fro(above, "z", -1), self.fro(below, "z", 1)]
 
     def z_scatter(self, parts):
-        return [parts[0], *self.z_scatter_go(parts, self.z_scatter_begin(parts))]
+        return [parts[0], *self.z_scatter_go(parts, self.z_scatter_begin(parts[len(parts) // 2]))]
 
 
 SEQ = ("u", "y", "c")
@@ -1037,11 +1039,19 @@
         )
         ways.what = "kv_sum"
         d_kv = d_kv.reshape(nz, nx, tok_rows, 2 * HD)
-        kv_parts = {}
-        for oz in sorted(range(nz), key=lambda o: abs(o - nz // 2)):
-            kv_parts[oz] = add_low(*[ways.fro(d_kv[oz, oa], ACROSS, -oa) for oa in range(nx)])
-        kv_parts[0], owned_down = lax.optimization_barrier((kv_parts[0], owned_down))
-        kv_parts = ways.z_scatter([kv_parts[oz] for oz in range(nz)])
+
+        def across(oz):
+            return [ways.fro(d_kv[oz, oa], ACROSS, -oa) for oa in range(nx)]
+
+        far = nz // 2
+        kv_parts = {far: add_low(*across(far))}
+        near = {oz: across(oz) for oz in range(nz) if oz != far}
+        begun = ways.z_scatter_begin(kv_parts[far])
+        if begun:
+            begun, near = lax.optimization_barrier((begun, near))
+        near[0], owned_down = lax.optimization_barrier((near[0], owned_down))
+        kv_parts.update({oz: add_low(*terms) for oz, terms in near.items()})
+        kv_parts = [kv_parts[0], *ways.z_scatter_go(kv_parts, begun)]
         lines, da_query, d_gq = query_side(
             flat, d_query, raw, cosine, sine, g_q, normed_in, w_qkv, heads, d_attn_out
         )
@@ -1051,33 +1061,30 @@
         )
 
         ways.what = "attn_grad_sum"
-        packed[0], owned_gate_up = lax.optimization_barrier((packed[0], owned_gate_up))
         packed = [part.reshape(-1, LANES) for part in packed]
-        plane_sum = add_low(
-            *ways.plane_scatter(
-                {p: packed[i * nc : (i + 1) * nc] for i, p in enumerate(places)}
-            )
-        )
-        plane_sum = to_outers(plane_sum)
-        red = sum(
-            part.astype(f32)
-            for part in ways.z_scatter(
-                [plane_sum[oz * flat.rows : (oz + 1) * flat.rows] for oz in range(nz)]
-            )
-        )
+        terms, owned_gate_up = ways.plane_scatter(
+            {p: packed[i * nc : (i + 1) * nc] for i, p in enumerate(places)}, owned_gate_up
+        )
+        own_rows = jnp.concatenate([owned_gate_up[:share], owned_down[:share]], axis=1)
+        by_cols = jnp.stack([own_rows[:, i * width : (i + 1) * width] for i in range(ns)])
+        terms, by_cols = lax.optimization_barrier((terms, by_cols))
+        plane_sum = to_outers(add_low(*terms))
+
+        ways.what = "grad_exchange"
+        mlp_red = seq_place_all(seq_send(by_cols)).astype(f32).reshape(units, width)
+        mlp_m_new, mlp_v_new, mlp_new = adam_update(
+            mlp_w, mlp_m, mlp_v, mlp_red, RATE_MATRIX, DECAY_MATRIX
+        )
+
+        ways.what = "attn_grad_sum"
+        terms = ways.z_scatter([plane_sum[oz * flat.rows : (oz + 1) * flat.rows] for oz in range(nz)])
+        terms, mlp_new = lax.optimization_barrier((terms, mlp_new))
+        red = sum(part.astype(f32) for part in terms)
         attn_red = red[: flat.lines].reshape(-1)
         gain_red = lax.dynamic_slice(red[flat.gain_at :].reshape(-1), (gain_offset,), (gain_piece,))
 
-        ways.what = "grad_exchange"
-        own_rows = jnp.concatenate([owned_gate_up[:share], owned_down[:share]], axis=1)
-        by_cols = jnp.stack([own_rows[:, i * width : (i + 1) * width] for i in range(ns)])
-        mlp_red = seq_place_all(seq_send(by_cols)).astype(f32).reshape(units, width)
-
         attn_m_new, attn_v_new, attn_new = adam_update(
             attn_w, attn_m, attn_v, attn_red, RATE_MATRIX, DECAY_MATRIX
-        )
-        mlp_m_new, mlp_v_new, mlp_new = adam_update(
-            mlp_w, mlp_m, mlp_v, mlp_red, RATE_MATRIX, DECAY_MATRIX
         )
         gain_m_new, gain_v_new, gain_new = adam_update(
             gains, gain_m, gain_v, gain_red, RATE_GAIN, 0.0

time: 509 us -> 494 us (0.971)
  waiting for transfers between devices: 214 us -> 200 us
    ppermute x78, waiting for transfers between devices: 213 us -> 198 us  [fro(): return lax.ppermute(value, axis, [((i + offset) % n, i) for i in range(n)])]
  transfers between devices with their start and end apart: 81 -> 81, of which waited for: 51 -> 50; matrix products, arithmetic and copies ran while one was open for 5% -> 6% of each run, Pallas kernels for 15% -> 16%
where the time goes in v3:
time: 494 us; the launch traced here: 487 us
  waiting for transfers between devices  200 us (40%)
  Pallas kernels  141 us (29%)
  starting transfers between devices  85.6 us (17%)
  other arithmetic  23.2 us (5%)
  local copies, waits for them, and re-layouts  21.1 us (4%)
  between operations  15.7 us (3%)
    ppermute x78, waiting for transfers between devices, fro(): return lax.ppermute(value, axis, [((i + offset) % n, i) for i in range(n)])  198 us
    ppermute x78, starting transfers between devices, fro(): return lax.ppermute(value, axis, [((i + offset) % n, i) for i in range(n)])  85.5 us
    pallas_call x2, Pallas kernels, ffn_call(): pl.pallas_call(kernel, grid=(chunks,), in_specs=[anywhere] * count + [chu...  49.2 us
    pallas_call x5, Pallas kernels, run(): pl.pallas_call(body, out_shape=tuple((jax.ShapeDtypeStruct(s, d) for s, d...  41.4 us
    pallas_call x2, Pallas kernels, unit_grads(): pl.pallas_call(body, grid=(n,), in_specs=[pl.BlockSpec((u.shape[0], per),...  26.9 us
    pallas_call x1, Pallas kernels, attend_back(): pl.pallas_call(body, grid_spec=pltpu.PrefetchScalarGridSpec(num_scalar_pr...  13.8 us
    pallas_call x1, Pallas kernels, attend(): pl.pallas_call(body, grid_spec=pltpu.PrefetchScalarGridSpec(num_scalar_pr...  10.2 us
  transfers between devices with their start and end apart: 81, of which 50 were waited for; matrix products, arithmetic and copies ran while one was open for 6% of the time, Pallas kernels for 16%

profile of v3, /device:TPU:0, one launch (start us, length us, event | category | flops | bytes accessed | tf_op | source)
XLA Modules:
  0.0 487.3 jit_solution(6539151901223796764)
XLA Ops:
  9.2 5.1 %collective-permute-start = (bf16[736,128]{1,0:T(8,128)(2,1)S(1)}, bf16[736,128]{1,0:T(8,128)(2,1)S(1)}, u32[]{:S(2)}, u32[]{:S(2)}) collective-permute-start(bf16[736,128]{1,0:T(8,128)(2,1)S(1)} %pad_maximum_fusion.10), channel_id=1, source_target_pairs={{2,0},{4,2},{6,4},{0,6},{3,1},{5,3},{7,5},{1,7},{10,8},{12,10},{14... | collective-permute-start | bytes 565256 | tf_op jit(solution)/shard_map/attn_gather_z1/ppermute | solution.py:774
  14.3 2.0 convert_element_type.294
  19.5 4.3 collective-permute-start.1
  26.9 3.4 collective-permute-done.3
  30.3 7.0 %collective-permute-done.5 = bf16[216,864]{1,0:T(8,128)(2,1)S(1)} collective-permute-done((bf16[216,864]{1,0:T(8,128)(2,1)}, bf16[216,864]{1,0:T(8,128)(2,1)S(1)}, u32[]{:S(2)}, u32[]{:S(2)}) %collective-permute-start.5) | collective-permute-done | bytes 373280 | tf_op jit(solution)/shard_map/unit_exchange_uyc2/ppermute | solution.py:774
  44.0 14.9 %collective-permute-done.10 = bf16[2944,128]{1,0:T(8,128)(2,1)S(1)} collective-permute-done((bf16[2944,128]{1,0:T(8,128)(2,1)S(1)}, bf16[2944,128]{1,0:T(8,128)(2,1)S(1)}, u32[]{:S(2)}, u32[]{:S(2)}) %collective-permute-start.10) | collective-permute-done | bytes 753696 | tf_op jit(solution)/shard_map/attn_gather_x1/ppermute | solution.py:774
  63.9 4.3 collective-permute-done.12
  74.4 8.9 %first_part.1 = (bf16[1152,1536]{1,0:T(8,128)(2,1)}, f32[1,1152]{1,0:T(1,128)}, f32[1,256]{1,0:T(1,128)}, f32[1,256]{1,0:T(1,128)}, f32[1,1152]{1,0:T(1,128)}, /...) custom-call(s32[32]{0:T(128)} %fusion.12.order_ref, ...), custom_call_target="tpu_custom_call" | custom-call | tf_op jit(solution)/shard_map/first_part/pallas_call | solution.py:89
  83.4 3.6 collective-permute-start.16
  90.4 6.0 %spread_out.1.w_ref.refs_6_ = bf16[1024,1152]{1,0:T(8,128)(2,1)} custom-call(s32[32]{0:T(128)} %fusion.12.order_ref, bf16[4,736,128]{2,1,0:T(8,128)(2,1)} %bitcast.142, bf16[4,736,128]{2,1,0:T(8,128)(2,1)} %bitcast.144, bf16[4,736,128]{2,1,0:T(8,128)(2,1)} %bitcast.138, bf16[4,736,128]{2,1,0:T(8,128)(2,1)} %bitcast.146, bf16[4,736,128]{2,1,0:T(8,128)(2,1)} %bitcast.136, ...), custom_call_target="tpu_custom_call" | custom-call | tf_op jit(solution)/shard_map/spread_out/pallas_call | solution.py:89
  96.5 11.3 %collective-permute-done.16 = bf16[256,512]{1,0:T(8,128)(2,1)S(1)} collective-permute-done((bf16[256,512]{1,0:T(8,128)(2,1)}, bf16[256,512]{1,0:T(8,128)(2,1)S(1)}, u32[]{:S(2)}, u32[]{:S(2)}) %collective-permute-start.16) | collective-permute-done | bytes 262176 | tf_op jit(solution)/shard_map/kv_gather_z1/ppermute | solution.py:774
  107.8 3.4 collective-permute-done.19
  111.2 2.5 collective-permute-start.20
  115.8 7.8 %collective-permute-done.18 = bf16[128,512]{1,0:T(8,128)(2,1)S(1)} collective-permute-done((bf16[128,512]{1,0:T(8,128)(2,1)S(1)}, bf16[128,512]{1,0:T(8,128)(2,1)S(1)}, u32[]{:S(2)}, u32[]{:S(2)}) %collective-permute-start.18) | collective-permute-done | bytes 131104 | tf_op jit(solution)/shard_map/kv_gather_z1/ppermute | solution.py:774
  124.9 7.6 %collective-permute-done.21 = bf16[256,512]{1,0:T(8,128)(2,1)S(1)} collective-permute-done((bf16[256,512]{1,0:T(8,128)(2,1)S(1)}, bf16[256,512]{1,0:T(8,128)(2,1)S(1)}, u32[]{:S(2)}, u32[]{:S(2)}) %collective-permute-start.21) | collective-permute-done | bytes 262176 | tf_op jit(solution)/shard_map/kv_gather_vx1/ppermute | solution.py:774
  133.9 10.2 %attend.1 = (bf16[256,1024]{1,0:T(8,128)(2,1)}, f32[8,256]{1,0:T(8,128)}, f32[256,1152]{1,0:T(8,128)}, f32[256,1152]{1,0:T(8,128)}, bf16[256,1152]{1,0:T(8,128)(2,1)}) custom-call(s32[2,8]{1,0:T(2,128)} %pad_add_fusion.info_ref, bf16[256,1024]{1,0:T(8,128)(2,1)} %get-tuple-element.120.q_ref, bf16[8,256,512]{2,1,0:T(8,128)(2,1)} %copy-done.1, ...), custom_call_target="tpu_custom_call" | custom-call | tf_op jit(solution)/shard_map/attend/pallas_call | solution.py:288
  144.1 2.3 collective-permute-start.26
  147.2 12.0 %collective-permute-done.26.refs_4_.refs_5_ = bf16[256,1152]{1,0:T(8,128)(2,1)S(1)} collective-permute-done((bf16[256,1152]{1,0:T(8,128)(2,1)}, bf16[256,1152]{1,0:T(8,128)(2,1)S(1)}, u32[]{:S(2)}, u32[]{:S(2)}) %collective-permute-start.26) | collective-permute-done | bytes 589856 | tf_op jit(solution)/shard_map/ffn_in_gather_x1/ppermute | solution.py:774
  161.9 5.1 %collective-permute-done.28 = bf16[128,1152]{1,0:T(8,128)(2,1)S(1)} collective-permute-done((bf16[128,1152]{1,0:T(8,128)(2,1)S(1)}, bf16[128,1152]{1,0:T(8,128)(2,1)S(1)}, u32[]{:S(2)}, u32[]{:S(2)}) %collective-permute-start.28) | collective-permute-done | bytes 294944 | tf_op jit(solution)/shard_map/ffn_in_gather_y1/ppermute | solution.py:774
  167.9 2.1 collective-permute-done.30.refs_7_.refs_8_
  171.7 24.9 %ffn_forward.1 = (bf16[2048,896]{1,0:T(8,128)(2,1)}, bf16[2048,896]{1,0:T(8,128)(2,1)}, bf16[2048,896]{1,0:T(8,128)(2,1)}, bf16[256,1152]{1,0:T(8,128)(2,1)}, bf...) custom-call(bf16[256,1152]{1,0:T(8,128)(2,1)} %get-tuple-element.132, ...), custom_call_target="tpu_custom_call" | custom-call | flops 12683575296 | tf_op jit(solution)/shard_map/ffn_forward/pallas_call | solution.py:512
  203.6 5.7 %collective-permute-done.37 = bf16[128,1152]{1,0:T(8,128)(2,1)S(1)} collective-permute-done((bf16[128,1152]{1,0:T(8,128)(2,1)S(1)}, bf16[128,1152]{1,0:T(8,128)(2,1)S(1)}, u32[]{:S(2)}, u32[]{:S(2)}) %collective-permute-start.37) | collective-permute-done | bytes 294944 | tf_op jit(solution)/shard_map/ffn_out_sum_x-1/ppermute | solution.py:774
  213.6 10.4 %collective-permute-done.38.refs_2_ = bf16[256,1152]{1,0:T(8,128)(2,1)S(1)} collective-permute-done((bf16[256,1152]{1,0:T(8,128)(2,1)S(1)}, bf16[256,1152]{1,0:T(8,128)(2,1)S(1)}, u32[]{:S(2)}, u32[]{:S(2)}) %collective-permute-start.38) | collective-permute-done | bytes 589856 | tf_op jit(solution)/shard_map/ffn_out_sum_y-1/ppermute | solution.py:774
  226.3 3.7 after_ffn.1
  232.0 11.5 %collective-permute-done.42.refs_5_.refs_4_ = bf16[256,1152]{1,0:T(8,128)(2,1)S(1)} collective-permute-done((bf16[256,1152]{1,0:T(8,128)(2,1)}, bf16[256,1152]{1,0:T(8,128)(2,1)S(1)}, u32[]{:S(2)}, u32[]{:S(2)}) %collective-permute-start.42) | collective-permute-done | bytes 589856 | tf_op jit(solution)/shard_map/d_out_gather_x1/ppermute | solution.py:774
  246.7 4.3 collective-permute-done.44
  255.7 10.7 %unit_grads.2 = bf16[896,1152]{1,0:T(8,128)(2,1)} custom-call(bf16[2048,896]{1,0:T(8,128)(2,1)} %get-tuple-element.151.refs_0_, bf16[256,1152]{1,0:T(8,128)(2,1)} %get-tuple-element.152.refs_1_.refs_0_, bf16[256,1152]{1,0:T(8,128)(2,1)} %copy-done.61, bf16[256,1152]{1,0:T(8,128)(2,1)} %copy-done.43, bf16[256,1152]{1,0:T(8,128)(2,1)} %copy-done.62, ...), custom_call_target="tpu_custom_call" | custom-call | flops 4227858432 | tf_op jit(solution)/shard_map/unit_grads/pallas_call | solution.py:594
  266.4 24.3 %ffn_backward.1 = (bf16[2048,1792]{1,0:T(8,128)(2,1)}, bf16[256,1152]{1,0:T(8,128)(2,1)}, bf16[256,1152]{1,0:T(8,128)(2,1)}, bf16[256,1152]{1,0:T(8,128)(2,1)}, ...) custom-call(bf16[256,1152]{1,0:T(8,128)(2,1)} %get-tuple-element.152, ...), custom_call_target="tpu_custom_call" | custom-call | flops 12683575296 | tf_op jit(solution)/shard_map/ffn_backward/pallas_call | solution.py:512
  295.4 6.8 %collective-permute-done.52 = bf16[128,1152]{1,0:T(8,128)(2,1)S(1)} collective-permute-done((bf16[128,1152]{1,0:T(8,128)(2,1)S(1)}, bf16[128,1152]{1,0:T(8,128)(2,1)S(1)}, u32[]{:S(2)}, u32[]{:S(2)}) %collective-permute-start.52) | collective-permute-done | bytes 294944 | tf_op jit(solution)/shard_map/d_in_sum_x-1/ppermute | solution.py:774
  304.7 16.2 %unit_grads.3 = bf16[896,2304]{1,0:T(8,128)(2,1)} custom-call(bf16[2048,1792]{1,0:T(8,128)(2,1)} %get-tuple-element.166.refs_0_, bf16[256,1152]{1,0:T(8,128)(2,1)} %get-tuple-element.132.refs_0_.refs_1_, bf16[256,1152]{1,0:T(8,128)(2,1)} %copy-done.57, bf16[256,1152]{1,0:T(8,128)(2,1)} %copy-done.41, bf16[256,1152]{1,0:T(8,128)(2,1)} %copy-done.58, ...), custom_call_target="tpu_custom_call" | custom-call | flops 8455716864 | tf_op jit(solution)/shard_map/unit_grads/pallas_call | solution.py:594
  324.1 13.8 %attend_back.1 = (f32[256,1024]{1,0:T(8,128)}, bf16[8,256,512]{2,1,0:T(8,128)(2,1)}, bf16[256,1152]{1,0:T(8,128)(2,1)}, f32[256,1152]{1,0:T(8,128)}, f32[1,1152]{1,0:T(1,128)}, /*index=5*/f32[1,1152]{1,0:T(1,128)}) custom-call(s32[2,8]{1,0:T(2,128)} %pad_add_fusion.info_ref, bf16[256,1024]{1,0:T(8,128)(2,1)} %get-tuple-element.120.q_ref, ...), custom_call_target="tpu_custom_call" | custom-call | tf_op jit(solution)/shard_map/attend_back/pallas_call | solution.py:398
  343.5 5.2 %collective-permute-done.55 = bf16[256,512]{1,0:T(8,128)(2,1)S(1)} collective-permute-done((bf16[256,512]{1,0:T(8,128)(2,1)S(1)}, bf16[256,512]{1,0:T(8,128)(2,1)S(1)}, u32[]{:S(2)}, u32[]{:S(2)}) %collective-permute-start.55) | collective-permute-done | bytes 262176 | tf_op jit(solution)/shard_map/kv_sum_vx-1/ppermute | solution.py:774
  349.8 2.2 collective-permute-start.56
  352.0 8.0 %collective-permute-start.57 = (bf16[128,512]{1,0:T(8,128)(2,1)S(1)}, bf16[128,512]{1,0:T(8,128)(2,1)S(1)}, u32[]{:S(2)}, u32[]{:S(2)}) collective-permute-start(bf16[128,512]{1,0:T(8,128)(2,1)S(1)} %get-tuple-element.265), channel_id=1, source_target_pairs={{2,0},{4,2},{6,4},{0,6},{3,1},{5,3},{7,5},{1,7},{10,8},{12,10},{14... | collective-permute-start | bytes 393224 | tf_op jit(solution)/shard_map/kv_sum_z1/ppermute | solution.py:774
  360.0 3.4 collective-permute-done.60
  363.4 3.4 collective-permute-done.56
  368.7 6.9 %collective-permute-start.62 = (bf16[256,512]{1,0:T(8,128)(2,1)S(1)}, bf16[256,512]{1,0:T(8,128)(2,1)S(1)}, u32[]{:S(2)}, u32[]{:S(2)}) collective-permute-start(bf16[256,512]{1,0:T(8,128)(2,1)S(1)} %pad_maximum_fusion.9), channel_id=1, source_target_pairs={{2,0},{4,2},{6,4},{0,6},{3,1},{5,3},{7,5},{1,7},{10,8},{12,10},{14... | collective-permute-start | bytes 786440 | tf_op jit(solution)/shard_map/kv_sum_z1/ppermute | solution.py:774
  376.1 10.2 %query_side.1 = (f32[23056,128]{1,0:T(8,128)}, f32[256,1152]{1,0:T(8,128)}, f32[1,256]{1,0:T(1,128)}) custom-call(f32[256,1024]{1,0:T(8,128)} %get-tuple-element.171.dq_ref, f32[256,1280]{1,0:T(8,128)} %get-tuple-element.172.raw_ref.refs_3_, f32[256,128]{1,0:T(8,128)} %get-tuple-element.268.refs_9_.cos_ref.refs_4_, ...), custom_call_target="tpu_custom_call" | custom-call | tf_op jit(solution)/shard_map/query_side/pallas_call | solution.py:89
  387.1 6.5 %collective-permute-done.62.refs_2_ = bf16[256,512]{1,0:T(8,128)(2,1)S(1)} collective-permute-done((bf16[256,512]{1,0:T(8,128)(2,1)S(1)}, bf16[256,512]{1,0:T(8,128)(2,1)S(1)}, u32[]{:S(2)}, u32[]{:S(2)}) %collective-permute-start.62) | collective-permute-done | bytes 262176 | tf_op jit(solution)/shard_map/kv_sum_z1/ppermute | solution.py:774
  393.6 4.6 collective-permute-done.61.refs_1_
  398.9 12.6 %last_part.1 = (bf16[256,1152]{1,0:T(8,128)(2,1)}, bf16[4,736,128]{2,1,0:T(8,128)(2,1)}, bf16[4,736,128]{2,1,0:T(8,128)(2,1)}, bf16[4,736,128]{2,1,0:T(8,128)(2,...) custom-call(s32[32]{0:T(128)} %fusion.12.order_ref, ...), custom_call_target="tpu_custom_call" | custom-call | tf_op jit(solution)/shard_map/last_part/pallas_call | solution.py:89
  417.7 7.6 %collective-permute-done.68 = bf16[1472,128]{1,0:T(8,128)(2,1)S(1)} collective-permute-done((bf16[1472,128]{1,0:T(8,128)(2,1)S(1)}, bf16[1472,128]{1,0:T(8,128)(2,1)S(1)}, u32[]{:S(2)}, u32[]{:S(2)}) %collective-permute-start.68) | collective-permute-done | bytes 376864 | tf_op jit(solution)/shard_map/attn_grad_sum_x-1/ppermute | solution.py:774
  433.9 13.6 %collective-permute-done.69 = bf16[2944,128]{1,0:T(8,128)(2,1)S(1)} collective-permute-done((bf16[2944,128]{1,0:T(8,128)(2,1)}, bf16[2944,128]{1,0:T(8,128)(2,1)S(1)}, u32[]{:S(2)}, u32[]{:S(2)}) %collective-permute-start.69) | collective-permute-done | bytes 753696 | tf_op jit(solution)/shard_map/attn_grad_sum_x-1/ppermute | solution.py:774
  450.4 2.3 collective-permute-start.73
  456.1 3.2 collective-permute-start.74
  459.3 2.1 collective-permute-done.75
  461.5 11.1 %collective-permute-done.76 = bf16[216,864]{1,0:T(8,128)(2,1)S(1)} collective-permute-done((bf16[216,864]{1,0:T(8,128)(2,1)S(1)}, bf16[216,864]{1,0:T(8,128)(2,1)S(1)}, u32[]{:S(2)}, u32[]{:S(2)}) %collective-permute-start.76) | collective-permute-done | bytes 373280 | tf_op jit(solution)/shard_map/grad_exchange_uyc2/ppermute | solution.py:774
  472.8 5.5 %multiply_subtract_fusion = (f32[864,864]{1,0:T(8,128)}, f32[864,864]{1,0:T(8,128)}, f32[864,864]{1,0:T(8,128)}, f32[864,864]{1,0:T(8,128)}) fusion(f32[864,864]{1,0:T(8,128)S(1)} %copy-done, f32[864,864]{1,0:T(8,128)S(1)} %copy-done.7, f32[864,864]{1,0:T(8,128)S(1)} %copy-done.8, bf16[4,216,864]{2,1,0:T(8,128)(2,1)S(1)} %bitcast_dynamic-update-slice_fusion), kind=kLoop, calls=%fused_computation.3 | loop fusion | flops 11197440 | bytes 22394880 | tf_op jit(solution)/shard_map/sub | solution.py:65
  (386 shorter events, 107.1 us)
Async XLA Ops:
  7.2 164.5 %all-gather.2.cloned.1.call-start = ((), (), s32[]{:S(2)}) async-start(), calls=%async_computation.2 | async-start | bytes 7741440 | tf_op jit(solution)/shard_map/all_gather | solution.py:981
  9.2 10.2 %collective-permute-start = (bf16[736,128]{1,0:T(8,128)(2,1)S(1)}, bf16[736,128]{1,0:T(8,128)(2,1)S(1)}, u32[]{:S(2)}, u32[]{:S(2)}) collective-permute-start(bf16[736,128]{1,0:T(8,128)(2,1)S(1)} %pad_maximum_fusion.10), channel_id=1, source_target_pairs={{2,0},{4,2},{6,4},{0,6},{3,1},{5,3},{7,5},{1,7},{10,8},{12,10},{14... | collective-permute-start | bytes 565256 | tf_op jit(solution)/shard_map/attn_gather_z1/ppermute | solution.py:774
  14.3 9.5 %collective-permute-start.2 = (bf16[736,128]{1,0:T(8,128)(2,1)S(1)}, bf16[736,128]{1,0:T(8,128)(2,1)S(1)}, u32[]{:S(2)}, u32[]{:S(2)}) collective-permute-start(bf16[736,128]{1,0:T(8,128)(2,1)S(1)} %pad_maximum_fusion.10), channel_id=1, source_target_pairs={{6,0},{0,2},{2,4},{4,6},{7,1},{1,3},{3,5},{5,7},{14,8},{8,10},{10,... | collective-permute-start | bytes 565256 | tf_op jit(solution)/shard_map/attn_gather_z-1/ppermute | solution.py:774
  17.4 12.8 %collective-permute-start.4 = (bf16[216,864]{1,0:T(8,128)(2,1)}, bf16[216,864]{1,0:T(8,128)(2,1)S(1)}, u32[]{:S(2)}, u32[]{:S(2)}) collective-permute-start(bf16[216,864]{1,0:T(8,128)(2,1)} %get-tuple-element.249), channel_id=1, source_target_pairs={{8,0},{16,8},{24,16},{0,24},{9,1},{17,9},{25,17},{1,25},{10,2},{18... | collective-permute-start | bytes 1119752 | tf_op jit(solution)/shard_map/unit_exchange_uyc1/ppermute | solution.py:774
  18.1 19.1 %collective-permute-start.5 = (bf16[216,864]{1,0:T(8,128)(2,1)}, bf16[216,864]{1,0:T(8,128)(2,1)S(1)}, u32[]{:S(2)}, u32[]{:S(2)}) collective-permute-start(bf16[216,864]{1,0:T(8,128)(2,1)} %get-tuple-element.248), channel_id=1, source_target_pairs={{16,0},{24,8},{0,16},{8,24},{17,1},{25,9},{1,17},{9,25},{18,2},{26... | collective-permute-start | bytes 1119752 | tf_op jit(solution)/shard_map/unit_exchange_uyc2/ppermute | solution.py:774
  19.0 18.3 %collective-permute-start.6 = (bf16[216,864]{1,0:T(8,128)(2,1)S(1)}, bf16[216,864]{1,0:T(8,128)(2,1)S(1)}, u32[]{:S(2)}, u32[]{:S(2)}) collective-permute-start(bf16[216,864]{1,0:T(8,128)(2,1)S(1)} %get-tuple-element.247), channel_id=1, source_target_pairs={{24,0},{0,8},{8,16},{16,24},{25,1},{1,9},{9,17},{17,25},{26,2},{2,... | collective-permute-start | bytes 1119752 | tf_op jit(solution)/shard_map/unit_exchange_uyc3/ppermute | solution.py:774
  40.2 346.1 %reduce-scatter.3.cloned.1.call-start = ((), (), s32[]{:S(2)}) async-start(), calls=%async_computation.3 | async-start | bytes 2580480 | tf_op jit(solution)/shard_map/reduce_scatter | solution.py:911
  41.3 17.6 %collective-permute-start.10 = (bf16[2944,128]{1,0:T(8,128)(2,1)S(1)}, bf16[2944,128]{1,0:T(8,128)(2,1)S(1)}, u32[]{:S(2)}, u32[]{:S(2)}) collective-permute-start(bf16[2944,128]{1,0:T(8,128)(2,1)S(1)} %constant_dynamic-update-slice_fusion), channel_id=1, source_target_pairs={{1,0},{0,1},{3,2},{2,3},{5,4},{4,5},{7,6},{6,7},{9,8},{8,9},{11,10... | collective-permute-start | bytes 2261000 | tf_op jit(solution)/shard_map/attn_gather_x1/ppermute | solution.py:774
  42.8 17.7 %collective-permute-start.8 = (bf16[2944,128]{1,0:T(8,128)(2,1)S(1)}, bf16[2944,128]{1,0:T(8,128)(2,1)S(1)}, u32[]{:S(2)}, u32[]{:S(2)}) collective-permute-start(bf16[2944,128]{1,0:T(8,128)(2,1)S(1)} %constant_dynamic-update-slice_fusion), channel_id=1, source_target_pairs={{16,0},{0,16},{17,1},{1,17},{18,2},{2,18},{19,3},{3,19},{20,4},{4,... | collective-permute-start | bytes 2261000 | tf_op jit(solution)/shard_map/attn_gather_y1/ppermute | solution.py:774
  58.9 9.3 %collective-permute-start.12 = (bf16[1472,128]{1,0:T(8,128)(2,1)S(1)}, bf16[1472,128]{1,0:T(8,128)(2,1)S(1)}, u32[]{:S(2)}, u32[]{:S(2)}) collective-permute-start(bf16[1472,128]{1,0:T(8,128)(2,1)S(1)} %slice.274), channel_id=1, source_target_pairs={{16,0},{0,16},{17,1},{1,17},{18,2},{2,18},{19,3},{3,19},{20,4},{4,... | collective-permute-start | bytes 1130504 | tf_op jit(solution)/shard_map/attn_gather_y1/ppermute | solution.py:774
  63.2 9.6 %collective-permute-start.7 = (bf16[2944,128]{1,0:T(8,128)(2,1)S(1)}, bf16[2944,128]{1,0:T(8,128)(2,1)S(1)}, u32[]{:S(2)}, u32[]{:S(2)}) collective-permute-start(bf16[2944,128]{1,0:T(8,128)(2,1)S(1)} %constant_dynamic-update-slice_fusion), channel_id=1, source_target_pairs={{8,0},{0,8},{9,1},{1,9},{10,2},{2,10},{11,3},{3,11},{12,4},{4,12},... | collective-permute-start | bytes 2261000 | tf_op jit(solution)/shard_map/attn_gather_c1/ppermute | solution.py:774
  63.3 9.5 %collective-permute-start.9 = (bf16[2944,128]{1,0:T(8,128)(2,1)S(1)}, bf16[2944,128]{1,0:T(8,128)(2,1)S(1)}, u32[]{:S(2)}, u32[]{:S(2)}) collective-permute-start(bf16[2944,128]{1,0:T(8,128)(2,1)S(1)} %collective-permute-done.8), channel_id=1, source_target_pairs={{8,0},{0,8},{9,1},{1,9},{10,2},{2,10},{11,3},{3,11},{12,4},{4,12},... | collective-permute-start | bytes 2261000 | tf_op jit(solution)/shard_map/attn_gather_c1/ppermute | solution.py:774
  83.4 24.4 %collective-permute-start.16 = (bf16[256,512]{1,0:T(8,128)(2,1)}, bf16[256,512]{1,0:T(8,128)(2,1)S(1)}, u32[]{:S(2)}, u32[]{:S(2)}) collective-permute-start(bf16[256,512]{1,0:T(8,128)(2,1)} %get-tuple-element.121), channel_id=1, source_target_pairs={{2,0},{4,2},{6,4},{0,6},{3,1},{5,3},{7,5},{1,7},{10,8},{12,10},{14... | collective-permute-start | bytes 786440 | tf_op jit(solution)/shard_map/kv_gather_z1/ppermute | solution.py:774
  87.0 24.2 %collective-permute-start.19 = (bf16[256,512]{1,0:T(8,128)(2,1)}, bf16[256,512]{1,0:T(8,128)(2,1)S(1)}, u32[]{:S(2)}, u32[]{:S(2)}) collective-permute-start(bf16[256,512]{1,0:T(8,128)(2,1)} %get-tuple-element.121), channel_id=1, source_target_pairs={{6,0},{0,2},{2,4},{4,6},{7,1},{1,3},{3,5},{5,7},{14,8},{8,10},{10,... | collective-permute-start | bytes 786440 | tf_op jit(solution)/shard_map/kv_gather_z-1/ppermute | solution.py:774
  87.0 28.8 %collective-permute-start.15 = (bf16[256,512]{1,0:T(8,128)(2,1)}, bf16[256,512]{1,0:T(8,128)(2,1)S(1)}, u32[]{:S(2)}, u32[]{:S(2)}) collective-permute-start(bf16[256,512]{1,0:T(8,128)(2,1)} %get-tuple-element.121), channel_id=1, source_target_pairs={{1,0},{0,1},{3,2},{2,3},{5,4},{4,5},{7,6},{6,7},{9,8},{8,9},{11,10... | collective-permute-start | bytes 786440 | tf_op jit(solution)/shard_map/kv_gather_vx1/ppermute | solution.py:774
  107.8 15.8 %collective-permute-start.18 = (bf16[128,512]{1,0:T(8,128)(2,1)S(1)}, bf16[128,512]{1,0:T(8,128)(2,1)S(1)}, u32[]{:S(2)}, u32[]{:S(2)}) collective-permute-start(bf16[128,512]{1,0:T(8,128)(2,1)S(1)} %slice.276), channel_id=1, source_target_pairs={{2,0},{4,2},{6,4},{0,6},{3,1},{5,3},{7,5},{1,7},{10,8},{12,10},{14... | collective-permute-start | bytes 393224 | tf_op jit(solution)/shard_map/kv_gather_z1/ppermute | solution.py:774
  111.2 12.4 %collective-permute-start.20 = (bf16[128,512]{1,0:T(8,128)(2,1)S(1)}, bf16[128,512]{1,0:T(8,128)(2,1)S(1)}, u32[]{:S(2)}, u32[]{:S(2)}) collective-permute-start(bf16[128,512]{1,0:T(8,128)(2,1)S(1)} %slice.277), channel_id=1, source_target_pairs={{6,0},{0,2},{2,4},{4,6},{7,1},{1,3},{3,5},{5,7},{14,8},{8,10},{10,... | collective-permute-start | bytes 393224 | tf_op jit(solution)/shard_map/kv_gather_z-1/ppermute | solution.py:774
  113.7 11.2 %collective-permute-start.17 = (bf16[256,512]{1,0:T(8,128)(2,1)S(1)}, bf16[256,512]{1,0:T(8,128)(2,1)S(1)}, u32[]{:S(2)}, u32[]{:S(2)}) collective-permute-start(bf16[256,512]{1,0:T(8,128)(2,1)S(1)} %collective-permute-done.16), channel_id=1, source_target_pairs={{1,0},{0,1},{3,2},{2,3},{5,4},{4,5},{7,6},{6,7},{9,8},{8,9},{11,10... | collective-permute-start | bytes 786440 | tf_op jit(solution)/shard_map/kv_gather_vx1/ppermute | solution.py:774
  115.2 17.3 %collective-permute-start.22 = (bf16[256,512]{1,0:T(8,128)(2,1)S(1)}, bf16[256,512]{1,0:T(8,128)(2,1)S(1)}, u32[]{:S(2)}, u32[]{:S(2)}) collective-permute-start(bf16[256,512]{1,0:T(8,128)(2,1)S(1)} %collective-permute-done.19), channel_id=1, source_target_pairs={{1,0},{0,1},{3,2},{2,3},{5,4},{4,5},{7,6},{6,7},{9,8},{8,9},{11,10... | collective-permute-start | bytes 786440 | tf_op jit(solution)/shard_map/kv_gather_vx1/ppermute | solution.py:774
  144.1 15.1 %collective-permute-start.26 = (bf16[256,1152]{1,0:T(8,128)(2,1)}, bf16[256,1152]{1,0:T(8,128)(2,1)S(1)}, u32[]{:S(2)}, u32[]{:S(2)}) collective-permute-start(bf16[256,1152]{1,0:T(8,128)(2,1)} %get-tuple-element.132.refs_0_.refs_1_), channel_id=1, source_target_pairs={{1,0},{0,1},{3,2},{2,3},{5,4},{4,5},{7,6},{6,7},{9,8},{8,9},{11,10... | collective-permute-start | bytes 1769480 | tf_op jit(solution)/shard_map/ffn_in_gather_x1/ppermute | solution.py:774
  146.5 14.4 %collective-permute-start.24 = (bf16[256,1152]{1,0:T(8,128)(2,1)}, bf16[256,1152]{1,0:T(8,128)(2,1)S(1)}, u32[]{:S(2)}, u32[]{:S(2)}) collective-permute-start(bf16[256,1152]{1,0:T(8,128)(2,1)} %get-tuple-element.132.refs_0_.refs_1_), channel_id=1, source_target_pairs={{16,0},{0,16},{17,1},{1,17},{18,2},{2,18},{19,3},{3,19},{20,4},{4,... | collective-permute-start | bytes 1769480 | tf_op jit(solution)/shard_map/ffn_in_gather_y1/ppermute | solution.py:774
  197.3 15.4 %collective-permute-start.31 = (bf16[256,1152]{1,0:T(8,128)(2,1)}, bf16[256,1152]{1,0:T(8,128)(2,1)S(1)}, u32[]{:S(2)}, u32[]{:S(2)}) collective-permute-start(bf16[256,1152]{1,0:T(8,128)(2,1)} %get-tuple-element.138), channel_id=1, source_target_pairs={{8,0},{0,8},{9,1},{1,9},{10,2},{2,10},{11,3},{3,11},{12,4},{4,12},... | collective-permute-start | bytes 1769480 | tf_op jit(solution)/shard_map/ffn_out_sum_c1/ppermute | solution.py:774
  200.2 9.1 %collective-permute-start.37 = (bf16[128,1152]{1,0:T(8,128)(2,1)S(1)}, bf16[128,1152]{1,0:T(8,128)(2,1)S(1)}, u32[]{:S(2)}, u32[]{:S(2)}) collective-permute-start(bf16[128,1152]{1,0:T(8,128)(2,1)S(1)} %get-tuple-element.263), channel_id=1, source_target_pairs={{1,0},{0,1},{3,2},{2,3},{5,4},{4,5},{7,6},{6,7},{9,8},{8,9},{11,10... | collective-permute-start | bytes 884744 | tf_op jit(solution)/shard_map/ffn_out_sum_x-1/ppermute | solution.py:774
  209.5 14.6 %collective-permute-start.38 = (bf16[256,1152]{1,0:T(8,128)(2,1)S(1)}, bf16[256,1152]{1,0:T(8,128)(2,1)S(1)}, u32[]{:S(2)}, u32[]{:S(2)}) collective-permute-start(bf16[256,1152]{1,0:T(8,128)(2,1)S(1)} %pad_maximum_fusion.4), channel_id=1, source_target_pairs={{16,0},{0,16},{17,1},{1,17},{18,2},{2,18},{19,3},{3,19},{20,4},{4,... | collective-permute-start | bytes 1769480 | tf_op jit(solution)/shard_map/ffn_out_sum_y-1/ppermute | solution.py:774
  211.1 14.3 %collective-permute-start.35 = (bf16[256,1152]{1,0:T(8,128)(2,1)S(1)}, bf16[256,1152]{1,0:T(8,128)(2,1)S(1)}, u32[]{:S(2)}, u32[]{:S(2)}) collective-permute-start(bf16[256,1152]{1,0:T(8,128)(2,1)S(1)} %pad_maximum_fusion.3), channel_id=1, source_target_pairs={{1,0},{0,1},{3,2},{2,3},{5,4},{4,5},{7,6},{6,7},{9,8},{8,9},{11,10... | collective-permute-start | bytes 1769480 | tf_op jit(solution)/shard_map/ffn_out_sum_x-1/ppermute | solution.py:774
  229.9 13.6 %collective-permute-start.42 = (bf16[256,1152]{1,0:T(8,128)(2,1)}, bf16[256,1152]{1,0:T(8,128)(2,1)S(1)}, u32[]{:S(2)}, u32[]{:S(2)}) collective-permute-start(bf16[256,1152]{1,0:T(8,128)(2,1)} %get-tuple-element.152.refs_1_.refs_0_), channel_id=1, source_target_pairs={{1,0},{0,1},{3,2},{2,3},{5,4},{4,5},{7,6},{6,7},{9,8},{8,9},{11,10... | collective-permute-start | bytes 1769480 | tf_op jit(solution)/shard_map/d_out_gather_x1/ppermute | solution.py:774
  231.4 14.5 %collective-permute-start.40 = (bf16[256,1152]{1,0:T(8,128)(2,1)}, bf16[256,1152]{1,0:T(8,128)(2,1)S(1)}, u32[]{:S(2)}, u32[]{:S(2)}) collective-permute-start(bf16[256,1152]{1,0:T(8,128)(2,1)} %get-tuple-element.152.refs_1_.refs_0_), channel_id=1, source_target_pairs={{16,0},{0,16},{17,1},{1,17},{18,2},{2,18},{19,3},{3,19},{20,4},{4,... | collective-permute-start | bytes 1769480 | tf_op jit(solution)/shard_map/d_out_gather_y1/ppermute | solution.py:774
  290.9 137.8 %reduce-scatter.5.cloned.1.call-start = ((), (), s32[]{:S(2)}) async-start(), calls=%async_computation.4 | async-start | bytes 5160960 | tf_op jit(solution)/shard_map/reduce_scatter | solution.py:911
  291.8 29.2 %collective-permute-start.47 = (bf16[256,1152]{1,0:T(8,128)(2,1)}, bf16[256,1152]{1,0:T(8,128)(2,1)S(1)}, u32[]{:S(2)}, u32[]{:S(2)}) collective-permute-start(bf16[256,1152]{1,0:T(8,128)(2,1)} %get-tuple-element.156), channel_id=1, source_target_pairs={{8,0},{0,8},{9,1},{1,9},{10,2},{2,10},{11,3},{3,11},{12,4},{4,12},... | collective-permute-start | bytes 1769480 | tf_op jit(solution)/shard_map/d_in_sum_c1/ppermute | solution.py:774
  303.2 19.8 %collective-permute-start.53 = (bf16[256,1152]{1,0:T(8,128)(2,1)S(1)}, bf16[256,1152]{1,0:T(8,128)(2,1)S(1)}, u32[]{:S(2)}, u32[]{:S(2)}) collective-permute-start(bf16[256,1152]{1,0:T(8,128)(2,1)S(1)} %pad_maximum_fusion.5), channel_id=1, source_target_pairs={{1,0},{0,1},{3,2},{2,3},{5,4},{4,5},{7,6},{6,7},{9,8},{8,9},{11,10... | collective-permute-start | bytes 1769480 | tf_op jit(solution)/shard_map/d_in_sum_x-1/ppermute | solution.py:774
  304.4 18.6 %collective-permute-start.54 = (bf16[256,1152]{1,0:T(8,128)(2,1)S(1)}, bf16[256,1152]{1,0:T(8,128)(2,1)S(1)}, u32[]{:S(2)}, u32[]{:S(2)}) collective-permute-start(bf16[256,1152]{1,0:T(8,128)(2,1)S(1)} %pad_maximum_fusion.6), channel_id=1, source_target_pairs={{16,0},{0,16},{17,1},{1,17},{18,2},{2,18},{19,3},{3,19},{20,4},{4,... | collective-permute-start | bytes 1769480 | tf_op jit(solution)/shard_map/d_in_sum_y-1/ppermute | solution.py:774
  339.4 9.3 %collective-permute-start.55 = (bf16[256,512]{1,0:T(8,128)(2,1)S(1)}, bf16[256,512]{1,0:T(8,128)(2,1)S(1)}, u32[]{:S(2)}, u32[]{:S(2)}) collective-permute-start(bf16[256,512]{1,0:T(8,128)(2,1)S(1)} %get-tuple-element.238), channel_id=1, source_target_pairs={{1,0},{0,1},{3,2},{2,3},{5,4},{4,5},{7,6},{6,7},{9,8},{8,9},{11,10... | collective-permute-start | bytes 786440 | tf_op jit(solution)/shard_map/kv_sum_vx-1/ppermute | solution.py:774
  341.4 18.6 %collective-permute-start.58 = (bf16[256,512]{1,0:T(8,128)(2,1)S(1)}, bf16[256,512]{1,0:T(8,128)(2,1)S(1)}, u32[]{:S(2)}, u32[]{:S(2)}) collective-permute-start(bf16[256,512]{1,0:T(8,128)(2,1)S(1)} %get-tuple-element.236), channel_id=1, source_target_pairs={{1,0},{0,1},{3,2},{2,3},{5,4},{4,5},{7,6},{6,7},{9,8},{8,9},{11,10... | collective-permute-start | bytes 786440 | tf_op jit(solution)/shard_map/kv_sum_vx-1/ppermute | solution.py:774
  341.5 18.5 %collective-permute-start.59 = (bf16[256,512]{1,0:T(8,128)(2,1)S(1)}, bf16[256,512]{1,0:T(8,128)(2,1)S(1)}, u32[]{:S(2)}, u32[]{:S(2)}) collective-permute-start(bf16[256,512]{1,0:T(8,128)(2,1)S(1)} %get-tuple-element.234), channel_id=1, source_target_pairs={{1,0},{0,1},{3,2},{2,3},{5,4},{4,5},{7,6},{6,7},{9,8},{8,9},{11,10... | collective-permute-start | bytes 786440 | tf_op jit(solution)/shard_map/kv_sum_vx-1/ppermute | solution.py:774
  343.4 20.0 %collective-permute-start.60 = (bf16[256,512]{1,0:T(8,128)(2,1)S(1)}, bf16[256,512]{1,0:T(8,128)(2,1)S(1)}, u32[]{:S(2)}, u32[]{:S(2)}) collective-permute-start(bf16[256,512]{1,0:T(8,128)(2,1)S(1)} %get-tuple-element.232), channel_id=1, source_target_pairs={{1,0},{0,1},{3,2},{2,3},{5,4},{4,5},{7,6},{6,7},{9,8},{8,9},{11,10... | collective-permute-start | bytes 786440 | tf_op jit(solution)/shard_map/kv_sum_vx-1/ppermute | solution.py:774
  349.8 17.0 %collective-permute-start.56 = (bf16[128,512]{1,0:T(8,128)(2,1)S(1)}, bf16[128,512]{1,0:T(8,128)(2,1)S(1)}, u32[]{:S(2)}, u32[]{:S(2)}) collective-permute-start(bf16[128,512]{1,0:T(8,128)(2,1)S(1)} %get-tuple-element.266), channel_id=1, source_target_pairs={{6,0},{0,2},{2,4},{4,6},{7,1},{1,3},{3,5},{5,7},{14,8},{8,10},{10,... | collective-permute-start | bytes 393224 | tf_op jit(solution)/shard_map/kv_sum_z-1/ppermute | solution.py:774
  352.0 16.6 %collective-permute-start.57 = (bf16[128,512]{1,0:T(8,128)(2,1)S(1)}, bf16[128,512]{1,0:T(8,128)(2,1)S(1)}, u32[]{:S(2)}, u32[]{:S(2)}) collective-permute-start(bf16[128,512]{1,0:T(8,128)(2,1)S(1)} %get-tuple-element.265), channel_id=1, source_target_pairs={{2,0},{4,2},{6,4},{0,6},{3,1},{5,3},{7,5},{1,7},{10,8},{12,10},{14... | collective-permute-start | bytes 393224 | tf_op jit(solution)/shard_map/kv_sum_z1/ppermute | solution.py:774
  368.7 25.0 %collective-permute-start.62 = (bf16[256,512]{1,0:T(8,128)(2,1)S(1)}, bf16[256,512]{1,0:T(8,128)(2,1)S(1)}, u32[]{:S(2)}, u32[]{:S(2)}) collective-permute-start(bf16[256,512]{1,0:T(8,128)(2,1)S(1)} %pad_maximum_fusion.9), channel_id=1, source_target_pairs={{2,0},{4,2},{6,4},{0,6},{3,1},{5,3},{7,5},{1,7},{10,8},{12,10},{14... | collective-permute-start | bytes 786440 | tf_op jit(solution)/shard_map/kv_sum_z1/ppermute | solution.py:774
  375.8 22.5 %collective-permute-start.61 = (bf16[256,512]{1,0:T(8,128)(2,1)S(1)}, bf16[256,512]{1,0:T(8,128)(2,1)S(1)}, u32[]{:S(2)}, u32[]{:S(2)}) collective-permute-start(bf16[256,512]{1,0:T(8,128)(2,1)S(1)} %pad_maximum_fusion.8), channel_id=1, source_target_pairs={{6,0},{0,2},{2,4},{4,6},{7,1},{1,3},{3,5},{5,7},{14,8},{8,10},{10,... | collective-permute-start | bytes 786440 | tf_op jit(solution)/shard_map/kv_sum_z-1/ppermute | solution.py:774
  412.2 19.4 %collective-permute-start.63 = (bf16[2944,128]{1,0:T(8,128)(2,1)}, bf16[2944,128]{1,0:T(8,128)(2,1)S(1)}, u32[]{:S(2)}, u32[]{:S(2)}) collective-permute-start(bf16[2944,128]{1,0:T(8,128)(2,1)} %bitcast.163), channel_id=1, source_target_pairs={{8,0},{0,8},{9,1},{1,9},{10,2},{2,10},{11,3},{3,11},{12,4},{4,12},... | collective-permute-start | bytes 2261000 | tf_op jit(solution)/shard_map/attn_grad_sum_c1/ppermute | solution.py:774
  414.4 10.9 %collective-permute-start.68 = (bf16[1472,128]{1,0:T(8,128)(2,1)S(1)}, bf16[1472,128]{1,0:T(8,128)(2,1)S(1)}, u32[]{:S(2)}, u32[]{:S(2)}) collective-permute-start(bf16[1472,128]{1,0:T(8,128)(2,1)S(1)} %get-tuple-element.259), channel_id=1, source_target_pairs={{1,0},{0,1},{3,2},{2,3},{5,4},{4,5},{7,6},{6,7},{9,8},{8,9},{11,10... | collective-permute-start | bytes 1130504 | tf_op jit(solution)/shard_map/attn_grad_sum_x-1/ppermute | solution.py:774
  416.3 10.6 %collective-permute-start.66 = (bf16[1472,128]{1,0:T(8,128)(2,1)S(1)}, bf16[1472,128]{1,0:T(8,128)(2,1)S(1)}, u32[]{:S(2)}, u32[]{:S(2)}) collective-permute-start(bf16[1472,128]{1,0:T(8,128)(2,1)S(1)} %get-tuple-element.260), channel_id=1, source_target_pairs={{16,0},{0,16},{17,1},{1,17},{18,2},{2,18},{19,3},{3,19},{20,4},{4,... | collective-permute-start | bytes 1130504 | tf_op jit(solution)/shard_map/attn_grad_sum_y-1/ppermute | solution.py:774
  428.7 18.9 %collective-permute-start.69 = (bf16[2944,128]{1,0:T(8,128)(2,1)}, bf16[2944,128]{1,0:T(8,128)(2,1)S(1)}, u32[]{:S(2)}, u32[]{:S(2)}) collective-permute-start(bf16[2944,128]{1,0:T(8,128)(2,1)} %pad_maximum_fusion.1), channel_id=1, source_target_pairs={{1,0},{0,1},{3,2},{2,3},{5,4},{4,5},{7,6},{6,7},{9,8},{8,9},{11,10... | collective-permute-start | bytes 2261000 | tf_op jit(solution)/shard_map/attn_grad_sum_x-1/ppermute | solution.py:774
  430.1 18.4 %collective-permute-start.70 = (bf16[2944,128]{1,0:T(8,128)(2,1)S(1)}, bf16[2944,128]{1,0:T(8,128)(2,1)S(1)}, u32[]{:S(2)}, u32[]{:S(2)}) collective-permute-start(bf16[2944,128]{1,0:T(8,128)(2,1)S(1)} %pad_maximum_fusion.2), channel_id=1, source_target_pairs={{16,0},{0,16},{17,1},{1,17},{18,2},{2,18},{19,3},{3,19},{20,4},{4,... | collective-permute-start | bytes 2261000 | tf_op jit(solution)/shard_map/attn_grad_sum_y-1/ppermute | solution.py:774
  453.1 19.5 %collective-permute-start.76 = (bf16[216,864]{1,0:T(8,128)(2,1)S(1)}, bf16[216,864]{1,0:T(8,128)(2,1)S(1)}, u32[]{:S(2)}, u32[]{:S(2)}) collective-permute-start(bf16[216,864]{1,0:T(8,128)(2,1)S(1)} %get-tuple-element.240), channel_id=1, source_target_pairs={{16,0},{24,8},{0,16},{8,24},{17,1},{25,9},{1,17},{9,25},{18,2},{26... | collective-permute-start | bytes 1119752 | tf_op jit(solution)/shard_map/grad_exchange_uyc2/ppermute | solution.py:774
  454.6 18.1 %collective-permute-start.77 = (bf16[216,864]{1,0:T(8,128)(2,1)S(1)}, bf16[216,864]{1,0:T(8,128)(2,1)S(1)}, u32[]{:S(2)}, u32[]{:S(2)}) collective-permute-start(bf16[216,864]{1,0:T(8,128)(2,1)S(1)} %get-tuple-element.239), channel_id=1, source_target_pairs={{24,0},{0,8},{8,16},{16,24},{25,1},{1,9},{9,17},{17,25},{26,2},{2,... | collective-permute-start | bytes 1119752 | tf_op jit(solution)/shard_map/grad_exchange_uyc3/ppermute | solution.py:774
  456.1 22.2 %collective-permute-start.74 = (bf16[736,128]{1,0:T(8,128)(2,1)S(1)}, bf16[736,128]{1,0:T(8,128)(2,1)S(1)}, u32[]{:S(2)}, u32[]{:S(2)}) collective-permute-start(bf16[736,128]{1,0:T(8,128)(2,1)S(1)} %pad_maximum_fusion.13), channel_id=1, source_target_pairs={{2,0},{4,2},{6,4},{0,6},{3,1},{5,3},{7,5},{1,7},{10,8},{12,10},{14... | collective-permute-start | bytes 565256 | tf_op jit(solution)/shard_map/attn_grad_sum_z1/ppermute | solution.py:774
  459.2 19.1 %collective-permute-start.72 = (bf16[736,128]{1,0:T(8,128)(2,1)S(1)}, bf16[736,128]{1,0:T(8,128)(2,1)S(1)}, u32[]{:S(2)}, u32[]{:S(2)}) collective-permute-start(bf16[736,128]{1,0:T(8,128)(2,1)S(1)} %pad_maximum_fusion.12), channel_id=1, source_target_pairs={{6,0},{0,2},{2,4},{4,6},{7,1},{1,3},{3,5},{5,7},{14,8},{8,10},{10,... | collective-permute-start | bytes 565256 | tf_op jit(solution)/shard_map/attn_grad_sum_z-1/ppermute | solution.py:774
  (101 other events, 728.4 us)
Sparse Core Ops, SparseCore 0:
  40.3 131.3 all-gather.1
  291.0 43.3 reduce-scatter.2
  336.8 91.8 reduce-scatter.4

commit v4 on v3

--- a/solution.py
+++ b/solution.py
@@ -85,7 +85,7 @@
 SPACES = {"v": pltpu.VMEM, "h": pl.ANY, "s": pltpu.SMEM}
 
 
-def run(name, body, operands, spaces, out_shape, scratch=(), out_spaces=None):
+def run(name, body, operands, spaces, out_shape, scratch=(), out_spaces=None, flops=0):
     return pl.pallas_call(
         body,
         out_shape=tuple(jax.ShapeDtypeStruct(s, d) for s, d in out_shape),
@@ -95,7 +95,7 @@
         ),
         scratch_shapes=list(scratch),
         compiler_params=pltpu.CompilerParams(vmem_limit_bytes=VMEM_LIMIT),
-        cost_estimate=pl.CostEstimate(flops=0, bytes_accessed=0, transcendentals=0),
+        cost_estimate=pl.CostEstimate(flops=flops, bytes_accessed=0, transcendentals=0),
         name=name,
     )(*operands)
 
@@ -112,6 +112,14 @@
         widths = [D, HD, HD, D, D, D]
         self.gain_rows = [w // LANES for w in widths]
         self.gain_lines = sum(self.gain_rows)
+
+        across, kv = self.q_across, 2 * HD // LANES
+        self.kv_across = kv
+        self.late_rows = self.lines // across + (2 if self.lines % across else 0)
+        self.late_lines = -(-self.late_rows * kv // 16) * 16
+
+    def first_row(self, device):
+        return self.lines * device // self.q_across
 
     def gain_line(self, device):
         return self.gain_piece * device // LANES
@@ -187,6 +195,7 @@
             pltpu.VMEM((-(-(flat.gain_lines + 3) // 8) * 8, LANES), f32),
             pltpu.SemaphoreType.DMA((flat.devices,)),
         ],
+        flops=8 * 2 * tok_rows * D * wide,
     )
 
 
@@ -321,7 +330,9 @@
             jax.ShapeDtypeStruct((rows, D), bf16),
         ),
         compiler_params=pltpu.CompilerParams(vmem_limit_bytes=VMEM_LIMIT),
-        cost_estimate=pl.CostEstimate(flops=0, bytes_accessed=0, transcendentals=0),
+        cost_estimate=pl.CostEstimate(
+            flops=8 * 4 * blocks * rows * rows * H * HD, bytes_accessed=0, transcendentals=0
+        ),
         name="attend",
     )(info, query, kv, key_docs, query_docs, w_out, tokens, g_post, g_fpre)
 
@@ -474,30 +485,47 @@
                 do(copy)
 
 
-def ffn_call(name, body, rows, streams, weights, outs):
+def ffn_call(name, body, rows, streams, weights, outs, order):
     count, (tok, wide) = len(rows), rows[0].shape
     chunks = -(-count * tok // 512)
     both = count * tok // chunks
-    per = weights.shape[0]
+    blocks = len(weights)
+    starts = np.cumsum([0] + [w.shape[0] for w in weights]).tolist()
+    per = starts[-1]
 
     def kernel(*refs):
         row_refs, refs = refs[:count], refs[count:]
         stream_refs, refs = refs[: len(streams)], refs[len(streams) :]
-        w_refs, refs = refs[:3], refs[3:]
+        w_refs, refs = refs[:blocks], refs[blocks:]
         out_refs, refs = refs[: len(outs)], refs[len(outs) :]
-        sum_refs, (held, given, sems_in, sems_out) = refs[:count], refs[count:]
+        sum_refs, (held, given, units, sems_in, sems_out, sems_w) = refs[:count], refs[count:]
         step = pl.program_id(0)
         coming = gather_rows(row_refs, held, sems_in)
         going = scatter_rows(given, sum_refs, sems_out)
+        brought = {
+            k: [
+                pltpu.make_async_copy(
+                    ref.at[:, k * D : (k + 1) * D],
+                    units.at[k, starts[i] : starts[i + 1]],
+                    sems_w.at[k * blocks + i],
+                )
+                for i, ref in enumerate(w_refs)
+            ]
+            for k in order
+        }
 
         @pl.when(step == 0)
         def _():
-            for copy in coming:
+            first = len(coming) // chunks
+            bringing = [c for k in order for c in brought[k]]
+            for copy in coming[:first] + bringing + coming[first:]:
                 copy.start()
+            for copy in bringing:
+                copy.wait()
 
         by_chunk(step, chunks, coming, lambda copy: copy.wait())
         here = pl.ds(pl.multiple_of(step * both, both), both)
-        given[here, :] = body(held[here, :], stream_refs, w_refs, out_refs)
+        given[here, :] = body(held[here, :], stream_refs, units, out_refs)
         by_chunk(step, chunks, going, lambda copy: copy.start())
 
         @pl.when(step == chunks - 1)
@@ -514,7 +542,7 @@
         grid=(chunks,),
         in_specs=[anywhere] * count
         + [chunk(s.shape[1]) for s in streams]
-        + [pl.BlockSpec((per, D), lambda i, k=k: (0, k)) for k in range(3)],
+        + [anywhere] * blocks,
         out_specs=tuple([chunk(w) for w in outs] + [anywhere] * count),
         out_shape=tuple(
             [jax.ShapeDtypeStruct((count * tok, w), bf16) for w in outs]
@@ -523,88 +551,83 @@
         scratch_shapes=[
             pltpu.VMEM((count * tok, wide), bf16),
             pltpu.VMEM((count * tok, wide), bf16),
+            pltpu.VMEM((3, per, D), bf16),
             pltpu.SemaphoreType.DMA((count,)),
             pltpu.SemaphoreType.DMA((count,)),
+            pltpu.SemaphoreType.DMA((3 * blocks,)),
         ],
         compiler_params=pltpu.CompilerParams(vmem_limit_bytes=VMEM_LIMIT),
         cost_estimate=pl.CostEstimate(
             flops=6 * count * tok * per * D, bytes_accessed=0, transcendentals=0
         ),
         name=name,
-    )(*rows, *streams, weights, weights, weights)
+    )(*rows, *streams, *weights)
 
 
 def ffn_forward(rows, weights):
-    def body(x, _, w_refs, out_refs):
+    def body(x, _, weight, out_refs):
         act_ref, gelu_ref, slope_ref = out_refs
-        gate = contract(x, w_refs[0][...], 1, 1)
-        up = contract(x, w_refs[1][...], 1, 1)
+        gate = contract(x, weight[0], 1, 1)
+        up = contract(x, weight[1], 1, 1)
         gelu, slope = gelu_parts(gate)
         act = (gelu * up).astype(bf16)
         act_ref[...] = act
         gelu_ref[...] = gelu.astype(bf16)
         slope_ref[...] = (slope * up).astype(bf16)
-        return contract(act, w_refs[2][...], 1, 0).astype(bf16)
-
-    per = weights.shape[0]
-    act, gelu, slope, *parts = ffn_call("ffn_forward", body, rows, [], weights, [per] * 3)
+        return contract(act, weight[2], 1, 0).astype(bf16)
+
+    units = sum(w.shape[0] for w in weights)
+    act, gelu, slope, *parts = ffn_call("ffn_forward", body, rows, [], weights, [units] * 3, (0, 1, 2))
     return act, gelu, slope, parts
 
 
 def ffn_backward(rows, gelu, slope, weights):
-    per = weights.shape[0]
-
-    def body(x, stream_refs, w_refs, out_refs):
+    units = sum(w.shape[0] for w in weights)
+
+    def body(x, stream_refs, weight, out_refs):
         gelu_ref, slope_ref = stream_refs
-        d_act = contract(x, w_refs[2][...], 1, 1)
+        d_act = contract(x, weight[2], 1, 1)
         d_gate = (d_act * slope_ref[...].astype(f32)).astype(bf16)
         d_up = (d_act * gelu_ref[...].astype(f32)).astype(bf16)
-        out_refs[0][:, :per] = d_gate
-        out_refs[0][:, per:] = d_up
-        return (contract(d_gate, w_refs[0][...], 1, 0) + contract(d_up, w_refs[1][...], 1, 0)).astype(bf16)
-
-    d_both, *parts = ffn_call("ffn_backward", body, rows, [gelu, slope], weights, [2 * per])
+        out_refs[0][:, :units] = d_gate
+        out_refs[0][:, units:] = d_up
+        return (contract(d_gate, weight[0], 1, 0) + contract(d_up, weight[1], 1, 0)).astype(bf16)
+
+    d_both, *parts = ffn_call(
+        "ffn_backward", body, rows, [gelu, slope], weights, [2 * units], (2, 0, 1)
+    )
     return d_both, parts
 
 
-def unit_grads(units, per, rows):
-    parts, count = len(units), len(rows)
-    tokens, wide = sum(u.shape[0] for u in units), units[0].shape[1]
-    n = wide // per
-
-    def body(*refs):
-        unit_refs, row_refs = refs[:parts], refs[parts : parts + count]
-        out_ref, held, sems = refs[parts + count :]
+def unit_grads(units, part, blocks, per, rows):
+    count = len(rows)
+    tokens, both = units.shape[0], blocks * per
+
+    def body(unit_ref, *refs):
+        row_refs, out_refs, (held, sems) = refs[:count], refs[count : count + blocks], refs[-2:]
         copies = gather_rows(row_refs, held, sems)
-
-        @pl.when(pl.program_id(0) == 0)
-        def _():
-            for copy in copies:
-                copy.start()
-            for copy in copies:
-                copy.wait()
-
-        total, at = None, 0
-        for ref in unit_refs:
-            part = contract(ref[...], held[at : at + ref.shape[0], :], 0, 0)
-            total = part if total is None else total + part
-            at += ref.shape[0]
-        out_ref[...] = total.astype(bf16)
+        for copy in copies:
+            copy.start()
+        for copy in copies:
+            copy.wait()
+        total = contract(unit_ref[...], held[...], 0, 0).astype(bf16)
+        for i, ref in enumerate(out_refs):
+            ref[...] = total[i * per : (i + 1) * per]
 
     return pl.pallas_call(
         body,
-        grid=(n,),
-        in_specs=[pl.BlockSpec((u.shape[0], per), lambda i: (0, i)) for u in units]
+        grid=(1,),
+        in_specs=[pl.BlockSpec((tokens, both), lambda i: (0, part))]
         + [pl.BlockSpec(memory_space=pl.ANY)] * count,
-        out_specs=pl.BlockSpec((per, D), lambda i: (0, i)),
-        out_shape=jax.ShapeDtypeStruct((per, n * D), bf16),
+        out_specs=[pl.BlockSpec((per, D), lambda i: (0, 0))] * blocks,
+        out_shape=[jax.ShapeDtypeStruct((per, D), bf16)] * blocks,
         scratch_shapes=[pltpu.VMEM((tokens, D), bf16), pltpu.SemaphoreType.DMA((count,))],
         compiler_params=pltpu.CompilerParams(vmem_limit_bytes=VMEM_LIMIT),
         cost_estimate=pl.CostEstimate(
-            flops=2 * tokens * wide * D, bytes_accessed=0, transcendentals=0
+            flops=2 * tokens * both * D, bytes_accessed=0, transcendentals=0
         ),
         name="unit_grads",
-    )(*units, *rows)
+    )(units, *rows)
 
 
 def after_ffn(out_parts, middle, cotangent, g_fpost):
@@ -780,7 +803,8 @@
     def outers(self):
         return [(ou, ov) for ou in range(self.sizes["u"]) for ov in range(self.sizes["v"])]
 
-    def plane_gather(self, value, beside=None):
+    def plane_gather(self, value, beside=(None, None)):
+        early, late = beside
         nx, ny = self.sizes["x"], self.sizes["y"]
         half = halfway(value.shape[0])
         found = {(0, 0): value}
@@ -788,22 +812,30 @@
             found[ox, 0] = self.fro(value, "x", ox)
         for oy in range(1, ny):
             found[0, oy] = self.fro(value, "y", oy)
-        if beside is not None:
-            found, beside = lax.optimization_barrier((found, beside))
+        if early is not None:
+            found, early = lax.optimization_barrier((found, early))
+        halves = {}
         for ox in range(1, nx):
             for oy in range(1, ny):
                 first = self.fro(found[ox, 0][:half], "y", oy)
                 second = self.fro(found[0, oy][half:], "x", ox)
-                found[ox, oy] = jnp.concatenate([first, second], axis=0)
+                halves[ox, oy] = [first, second]
+        if late is not None:
+            halves, late = lax.optimization_barrier((halves, late))
+        found.update({at: jnp.concatenate(v, axis=0) for at, v in halves.items()})
         found = {at: [block, self.fro(block, "c", 1)] for at, block in found.items()}
-        return found if beside is None else (found, beside)
-
-    def plane_scatter(self, parts, beside=None):
+        return found, (early, late)
+
+    def plane_scatter(self, parts, first=None, second=None):
         nx, ny = self.sizes["x"], self.sizes["y"]
         low = {
             at: add_low(parts[at][0], self.fro(parts[at][1], "c", 1))
             for at in sorted(parts, reverse=True)
         }
+        what = self.what
+        if first is not None:
+            low = first(low)
+            self.what = what
         half = halfway(low[0, 0].shape[0])
         along_x = {ox: [low[ox, 0][:half]] for ox in range(1, nx)}
         along_y = {oy: [low[0, oy][half:]] for oy in range(1, ny)}
@@ -817,12 +849,13 @@
         by_y = {
             oy: jnp.concatenate([low[0, oy][:half], add_low(*v)], axis=0) for oy, v in along_y.items()
         }
-        if beside is not None:
-            by_x, by_y, beside = lax.optimization_barrier((by_x, by_y, beside))
+        if second is not None:
+            by_x, by_y = second((by_x, by_y))
+            self.what = what
         terms = [low[0, 0]]
         terms += [self.fro(v, "x", -ox) for ox, v in by_x.items()]
         terms += [self.fro(v, "y", -oy) for oy, v in by_y.items()]
-        return terms if beside is None else (terms, beside)
+        return terms
 
     def z_begin(self, value):
         n = self.sizes["z"]
@@ -900,15 +933,12 @@
             ]
         )
 
-    def plane_rows(value):
-        found = ways.plane_gather(value)
-        return [block for p in places for block in found[p]]
+    def plane_rows(value, *beside):
+        found, beside = ways.plane_gather(value, beside or (None, None))
+        return [block for p in places for block in found[p]], beside
 
     def by_device(parts):
         return {p: parts[i * nc : (i + 1) * nc] for i, p in enumerate(places)}
-
-    def own_units(grad):
-        return lax.psum_scatter(to_outers(grad), "z", scatter_dimension=0, tiled=True)
 
     def shards(
         tokens, cotangent, segments, positions, attn_w, attn_m, attn_v,
@@ -975,10 +1005,31 @@
         rows_own = jnp.concatenate([by_cols[i] for i in range(ns)], axis=1)
         rows_own = jnp.pad(rows_own, ((0, held - share), (0, 0)))
         ways.what = "attn_gather"
-        line_z = from_outers(jnp.concatenate(line_blocks, axis=0))
-        gathered = ways.plane_gather(line_z)
+        line_z, rows_own = lax.optimization_barrier(
+            (from_outers(jnp.concatenate(line_blocks, axis=0)), rows_own)
+        )
+        def next_units(ring, *beside):
+            if beside:
+                ring[-1], *beside = lax.optimization_barrier((ring[-1],) + beside)
+            what, ways.what = ways.what, "unit_gather"
+            ring.append(ways.fro(ring[-1], "z", 1))
+            ways.what = what
+            return beside[0] if len(beside) == 1 else beside
+
+        steps = nz == 4
+        cut = halfway(held)
+        whole = [rows_own]
+        next_units(whole)
+        gathered, _ = ways.plane_gather(line_z)
         line_parts = [part.reshape(-1, flat.rows, LANES) for p in places for part in gathered[p]]
-        units_here = from_outers(lax.all_gather(rows_own, "z", axis=0, tiled=True))
+        line_parts, whole[-1] = lax.optimization_barrier((line_parts, whole[-1]))
+        rings = [[v[:cut] for v in whole], [v[cut:] for v in whole]]
+        if steps:
+            next_units(rings[0])
+        else:
+            for ring in rings:
+                for _ in range(2, nz):
+                    next_units(ring)
 
         tok_rows = tokens.shape[1]
         cosine, sine = angles(positions[0])
@@ -987,9 +1038,16 @@
         ) = first_part(flat, line_parts, order, tokens[0], cosine, sine)
         w_out = spread_out(flat, [after(part, kv_local) for part in line_parts], order)
         ways.what = "kv_gather"
-        kv_all = jnp.stack(
-            [ways.fro(block, ACROSS, oa) for block in ways.z_gather(kv_local) for oa in range(nx)]
-        )
+        if steps:
+            half = halfway(tok_rows)
+            above, below = ways.z_begin(kv_local)
+            above, below, rings[0][-1] = next_units(rings[1], above, below, rings[0][-1])
+            far = ways.fro(above[:half], "z", 1), ways.fro(below[half:], "z", -1)
+            far = next_units(rings[0], *far)
+            kv_blocks = [kv_local, above, jnp.concatenate(far, axis=0), below]
+        else:
+            kv_blocks = ways.z_gather(kv_local)
+        kv_all = jnp.stack([ways.fro(block, ACROSS, oa) for block in kv_blocks for oa in range(nx)])
 
         doc_all = segments[0]
         first_docs, last_docs = doc_all[::tok_rows], doc_all[tok_rows - 1 :: tok_rows]
@@ -1012,31 +1070,81 @@
         )
 
         ways.what = "ffn_in_gather"
-        ffn_rows = plane_rows(ffn_in)
+        if steps:
+            ffn_in = next_units(rings[1], ffn_in)
+            ffn_rows, (rings[0][-1], rings[1][-1]) = plane_rows(ffn_in, rings[0][-1], rings[1][-1])
+        else:
+            ffn_rows, _ = plane_rows(ffn_in)
+        units_here = [from_outers(block) for block in whole[:nz]]
+        units_here += [from_outers(block) for pair in zip(rings[0][2:], rings[1][2:]) for block in pair]
         act, gelu, slope, parts = ffn_forward(ffn_rows, units_here)
         ways.what = "ffn_out_sum"
         out_parts = ways.plane_scatter(by_device(parts))
         mixed, d_mlp_out, d_gfpost = after_ffn(out_parts, middle, cotangent[0], g_fpost)
 
         ways.what = "d_out_gather"
-        d_out_rows = plane_rows(d_mlp_out)
-        held_here = units_here.shape[0]
-        d_w_down = unit_grads([act], held_here, d_out_rows)
-        ways.what = "ffn_grad_sum"
-        owned_down = own_units(d_w_down)
-        d_out_rows[0] = after(d_out_rows[0], d_w_down)
+        d_out_rows, _ = plane_rows(d_mlp_out)
+        per = units_here[0].shape[0]
+
+        def z_step(blocks, far, *earlier):
+            value = blocks[far] if not earlier else add_low(blocks[far], *earlier)
+            return ways.fro(value, "z", -1)
+
+        class Ring:
+            def __init__(self, name, blocks):
+                self.name, self.blocks, self.at, self.heard = name, [to_outers(b) for b in blocks], nz, None
+
+            def step(self, beside=None):
+                if not steps:
+                    return beside
+                if self.heard is not None and beside is not None:
+                    self.heard, beside = lax.optimization_barrier((self.heard, beside))
+                self.at -= 1
+                if self.at > 0:
+                    value = self.blocks[self.at]
+                    if self.heard is not None:
+                        value = add_low(value, self.heard)
+                    what, ways.what = ways.what, self.name
+                    self.heard = ways.fro(value, "z", -1)
+                    ways.what = what
+                return beside
+
+            def result(self):
+                if steps:
+                    return add_low(self.blocks[0], self.heard)
+                return add_low(*[ways.fro(v, "z", -i) for i, v in enumerate(self.blocks)])
+
+        down = Ring("down_grad_sum", unit_grads(act, 0, nz, per, d_out_rows))
+        down.step()
+        d_out_rows[0] = after(d_out_rows[0], down.blocks[0])
         d_both, parts = ffn_backward(d_out_rows, gelu, slope, units_here)
+        parts[-1] = down.step(parts[-1])
+        rings = {}
+
+        def gate_then(low):
+            low, both = lax.optimization_barrier((low, d_both))
+            rings["gate"] = Ring("gate_grad_sum", unit_grads(both, 0, nz, per, ffn_rows))
+            rings["gate"].step()
+            return low
+
+        def up_then(summed):
+            summed = down.step(summed)
+            summed, both = lax.optimization_barrier((summed, d_both))
+            rings["up"] = Ring("up_grad_sum", unit_grads(both, 1, nz, per, ffn_rows))
+            rings["up"].step()
+            return summed
+
         ways.what = "d_in_sum"
-        d_in_parts, d_both = ways.plane_scatter(by_device(parts), d_both)
-
-        d_w_gate_up = unit_grads([d_both], held_here, ffn_rows)
-        owned_gate_up = own_units(d_w_gate_up)
-        d_in_parts = lax.optimization_barrier((d_in_parts, d_w_gate_up))[0]
+        d_in_parts = ways.plane_scatter(by_device(parts), gate_then, up_then)
+        d_in_parts = lax.optimization_barrier((d_in_parts, rings["up"].blocks[0]))[0]
+        d_in_parts = rings["gate"].step(d_in_parts)
 
         d_query, d_kv, d_attn_out, d_middle, d_gfpre, d_gpost = attend_back(
             info, query, kv_all, key_docs, query_docs, heads, log_total, d_in_parts, middle, attn_out,
             cotangent[0], w_out, g_post, g_fpre,
         )
+        d_kv = rings["up"].step(d_kv)
+        d_kv = down.step(d_kv)
         ways.what = "kv_sum"
         d_kv = d_kv.reshape(nz, nx, tok_rows, 2 * HD)
 
@@ -1047,13 +1155,12 @@
         kv_parts = {far: add_low(*across(far))}
         near = {oz: across(oz) for oz in range(nz) if oz != far}
         begun = ways.z_scatter_begin(kv_parts[far])
-        if begun:
-            begun, near = lax.optimization_barrier((begun, near))
-        near[0], owned_down = lax.optimization_barrier((near[0], owned_down))
+        near, begun = rings["gate"].step(lax.optimization_barrier((near, begun)))
         kv_parts.update({oz: add_low(*terms) for oz, terms in near.items()})
         kv_parts = [kv_parts[0], *ways.z_scatter_go(kv_parts, begun)]
+        kv_parts = rings["up"].step(kv_parts)
         lines, da_query, d_gq = query_side(
-            flat, d_query, raw, cosine, sine, g_q, normed_in, w_qkv, heads, d_attn_out
+            flat, after(d_query, *near[0]), raw, cosine, sine, g_q, normed_in, w_qkv, heads, d_attn_out
         )
         input_grad, *packed = last_part(
             flat, order, len(places) * nc, lines, kv_parts, raw, cosine, sine, g_k, normed_in, w_qkv, tokens[0],
@@ -1062,10 +1169,9 @@
 
         ways.what = "attn_grad_sum"
         packed = [part.reshape(-1, LANES) for part in packed]
-        terms, owned_gate_up = ways.plane_scatter(
-            {p: packed[i * nc : (i + 1) * nc] for i, p in enumerate(places)}, owned_gate_up
-        )
-        own_rows = jnp.concatenate([owned_gate_up[:share], owned_down[:share]], axis=1)
+        terms = ways.plane_scatter({p: packed[i * nc : (i + 1) * nc] for i, p in enumerate(places)})
+        owned = [rings["gate"].result(), rings["up"].result(), down.result()]
+        own_rows = jnp.concatenate([v[:share] for v in owned], axis=1)
         by_cols = jnp.stack([own_rows[:, i * width : (i + 1) * width] for i in range(ns)])
         terms, by_cols = lax.optimization_barrier((terms, by_cols))
         plane_sum = to_outers(add_low(*terms))

time: 494 us -> 484 us (0.980)
  waiting for transfers between devices: 200 us -> 184 us
  between operations: 15.7 us -> 2.74 us
  starting transfers between devices: 85.6 us -> 97.6 us
  Pallas kernels: 141 us -> 147 us
    ppermute x78 -> x92, waiting for transfers between devices: 198 us -> 184 us  [fro(): return lax.ppermute(value, axis, [((i + offset) % n, i) for i in range(n)])]
    ppermute x78 -> x92, starting transfers between devices: 85.5 us -> 97.6 us  [fro(): return lax.ppermute(value, axis, [((i + offset) % n, i) for i in range(n)])]
    pallas_call x2 -> x3, Pallas kernels: 26.9 us -> 31.6 us  [unit_grads(): pl.pallas_call(body, grid=(1,), in_specs=[pl.BlockSpec((tokens, both), la...]
  transfers between devices with their start and end apart: 81 -> 92, of which waited for: 50 -> 47; matrix products, arithmetic and copies ran while one was open for 6% -> 6% of each run, Pallas kernels for 16% -> 23%
where the time goes in v4:
time: 484 us; the launch traced here: 477 us
  waiting for transfers between devices  184 us (38%)
  Pallas kernels  147 us (30%)
  starting transfers between devices  97.6 us (20%)
  other arithmetic  23.7 us (5%)
  local copies, waits for them, and re-layouts  22.2 us (5%)
    ppermute x92, waiting for transfers between devices, fro(): return lax.ppermute(value, axis, [((i + offset) % n, i) for i in range(n)])  184 us
    ppermute x92, starting transfers between devices, fro(): return lax.ppermute(value, axis, [((i + offset) % n, i) for i in range(n)])  97.6 us
    pallas_call x2, Pallas kernels, ffn_call(): pl.pallas_call(kernel, grid=(chunks,), in_specs=[anywhere] * count + [chu...  50 us
    pallas_call x5, Pallas kernels, run(): pl.pallas_call(body, out_shape=tuple((jax.ShapeDtypeStruct(s, d) for s, d...  41.1 us
    pallas_call x3, Pallas kernels, unit_grads(): pl.pallas_call(body, grid=(1,), in_specs=[pl.BlockSpec((tokens, both), la...  31.6 us
    pallas_call x1, Pallas kernels, attend_back(): pl.pallas_call(body, grid_spec=pltpu.PrefetchScalarGridSpec(num_scalar_pr...  13.8 us
    pallas_call x1, Pallas kernels, attend(): pl.pallas_call(body, grid_spec=pltpu.PrefetchScalarGridSpec(num_scalar_pr...  10.2 us
  transfers between devices with their start and end apart: 92, of which 47 were waited for; matrix products, arithmetic and copies ran while one was open for 6% of the time, Pallas kernels for 23%

profile of v4, /device:TPU:0, one launch (start us, length us, event | category | flops | bytes accessed | tf_op | source)
XLA Modules:
  0.0 476.9 jit_solution(6382184780483310816)
XLA Ops:
  2.7 5.1 %collective-permute-start = (bf16[736,128]{1,0:T(8,128)(2,1)S(1)}, bf16[736,128]{1,0:T(8,128)(2,1)S(1)}, u32[]{:S(2)}, u32[]{:S(2)}) collective-permute-start(bf16[736,128]{1,0:T(8,128)(2,1)S(1)} %pad_maximum_fusion.12), channel_id=1, source_target_pairs={{2,0},{4,2},{6,4},{0,6},{3,1},{5,3},{7,5},{1,7},{10,8},{12,10},{14... | collective-permute-start | bytes 565256 | tf_op jit(solution)/shard_map/attn_gather_z1/ppermute | solution.py:797
  12.9 4.3 collective-permute-start.1
  20.3 3.4 collective-permute-done.3
  23.7 7.0 %collective-permute-done.5 = bf16[216,864]{1,0:T(8,128)(2,1)S(1)} collective-permute-done((bf16[216,864]{1,0:T(8,128)(2,1)}, bf16[216,864]{1,0:T(8,128)(2,1)S(1)}, u32[]{:S(2)}, u32[]{:S(2)}) %collective-permute-start.5) | collective-permute-done | bytes 373280 | tf_op jit(solution)/shard_map/unit_exchange_uyc2/ppermute | solution.py:797
  36.5 3.5 collective-permute-start.15
  40.0 11.3 %collective-permute-done.10 = bf16[2944,128]{1,0:T(8,128)(2,1)S(1)} collective-permute-done((bf16[2944,128]{1,0:T(8,128)(2,1)S(1)}, bf16[2944,128]{1,0:T(8,128)(2,1)S(1)}, u32[]{:S(2)}, u32[]{:S(2)}) %collective-permute-start.10) | collective-permute-done | bytes 753696 | tf_op jit(solution)/shard_map/attn_gather_x1/ppermute | solution.py:797
  56.2 4.5 collective-permute-done.12
  65.2 6.7 %collective-permute-done.15.refs_9_.refs_11_ = bf16[224,3456]{1,0:T(8,128)(2,1)} collective-permute-done((bf16[224,3456]{1,0:T(8,128)(2,1)}, bf16[224,3456]{1,0:T(8,128)(2,1)}, u32[]{:S(2)}, u32[]{:S(2)}) %collective-permute-start.15) | collective-permute-done | bytes 1548320 | tf_op jit(solution)/shard_map/unit_gather_z1/ppermute | solution.py:797
  71.9 2.6 fusion.28
  74.5 4.3 collective-permute-start.18
  78.9 8.9 %first_part.1 = (bf16[1152,1536]{1,0:T(8,128)(2,1)}, f32[1,1152]{1,0:T(1,128)}, f32[1,256]{1,0:T(1,128)}, f32[1,256]{1,0:T(1,128)}, f32[1,1152]{1,0:T(1,128)}, /...) custom-call(s32[32]{0:T(128)} %fusion.12.order_ref, ...), custom_call_target="tpu_custom_call" | custom-call | flops 7247757312 | tf_op jit(solution)/shard_map/first_part/pallas_call | solution.py:89
  93.4 5.9 %spread_out.1.w_ref.refs_6_ = bf16[1024,1152]{1,0:T(8,128)(2,1)} custom-call(s32[32]{0:T(128)} %fusion.12.order_ref, bf16[4,736,128]{2,1,0:T(8,128)(2,1)} %bitcast.133, bf16[4,736,128]{2,1,0:T(8,128)(2,1)} %bitcast.145, bf16[4,736,128]{2,1,0:T(8,128)(2,1)} %bitcast.141, bf16[4,736,128]{2,1,0:T(8,128)(2,1)} %bitcast.147, bf16[4,736,128]{2,1,0:T(8,128)(2,1)} %bitcast.139, ...), custom_call_target="tpu_custom_call" | custom-call | tf_op jit(solution)/shard_map/spread_out/pallas_call | solution.py:89
  101.7 3.4 collective-permute-done.17
  107.2 3.5 collective-permute-start.22
  110.8 3.9 collective-permute-start.19
  114.7 4.3 collective-permute-done.23
  120.2 5.3 %collective-permute-done.24 = bf16[256,512]{1,0:T(8,128)(2,1)S(1)} collective-permute-done((bf16[256,512]{1,0:T(8,128)(2,1)S(1)}, bf16[256,512]{1,0:T(8,128)(2,1)S(1)}, u32[]{:S(2)}, u32[]{:S(2)}) %collective-permute-start.24) | collective-permute-done | bytes 262176 | tf_op jit(solution)/shard_map/kv_gather_vx1/ppermute | solution.py:797
  126.9 10.2 %attend.1 = (bf16[256,1024]{1,0:T(8,128)(2,1)}, f32[8,256]{1,0:T(8,128)}, f32[256,1152]{1,0:T(8,128)}, f32[256,1152]{1,0:T(8,128)}, bf16[256,1152]{1,0:T(8,128)(2,1)}) custom-call(s32[2,8]{1,0:T(2,128)} %pad_add_fusion.info_ref, bf16[256,1024]{1,0:T(8,128)(2,1)} %get-tuple-element.202.q_ref, bf16[8,256,512]{2,1,0:T(8,128)(2,1)} %copy-done.6, ...), custom_call_target="tpu_custom_call" | custom-call | flops 17179869184 | tf_op jit(solution)/shard_map/attend/pallas_call | solution.py:297
  139.3 5.7 %collective-permute-start.34 = (bf16[112,3456]{1,0:T(8,128)(2,1)S(1)}, bf16[112,3456]{1,0:T(8,128)(2,1)S(1)}, u32[]{:S(2)}, u32[]{:S(2)}) collective-permute-start(bf16[112,3456]{1,0:T(8,128)(2,1)S(1)} %collective-permute-done.19.refs_11_.refs_13_), channel_id=1, source_target_pairs={{2,0},{4,2},{6,4},{0,6},{3,1},{5,3},{7,5},{1,7},{10,8},{12,10},{14... | collective-permute-start | bytes 2322440 | tf_op jit(solution)/shard_map/unit_gather_z1/ppermute | solution.py:797
  144.9 5.8 %collective-permute-done.28.refs_12_.refs_14_ = bf16[112,3456]{1,0:T(8,128)(2,1)S(1)} collective-permute-done((bf16[112,3456]{1,0:T(8,128)(2,1)S(1)}, bf16[112,3456]{1,0:T(8,128)(2,1)S(1)}, u32[]{:S(2)}, u32[]{:S(2)}) %collective-permute-start.28) | collective-permute-done | bytes 774176 | tf_op jit(solution)/shard_map/unit_gather_z1/ppermute | solution.py:797
  152.6 13.0 %collective-permute-done.34.refs_13_.refs_15_ = bf16[112,3456]{1,0:T(8,128)(2,1)S(1)} collective-permute-done((bf16[112,3456]{1,0:T(8,128)(2,1)S(1)}, bf16[112,3456]{1,0:T(8,128)(2,1)S(1)}, u32[]{:S(2)}, u32[]{:S(2)}) %collective-permute-start.34) | collective-permute-done | bytes 774176 | tf_op jit(solution)/shard_map/unit_gather_z1/ppermute | solution.py:797
  169.9 24.7 %ffn_forward.1 = (bf16[2048,896]{1,0:T(8,128)(2,1)}, bf16[2048,896]{1,0:T(8,128)(2,1)}, bf16[2048,896]{1,0:T(8,128)(2,1)}, bf16[256,1152]{1,0:T(8,128)(2,1)}, bf...) custom-call(bf16[256,1152]{1,0:T(8,128)(2,1)} %get-tuple-element.221, ...), custom_call_target="tpu_custom_call" | custom-call | flops 12683575296 | tf_op jit(solution)/shard_map/ffn_forward/pallas_call | solution.py:540
  199.9 7.4 %collective-permute-done.42 = bf16[128,1152]{1,0:T(8,128)(2,1)S(1)} collective-permute-done((bf16[128,1152]{1,0:T(8,128)(2,1)S(1)}, bf16[128,1152]{1,0:T(8,128)(2,1)S(1)}, u32[]{:S(2)}, u32[]{:S(2)}) %collective-permute-start.42) | collective-permute-done | bytes 294944 | tf_op jit(solution)/shard_map/ffn_out_sum_x-1/ppermute | solution.py:797
  210.5 11.6 %collective-permute-done.43.refs_2_ = bf16[256,1152]{1,0:T(8,128)(2,1)S(1)} collective-permute-done((bf16[256,1152]{1,0:T(8,128)(2,1)S(1)}, bf16[256,1152]{1,0:T(8,128)(2,1)S(1)}, u32[]{:S(2)}, u32[]{:S(2)}) %collective-permute-start.43) | collective-permute-done | bytes 589856 | tf_op jit(solution)/shard_map/ffn_out_sum_y-1/ppermute | solution.py:797
  223.4 3.7 after_ffn.1
  229.1 11.6 %collective-permute-done.47.refs_4_ = bf16[256,1152]{1,0:T(8,128)(2,1)S(1)} collective-permute-done((bf16[256,1152]{1,0:T(8,128)(2,1)}, bf16[256,1152]{1,0:T(8,128)(2,1)S(1)}, u32[]{:S(2)}, u32[]{:S(2)}) %collective-permute-start.47) | collective-permute-done | bytes 589856 | tf_op jit(solution)/shard_map/d_out_gather_x1/ppermute | solution.py:797
  243.8 3.9 collective-permute-done.49
  252.1 10.5 %unit_grads.3 = (bf16[224,1152]{1,0:T(8,128)(2,1)}, bf16[224,1152]{1,0:T(8,128)(2,1)}, bf16[224,1152]{1,0:T(8,128)(2,1)}, bf16[224,1152]{1,0:T(8,128)(2,1)}) custom-call(bf16[2048,896]{1,0:T(8,128)(2,1)} %get-tuple-element.243.unit_ref, bf16[256,1152]{1,0:T(8,128)(2,1)} %get-tuple-element.245.refs_0_, bf16[256,1152]{1,0:T(8,128)(2,1)} %copy-done.72, ...), custom_call_target="tpu_custom_call" | custom-call | flops 4227858432 | tf_op jit(solution)/shard_map/unit_grads/pallas_call | solution.py:617
  263.5 25.3 %ffn_backward.1 = (bf16[2048,1792]{1,0:T(8,128)(2,1)}, bf16[256,1152]{1,0:T(8,128)(2,1)}, bf16[256,1152]{1,0:T(8,128)(2,1)}, bf16[256,1152]{1,0:T(8,128)(2,1)}, ...) custom-call(bf16[256,1152]{1,0:T(8,128)(2,1)} %get-tuple-element.245, ...), custom_call_target="tpu_custom_call" | custom-call | flops 12683575296 | tf_op jit(solution)/shard_map/ffn_backward/pallas_call | solution.py:540
  296.9 10.5 %unit_grads.4 = (bf16[224,1152]{1,0:T(8,128)(2,1)}, bf16[224,1152]{1,0:T(8,128)(2,1)}, bf16[224,1152]{1,0:T(8,128)(2,1)}, bf16[224,1152]{1,0:T(8,128)(2,1)}) custom-call(bf16[2048,1792]{1,0:T(8,128)(2,1)} %get-tuple-element.271.unit_ref, bf16[256,1152]{1,0:T(8,128)(2,1)} %get-tuple-element.221.refs_0_, bf16[256,1152]{1,0:T(8,128)(2,1)} %copy-done.70, ...), custom_call_target="tpu_custom_call" | custom-call | flops 4227858432 | tf_op jit(solution)/shard_map/unit_grads/pallas_call | solution.py:617
  307.4 3.1 collective-permute-start.57
  312.1 10.6 %unit_grads.5 = (bf16[224,1152]{1,0:T(8,128)(2,1)}, bf16[224,1152]{1,0:T(8,128)(2,1)}, bf16[224,1152]{1,0:T(8,128)(2,1)}, bf16[224,1152]{1,0:T(8,128)(2,1)}) custom-call(bf16[2048,1792]{1,0:T(8,128)(2,1)} %get-tuple-element.271.unit_ref, bf16[256,1152]{1,0:T(8,128)(2,1)} %get-tuple-element.221.refs_0_, bf16[256,1152]{1,0:T(8,128)(2,1)} %copy-done.70, ...), custom_call_target="tpu_custom_call" | custom-call | flops 4227858432 | tf_op jit(solution)/shard_map/unit_grads/pallas_call | solution.py:617
  326.2 13.8 %attend_back.1 = (f32[256,1024]{1,0:T(8,128)}, bf16[8,256,512]{2,1,0:T(8,128)(2,1)}, bf16[256,1152]{1,0:T(8,128)(2,1)}, f32[256,1152]{1,0:T(8,128)}, f32[1,1152]{1,0:T(1,128)}, /*index=5*/f32[1,1152]{1,0:T(1,128)}) custom-call(s32[2,8]{1,0:T(2,128)} %pad_add_fusion.info_ref, bf16[256,1024]{1,0:T(8,128)(2,1)} %get-tuple-element.202.q_ref, ...), custom_call_target="tpu_custom_call" | custom-call | tf_op jit(solution)/shard_map/attend_back/pallas_call | solution.py:409
  340.0 7.9 %collective-permute-done.64 = bf16[224,1152]{1,0:T(8,128)(2,1)S(1)} collective-permute-done((bf16[224,1152]{1,0:T(8,128)(2,1)S(1)}, bf16[224,1152]{1,0:T(8,128)(2,1)S(1)}, u32[]{:S(2)}, u32[]{:S(2)}) %collective-permute-start.64) | collective-permute-done | bytes 516128 | tf_op jit(solution)/shard_map/down_grad_sum_z-1/ppermute | solution.py:797
  354.9 3.9 collective-permute-done.69
  360.0 4.4 collective-permute-done.66
  365.6 3.6 collective-permute-done.67
  372.3 8.9 %collective-permute-done.71 = bf16[128,512]{1,0:T(8,128)(2,1)S(1)} collective-permute-done((bf16[128,512]{1,0:T(8,128)(2,1)S(1)}, bf16[128,512]{1,0:T(8,128)(2,1)S(1)}, u32[]{:S(2)}, u32[]{:S(2)}) %collective-permute-start.71) | collective-permute-done | bytes 131104 | tf_op jit(solution)/shard_map/kv_sum_z1/ppermute | solution.py:797
  384.4 10.2 %query_side.1 = (f32[23056,128]{1,0:T(8,128)}, f32[256,1152]{1,0:T(8,128)}, f32[1,256]{1,0:T(1,128)}) custom-call(f32[256,1024]{1,0:T(8,128)} %get-tuple-element.299.dq_ref, f32[256,1280]{1,0:T(8,128)} %get-tuple-element.300.raw_ref.refs_3_, f32[256,128]{1,0:T(8,128)} %get-tuple-element.400.refs_9_.cos_ref.refs_4_, ...), custom_call_target="tpu_custom_call" | custom-call | tf_op jit(solution)/shard_map/query_side/pallas_call | solution.py:89
  398.1 12.5 %last_part.1 = (bf16[256,1152]{1,0:T(8,128)(2,1)}, bf16[4,736,128]{2,1,0:T(8,128)(2,1)}, bf16[4,736,128]{2,1,0:T(8,128)(2,1)}, bf16[4,736,128]{2,1,0:T(8,128)(2,...) custom-call(s32[32]{0:T(128)} %fusion.12.order_ref, ...), custom_call_target="tpu_custom_call" | custom-call | tf_op jit(solution)/shard_map/last_part/pallas_call | solution.py:89
  411.9 3.8 collective-permute-done.84
  420.2 5.1 %collective-permute-done.81 = bf16[1472,128]{1,0:T(8,128)(2,1)S(1)} collective-permute-done((bf16[1472,128]{1,0:T(8,128)(2,1)S(1)}, bf16[1472,128]{1,0:T(8,128)(2,1)S(1)}, u32[]{:S(2)}, u32[]{:S(2)}) %collective-permute-start.81) | collective-permute-done | bytes 376864 | tf_op jit(solution)/shard_map/attn_grad_sum_x-1/ppermute | solution.py:797
  430.3 12.5 %collective-permute-done.82 = bf16[2944,128]{1,0:T(8,128)(2,1)S(1)} collective-permute-done((bf16[2944,128]{1,0:T(8,128)(2,1)S(1)}, bf16[2944,128]{1,0:T(8,128)(2,1)S(1)}, u32[]{:S(2)}, u32[]{:S(2)}) %collective-permute-start.82) | collective-permute-done | bytes 753696 | tf_op jit(solution)/shard_map/attn_grad_sum_y-1/ppermute | solution.py:797
  443.2 2.7 collective-permute-start.85
  445.8 3.1 collective-permute-start.87
  451.7 3.7 collective-permute-start.88
  457.6 11.1 %collective-permute-done.90 = bf16[216,864]{1,0:T(8,128)(2,1)S(1)} collective-permute-done((bf16[216,864]{1,0:T(8,128)(2,1)S(1)}, bf16[216,864]{1,0:T(8,128)(2,1)S(1)}, u32[]{:S(2)}, u32[]{:S(2)}) %collective-permute-start.90) | collective-permute-done | bytes 373280 | tf_op jit(solution)/shard_map/grad_exchange_uyc2/ppermute | solution.py:797
  469.0 5.5 %multiply_subtract_fusion = (f32[864,864]{1,0:T(8,128)}, f32[864,864]{1,0:T(8,128)}, f32[864,864]{1,0:T(8,128)}, f32[864,864]{1,0:T(8,128)}) fusion(f32[864,864]{1,0:T(8,128)S(1)} %copy-done, f32[864,864]{1,0:T(8,128)S(1)} %copy-done.2, f32[864,864]{1,0:T(8,128)S(1)} %copy-done.3, bf16[4,216,864]{2,1,0:T(8,128)(2,1)S(1)} %bitcast_dynamic-update-slice_fusion), kind=kLoop, calls=%fused_computation.3 | loop fusion | flops 11197440 | bytes 22394880 | tf_op jit(solution)/shard_map/sub | solution.py:65
  (434 shorter events, 116.3 us)
Async XLA Ops:
  11.5 19.1 %collective-permute-start.5 = (bf16[216,864]{1,0:T(8,128)(2,1)}, bf16[216,864]{1,0:T(8,128)(2,1)S(1)}, u32[]{:S(2)}, u32[]{:S(2)}) collective-permute-start(bf16[216,864]{1,0:T(8,128)(2,1)} %get-tuple-element.380), channel_id=1, source_target_pairs={{16,0},{24,8},{0,16},{8,24},{17,1},{25,9},{1,17},{9,25},{18,2},{26... | collective-permute-start | bytes 1119752 | tf_op jit(solution)/shard_map/unit_exchange_uyc2/ppermute | solution.py:797
  12.4 18.3 %collective-permute-start.6 = (bf16[216,864]{1,0:T(8,128)(2,1)S(1)}, bf16[216,864]{1,0:T(8,128)(2,1)S(1)}, u32[]{:S(2)}, u32[]{:S(2)}) collective-permute-start(bf16[216,864]{1,0:T(8,128)(2,1)S(1)} %get-tuple-element.379), channel_id=1, source_target_pairs={{24,0},{0,8},{8,16},{16,24},{25,1},{1,9},{9,17},{17,25},{26,2},{2,... | collective-permute-start | bytes 1119752 | tf_op jit(solution)/shard_map/unit_exchange_uyc3/ppermute | solution.py:797
  33.7 17.6 %collective-permute-start.10 = (bf16[2944,128]{1,0:T(8,128)(2,1)S(1)}, bf16[2944,128]{1,0:T(8,128)(2,1)S(1)}, u32[]{:S(2)}, u32[]{:S(2)}) collective-permute-start(bf16[2944,128]{1,0:T(8,128)(2,1)S(1)} %pad_maximum_fusion.1), channel_id=1, source_target_pairs={{1,0},{0,1},{3,2},{2,3},{5,4},{4,5},{7,6},{6,7},{9,8},{8,9},{11,10... | collective-permute-start | bytes 2261000 | tf_op jit(solution)/shard_map/attn_gather_x1/ppermute | solution.py:797
  35.3 17.7 %collective-permute-start.8 = (bf16[2944,128]{1,0:T(8,128)(2,1)S(1)}, bf16[2944,128]{1,0:T(8,128)(2,1)S(1)}, u32[]{:S(2)}, u32[]{:S(2)}) collective-permute-start(bf16[2944,128]{1,0:T(8,128)(2,1)S(1)} %pad_maximum_fusion.1), channel_id=1, source_target_pairs={{16,0},{0,16},{17,1},{1,17},{18,2},{2,18},{19,3},{3,19},{20,4},{4,... | collective-permute-start | bytes 2261000 | tf_op jit(solution)/shard_map/attn_gather_y1/ppermute | solution.py:797
  36.5 35.4 %collective-permute-start.15 = (bf16[224,3456]{1,0:T(8,128)(2,1)}, bf16[224,3456]{1,0:T(8,128)(2,1)}, u32[]{:S(2)}, u32[]{:S(2)}) collective-permute-start(bf16[224,3456]{1,0:T(8,128)(2,1)} %pad.4.refs_8_.refs_10_), channel_id=1, source_target_pairs={{2,0},{4,2},{6,4},{0,6},{3,1},{5,3},{7,5},{1,7},{10,8},{12,10},{14... | collective-permute-start | bytes 4644872 | tf_op jit(solution)/shard_map/unit_gather_z1/ppermute | solution.py:797
  74.5 30.5 %collective-permute-start.18 = (bf16[112,3456]{1,0:T(8,128)(2,1)}, bf16[112,3456]{1,0:T(8,128)(2,1)S(1)}, u32[]{:S(2)}, u32[]{:S(2)}) collective-permute-start(bf16[112,3456]{1,0:T(8,128)(2,1)} %get-tuple-element.373), channel_id=1, source_target_pairs={{2,0},{4,2},{6,4},{0,6},{3,1},{5,3},{7,5},{1,7},{10,8},{12,10},{14... | collective-permute-start | bytes 2322440 | tf_op jit(solution)/shard_map/unit_gather_z1/ppermute | solution.py:797
  90.4 14.7 %collective-permute-start.17 = (bf16[256,512]{1,0:T(8,128)(2,1)}, bf16[256,512]{1,0:T(8,128)(2,1)S(1)}, u32[]{:S(2)}, u32[]{:S(2)}) collective-permute-start(bf16[256,512]{1,0:T(8,128)(2,1)} %get-tuple-element.200), channel_id=1, source_target_pairs={{6,0},{0,2},{2,4},{4,6},{7,1},{1,3},{3,5},{5,7},{14,8},{8,10},{10,... | collective-permute-start | bytes 786440 | tf_op jit(solution)/shard_map/kv_gather_z-1/ppermute | solution.py:797
  105.1 15.0 %collective-permute-start.21 = (bf16[256,512]{1,0:T(8,128)(2,1)S(1)}, bf16[256,512]{1,0:T(8,128)(2,1)S(1)}, u32[]{:S(2)}, u32[]{:S(2)}) collective-permute-start(bf16[256,512]{1,0:T(8,128)(2,1)S(1)} %collective-permute-done.16), channel_id=1, source_target_pairs={{1,0},{0,1},{3,2},{2,3},{5,4},{4,5},{7,6},{6,7},{9,8},{8,9},{11,10... | collective-permute-start | bytes 786440 | tf_op jit(solution)/shard_map/kv_gather_vx1/ppermute | solution.py:797
  105.7 19.9 %collective-permute-start.25 = (bf16[256,512]{1,0:T(8,128)(2,1)S(1)}, bf16[256,512]{1,0:T(8,128)(2,1)S(1)}, u32[]{:S(2)}, u32[]{:S(2)}) collective-permute-start(bf16[256,512]{1,0:T(8,128)(2,1)S(1)} %collective-permute-done.17), channel_id=1, source_target_pairs={{1,0},{0,1},{3,2},{2,3},{5,4},{4,5},{7,6},{6,7},{9,8},{8,9},{11,10... | collective-permute-start | bytes 786440 | tf_op jit(solution)/shard_map/kv_gather_vx1/ppermute | solution.py:797
  110.8 26.3 %collective-permute-start.19 = (bf16[112,3456]{1,0:T(8,128)(2,1)S(1)}, bf16[112,3456]{1,0:T(8,128)(2,1)S(1)}, u32[]{:S(2)}, u32[]{:S(2)}) collective-permute-start(bf16[112,3456]{1,0:T(8,128)(2,1)S(1)} %get-tuple-element.201), channel_id=1, source_target_pairs={{2,0},{4,2},{6,4},{0,6},{3,1},{5,3},{7,5},{1,7},{10,8},{12,10},{14... | collective-permute-start | bytes 2322440 | tf_op jit(solution)/shard_map/unit_gather_z1/ppermute | solution.py:797
  119.7 31.1 %collective-permute-start.28 = (bf16[112,3456]{1,0:T(8,128)(2,1)S(1)}, bf16[112,3456]{1,0:T(8,128)(2,1)S(1)}, u32[]{:S(2)}, u32[]{:S(2)}) collective-permute-start(bf16[112,3456]{1,0:T(8,128)(2,1)S(1)} %collective-permute-done.18.refs_10_.refs_12_), channel_id=1, source_target_pairs={{2,0},{4,2},{6,4},{0,6},{3,1},{5,3},{7,5},{1,7},{10,8},{12,10},{14... | collective-permute-start | bytes 2322440 | tf_op jit(solution)/shard_map/unit_gather_z1/ppermute | solution.py:797
  137.2 13.6 %collective-permute-start.26 = (bf16[256,1152]{1,0:T(8,128)(2,1)}, bf16[256,1152]{1,0:T(8,128)(2,1)S(1)}, u32[]{:S(2)}, u32[]{:S(2)}) collective-permute-start(bf16[256,1152]{1,0:T(8,128)(2,1)} %get-tuple-element.221.refs_0_), channel_id=1, source_target_pairs={{16,0},{0,16},{17,1},{1,17},{18,2},{2,18},{19,3},{3,19},{20,4},{4,... | collective-permute-start | bytes 1769480 | tf_op jit(solution)/shard_map/ffn_in_gather_y1/ppermute | solution.py:797
  139.3 26.4 %collective-permute-start.34 = (bf16[112,3456]{1,0:T(8,128)(2,1)S(1)}, bf16[112,3456]{1,0:T(8,128)(2,1)S(1)}, u32[]{:S(2)}, u32[]{:S(2)}) collective-permute-start(bf16[112,3456]{1,0:T(8,128)(2,1)S(1)} %collective-permute-done.19.refs_11_.refs_13_), channel_id=1, source_target_pairs={{2,0},{4,2},{6,4},{0,6},{3,1},{5,3},{7,5},{1,7},{10,8},{12,10},{14... | collective-permute-start | bytes 2322440 | tf_op jit(solution)/shard_map/unit_gather_z1/ppermute | solution.py:797
  150.8 14.9 %collective-permute-start.32 = (bf16[128,1152]{1,0:T(8,128)(2,1)S(1)}, bf16[128,1152]{1,0:T(8,128)(2,1)S(1)}, u32[]{:S(2)}, u32[]{:S(2)}) collective-permute-start(bf16[128,1152]{1,0:T(8,128)(2,1)S(1)} %slice.233), channel_id=1, source_target_pairs={{16,0},{0,16},{17,1},{1,17},{18,2},{2,18},{19,3},{3,19},{20,4},{4,... | collective-permute-start | bytes 884744 | tf_op jit(solution)/shard_map/ffn_in_gather_y1/ppermute | solution.py:797
  151.5 14.1 %collective-permute-start.33 = (bf16[128,1152]{1,0:T(8,128)(2,1)S(1)}, bf16[128,1152]{1,0:T(8,128)(2,1)S(1)}, u32[]{:S(2)}, u32[]{:S(2)}) collective-permute-start(bf16[128,1152]{1,0:T(8,128)(2,1)S(1)} %slice.234), channel_id=1, source_target_pairs={{1,0},{0,1},{3,2},{2,3},{5,4},{4,5},{7,6},{6,7},{9,8},{8,9},{11,10... | collective-permute-start | bytes 884744 | tf_op jit(solution)/shard_map/ffn_in_gather_x1/ppermute | solution.py:797
  152.1 15.8 %collective-permute-start.30 = (bf16[256,1152]{1,0:T(8,128)(2,1)S(1)}, bf16[256,1152]{1,0:T(8,128)(2,1)S(1)}, u32[]{:S(2)}, u32[]{:S(2)}) collective-permute-start(bf16[256,1152]{1,0:T(8,128)(2,1)S(1)} %collective-permute-done.26.refs_2_), channel_id=1, source_target_pairs={{8,0},{0,8},{9,1},{1,9},{10,2},{2,10},{11,3},{3,11},{12,4},{4,12},... | collective-permute-start | bytes 1769480 | tf_op jit(solution)/shard_map/ffn_in_gather_c1/ppermute | solution.py:797
  152.1 15.8 %collective-permute-start.31 = (bf16[256,1152]{1,0:T(8,128)(2,1)S(1)}, bf16[256,1152]{1,0:T(8,128)(2,1)S(1)}, u32[]{:S(2)}, u32[]{:S(2)}) collective-permute-start(bf16[256,1152]{1,0:T(8,128)(2,1)S(1)} %collective-permute-done.27.refs_4_), channel_id=1, source_target_pairs={{8,0},{0,8},{9,1},{1,9},{10,2},{2,10},{11,3},{3,11},{12,4},{4,12},... | collective-permute-start | bytes 1769480 | tf_op jit(solution)/shard_map/ffn_in_gather_c1/ppermute | solution.py:797
  195.3 14.2 %collective-permute-start.36 = (bf16[256,1152]{1,0:T(8,128)(2,1)}, bf16[256,1152]{1,0:T(8,128)(2,1)S(1)}, u32[]{:S(2)}, u32[]{:S(2)}) collective-permute-start(bf16[256,1152]{1,0:T(8,128)(2,1)} %get-tuple-element.230), channel_id=1, source_target_pairs={{8,0},{0,8},{9,1},{1,9},{10,2},{2,10},{11,3},{3,11},{12,4},{4,12},... | collective-permute-start | bytes 1769480 | tf_op jit(solution)/shard_map/ffn_out_sum_c1/ppermute | solution.py:797
  207.5 14.6 %collective-permute-start.43 = (bf16[256,1152]{1,0:T(8,128)(2,1)S(1)}, bf16[256,1152]{1,0:T(8,128)(2,1)S(1)}, u32[]{:S(2)}, u32[]{:S(2)}) collective-permute-start(bf16[256,1152]{1,0:T(8,128)(2,1)S(1)} %pad_maximum_fusion.5), channel_id=1, source_target_pairs={{16,0},{0,16},{17,1},{1,17},{18,2},{2,18},{19,3},{3,19},{20,4},{4,... | collective-permute-start | bytes 1769480 | tf_op jit(solution)/shard_map/ffn_out_sum_y-1/ppermute | solution.py:797
  208.3 14.3 %collective-permute-start.40 = (bf16[256,1152]{1,0:T(8,128)(2,1)S(1)}, bf16[256,1152]{1,0:T(8,128)(2,1)S(1)}, u32[]{:S(2)}, u32[]{:S(2)}) collective-permute-start(bf16[256,1152]{1,0:T(8,128)(2,1)S(1)} %pad_maximum_fusion.4), channel_id=1, source_target_pairs={{1,0},{0,1},{3,2},{2,3},{5,4},{4,5},{7,6},{6,7},{9,8},{8,9},{11,10... | collective-permute-start | bytes 1769480 | tf_op jit(solution)/shard_map/ffn_out_sum_x-1/ppermute | solution.py:797
  227.1 13.6 %collective-permute-start.47 = (bf16[256,1152]{1,0:T(8,128)(2,1)}, bf16[256,1152]{1,0:T(8,128)(2,1)S(1)}, u32[]{:S(2)}, u32[]{:S(2)}) collective-permute-start(bf16[256,1152]{1,0:T(8,128)(2,1)} %get-tuple-element.245.refs_0_), channel_id=1, source_target_pairs={{1,0},{0,1},{3,2},{2,3},{5,4},{4,5},{7,6},{6,7},{9,8},{8,9},{11,10... | collective-permute-start | bytes 1769480 | tf_op jit(solution)/shard_map/d_out_gather_x1/ppermute | solution.py:797
  228.2 14.1 %collective-permute-start.45 = (bf16[256,1152]{1,0:T(8,128)(2,1)}, bf16[256,1152]{1,0:T(8,128)(2,1)S(1)}, u32[]{:S(2)}, u32[]{:S(2)}) collective-permute-start(bf16[256,1152]{1,0:T(8,128)(2,1)} %get-tuple-element.245.refs_0_), channel_id=1, source_target_pairs={{16,0},{0,16},{17,1},{1,17},{18,2},{2,18},{19,3},{3,19},{20,4},{4,... | collective-permute-start | bytes 1769480 | tf_op jit(solution)/shard_map/d_out_gather_y1/ppermute | solution.py:797
  262.6 26.9 %collective-permute-start.55 = (bf16[224,1152]{1,0:T(8,128)(2,1)}, bf16[224,1152]{1,0:T(8,128)(2,1)S(1)}, u32[]{:S(2)}, u32[]{:S(2)}) collective-permute-start(bf16[224,1152]{1,0:T(8,128)(2,1)} %get-tuple-element.255), channel_id=1, source_target_pairs={{6,0},{0,2},{2,4},{4,6},{7,1},{1,3},{3,5},{5,7},{14,8},{8,10},{10,... | collective-permute-start | bytes 1548296 | tf_op jit(solution)/shard_map/down_grad_sum_z-1/ppermute | solution.py:797
  290.0 20.8 %collective-permute-start.58 = (bf16[224,1152]{1,0:T(8,128)(2,1)S(1)}, bf16[224,1152]{1,0:T(8,128)(2,1)S(1)}, u32[]{:S(2)}, u32[]{:S(2)}) collective-permute-start(bf16[224,1152]{1,0:T(8,128)(2,1)S(1)} %add_convert_fusion.16), channel_id=1, source_target_pairs={{6,0},{0,2},{2,4},{4,6},{7,1},{1,3},{3,5},{5,7},{14,8},{8,10},{10,... | collective-permute-start | bytes 1548296 | tf_op jit(solution)/shard_map/down_grad_sum_z-1/ppermute | solution.py:797
  294.1 16.5 %collective-permute-start.60 = (bf16[128,1152]{1,0:T(8,128)(2,1)S(1)}, bf16[128,1152]{1,0:T(8,128)(2,1)S(1)}, u32[]{:S(2)}, u32[]{:S(2)}) collective-permute-start(bf16[128,1152]{1,0:T(8,128)(2,1)S(1)} %get-tuple-element.391), channel_id=1, source_target_pairs={{1,0},{0,1},{3,2},{2,3},{5,4},{4,5},{7,6},{6,7},{9,8},{8,9},{11,10... | collective-permute-start | bytes 884744 | tf_op jit(solution)/shard_map/d_in_sum_x-1/ppermute | solution.py:797
  295.1 15.5 %collective-permute-start.59 = (bf16[128,1152]{1,0:T(8,128)(2,1)S(1)}, bf16[128,1152]{1,0:T(8,128)(2,1)S(1)}, u32[]{:S(2)}, u32[]{:S(2)}) collective-permute-start(bf16[128,1152]{1,0:T(8,128)(2,1)S(1)} %get-tuple-element.392), channel_id=1, source_target_pairs={{16,0},{0,16},{17,1},{1,17},{18,2},{2,18},{19,3},{3,19},{20,4},{4,... | collective-permute-start | bytes 884744 | tf_op jit(solution)/shard_map/d_in_sum_y-1/ppermute | solution.py:797
  307.4 17.8 %collective-permute-start.57 = (bf16[224,1152]{1,0:T(8,128)(2,1)}, bf16[224,1152]{1,0:T(8,128)(2,1)S(1)}, u32[]{:S(2)}, u32[]{:S(2)}) collective-permute-start(bf16[224,1152]{1,0:T(8,128)(2,1)} %get-tuple-element.260), channel_id=1, source_target_pairs={{6,0},{0,2},{2,4},{4,6},{7,1},{1,3},{3,5},{5,7},{14,8},{8,10},{10,... | collective-permute-start | bytes 1548296 | tf_op jit(solution)/shard_map/gate_grad_sum_z-1/ppermute | solution.py:797
  310.9 14.3 %collective-permute-start.61 = (bf16[256,1152]{1,0:T(8,128)(2,1)S(1)}, bf16[256,1152]{1,0:T(8,128)(2,1)S(1)}, u32[]{:S(2)}, u32[]{:S(2)}) collective-permute-start(bf16[256,1152]{1,0:T(8,128)(2,1)S(1)} %pad_maximum_fusion.6), channel_id=1, source_target_pairs={{1,0},{0,1},{3,2},{2,3},{5,4},{4,5},{7,6},{6,7},{9,8},{8,9},{11,10... | collective-permute-start | bytes 1769480 | tf_op jit(solution)/shard_map/d_in_sum_x-1/ppermute | solution.py:797
  310.9 14.3 %collective-permute-start.62 = (bf16[256,1152]{1,0:T(8,128)(2,1)S(1)}, bf16[256,1152]{1,0:T(8,128)(2,1)S(1)}, u32[]{:S(2)}, u32[]{:S(2)}) collective-permute-start(bf16[256,1152]{1,0:T(8,128)(2,1)S(1)} %pad_maximum_fusion.7), channel_id=1, source_target_pairs={{16,0},{0,16},{17,1},{1,17},{18,2},{2,18},{19,3},{3,19},{20,4},{4,... | collective-permute-start | bytes 1769480 | tf_op jit(solution)/shard_map/d_in_sum_y-1/ppermute | solution.py:797
  322.6 17.3 %collective-permute-start.65 = (bf16[224,1152]{1,0:T(8,128)(2,1)}, bf16[224,1152]{1,0:T(8,128)(2,1)S(1)}, u32[]{:S(2)}, u32[]{:S(2)}) collective-permute-start(bf16[224,1152]{1,0:T(8,128)(2,1)} %get-tuple-element.285), channel_id=1, source_target_pairs={{6,0},{0,2},{2,4},{4,6},{7,1},{1,3},{3,5},{5,7},{14,8},{8,10},{10,... | collective-permute-start | bytes 1548296 | tf_op jit(solution)/shard_map/up_grad_sum_z-1/ppermute | solution.py:797
  324.4 23.4 %collective-permute-start.64 = (bf16[224,1152]{1,0:T(8,128)(2,1)S(1)}, bf16[224,1152]{1,0:T(8,128)(2,1)S(1)}, u32[]{:S(2)}, u32[]{:S(2)}) collective-permute-start(bf16[224,1152]{1,0:T(8,128)(2,1)S(1)} %add_convert_fusion.14), channel_id=1, source_target_pairs={{6,0},{0,2},{2,4},{4,6},{7,1},{1,3},{3,5},{5,7},{14,8},{8,10},{10,... | collective-permute-start | bytes 1548296 | tf_op jit(solution)/shard_map/down_grad_sum_z-1/ppermute | solution.py:797
  350.7 13.6 %collective-permute-start.66 = (bf16[256,512]{1,0:T(8,128)(2,1)S(1)}, bf16[256,512]{1,0:T(8,128)(2,1)S(1)}, u32[]{:S(2)}, u32[]{:S(2)}) collective-permute-start(bf16[256,512]{1,0:T(8,128)(2,1)S(1)} %get-tuple-element.367), channel_id=1, source_target_pairs={{1,0},{0,1},{3,2},{2,3},{5,4},{4,5},{7,6},{6,7},{9,8},{8,9},{11,10... | collective-permute-start | bytes 786440 | tf_op jit(solution)/shard_map/kv_sum_vx-1/ppermute | solution.py:797
  351.5 17.7 %collective-permute-start.67 = (bf16[256,512]{1,0:T(8,128)(2,1)S(1)}, bf16[256,512]{1,0:T(8,128)(2,1)S(1)}, u32[]{:S(2)}, u32[]{:S(2)}) collective-permute-start(bf16[256,512]{1,0:T(8,128)(2,1)S(1)} %get-tuple-element.365), channel_id=1, source_target_pairs={{1,0},{0,1},{3,2},{2,3},{5,4},{4,5},{7,6},{6,7},{9,8},{8,9},{11,10... | collective-permute-start | bytes 786440 | tf_op jit(solution)/shard_map/kv_sum_vx-1/ppermute | solution.py:797
  352.8 19.3 %collective-permute-start.68 = (bf16[256,512]{1,0:T(8,128)(2,1)S(1)}, bf16[256,512]{1,0:T(8,128)(2,1)S(1)}, u32[]{:S(2)}, u32[]{:S(2)}) collective-permute-start(bf16[256,512]{1,0:T(8,128)(2,1)S(1)} %get-tuple-element.363), channel_id=1, source_target_pairs={{1,0},{0,1},{3,2},{2,3},{5,4},{4,5},{7,6},{6,7},{9,8},{8,9},{11,10... | collective-permute-start | bytes 786440 | tf_op jit(solution)/shard_map/kv_sum_vx-1/ppermute | solution.py:797
  353.7 27.5 %collective-permute-start.63 = (bf16[224,1152]{1,0:T(8,128)(2,1)S(1)}, bf16[224,1152]{1,0:T(8,128)(2,1)S(1)}, u32[]{:S(2)}, u32[]{:S(2)}) collective-permute-start(bf16[224,1152]{1,0:T(8,128)(2,1)S(1)} %add_convert_fusion.15), channel_id=1, source_target_pairs={{6,0},{0,2},{2,4},{4,6},{7,1},{1,3},{3,5},{5,7},{14,8},{8,10},{10,... | collective-permute-start | bytes 1548296 | tf_op jit(solution)/shard_map/gate_grad_sum_z-1/ppermute | solution.py:797
  364.3 16.9 %collective-permute-start.71 = (bf16[128,512]{1,0:T(8,128)(2,1)S(1)}, bf16[128,512]{1,0:T(8,128)(2,1)S(1)}, u32[]{:S(2)}, u32[]{:S(2)}) collective-permute-start(bf16[128,512]{1,0:T(8,128)(2,1)S(1)} %get-tuple-element.397), channel_id=1, source_target_pairs={{2,0},{4,2},{6,4},{0,6},{3,1},{5,3},{7,5},{1,7},{10,8},{12,10},{14... | collective-permute-start | bytes 393224 | tf_op jit(solution)/shard_map/kv_sum_z1/ppermute | solution.py:797
  369.2 26.2 %collective-permute-start.72 = (bf16[224,1152]{1,0:T(8,128)(2,1)S(1)}, bf16[224,1152]{1,0:T(8,128)(2,1)S(1)}, u32[]{:S(2)}, u32[]{:S(2)}) collective-permute-start(bf16[224,1152]{1,0:T(8,128)(2,1)S(1)} %add_convert_fusion.13), channel_id=1, source_target_pairs={{6,0},{0,2},{2,4},{4,6},{7,1},{1,3},{3,5},{5,7},{14,8},{8,10},{10,... | collective-permute-start | bytes 1548296 | tf_op jit(solution)/shard_map/up_grad_sum_z-1/ppermute | solution.py:797
  381.4 14.0 %collective-permute-start.74 = (bf16[256,512]{1,0:T(8,128)(2,1)S(1)}, bf16[256,512]{1,0:T(8,128)(2,1)S(1)}, u32[]{:S(2)}, u32[]{:S(2)}) collective-permute-start(bf16[256,512]{1,0:T(8,128)(2,1)S(1)} %pad_maximum_fusion.11), channel_id=1, source_target_pairs={{2,0},{4,2},{6,4},{0,6},{3,1},{5,3},{7,5},{1,7},{10,8},{12,10},{14... | collective-permute-start | bytes 786440 | tf_op jit(solution)/shard_map/kv_sum_z1/ppermute | solution.py:797
  381.6 15.7 %collective-permute-start.73 = (bf16[256,512]{1,0:T(8,128)(2,1)S(1)}, bf16[256,512]{1,0:T(8,128)(2,1)S(1)}, u32[]{:S(2)}, u32[]{:S(2)}) collective-permute-start(bf16[256,512]{1,0:T(8,128)(2,1)S(1)} %pad_maximum_fusion.10), channel_id=1, source_target_pairs={{6,0},{0,2},{2,4},{4,6},{7,1},{1,3},{3,5},{5,7},{14,8},{8,10},{10,... | collective-permute-start | bytes 786440 | tf_op jit(solution)/shard_map/kv_sum_z-1/ppermute | solution.py:797
  383.8 27.4 %collective-permute-start.83 = (bf16[224,1152]{1,0:T(8,128)(2,1)S(1)}, bf16[224,1152]{1,0:T(8,128)(2,1)S(1)}, u32[]{:S(2)}, u32[]{:S(2)}) collective-permute-start(bf16[224,1152]{1,0:T(8,128)(2,1)S(1)} %add_convert_fusion.12), channel_id=1, source_target_pairs={{6,0},{0,2},{2,4},{4,6},{7,1},{1,3},{3,5},{5,7},{14,8},{8,10},{10,... | collective-permute-start | bytes 1548296 | tf_op jit(solution)/shard_map/gate_grad_sum_z-1/ppermute | solution.py:797
  397.5 18.2 %collective-permute-start.84 = (bf16[224,1152]{1,0:T(8,128)(2,1)S(1)}, bf16[224,1152]{1,0:T(8,128)(2,1)S(1)}, u32[]{:S(2)}, u32[]{:S(2)}) collective-permute-start(bf16[224,1152]{1,0:T(8,128)(2,1)S(1)} %add_convert_fusion.10), channel_id=1, source_target_pairs={{6,0},{0,2},{2,4},{4,6},{7,1},{1,3},{3,5},{5,7},{14,8},{8,10},{10,... | collective-permute-start | bytes 1548296 | tf_op jit(solution)/shard_map/up_grad_sum_z-1/ppermute | solution.py:797
  411.2 18.0 %collective-permute-start.75 = (bf16[2944,128]{1,0:T(8,128)(2,1)}, bf16[2944,128]{1,0:T(8,128)(2,1)S(1)}, u32[]{:S(2)}, u32[]{:S(2)}) collective-permute-start(bf16[2944,128]{1,0:T(8,128)(2,1)} %bitcast.163), channel_id=1, source_target_pairs={{8,0},{0,8},{9,1},{1,9},{10,2},{2,10},{11,3},{3,11},{12,4},{4,12},... | collective-permute-start | bytes 2261000 | tf_op jit(solution)/shard_map/attn_grad_sum_c1/ppermute | solution.py:797
  425.5 17.3 %collective-permute-start.82 = (bf16[2944,128]{1,0:T(8,128)(2,1)S(1)}, bf16[2944,128]{1,0:T(8,128)(2,1)S(1)}, u32[]{:S(2)}, u32[]{:S(2)}) collective-permute-start(bf16[2944,128]{1,0:T(8,128)(2,1)S(1)} %pad_maximum_fusion.3), channel_id=1, source_target_pairs={{16,0},{0,16},{17,1},{1,17},{18,2},{2,18},{19,3},{3,19},{20,4},{4,... | collective-permute-start | bytes 2261000 | tf_op jit(solution)/shard_map/attn_grad_sum_y-1/ppermute | solution.py:797
  428.1 14.7 %collective-permute-start.79 = (bf16[2944,128]{1,0:T(8,128)(2,1)S(1)}, bf16[2944,128]{1,0:T(8,128)(2,1)S(1)}, u32[]{:S(2)}, u32[]{:S(2)}) collective-permute-start(bf16[2944,128]{1,0:T(8,128)(2,1)S(1)} %pad_maximum_fusion.2), channel_id=1, source_target_pairs={{1,0},{0,1},{3,2},{2,3},{5,4},{4,5},{7,6},{6,7},{9,8},{8,9},{11,10... | collective-permute-start | bytes 2261000 | tf_op jit(solution)/shard_map/attn_grad_sum_x-1/ppermute | solution.py:797
  449.3 19.5 %collective-permute-start.90 = (bf16[216,864]{1,0:T(8,128)(2,1)S(1)}, bf16[216,864]{1,0:T(8,128)(2,1)S(1)}, u32[]{:S(2)}, u32[]{:S(2)}) collective-permute-start(bf16[216,864]{1,0:T(8,128)(2,1)S(1)} %get-tuple-element.370), channel_id=1, source_target_pairs={{16,0},{24,8},{0,16},{8,24},{17,1},{25,9},{1,17},{9,25},{18,2},{26... | collective-permute-start | bytes 1119752 | tf_op jit(solution)/shard_map/grad_exchange_uyc2/ppermute | solution.py:797
  450.8 18.1 %collective-permute-start.91 = (bf16[216,864]{1,0:T(8,128)(2,1)S(1)}, bf16[216,864]{1,0:T(8,128)(2,1)S(1)}, u32[]{:S(2)}, u32[]{:S(2)}) collective-permute-start(bf16[216,864]{1,0:T(8,128)(2,1)S(1)} %get-tuple-element.369), channel_id=1, source_target_pairs={{24,0},{0,8},{8,16},{16,24},{25,1},{1,9},{9,17},{17,25},{26,2},{2,... | collective-permute-start | bytes 1119752 | tf_op jit(solution)/shard_map/grad_exchange_uyc3/ppermute | solution.py:797
  451.7 22.8 %collective-permute-start.88 = (bf16[736,128]{1,0:T(8,128)(2,1)S(1)}, bf16[736,128]{1,0:T(8,128)(2,1)S(1)}, u32[]{:S(2)}, u32[]{:S(2)}) collective-permute-start(bf16[736,128]{1,0:T(8,128)(2,1)S(1)} %pad_maximum_fusion.15), channel_id=1, source_target_pairs={{2,0},{4,2},{6,4},{0,6},{3,1},{5,3},{7,5},{1,7},{10,8},{12,10},{14... | collective-permute-start | bytes 565256 | tf_op jit(solution)/shard_map/attn_grad_sum_z1/ppermute | solution.py:797
  455.4 19.1 %collective-permute-start.86 = (bf16[736,128]{1,0:T(8,128)(2,1)S(1)}, bf16[736,128]{1,0:T(8,128)(2,1)S(1)}, u32[]{:S(2)}, u32[]{:S(2)}) collective-permute-start(bf16[736,128]{1,0:T(8,128)(2,1)S(1)} %pad_maximum_fusion.14), channel_id=1, source_target_pairs={{6,0},{0,2},{2,4},{4,6},{7,1},{1,3},{3,5},{5,7},{14,8},{8,10},{10,... | collective-permute-start | bytes 565256 | tf_op jit(solution)/shard_map/attn_grad_sum_z-1/ppermute | solution.py:797
  (122 other events, 1040.9 us)

commit v5 on v4

--- a/solution.py
+++ b/solution.py
@@ -81,6 +81,7 @@
 
 
 VMEM_LIMIT = 56 * 1024 * 1024
+VMEM_LIMITS = {"after_ffn": 40 * 1024 * 1024}
 SCORE_SCALE = HD ** (-0.5)
 SPACES = {"v": pltpu.VMEM, "h": pl.ANY, "s": pltpu.SMEM}
 
@@ -94,7 +95,7 @@
             pl.BlockSpec(memory_space=SPACES[s]) for s in out_spaces or "v" * len(out_shape)
         ),
         scratch_shapes=list(scratch),
-        compiler_params=pltpu.CompilerParams(vmem_limit_bytes=VMEM_LIMIT),
+        compiler_params=pltpu.CompilerParams(vmem_limit_bytes=VMEM_LIMITS.get(name, VMEM_LIMIT)),
         cost_estimate=pl.CostEstimate(flops=flops, bytes_accessed=0, transcendentals=0),
         name=name,
     )(*operands)
@@ -329,7 +330,7 @@
             jax.ShapeDtypeStruct((rows, D), f32),
             jax.ShapeDtypeStruct((rows, D), bf16),
         ),
-        compiler_params=pltpu.CompilerParams(vmem_limit_bytes=VMEM_LIMIT),
+        compiler_params=pltpu.CompilerParams(vmem_limit_bytes=44 * 1024 * 1024),
         cost_estimate=pl.CostEstimate(
             flops=8 * 4 * blocks * rows * rows * H * HD, bytes_accessed=0, transcendentals=0
         ),
@@ -348,9 +349,17 @@
         terms_ref = refs[:terms]
         (
             mid_ref, out_ref, cot_ref, w_ref, g_post_ref, g_fpre_ref,
-            dq_ref, dkv_ref, dout_ref, dmid_ref, dg_fpre_ref, dg_post_ref, do_ref, delta_ref,
+            dq_ref, dout_ref, dmid_ref, dg_fpre_ref, dg_post_ref, *dkv_refs, do_ref, delta_ref,
         ) = refs[terms:]
         step = pl.program_id(0)
+
+        def give(d_key, d_value):
+            for k, ref in enumerate(dkv_refs):
+
+                @pl.when(step == k)
+                def _(ref=ref):
+                    ref[:, :HD] = d_key.astype(bf16)
+                    ref[:, HD:] = d_value.astype(bf16)
 
         @pl.when(step == 0)
         def _():
@@ -391,15 +400,14 @@
                 d_score = (prob * (d_prob - delta_ref[h : h + 1, :])).astype(bf16)
                 d_key = d_key + contract(d_score, q, 1, 0)
                 dq_ref[:, cols] = dq_ref[:, cols] + contract(d_score, key, 0, 0)
-            dkv_ref[0, :, :HD] = d_key.astype(bf16)
-            dkv_ref[0, :, HD:] = d_value.astype(bf16)
+            give(d_key, d_value)
 
         pl.when(info_ref[1, step] == WHOLE)(lambda: visit(False))
         pl.when(info_ref[1, step] == MASKED)(lambda: visit(True))
 
         @pl.when(info_ref[1, step] == DEAD)
         def _():
-            dkv_ref[...] = jnp.zeros_like(dkv_ref)
+            give(jnp.zeros((rows, HD), f32), jnp.zeros((rows, HD), f32))
 
         @pl.when(step == blocks - 1)
         def _():
@@ -425,21 +433,21 @@
             ],
             out_specs=[
                 same((rows, H * HD)),
-                block,
                 same((rows, D)),
                 same((rows, D)),
                 same((1, D)),
                 same((1, D)),
+                *[same((rows, 2 * HD))] * blocks,
             ],
             scratch_shapes=[pltpu.VMEM((rows, H * HD), bf16), pltpu.VMEM((8, rows), f32)],
         ),
         out_shape=(
             jax.ShapeDtypeStruct((rows, H * HD), f32),
-            jax.ShapeDtypeStruct(kv.shape, bf16),
             jax.ShapeDtypeStruct((rows, D), bf16),
             jax.ShapeDtypeStruct((rows, D), f32),
             jax.ShapeDtypeStruct((1, D), f32),
             jax.ShapeDtypeStruct((1, D), f32),
+            *[jax.ShapeDtypeStruct((rows, 2 * HD), bf16)] * blocks,
         ),
         compiler_params=pltpu.CompilerParams(vmem_limit_bytes=VMEM_LIMIT),
         cost_estimate=pl.CostEstimate(flops=0, bytes_accessed=0, transcendentals=0),
@@ -520,12 +528,23 @@
             bringing = [c for k in order for c in brought[k]]
             for copy in coming[:first] + bringing + coming[first:]:
                 copy.start()
-            for copy in bringing:
-                copy.wait()
 
         by_chunk(step, chunks, coming, lambda copy: copy.wait())
         here = pl.ds(pl.multiple_of(step * both, both), both)
-        given[here, :] = body(held[here, :], stream_refs, units, out_refs)
+
+        def arrived(k):
+            for copy in brought[k]:
+                copy.wait()
+            return units[k]
+
+        @pl.when(step == 0)
+        def _():
+            given[here, :] = body(held[here, :], stream_refs, arrived, out_refs)
+
+        @pl.when(step > 0)
+        def _():
+            given[here, :] = body(held[here, :], stream_refs, lambda k: units[k], out_refs)
+
         by_chunk(step, chunks, going, lambda copy: copy.start())
 
         @pl.when(step == chunks - 1)
@@ -567,14 +586,14 @@
 def ffn_forward(rows, weights):
     def body(x, _, weight, out_refs):
         act_ref, gelu_ref, slope_ref = out_refs
-        gate = contract(x, weight[0], 1, 1)
-        up = contract(x, weight[1], 1, 1)
+        gate = contract(x, weight(0), 1, 1)
+        up = contract(x, weight(1), 1, 1)
         gelu, slope = gelu_parts(gate)
         act = (gelu * up).astype(bf16)
         act_ref[...] = act
         gelu_ref[...] = gelu.astype(bf16)
         slope_ref[...] = (slope * up).astype(bf16)
-        return contract(act, weight[2], 1, 0).astype(bf16)
+        return contract(act, weight(2), 1, 0).astype(bf16)
 
     units = sum(w.shape[0] for w in weights)
     act, gelu, slope, *parts = ffn_call("ffn_forward", body, rows, [], weights, [units] * 3, (0, 1, 2))
@@ -586,12 +605,12 @@
 
     def body(x, stream_refs, weight, out_refs):
         gelu_ref, slope_ref = stream_refs
-        d_act = contract(x, weight[2], 1, 1)
+        d_act = contract(x, weight(2), 1, 1)
         d_gate = (d_act * slope_ref[...].astype(f32)).astype(bf16)
         d_up = (d_act * gelu_ref[...].astype(f32)).astype(bf16)
         out_refs[0][:, :units] = d_gate
         out_refs[0][:, units:] = d_up
-        return (contract(d_gate, weight[0], 1, 0) + contract(d_up, weight[1], 1, 0)).astype(bf16)
+        return (contract(d_gate, weight(0), 1, 0) + contract(d_up, weight(1), 1, 0)).astype(bf16)
 
     d_both, *parts = ffn_call(
         "ffn_backward", body, rows, [gelu, slope], weights, [2 * units], (2, 0, 1)
@@ -622,7 +641,7 @@
         out_specs=[pl.BlockSpec((per, D), lambda i: (0, 0))] * blocks,
         out_shape=[jax.ShapeDtypeStruct((per, D), bf16)] * blocks,
         scratch_shapes=[pltpu.VMEM((tokens, D), bf16), pltpu.SemaphoreType.DMA((count,))],
-        compiler_params=pltpu.CompilerParams(vmem_limit_bytes=VMEM_LIMIT),
+        compiler_params=pltpu.CompilerParams(vmem_limit_bytes=40 * 1024 * 1024),
         cost_estimate=pl.CostEstimate(
             flops=2 * tokens * both * D, bytes_accessed=0, transcendentals=0
         ),
@@ -834,7 +853,8 @@
         }
         what = self.what
         if first is not None:
-            low = first(low)
+            last = max(low)
+            low[last] = first(low[last])
             self.what = what
         half = halfway(low[0, 0].shape[0])
         along_x = {ox: [low[ox, 0][:half]] for ox in range(1, nx)}
@@ -976,20 +996,17 @@
             ],
             axis=0,
         )
-        line_blocks = ways.z_gather(low_piece)
-
         ways.what = "unit_exchange"
         units, width = mlp_w.shape
         share = units // ns
         held = -(-share // 32) * 32
 
         def seq_send(by_place):
+            return [ways.fro(v, SEQ, offset) for offset, v in enumerate(seq_parts(by_place))]
+
+        def seq_parts(by_place):
             return [
-                ways.fro(
-                    lax.dynamic_index_in_dim(by_place, (seq_place - offset) % ns, 0, keepdims=False),
-                    SEQ,
-                    offset,
-                )
+                lax.dynamic_index_in_dim(by_place, (seq_place - offset) % ns, 0, keepdims=False)
                 for offset in range(ns)
             ]
 
@@ -999,7 +1016,11 @@
                 kept = lax.dynamic_update_index_in_dim(kept, value, (seq_place + offset) % ns, 0)
             return kept
 
-        heard = seq_send(mlp_w.astype(bf16).reshape(ns, share, width))
+        sent = seq_parts(mlp_w.astype(bf16).reshape(ns, share, width))
+        sent, low_piece = lax.optimization_barrier((sent, low_piece))
+        heard = [ways.fro(v, SEQ, offset) for offset, v in enumerate(sent)]
+        ways.what = "attn_gather"
+        line_blocks = ways.z_gather(low_piece)
         line_blocks, heard = lax.optimization_barrier((line_blocks, heard))
         by_cols = seq_place_all(heard)
         rows_own = jnp.concatenate([by_cols[i] for i in range(ns)], axis=1)
@@ -1139,17 +1160,16 @@
         d_in_parts = lax.optimization_barrier((d_in_parts, rings["up"].blocks[0]))[0]
         d_in_parts = rings["gate"].step(d_in_parts)
 
-        d_query, d_kv, d_attn_out, d_middle, d_gfpre, d_gpost = attend_back(
+        d_query, d_attn_out, d_middle, d_gfpre, d_gpost, *d_kv = attend_back(
             info, query, kv_all, key_docs, query_docs, heads, log_total, d_in_parts, middle, attn_out,
             cotangent[0], w_out, g_post, g_fpre,
         )
         d_kv = rings["up"].step(d_kv)
         d_kv = down.step(d_kv)
         ways.what = "kv_sum"
-        d_kv = d_kv.reshape(nz, nx, tok_rows, 2 * HD)
 
         def across(oz):
-            return [ways.fro(d_kv[oz, oa], ACROSS, -oa) for oa in range(nx)]
+            return [ways.fro(d_kv[oz * nx + oa], ACROSS, -oa) for oa in range(nx)]
 
         far = nz // 2
         kv_parts = {far: add_low(*across(far))}

time: 484 us -> 466 us (0.963)
  Pallas kernels: 147 us -> 124 us
  waiting for transfers between devices: 184 us -> 196 us
    pallas_call x3, Pallas kernels: 31.6 us -> 18.9 us  [unit_grads(): pl.pallas_call(body, grid=(1,), in_specs=[pl.BlockSpec((tokens, both), la...]
    ppermute x92, waiting for transfers between devices: 184 us -> 196 us  [fro(): return lax.ppermute(value, axis, [((i + offset) % n, i) for i in range(n)])]
    pallas_call x1, Pallas kernels: 10.2 us -> 3.18 us  [attend(): pl.pallas_call(body, grid_spec=pltpu.PrefetchScalarGridSpec(num_scalar_pr...]
  transfers between devices with their start and end apart: 92 -> 92, of which waited for: 47 -> 48; matrix products, arithmetic and copies ran while one was open for 6% -> 5% of each run, Pallas kernels for 23% -> 20%
where the time goes in v5:
time: 466 us; the launch traced here: 459 us
  waiting for transfers between devices  196 us (42%)
  Pallas kernels  124 us (27%)
  starting transfers between devices  95.2 us (20%)
  other arithmetic  20.5 us (4%)
  local copies, waits for them, and re-layouts  19.9 us (4%)
    ppermute x92, waiting for transfers between devices, fro(): return lax.ppermute(value, axis, [((i + offset) % n, i) for i in range(n)])  196 us
    ppermute x92, starting transfers between devices, fro(): return lax.ppermute(value, axis, [((i + offset) % n, i) for i in range(n)])  95.2 us
    pallas_call x2, Pallas kernels, ffn_call(): pl.pallas_call(kernel, grid=(chunks,), in_specs=[anywhere] * count + [chu...  49.1 us
    pallas_call x5, Pallas kernels, run(): pl.pallas_call(body, out_shape=tuple((jax.ShapeDtypeStruct(s, d) for s, d...  38.8 us
    pallas_call x3, Pallas kernels, unit_grads(): pl.pallas_call(body, grid=(1,), in_specs=[pl.BlockSpec((tokens, both), la...  18.9 us
    pallas_call x1, Pallas kernels, attend_back(): pl.pallas_call(body, grid_spec=pltpu.PrefetchScalarGridSpec(num_scalar_pr...  14.2 us
  transfers between devices with their start and end apart: 92, of which 48 were waited for; matrix products, arithmetic and copies ran while one was open for 5% of the time, Pallas kernels for 20%

profile of v5, /device:TPU:0, one launch (start us, length us, event | category | flops | bytes accessed | tf_op | source)
XLA Modules:
  0.0 459.0 jit_solution(4635136884445514213)
XLA Ops:
  4.3 5.0 %collective-permute-start = (bf16[736,128]{1,0:T(8,128)(2,1)S(1)}, bf16[736,128]{1,0:T(8,128)(2,1)S(1)}, u32[]{:S(2)}, u32[]{:S(2)}) collective-permute-start(bf16[736,128]{1,0:T(8,128)(2,1)S(1)} %pad_maximum_fusion.12), channel_id=1, source_target_pairs={{2,0},{4,2},{6,4},{0,6},{3,1},{5,3},{7,5},{1,7},{10,8},{12,10},{14... | collective-permute-start | bytes 565256 | tf_op jit(solution)/shard_map/attn_gather_z1/ppermute | solution.py:816
  11.1 3.4 collective-permute-done
  14.5 4.3 collective-permute-start.1
  21.1 4.3 collective-permute-done.3
  25.4 3.7 collective-permute-done.5
  35.0 3.5 collective-permute-start.15
  38.5 11.3 %collective-permute-done.10 = bf16[2944,128]{1,0:T(8,128)(2,1)S(1)} collective-permute-done((bf16[2944,128]{1,0:T(8,128)(2,1)S(1)}, bf16[2944,128]{1,0:T(8,128)(2,1)S(1)}, u32[]{:S(2)}, u32[]{:S(2)}) %collective-permute-start.10) | collective-permute-done | bytes 753696 | tf_op jit(solution)/shard_map/attn_gather_x1/ppermute | solution.py:816
  54.1 5.0 %collective-permute-done.12 = bf16[1472,128]{1,0:T(8,128)(2,1)S(1)} collective-permute-done((bf16[1472,128]{1,0:T(8,128)(2,1)S(1)}, bf16[1472,128]{1,0:T(8,128)(2,1)S(1)}, u32[]{:S(2)}, u32[]{:S(2)}) %collective-permute-start.12) | collective-permute-done | bytes 376864 | tf_op jit(solution)/shard_map/attn_gather_y1/ppermute | solution.py:816
  63.7 6.6 %collective-permute-done.15.refs_9_.refs_11_ = bf16[224,3456]{1,0:T(8,128)(2,1)} collective-permute-done((bf16[224,3456]{1,0:T(8,128)(2,1)}, bf16[224,3456]{1,0:T(8,128)(2,1)}, u32[]{:S(2)}, u32[]{:S(2)}) %collective-permute-start.15) | collective-permute-done | bytes 1548320 | tf_op jit(solution)/shard_map/unit_gather_z1/ppermute | solution.py:816
  73.3 4.3 collective-permute-start.18
  77.6 8.9 %first_part.1 = (bf16[1152,1536]{1,0:T(8,128)(2,1)}, f32[1,1152]{1,0:T(1,128)}, f32[1,256]{1,0:T(1,128)}, f32[1,256]{1,0:T(1,128)}, f32[1,1152]{1,0:T(1,128)}, /...) custom-call(s32[32]{0:T(128)} %fusion.11.order_ref, ...), custom_call_target="tpu_custom_call" | custom-call | flops 7247757312 | tf_op jit(solution)/shard_map/first_part/pallas_call | solution.py:90
  90.6 5.9 %spread_out.1.w_ref.refs_6_ = bf16[1024,1152]{1,0:T(8,128)(2,1)} custom-call(s32[32]{0:T(128)} %fusion.11.order_ref, bf16[4,736,128]{2,1,0:T(8,128)(2,1)} %bitcast.118, bf16[4,736,128]{2,1,0:T(8,128)(2,1)} %bitcast.126, bf16[4,736,128]{2,1,0:T(8,128)(2,1)} %bitcast.122, bf16[4,736,128]{2,1,0:T(8,128)(2,1)} %bitcast.128, bf16[4,736,128]{2,1,0:T(8,128)(2,1)} %bitcast.120, ...), custom_call_target="tpu_custom_call" | custom-call | tf_op jit(solution)/shard_map/spread_out/pallas_call | solution.py:90
  96.5 3.9 collective-permute-done.16
  100.4 3.4 collective-permute-done.17
  106.0 3.5 collective-permute-start.22
  109.6 3.9 collective-permute-start.19
  113.5 4.3 collective-permute-done.23
  118.9 5.3 %collective-permute-done.24 = bf16[256,512]{1,0:T(8,128)(2,1)S(1)} collective-permute-done((bf16[256,512]{1,0:T(8,128)(2,1)S(1)}, bf16[256,512]{1,0:T(8,128)(2,1)S(1)}, u32[]{:S(2)}, u32[]{:S(2)}) %collective-permute-start.24) | collective-permute-done | bytes 262176 | tf_op jit(solution)/shard_map/kv_gather_vx1/ppermute | solution.py:816
  124.4 3.2 attend.1
  129.0 3.9 collective-permute-done.19.refs_11_.refs_13_
  134.1 5.5 %collective-permute-start.34 = (bf16[112,3456]{1,0:T(8,128)(2,1)S(1)}, bf16[112,3456]{1,0:T(8,128)(2,1)S(1)}, u32[]{:S(2)}, u32[]{:S(2)}) collective-permute-start(bf16[112,3456]{1,0:T(8,128)(2,1)S(1)} %collective-permute-done.19.refs_11_.refs_13_), channel_id=1, source_target_pairs={{2,0},{4,2},{6,4},{0,6},{3,1},{5,3},{7,5},{1,7},{10,8},{12,10},{14... | collective-permute-start | bytes 2322440 | tf_op jit(solution)/shard_map/unit_gather_z1/ppermute | solution.py:816
  139.5 10.0 %collective-permute-done.28.refs_12_.refs_14_ = bf16[112,3456]{1,0:T(8,128)(2,1)S(1)} collective-permute-done((bf16[112,3456]{1,0:T(8,128)(2,1)}, bf16[112,3456]{1,0:T(8,128)(2,1)S(1)}, u32[]{:S(2)}, u32[]{:S(2)}) %collective-permute-start.28) | collective-permute-done | bytes 774176 | tf_op jit(solution)/shard_map/unit_gather_z1/ppermute | solution.py:816
  151.5 12.9 %collective-permute-done.34.refs_13_.refs_15_ = bf16[112,3456]{1,0:T(8,128)(2,1)S(1)} collective-permute-done((bf16[112,3456]{1,0:T(8,128)(2,1)S(1)}, bf16[112,3456]{1,0:T(8,128)(2,1)S(1)}, u32[]{:S(2)}, u32[]{:S(2)}) %collective-permute-start.34) | collective-permute-done | bytes 774176 | tf_op jit(solution)/shard_map/unit_gather_z1/ppermute | solution.py:816
  168.4 24.6 %ffn_forward.1 = (bf16[2048,896]{1,0:T(8,128)(2,1)}, bf16[2048,896]{1,0:T(8,128)(2,1)}, bf16[2048,896]{1,0:T(8,128)(2,1)}, bf16[256,1152]{1,0:T(8,128)(2,1)}, bf...) custom-call(bf16[256,1152]{1,0:T(8,128)(2,1)} %copy-done.25, ...), custom_call_target="tpu_custom_call" | custom-call | flops 12683575296 | tf_op jit(solution)/shard_map/ffn_forward/pallas_call | solution.py:559
  198.3 7.4 %collective-permute-done.42 = bf16[128,1152]{1,0:T(8,128)(2,1)S(1)} collective-permute-done((bf16[128,1152]{1,0:T(8,128)(2,1)S(1)}, bf16[128,1152]{1,0:T(8,128)(2,1)S(1)}, u32[]{:S(2)}, u32[]{:S(2)}) %collective-permute-start.42) | collective-permute-done | bytes 294944 | tf_op jit(solution)/shard_map/ffn_out_sum_x-1/ppermute | solution.py:816
  208.1 12.4 %collective-permute-done.43.refs_2_ = bf16[256,1152]{1,0:T(8,128)(2,1)S(1)} collective-permute-done((bf16[256,1152]{1,0:T(8,128)(2,1)S(1)}, bf16[256,1152]{1,0:T(8,128)(2,1)S(1)}, u32[]{:S(2)}, u32[]{:S(2)}) %collective-permute-start.43) | collective-permute-done | bytes 589856 | tf_op jit(solution)/shard_map/ffn_out_sum_y-1/ppermute | solution.py:816
  224.5 11.4 %collective-permute-done.47.refs_4_ = bf16[256,1152]{1,0:T(8,128)(2,1)S(1)} collective-permute-done((bf16[256,1152]{1,0:T(8,128)(2,1)S(1)}, bf16[256,1152]{1,0:T(8,128)(2,1)S(1)}, u32[]{:S(2)}, u32[]{:S(2)}) %collective-permute-start.47) | collective-permute-done | bytes 589856 | tf_op jit(solution)/shard_map/d_out_gather_x1/ppermute | solution.py:816
  239.1 3.9 collective-permute-done.49
  246.5 6.2 %unit_grads.3 = (bf16[224,1152]{1,0:T(8,128)(2,1)S(1)}, bf16[224,1152]{1,0:T(8,128)(2,1)S(1)}, bf16[224,1152]{1,0:T(8,128)(2,1)S(1)}, bf16[224,1152]{1,0:T(8,128)(2,1)S(1)}) custom-call(bf16[2048,896]{1,0:T(8,128)(2,1)S(1)} %copy-done.41, bf16[256,1152]{1,0:T(8,128)(2,1)S(1)} %get-tuple-element.273.refs_0_, ...), custom_call_target="tpu_custom_call" | custom-call | flops 4227858432 | tf_op jit(solution)/shard_map/unit_grads/pallas_call | solution.py:636
  253.5 24.5 %ffn_backward.1 = (bf16[2048,1792]{1,0:T(8,128)(2,1)}, bf16[256,1152]{1,0:T(8,128)(2,1)}, bf16[256,1152]{1,0:T(8,128)(2,1)}, bf16[256,1152]{1,0:T(8,128)(2,1)}, ...) custom-call(bf16[256,1152]{1,0:T(8,128)(2,1)} %copy-done.35, ...), custom_call_target="tpu_custom_call" | custom-call | flops 12683575296 | tf_op jit(solution)/shard_map/ffn_backward/pallas_call | solution.py:559
  285.9 3.1 copy-done.40
  289.0 6.5 %unit_grads.4 = (bf16[224,1152]{1,0:T(8,128)(2,1)S(1)}, bf16[224,1152]{1,0:T(8,128)(2,1)S(1)}, bf16[224,1152]{1,0:T(8,128)(2,1)S(1)}, bf16[224,1152]{1,0:T(8,128)(2,1)S(1)}) custom-call(bf16[2048,1792]{1,0:T(8,128)(2,1)S(1)} %copy-done.40, bf16[256,1152]{1,0:T(8,128)(2,1)S(1)} %copy-done.26, bf16[256,1152]{1,0:T(8,128)(2,1)S(1)} %copy-done.32, ...), custom_call_target="tpu_custom_call" | custom-call | flops 4227858432 | tf_op jit(solution)/shard_map/unit_grads/pallas_call | solution.py:636
  299.5 6.3 %unit_grads.5 = (bf16[224,1152]{1,0:T(8,128)(2,1)S(1)}, bf16[224,1152]{1,0:T(8,128)(2,1)S(1)}, bf16[224,1152]{1,0:T(8,128)(2,1)S(1)}, bf16[224,1152]{1,0:T(8,128)(2,1)S(1)}) custom-call(bf16[2048,1792]{1,0:T(8,128)(2,1)S(1)} %copy-done.40, bf16[256,1152]{1,0:T(8,128)(2,1)S(1)} %copy-done.26, bf16[256,1152]{1,0:T(8,128)(2,1)S(1)} %copy-done.32, ...), custom_call_target="tpu_custom_call" | custom-call | flops 4227858432 | tf_op jit(solution)/shard_map/unit_grads/pallas_call | solution.py:636
  313.5 14.2 %attend_back.1 = (f32[256,1024]{1,0:T(8,128)}, bf16[256,1152]{1,0:T(8,128)(2,1)}, f32[256,1152]{1,0:T(8,128)}, f32[1,1152]{1,0:T(1,128)}, f32[1,1152]{1,0:T(1,12...) custom-call(s32[2,8]{1,0:T(2,128)} %copy-done.24, ...), custom_call_target="tpu_custom_call" | custom-call | tf_op jit(solution)/shard_map/attend_back/pallas_call | solution.py:417
  327.6 5.1 %collective-permute-done.64 = bf16[224,1152]{1,0:T(8,128)(2,1)S(1)} collective-permute-done((bf16[224,1152]{1,0:T(8,128)(2,1)}, bf16[224,1152]{1,0:T(8,128)(2,1)S(1)}, u32[]{:S(2)}, u32[]{:S(2)}) %collective-permute-start.64) | collective-permute-done | bytes 516128 | tf_op jit(solution)/shard_map/down_grad_sum_z-1/ppermute | solution.py:816
  337.7 4.5 collective-permute-done.69
  342.8 5.0 %collective-permute-done.66 = bf16[256,512]{1,0:T(8,128)(2,1)S(1)} collective-permute-done((bf16[256,512]{1,0:T(8,128)(2,1)}, bf16[256,512]{1,0:T(8,128)(2,1)S(1)}, u32[]{:S(2)}, u32[]{:S(2)}) %collective-permute-start.66) | collective-permute-done | bytes 262176 | tf_op jit(solution)/shard_map/kv_sum_vx-1/ppermute | solution.py:816
  347.8 3.2 collective-permute-start.71
  361.1 10.2 %query_side.1 = (f32[23056,128]{1,0:T(8,128)}, f32[256,1152]{1,0:T(8,128)}, f32[1,256]{1,0:T(1,128)}) custom-call(f32[256,1024]{1,0:T(8,128)} %get-tuple-element.345.dq_ref, f32[256,1280]{1,0:T(8,128)} %get-tuple-element.346.raw_ref.refs_3_, f32[256,128]{1,0:T(8,128)} %get-tuple-element.439.refs_9_.cos_ref.refs_4_, ...), custom_call_target="tpu_custom_call" | custom-call | tf_op jit(solution)/shard_map/query_side/pallas_call | solution.py:90
  372.1 3.7 collective-permute-done.74.refs_2_
  375.8 5.4 %collective-permute-done.73.refs_1_ = bf16[256,512]{1,0:T(8,128)(2,1)S(1)} collective-permute-done((bf16[256,512]{1,0:T(8,128)(2,1)S(1)}, bf16[256,512]{1,0:T(8,128)(2,1)S(1)}, u32[]{:S(2)}, u32[]{:S(2)}) %collective-permute-start.73) | collective-permute-done | bytes 262176 | tf_op jit(solution)/shard_map/kv_sum_z-1/ppermute | solution.py:816
  381.9 12.4 %last_part.1 = (bf16[256,1152]{1,0:T(8,128)(2,1)}, bf16[4,736,128]{2,1,0:T(8,128)(2,1)}, bf16[4,736,128]{2,1,0:T(8,128)(2,1)}, bf16[4,736,128]{2,1,0:T(8,128)(2,...) custom-call(s32[32]{0:T(128)} %fusion.11.order_ref, ...), custom_call_target="tpu_custom_call" | custom-call | tf_op jit(solution)/shard_map/last_part/pallas_call | solution.py:90
  395.6 4.5 collective-permute-done.84
  403.9 5.2 %collective-permute-done.81 = bf16[1472,128]{1,0:T(8,128)(2,1)S(1)} collective-permute-done((bf16[1472,128]{1,0:T(8,128)(2,1)S(1)}, bf16[1472,128]{1,0:T(8,128)(2,1)S(1)}, u32[]{:S(2)}, u32[]{:S(2)}) %collective-permute-start.81) | collective-permute-done | bytes 376864 | tf_op jit(solution)/shard_map/attn_grad_sum_x-1/ppermute | solution.py:816
  414.9 11.9 %collective-permute-done.82 = bf16[2944,128]{1,0:T(8,128)(2,1)S(1)} collective-permute-done((bf16[2944,128]{1,0:T(8,128)(2,1)S(1)}, bf16[2944,128]{1,0:T(8,128)(2,1)S(1)}, u32[]{:S(2)}, u32[]{:S(2)}) %collective-permute-start.82) | collective-permute-done | bytes 753696 | tf_op jit(solution)/shard_map/attn_grad_sum_y-1/ppermute | solution.py:816
  435.2 2.9 collective-permute-start.88
  440.9 9.8 %collective-permute-done.90 = bf16[216,864]{1,0:T(8,128)(2,1)S(1)} collective-permute-done((bf16[216,864]{1,0:T(8,128)(2,1)S(1)}, bf16[216,864]{1,0:T(8,128)(2,1)S(1)}, u32[]{:S(2)}, u32[]{:S(2)}) %collective-permute-start.90) | collective-permute-done | bytes 373280 | tf_op jit(solution)/shard_map/grad_exchange_uyc2/ppermute | solution.py:816
  451.3 5.5 %multiply_subtract_fusion = (f32[864,864]{1,0:T(8,128)}, f32[864,864]{1,0:T(8,128)}, f32[864,864]{1,0:T(8,128)}, f32[864,864]{1,0:T(8,128)}) fusion(f32[864,864]{1,0:T(8,128)S(1)} %copy-done.42, f32[864,864]{1,0:T(8,128)S(1)} %copy-done.44, f32[864,864]{1,0:T(8,128)S(1)} %copy-done.45, bf16[4,216,864]{2,1,0:T(8,128)(2,1)S(1)} %bitcast_dynamic-update-slice_fusion), kind=kLoop, calls=%fused_computation.3 | loop fusion | flops 11197440 | bytes 22394880 | tf_op jit(solution)/shard_map/sub | solution.py:65
  (475 shorter events, 120.3 us)
Async XLA Ops:
  9.3 16.1 %collective-permute-start.4 = (bf16[216,864]{1,0:T(8,128)(2,1)}, bf16[216,864]{1,0:T(8,128)(2,1)S(1)}, u32[]{:S(2)}, u32[]{:S(2)}) collective-permute-start(bf16[216,864]{1,0:T(8,128)(2,1)} %get-tuple-element.206), channel_id=1, source_target_pairs={{8,0},{16,8},{24,16},{0,24},{9,1},{17,9},{25,17},{1,25},{10,2},{18... | collective-permute-start | bytes 1119752 | tf_op jit(solution)/shard_map/unit_exchange_uyc1/ppermute | solution.py:816
  10.0 19.1 %collective-permute-start.5 = (bf16[216,864]{1,0:T(8,128)(2,1)}, bf16[216,864]{1,0:T(8,128)(2,1)S(1)}, u32[]{:S(2)}, u32[]{:S(2)}) collective-permute-start(bf16[216,864]{1,0:T(8,128)(2,1)} %get-tuple-element.207), channel_id=1, source_target_pairs={{16,0},{24,8},{0,16},{8,24},{17,1},{25,9},{1,17},{9,25},{18,2},{26... | collective-permute-start | bytes 1119752 | tf_op jit(solution)/shard_map/unit_exchange_uyc2/ppermute | solution.py:816
  10.8 18.3 %collective-permute-start.6 = (bf16[216,864]{1,0:T(8,128)(2,1)S(1)}, bf16[216,864]{1,0:T(8,128)(2,1)S(1)}, u32[]{:S(2)}, u32[]{:S(2)}) collective-permute-start(bf16[216,864]{1,0:T(8,128)(2,1)S(1)} %get-tuple-element.208), channel_id=1, source_target_pairs={{24,0},{0,8},{8,16},{16,24},{25,1},{1,9},{9,17},{17,25},{26,2},{2,... | collective-permute-start | bytes 1119752 | tf_op jit(solution)/shard_map/unit_exchange_uyc3/ppermute | solution.py:816
  32.2 17.6 %collective-permute-start.10 = (bf16[2944,128]{1,0:T(8,128)(2,1)S(1)}, bf16[2944,128]{1,0:T(8,128)(2,1)S(1)}, u32[]{:S(2)}, u32[]{:S(2)}) collective-permute-start(bf16[2944,128]{1,0:T(8,128)(2,1)S(1)} %pad_maximum_fusion.1), channel_id=1, source_target_pairs={{1,0},{0,1},{3,2},{2,3},{5,4},{4,5},{7,6},{6,7},{9,8},{8,9},{11,10... | collective-permute-start | bytes 2261000 | tf_op jit(solution)/shard_map/attn_gather_x1/ppermute | solution.py:816
  33.8 17.7 %collective-permute-start.8 = (bf16[2944,128]{1,0:T(8,128)(2,1)S(1)}, bf16[2944,128]{1,0:T(8,128)(2,1)S(1)}, u32[]{:S(2)}, u32[]{:S(2)}) collective-permute-start(bf16[2944,128]{1,0:T(8,128)(2,1)S(1)} %pad_maximum_fusion.1), channel_id=1, source_target_pairs={{16,0},{0,16},{17,1},{1,17},{18,2},{2,18},{19,3},{3,19},{20,4},{4,... | collective-permute-start | bytes 2261000 | tf_op jit(solution)/shard_map/attn_gather_y1/ppermute | solution.py:816
  35.0 35.4 %collective-permute-start.15 = (bf16[224,3456]{1,0:T(8,128)(2,1)}, bf16[224,3456]{1,0:T(8,128)(2,1)}, u32[]{:S(2)}, u32[]{:S(2)}) collective-permute-start(bf16[224,3456]{1,0:T(8,128)(2,1)} %pad.4.refs_8_.refs_10_), channel_id=1, source_target_pairs={{2,0},{4,2},{6,4},{0,6},{3,1},{5,3},{7,5},{1,7},{10,8},{12,10},{14... | collective-permute-start | bytes 4644872 | tf_op jit(solution)/shard_map/unit_gather_z1/ppermute | solution.py:816
  73.3 30.5 %collective-permute-start.18 = (bf16[112,3456]{1,0:T(8,128)(2,1)}, bf16[112,3456]{1,0:T(8,128)(2,1)}, u32[]{:S(2)}, u32[]{:S(2)}) collective-permute-start(bf16[112,3456]{1,0:T(8,128)(2,1)} %get-tuple-element.412), channel_id=1, source_target_pairs={{2,0},{4,2},{6,4},{0,6},{3,1},{5,3},{7,5},{1,7},{10,8},{12,10},{14... | collective-permute-start | bytes 2322440 | tf_op jit(solution)/shard_map/unit_gather_z1/ppermute | solution.py:816
  87.6 16.2 %collective-permute-start.17 = (bf16[256,512]{1,0:T(8,128)(2,1)}, bf16[256,512]{1,0:T(8,128)(2,1)S(1)}, u32[]{:S(2)}, u32[]{:S(2)}) collective-permute-start(bf16[256,512]{1,0:T(8,128)(2,1)} %get-tuple-element.228), channel_id=1, source_target_pairs={{6,0},{0,2},{2,4},{4,6},{7,1},{1,3},{3,5},{5,7},{14,8},{8,10},{10,... | collective-permute-start | bytes 786440 | tf_op jit(solution)/shard_map/kv_gather_z-1/ppermute | solution.py:816
  103.8 15.0 %collective-permute-start.21 = (bf16[256,512]{1,0:T(8,128)(2,1)S(1)}, bf16[256,512]{1,0:T(8,128)(2,1)S(1)}, u32[]{:S(2)}, u32[]{:S(2)}) collective-permute-start(bf16[256,512]{1,0:T(8,128)(2,1)S(1)} %collective-permute-done.16), channel_id=1, source_target_pairs={{1,0},{0,1},{3,2},{2,3},{5,4},{4,5},{7,6},{6,7},{9,8},{8,9},{11,10... | collective-permute-start | bytes 786440 | tf_op jit(solution)/shard_map/kv_gather_vx1/ppermute | solution.py:816
  104.4 19.9 %collective-permute-start.25 = (bf16[256,512]{1,0:T(8,128)(2,1)S(1)}, bf16[256,512]{1,0:T(8,128)(2,1)S(1)}, u32[]{:S(2)}, u32[]{:S(2)}) collective-permute-start(bf16[256,512]{1,0:T(8,128)(2,1)S(1)} %collective-permute-done.17), channel_id=1, source_target_pairs={{1,0},{0,1},{3,2},{2,3},{5,4},{4,5},{7,6},{6,7},{9,8},{8,9},{11,10... | collective-permute-start | bytes 786440 | tf_op jit(solution)/shard_map/kv_gather_vx1/ppermute | solution.py:816
  109.6 23.3 %collective-permute-start.19 = (bf16[112,3456]{1,0:T(8,128)(2,1)S(1)}, bf16[112,3456]{1,0:T(8,128)(2,1)S(1)}, u32[]{:S(2)}, u32[]{:S(2)}) collective-permute-start(bf16[112,3456]{1,0:T(8,128)(2,1)S(1)} %copy-done.53), channel_id=1, source_target_pairs={{2,0},{4,2},{6,4},{0,6},{3,1},{5,3},{7,5},{1,7},{10,8},{12,10},{14... | collective-permute-start | bytes 2322440 | tf_op jit(solution)/shard_map/unit_gather_z1/ppermute | solution.py:816
  118.4 31.2 %collective-permute-start.28 = (bf16[112,3456]{1,0:T(8,128)(2,1)}, bf16[112,3456]{1,0:T(8,128)(2,1)S(1)}, u32[]{:S(2)}, u32[]{:S(2)}) collective-permute-start(bf16[112,3456]{1,0:T(8,128)(2,1)} %collective-permute-done.18.refs_10_.refs_12_), channel_id=1, source_target_pairs={{2,0},{4,2},{6,4},{0,6},{3,1},{5,3},{7,5},{1,7},{10,8},{12,10},{14... | collective-permute-start | bytes 2322440 | tf_op jit(solution)/shard_map/unit_gather_z1/ppermute | solution.py:816
  132.9 16.7 %collective-permute-start.26 = (bf16[256,1152]{1,0:T(8,128)(2,1)S(1)}, bf16[256,1152]{1,0:T(8,128)(2,1)S(1)}, u32[]{:S(2)}, u32[]{:S(2)}) collective-permute-start(bf16[256,1152]{1,0:T(8,128)(2,1)S(1)} %get-tuple-element.249.refs_0_), channel_id=1, source_target_pairs={{16,0},{0,16},{17,1},{1,17},{18,2},{2,18},{19,3},{3,19},{20,4},{4,... | collective-permute-start | bytes 1769480 | tf_op jit(solution)/shard_map/ffn_in_gather_y1/ppermute | solution.py:816
  133.5 16.1 %collective-permute-start.27 = (bf16[256,1152]{1,0:T(8,128)(2,1)S(1)}, bf16[256,1152]{1,0:T(8,128)(2,1)S(1)}, u32[]{:S(2)}, u32[]{:S(2)}) collective-permute-start(bf16[256,1152]{1,0:T(8,128)(2,1)S(1)} %get-tuple-element.249.refs_0_), channel_id=1, source_target_pairs={{1,0},{0,1},{3,2},{2,3},{5,4},{4,5},{7,6},{6,7},{9,8},{8,9},{11,10... | collective-permute-start | bytes 1769480 | tf_op jit(solution)/shard_map/ffn_in_gather_x1/ppermute | solution.py:816
  134.1 30.3 %collective-permute-start.34 = (bf16[112,3456]{1,0:T(8,128)(2,1)S(1)}, bf16[112,3456]{1,0:T(8,128)(2,1)S(1)}, u32[]{:S(2)}, u32[]{:S(2)}) collective-permute-start(bf16[112,3456]{1,0:T(8,128)(2,1)S(1)} %collective-permute-done.19.refs_11_.refs_13_), channel_id=1, source_target_pairs={{2,0},{4,2},{6,4},{0,6},{3,1},{5,3},{7,5},{1,7},{10,8},{12,10},{14... | collective-permute-start | bytes 2322440 | tf_op jit(solution)/shard_map/unit_gather_z1/ppermute | solution.py:816
  149.6 14.8 %collective-permute-start.32 = (bf16[128,1152]{1,0:T(8,128)(2,1)S(1)}, bf16[128,1152]{1,0:T(8,128)(2,1)S(1)}, u32[]{:S(2)}, u32[]{:S(2)}) collective-permute-start(bf16[128,1152]{1,0:T(8,128)(2,1)S(1)} %slice.209), channel_id=1, source_target_pairs={{16,0},{0,16},{17,1},{1,17},{18,2},{2,18},{19,3},{3,19},{20,4},{4,... | collective-permute-start | bytes 884744 | tf_op jit(solution)/shard_map/ffn_in_gather_y1/ppermute | solution.py:816
  150.4 14.0 %collective-permute-start.33 = (bf16[128,1152]{1,0:T(8,128)(2,1)S(1)}, bf16[128,1152]{1,0:T(8,128)(2,1)S(1)}, u32[]{:S(2)}, u32[]{:S(2)}) collective-permute-start(bf16[128,1152]{1,0:T(8,128)(2,1)S(1)} %slice.210), channel_id=1, source_target_pairs={{1,0},{0,1},{3,2},{2,3},{5,4},{4,5},{7,6},{6,7},{9,8},{8,9},{11,10... | collective-permute-start | bytes 884744 | tf_op jit(solution)/shard_map/ffn_in_gather_x1/ppermute | solution.py:816
  151.0 15.4 %collective-permute-start.30 = (bf16[256,1152]{1,0:T(8,128)(2,1)S(1)}, bf16[256,1152]{1,0:T(8,128)(2,1)S(1)}, u32[]{:S(2)}, u32[]{:S(2)}) collective-permute-start(bf16[256,1152]{1,0:T(8,128)(2,1)S(1)} %collective-permute-done.26.refs_2_), channel_id=1, source_target_pairs={{8,0},{0,8},{9,1},{1,9},{10,2},{2,10},{11,3},{3,11},{12,4},{4,12},... | collective-permute-start | bytes 1769480 | tf_op jit(solution)/shard_map/ffn_in_gather_c1/ppermute | solution.py:816
  151.0 15.4 %collective-permute-start.31 = (bf16[256,1152]{1,0:T(8,128)(2,1)S(1)}, bf16[256,1152]{1,0:T(8,128)(2,1)S(1)}, u32[]{:S(2)}, u32[]{:S(2)}) collective-permute-start(bf16[256,1152]{1,0:T(8,128)(2,1)S(1)} %collective-permute-done.27.refs_4_), channel_id=1, source_target_pairs={{8,0},{0,8},{9,1},{1,9},{10,2},{2,10},{11,3},{3,11},{12,4},{4,12},... | collective-permute-start | bytes 1769480 | tf_op jit(solution)/shard_map/ffn_in_gather_c1/ppermute | solution.py:816
  193.8 14.2 %collective-permute-start.36 = (bf16[256,1152]{1,0:T(8,128)(2,1)}, bf16[256,1152]{1,0:T(8,128)(2,1)S(1)}, u32[]{:S(2)}, u32[]{:S(2)}) collective-permute-start(bf16[256,1152]{1,0:T(8,128)(2,1)} %get-tuple-element.258), channel_id=1, source_target_pairs={{8,0},{0,8},{9,1},{1,9},{10,2},{2,10},{11,3},{3,11},{12,4},{4,12},... | collective-permute-start | bytes 1769480 | tf_op jit(solution)/shard_map/ffn_out_sum_c1/ppermute | solution.py:816
  205.9 14.6 %collective-permute-start.43 = (bf16[256,1152]{1,0:T(8,128)(2,1)S(1)}, bf16[256,1152]{1,0:T(8,128)(2,1)S(1)}, u32[]{:S(2)}, u32[]{:S(2)}) collective-permute-start(bf16[256,1152]{1,0:T(8,128)(2,1)S(1)} %pad_maximum_fusion.5), channel_id=1, source_target_pairs={{16,0},{0,16},{17,1},{1,17},{18,2},{2,18},{19,3},{3,19},{20,4},{4,... | collective-permute-start | bytes 1769480 | tf_op jit(solution)/shard_map/ffn_out_sum_y-1/ppermute | solution.py:816
  206.7 14.3 %collective-permute-start.40 = (bf16[256,1152]{1,0:T(8,128)(2,1)S(1)}, bf16[256,1152]{1,0:T(8,128)(2,1)S(1)}, u32[]{:S(2)}, u32[]{:S(2)}) collective-permute-start(bf16[256,1152]{1,0:T(8,128)(2,1)S(1)} %pad_maximum_fusion.4), channel_id=1, source_target_pairs={{1,0},{0,1},{3,2},{2,3},{5,4},{4,5},{7,6},{6,7},{9,8},{8,9},{11,10... | collective-permute-start | bytes 1769480 | tf_op jit(solution)/shard_map/ffn_out_sum_x-1/ppermute | solution.py:816
  252.7 26.0 %collective-permute-start.52 = (bf16[224,1152]{1,0:T(8,128)(2,1)S(1)}, bf16[224,1152]{1,0:T(8,128)(2,1)S(1)}, u32[]{:S(2)}, u32[]{:S(2)}) collective-permute-start(bf16[224,1152]{1,0:T(8,128)(2,1)S(1)} %get-tuple-element.277), channel_id=1, source_target_pairs={{6,0},{0,2},{2,4},{4,6},{7,1},{1,3},{3,5},{5,7},{14,8},{8,10},{10,... | collective-permute-start | bytes 1548296 | tf_op jit(solution)/shard_map/down_grad_sum_z-1/ppermute | solution.py:816
  278.6 30.5 %collective-permute-start.55 = (bf16[256,1152]{1,0:T(8,128)(2,1)}, bf16[256,1152]{1,0:T(8,128)(2,1)S(1)}, u32[]{:S(2)}, u32[]{:S(2)}) collective-permute-start(bf16[256,1152]{1,0:T(8,128)(2,1)} %get-tuple-element.284), channel_id=1, source_target_pairs={{8,0},{0,8},{9,1},{1,9},{10,2},{2,10},{11,3},{3,11},{12,4},{4,12},... | collective-permute-start | bytes 1769480 | tf_op jit(solution)/shard_map/d_in_sum_c1/ppermute | solution.py:816
  279.3 18.9 %collective-permute-start.56 = (bf16[224,1152]{1,0:T(8,128)(2,1)S(1)}, bf16[224,1152]{1,0:T(8,128)(2,1)S(1)}, u32[]{:S(2)}, u32[]{:S(2)}) collective-permute-start(bf16[224,1152]{1,0:T(8,128)(2,1)S(1)} %add_convert_fusion.16), channel_id=1, source_target_pairs={{6,0},{0,2},{2,4},{4,6},{7,1},{1,3},{3,5},{5,7},{14,8},{8,10},{10,... | collective-permute-start | bytes 1548296 | tf_op jit(solution)/shard_map/down_grad_sum_z-1/ppermute | solution.py:816
  283.0 14.9 %collective-permute-start.60 = (bf16[128,1152]{1,0:T(8,128)(2,1)S(1)}, bf16[128,1152]{1,0:T(8,128)(2,1)S(1)}, u32[]{:S(2)}, u32[]{:S(2)}) collective-permute-start(bf16[128,1152]{1,0:T(8,128)(2,1)S(1)} %get-tuple-element.430), channel_id=1, source_target_pairs={{1,0},{0,1},{3,2},{2,3},{5,4},{4,5},{7,6},{6,7},{9,8},{8,9},{11,10... | collective-permute-start | bytes 884744 | tf_op jit(solution)/shard_map/d_in_sum_x-1/ppermute | solution.py:816
  284.0 14.0 %collective-permute-start.58 = (bf16[128,1152]{1,0:T(8,128)(2,1)S(1)}, bf16[128,1152]{1,0:T(8,128)(2,1)S(1)}, u32[]{:S(2)}, u32[]{:S(2)}) collective-permute-start(bf16[128,1152]{1,0:T(8,128)(2,1)S(1)} %get-tuple-element.431), channel_id=1, source_target_pairs={{16,0},{0,16},{17,1},{1,17},{18,2},{2,18},{19,3},{3,19},{20,4},{4,... | collective-permute-start | bytes 884744 | tf_op jit(solution)/shard_map/d_in_sum_y-1/ppermute | solution.py:816
  295.5 17.0 %collective-permute-start.54 = (bf16[224,1152]{1,0:T(8,128)(2,1)S(1)}, bf16[224,1152]{1,0:T(8,128)(2,1)S(1)}, u32[]{:S(2)}, u32[]{:S(2)}) collective-permute-start(bf16[224,1152]{1,0:T(8,128)(2,1)S(1)} %get-tuple-element.282), channel_id=1, source_target_pairs={{6,0},{0,2},{2,4},{4,6},{7,1},{1,3},{3,5},{5,7},{14,8},{8,10},{10,... | collective-permute-start | bytes 1548296 | tf_op jit(solution)/shard_map/gate_grad_sum_z-1/ppermute | solution.py:816
  298.2 14.3 %collective-permute-start.61 = (bf16[256,1152]{1,0:T(8,128)(2,1)S(1)}, bf16[256,1152]{1,0:T(8,128)(2,1)S(1)}, u32[]{:S(2)}, u32[]{:S(2)}) collective-permute-start(bf16[256,1152]{1,0:T(8,128)(2,1)S(1)} %pad_maximum_fusion.6), channel_id=1, source_target_pairs={{1,0},{0,1},{3,2},{2,3},{5,4},{4,5},{7,6},{6,7},{9,8},{8,9},{11,10... | collective-permute-start | bytes 1769480 | tf_op jit(solution)/shard_map/d_in_sum_x-1/ppermute | solution.py:816
  298.3 14.2 %collective-permute-start.62 = (bf16[256,1152]{1,0:T(8,128)(2,1)S(1)}, bf16[256,1152]{1,0:T(8,128)(2,1)S(1)}, u32[]{:S(2)}, u32[]{:S(2)}) collective-permute-start(bf16[256,1152]{1,0:T(8,128)(2,1)S(1)} %pad_maximum_fusion.7), channel_id=1, source_target_pairs={{16,0},{0,16},{17,1},{1,17},{18,2},{2,18},{19,3},{3,19},{20,4},{4,... | collective-permute-start | bytes 1769480 | tf_op jit(solution)/shard_map/d_in_sum_y-1/ppermute | solution.py:816
  305.8 21.8 %collective-permute-start.65 = (bf16[224,1152]{1,0:T(8,128)(2,1)S(1)}, bf16[224,1152]{1,0:T(8,128)(2,1)S(1)}, u32[]{:S(2)}, u32[]{:S(2)}) collective-permute-start(bf16[224,1152]{1,0:T(8,128)(2,1)S(1)} %get-tuple-element.310), channel_id=1, source_target_pairs={{6,0},{0,2},{2,4},{4,6},{7,1},{1,3},{3,5},{5,7},{14,8},{8,10},{10,... | collective-permute-start | bytes 1548296 | tf_op jit(solution)/shard_map/up_grad_sum_z-1/ppermute | solution.py:816
  309.1 23.6 %collective-permute-start.64 = (bf16[224,1152]{1,0:T(8,128)(2,1)}, bf16[224,1152]{1,0:T(8,128)(2,1)S(1)}, u32[]{:S(2)}, u32[]{:S(2)}) collective-permute-start(bf16[224,1152]{1,0:T(8,128)(2,1)} %add_convert_fusion.14), channel_id=1, source_target_pairs={{6,0},{0,2},{2,4},{4,6},{7,1},{1,3},{3,5},{5,7},{14,8},{8,10},{10,... | collective-permute-start | bytes 1548296 | tf_op jit(solution)/shard_map/down_grad_sum_z-1/ppermute | solution.py:816
  333.1 14.7 %collective-permute-start.66 = (bf16[256,512]{1,0:T(8,128)(2,1)}, bf16[256,512]{1,0:T(8,128)(2,1)S(1)}, u32[]{:S(2)}, u32[]{:S(2)}) collective-permute-start(bf16[256,512]{1,0:T(8,128)(2,1)} %get-tuple-element.328), channel_id=1, source_target_pairs={{1,0},{0,1},{3,2},{2,3},{5,4},{4,5},{7,6},{6,7},{9,8},{8,9},{11,10... | collective-permute-start | bytes 786440 | tf_op jit(solution)/shard_map/kv_sum_vx-1/ppermute | solution.py:816
  334.8 18.7 %collective-permute-start.67 = (bf16[256,512]{1,0:T(8,128)(2,1)}, bf16[256,512]{1,0:T(8,128)(2,1)S(1)}, u32[]{:S(2)}, u32[]{:S(2)}) collective-permute-start(bf16[256,512]{1,0:T(8,128)(2,1)} %get-tuple-element.330), channel_id=1, source_target_pairs={{1,0},{0,1},{3,2},{2,3},{5,4},{4,5},{7,6},{6,7},{9,8},{8,9},{11,10... | collective-permute-start | bytes 786440 | tf_op jit(solution)/shard_map/kv_sum_vx-1/ppermute | solution.py:816
  335.1 21.6 %collective-permute-start.68 = (bf16[256,512]{1,0:T(8,128)(2,1)}, bf16[256,512]{1,0:T(8,128)(2,1)S(1)}, u32[]{:S(2)}, u32[]{:S(2)}) collective-permute-start(bf16[256,512]{1,0:T(8,128)(2,1)} %get-tuple-element.332), channel_id=1, source_target_pairs={{1,0},{0,1},{3,2},{2,3},{5,4},{4,5},{7,6},{6,7},{9,8},{8,9},{11,10... | collective-permute-start | bytes 786440 | tf_op jit(solution)/shard_map/kv_sum_vx-1/ppermute | solution.py:816
  336.9 21.0 %collective-permute-start.63 = (bf16[224,1152]{1,0:T(8,128)(2,1)S(1)}, bf16[224,1152]{1,0:T(8,128)(2,1)S(1)}, u32[]{:S(2)}, u32[]{:S(2)}) collective-permute-start(bf16[224,1152]{1,0:T(8,128)(2,1)S(1)} %add_convert_fusion.15), channel_id=1, source_target_pairs={{6,0},{0,2},{2,4},{4,6},{7,1},{1,3},{3,5},{5,7},{14,8},{8,10},{10,... | collective-permute-start | bytes 1548296 | tf_op jit(solution)/shard_map/gate_grad_sum_z-1/ppermute | solution.py:816
  342.3 14.4 %collective-permute-start.70 = (bf16[128,512]{1,0:T(8,128)(2,1)S(1)}, bf16[128,512]{1,0:T(8,128)(2,1)S(1)}, u32[]{:S(2)}, u32[]{:S(2)}) collective-permute-start(bf16[128,512]{1,0:T(8,128)(2,1)S(1)} %get-tuple-element.437), channel_id=1, source_target_pairs={{6,0},{0,2},{2,4},{4,6},{7,1},{1,3},{3,5},{5,7},{14,8},{8,10},{10,... | collective-permute-start | bytes 393224 | tf_op jit(solution)/shard_map/kv_sum_z-1/ppermute | solution.py:816
  353.4 18.7 %collective-permute-start.72 = (bf16[224,1152]{1,0:T(8,128)(2,1)S(1)}, bf16[224,1152]{1,0:T(8,128)(2,1)S(1)}, u32[]{:S(2)}, u32[]{:S(2)}) collective-permute-start(bf16[224,1152]{1,0:T(8,128)(2,1)S(1)} %add_convert_fusion.13), channel_id=1, source_target_pairs={{6,0},{0,2},{2,4},{4,6},{7,1},{1,3},{3,5},{5,7},{14,8},{8,10},{10,... | collective-permute-start | bytes 1548296 | tf_op jit(solution)/shard_map/up_grad_sum_z-1/ppermute | solution.py:816
  358.1 17.7 %collective-permute-start.74 = (bf16[256,512]{1,0:T(8,128)(2,1)S(1)}, bf16[256,512]{1,0:T(8,128)(2,1)S(1)}, u32[]{:S(2)}, u32[]{:S(2)}) collective-permute-start(bf16[256,512]{1,0:T(8,128)(2,1)S(1)} %pad_maximum_fusion.11), channel_id=1, source_target_pairs={{2,0},{4,2},{6,4},{0,6},{3,1},{5,3},{7,5},{1,7},{10,8},{12,10},{14... | collective-permute-start | bytes 786440 | tf_op jit(solution)/shard_map/kv_sum_z1/ppermute | solution.py:816
  360.3 20.9 %collective-permute-start.73 = (bf16[256,512]{1,0:T(8,128)(2,1)S(1)}, bf16[256,512]{1,0:T(8,128)(2,1)S(1)}, u32[]{:S(2)}, u32[]{:S(2)}) collective-permute-start(bf16[256,512]{1,0:T(8,128)(2,1)S(1)} %pad_maximum_fusion.10), channel_id=1, source_target_pairs={{6,0},{0,2},{2,4},{4,6},{7,1},{1,3},{3,5},{5,7},{14,8},{8,10},{10,... | collective-permute-start | bytes 786440 | tf_op jit(solution)/shard_map/kv_sum_z-1/ppermute | solution.py:816
  360.5 34.5 %collective-permute-start.83 = (bf16[224,1152]{1,0:T(8,128)(2,1)S(1)}, bf16[224,1152]{1,0:T(8,128)(2,1)S(1)}, u32[]{:S(2)}, u32[]{:S(2)}) collective-permute-start(bf16[224,1152]{1,0:T(8,128)(2,1)S(1)} %add_convert_fusion.12), channel_id=1, source_target_pairs={{6,0},{0,2},{2,4},{4,6},{7,1},{1,3},{3,5},{5,7},{14,8},{8,10},{10,... | collective-permute-start | bytes 1548296 | tf_op jit(solution)/shard_map/gate_grad_sum_z-1/ppermute | solution.py:816
  381.3 18.8 %collective-permute-start.84 = (bf16[224,1152]{1,0:T(8,128)(2,1)S(1)}, bf16[224,1152]{1,0:T(8,128)(2,1)S(1)}, u32[]{:S(2)}, u32[]{:S(2)}) collective-permute-start(bf16[224,1152]{1,0:T(8,128)(2,1)S(1)} %add_convert_fusion.10), channel_id=1, source_target_pairs={{6,0},{0,2},{2,4},{4,6},{7,1},{1,3},{3,5},{5,7},{14,8},{8,10},{10,... | collective-permute-start | bytes 1548296 | tf_op jit(solution)/shard_map/up_grad_sum_z-1/ppermute | solution.py:816
  395.0 18.8 %collective-permute-start.75 = (bf16[2944,128]{1,0:T(8,128)(2,1)}, bf16[2944,128]{1,0:T(8,128)(2,1)S(1)}, u32[]{:S(2)}, u32[]{:S(2)}) collective-permute-start(bf16[2944,128]{1,0:T(8,128)(2,1)} %bitcast.141), channel_id=1, source_target_pairs={{8,0},{0,8},{9,1},{1,9},{10,2},{2,10},{11,3},{3,11},{12,4},{4,12},... | collective-permute-start | bytes 2261000 | tf_op jit(solution)/shard_map/attn_grad_sum_c1/ppermute | solution.py:816
  409.3 17.5 %collective-permute-start.82 = (bf16[2944,128]{1,0:T(8,128)(2,1)S(1)}, bf16[2944,128]{1,0:T(8,128)(2,1)S(1)}, u32[]{:S(2)}, u32[]{:S(2)}) collective-permute-start(bf16[2944,128]{1,0:T(8,128)(2,1)S(1)} %pad_maximum_fusion.3), channel_id=1, source_target_pairs={{16,0},{0,16},{17,1},{1,17},{18,2},{2,18},{19,3},{3,19},{20,4},{4,... | collective-permute-start | bytes 2261000 | tf_op jit(solution)/shard_map/attn_grad_sum_y-1/ppermute | solution.py:816
  432.0 18.7 %collective-permute-start.90 = (bf16[216,864]{1,0:T(8,128)(2,1)S(1)}, bf16[216,864]{1,0:T(8,128)(2,1)S(1)}, u32[]{:S(2)}, u32[]{:S(2)}) collective-permute-start(bf16[216,864]{1,0:T(8,128)(2,1)S(1)} %get-tuple-element.409), channel_id=1, source_target_pairs={{16,0},{24,8},{0,16},{8,24},{17,1},{25,9},{1,17},{9,25},{18,2},{26... | collective-permute-start | bytes 1119752 | tf_op jit(solution)/shard_map/grad_exchange_uyc2/ppermute | solution.py:816
  433.2 18.1 %collective-permute-start.91 = (bf16[216,864]{1,0:T(8,128)(2,1)S(1)}, bf16[216,864]{1,0:T(8,128)(2,1)S(1)}, u32[]{:S(2)}, u32[]{:S(2)}) collective-permute-start(bf16[216,864]{1,0:T(8,128)(2,1)S(1)} %get-tuple-element.408), channel_id=1, source_target_pairs={{24,0},{0,8},{8,16},{16,24},{25,1},{1,9},{9,17},{17,25},{26,2},{2,... | collective-permute-start | bytes 1119752 | tf_op jit(solution)/shard_map/grad_exchange_uyc3/ppermute | solution.py:816
  435.2 21.6 %collective-permute-start.88 = (bf16[736,128]{1,0:T(8,128)(2,1)S(1)}, bf16[736,128]{1,0:T(8,128)(2,1)S(1)}, u32[]{:S(2)}, u32[]{:S(2)}) collective-permute-start(bf16[736,128]{1,0:T(8,128)(2,1)S(1)} %pad_maximum_fusion.15), channel_id=1, source_target_pairs={{2,0},{4,2},{6,4},{0,6},{3,1},{5,3},{7,5},{1,7},{10,8},{12,10},{14... | collective-permute-start | bytes 565256 | tf_op jit(solution)/shard_map/attn_grad_sum_z1/ppermute | solution.py:816
  438.2 18.6 %collective-permute-start.86 = (bf16[736,128]{1,0:T(8,128)(2,1)S(1)}, bf16[736,128]{1,0:T(8,128)(2,1)S(1)}, u32[]{:S(2)}, u32[]{:S(2)}) collective-permute-start(bf16[736,128]{1,0:T(8,128)(2,1)S(1)} %pad_maximum_fusion.14), channel_id=1, source_target_pairs={{6,0},{0,2},{2,4},{4,6},{7,1},{1,3},{3,5},{5,7},{14,8},{8,10},{10,... | collective-permute-start | bytes 565256 | tf_op jit(solution)/shard_map/attn_grad_sum_z-1/ppermute | solution.py:816
  (143 other events, 1620.2 us)

commit v6 on v5

--- a/solution.py
+++ b/solution.py
@@ -192,7 +192,7 @@
         + [((tok_rows, (H + 1) * HD), f32)],
         [
             pltpu.VMEM((flat.devices, flat.rows, LANES), bf16),
-            pltpu.VMEM((blocks * flat.lines, LANES), f32),
+            pltpu.VMEM((blocks * flat.lines + 16, LANES), f32),
             pltpu.VMEM((-(-(flat.gain_lines + 3) // 8) * 8, LANES), f32),
             pltpu.SemaphoreType.DMA((flat.devices,)),
         ],
@@ -224,7 +224,7 @@
         [((H * HD, D), bf16)],
         [
             pltpu.VMEM((flat.devices, flat.rows, LANES), bf16),
-            pltpu.VMEM(((flat.devices - start) * flat.lines, LANES), f32),
+            pltpu.VMEM(((flat.devices - start) * flat.lines + 16, LANES), f32),
             pltpu.SemaphoreType.DMA((flat.devices,)),
         ],
     )[0]
@@ -414,30 +414,31 @@
             dq_ref[...] = dq_ref[...] * SCORE_SCALE
 
     block = pl.BlockSpec((1, rows, 2 * HD), lambda i, info: (i, 0, 0))
+    resident = pl.BlockSpec(memory_space=pltpu.VMEM)
     return pl.pallas_call(
         body,
         grid_spec=pltpu.PrefetchScalarGridSpec(
             num_scalar_prefetch=1,
             grid=(blocks,),
             in_specs=[
-                same((rows, H * HD)),
+                resident,
                 block,
                 pl.BlockSpec((rows, 1), lambda i, info: (info[0, i], 0)),
-                same((1, rows)),
-                same((rows, H * HD)),
-                same((8, rows)),
-                *[same((rows, D))] * (terms + 3),
-                same((H * HD, D)),
-                same((1, D)),
-                same((1, D)),
+                resident,
+                resident,
+                resident,
+                *[resident] * (terms + 3),
+                resident,
+                resident,
+                resident,
             ],
             out_specs=[
-                same((rows, H * HD)),
-                same((rows, D)),
-                same((rows, D)),
-                same((1, D)),
-                same((1, D)),
-                *[same((rows, 2 * HD))] * blocks,
+                resident,
+                resident,
+                resident,
+                resident,
+                resident,
+                *[resident] * blocks,
             ],
             scratch_shapes=[pltpu.VMEM((rows, H * HD), bf16), pltpu.VMEM((8, rows), f32)],
         ),
@@ -449,7 +450,7 @@
             jax.ShapeDtypeStruct((1, D), f32),
             *[jax.ShapeDtypeStruct((rows, 2 * HD), bf16)] * blocks,
         ),
-        compiler_params=pltpu.CompilerParams(vmem_limit_bytes=VMEM_LIMIT),
+        compiler_params=pltpu.CompilerParams(vmem_limit_bytes=44 * 1024 * 1024),
         cost_estimate=pl.CostEstimate(flops=0, bytes_accessed=0, transcendentals=0),
         name="attend_back",
     )(
@@ -575,7 +576,7 @@
             pltpu.SemaphoreType.DMA((count,)),
             pltpu.SemaphoreType.DMA((3 * blocks,)),
         ],
-        compiler_params=pltpu.CompilerParams(vmem_limit_bytes=VMEM_LIMIT),
+        compiler_params=pltpu.CompilerParams(vmem_limit_bytes={"ffn_forward": 46, "ffn_backward": 46}[name] * 1024 * 1024),
         cost_estimate=pl.CostEstimate(
             flops=6 * count * tok * per * D, bytes_accessed=0, transcendentals=0
         ),
@@ -1130,6 +1131,11 @@
                     ways.what = what
                 return beside
 
+            def settle(self, beside):
+                if steps:
+                    self.heard, beside = lax.optimization_barrier((self.heard, beside))
+                return beside
+
             def result(self):
                 if steps:
                     return add_low(self.blocks[0], self.heard)
@@ -1164,8 +1170,7 @@
             info, query, kv_all, key_docs, query_docs, heads, log_total, d_in_parts, middle, attn_out,
             cotangent[0], w_out, g_post, g_fpre,
         )
-        d_kv = rings["up"].step(d_kv)
-        d_kv = down.step(d_kv)
+        d_kv = down.step(rings["up"].settle(d_kv))
         ways.what = "kv_sum"
 
         def across(oz):
@@ -1175,13 +1180,13 @@
         kv_parts = {far: add_low(*across(far))}
         near = {oz: across(oz) for oz in range(nz) if oz != far}
         begun = ways.z_scatter_begin(kv_parts[far])
-        near, begun = rings["gate"].step(lax.optimization_barrier((near, begun)))
+        near, begun = lax.optimization_barrier((near, begun))
         kv_parts.update({oz: add_low(*terms) for oz, terms in near.items()})
         kv_parts = [kv_parts[0], *ways.z_scatter_go(kv_parts, begun)]
-        kv_parts = rings["up"].step(kv_parts)
         lines, da_query, d_gq = query_side(
             flat, after(d_query, *near[0]), raw, cosine, sine, g_q, normed_in, w_qkv, heads, d_attn_out
         )
+        da_query = rings["up"].step(rings["gate"].step(da_query))
         input_grad, *packed = last_part(
             flat, order, len(places) * nc, lines, kv_parts, raw, cosine, sine, g_k, normed_in, w_qkv, tokens[0],
             g_pre, d_middle, da_query, [d_gq, d_gpost, d_gfpre, d_gfpost],
@@ -1189,7 +1194,9 @@
 
         ways.what = "attn_grad_sum"
         packed = [part.reshape(-1, LANES) for part in packed]
-        terms = ways.plane_scatter({p: packed[i * nc : (i + 1) * nc] for i, p in enumerate(places)})
+        terms = ways.plane_scatter(
+            {p: packed[i * nc : (i + 1) * nc] for i, p in enumerate(places)}, rings["up"].step
+        )
         owned = [rings["gate"].result(), rings["up"].result(), down.result()]
         own_rows = jnp.concatenate([v[:share] for v in owned], axis=1)
         by_cols = jnp.stack([own_rows[:, i * width : (i + 1) * width] for i in range(ns)])

time: 466 us -> 457 us (0.981)
  waiting for transfers between devices: 196 us -> 187 us
  Pallas kernels: 124 us -> 118 us
    ppermute x92, waiting for transfers between devices: 196 us -> 187 us  [fro(): return lax.ppermute(value, axis, [((i + offset) % n, i) for i in range(n)])]
    unnamed x205 -> x167, local copies, waits for them, and re-layouts: 9.29 us -> 11.4 us
  transfers between devices with their start and end apart: 92 -> 92, of which waited for: 48 -> 44; matrix products, arithmetic and copies ran while one was open for 5% -> 5% of each run, Pallas kernels for 20% -> 19%
where the time goes in v6:
time: 457 us; the launch traced here: 450 us
  waiting for transfers between devices  187 us (41%)
  Pallas kernels  118 us (26%)
  starting transfers between devices  98.5 us (22%)
  local copies, waits for them, and re-layouts  22.5 us (5%)
  other arithmetic  20.8 us (5%)
    ppermute x92, waiting for transfers between devices, fro(): return lax.ppermute(value, axis, [((i + offset) % n, i) for i in range(n)])  187 us
    ppermute x92, starting transfers between devices, fro(): return lax.ppermute(value, axis, [((i + offset) % n, i) for i in range(n)])  98.5 us
    pallas_call x2, Pallas kernels, ffn_call(): pl.pallas_call(kernel, grid=(chunks,), in_specs=[anywhere] * count + [chu...  47 us
    pallas_call x5, Pallas kernels, run(): pl.pallas_call(body, out_shape=tuple((jax.ShapeDtypeStruct(s, d) for s, d...  38.8 us
    pallas_call x3, Pallas kernels, unit_grads(): pl.pallas_call(body, grid=(1,), in_specs=[pl.BlockSpec((tokens, both), la...  18.9 us
    unnamed x167, local copies, waits for them, and re-layouts  11.4 us
    pallas_call x1, Pallas kernels, attend_back(): pl.pallas_call(body, grid_spec=pltpu.PrefetchScalarGridSpec(num_scalar_pr...  10.3 us
  transfers between devices with their start and end apart: 92, of which 44 were waited for; matrix products, arithmetic and copies ran while one was open for 5% of the time, Pallas kernels for 19%

profile of v6, /device:TPU:0, one launch (start us, length us, event | category | flops | bytes accessed | tf_op | source)
XLA Modules:
  0.0 449.6 jit_solution(9902814823326618649)
XLA Ops:
  4.3 5.0 %collective-permute-start = (bf16[736,128]{1,0:T(8,128)(2,1)S(1)}, bf16[736,128]{1,0:T(8,128)(2,1)S(1)}, u32[]{:S(2)}, u32[]{:S(2)}) collective-permute-start(bf16[736,128]{1,0:T(8,128)(2,1)S(1)} %pad_maximum_fusion.12), channel_id=1, source_target_pairs={{2,0},{4,2},{6,4},{0,6},{3,1},{5,3},{7,5},{1,7},{10,8},{12,10},{14... | collective-permute-start | bytes 565256 | tf_op jit(solution)/shard_map/attn_gather_z1/ppermute | solution.py:817
  11.1 3.4 collective-permute-done
  14.5 4.3 collective-permute-start.1
  21.1 4.3 collective-permute-done.3
  25.4 3.7 collective-permute-done.5
  35.0 3.5 collective-permute-start.15
  38.5 11.3 %collective-permute-done.10 = bf16[2944,128]{1,0:T(8,128)(2,1)S(1)} collective-permute-done((bf16[2944,128]{1,0:T(8,128)(2,1)S(1)}, bf16[2944,128]{1,0:T(8,128)(2,1)S(1)}, u32[]{:S(2)}, u32[]{:S(2)}) %collective-permute-start.10) | collective-permute-done | bytes 753696 | tf_op jit(solution)/shard_map/attn_gather_x1/ppermute | solution.py:817
  54.8 4.7 %collective-permute-done.12 = bf16[1472,128]{1,0:T(8,128)(2,1)S(1)} collective-permute-done((bf16[1472,128]{1,0:T(8,128)(2,1)}, bf16[1472,128]{1,0:T(8,128)(2,1)S(1)}, u32[]{:S(2)}, u32[]{:S(2)}) %collective-permute-start.12) | collective-permute-done | bytes 376864 | tf_op jit(solution)/shard_map/attn_gather_y1/ppermute | solution.py:817
  63.9 6.5 %collective-permute-done.15.refs_9_.refs_11_ = bf16[224,3456]{1,0:T(8,128)(2,1)} collective-permute-done((bf16[224,3456]{1,0:T(8,128)(2,1)}, bf16[224,3456]{1,0:T(8,128)(2,1)}, u32[]{:S(2)}, u32[]{:S(2)}) %collective-permute-start.15) | collective-permute-done | bytes 1548320 | tf_op jit(solution)/shard_map/unit_gather_z1/ppermute | solution.py:817
  72.1 4.3 collective-permute-start.18
  76.5 8.9 %first_part.1 = (bf16[1152,1536]{1,0:T(8,128)(2,1)}, f32[1,1152]{1,0:T(1,128)}, f32[1,256]{1,0:T(1,128)}, f32[1,256]{1,0:T(1,128)}, f32[1,1152]{1,0:T(1,128)}, /...) custom-call(s32[32]{0:T(128)} %fusion.11.order_ref, ...), custom_call_target="tpu_custom_call" | custom-call | flops 7247757312 | tf_op jit(solution)/shard_map/first_part/pallas_call | solution.py:90
  89.5 5.9 %spread_out.1.w_ref.refs_6_ = bf16[1024,1152]{1,0:T(8,128)(2,1)} custom-call(s32[32]{0:T(128)} %fusion.11.order_ref, bf16[4,736,128]{2,1,0:T(8,128)(2,1)} %bitcast.118, bf16[4,736,128]{2,1,0:T(8,128)(2,1)} %bitcast.126, bf16[4,736,128]{2,1,0:T(8,128)(2,1)} %bitcast.122, bf16[4,736,128]{2,1,0:T(8,128)(2,1)} %bitcast.128, bf16[4,736,128]{2,1,0:T(8,128)(2,1)} %bitcast.120, ...), custom_call_target="tpu_custom_call" | custom-call | tf_op jit(solution)/shard_map/spread_out/pallas_call | solution.py:90
  95.3 3.7 collective-permute-done.16
  99.1 3.4 collective-permute-done.17
  104.6 3.5 collective-permute-start.22
  108.3 3.9 collective-permute-start.19
  112.1 4.3 collective-permute-done.23
  117.6 5.3 %collective-permute-done.24 = bf16[256,512]{1,0:T(8,128)(2,1)S(1)} collective-permute-done((bf16[256,512]{1,0:T(8,128)(2,1)S(1)}, bf16[256,512]{1,0:T(8,128)(2,1)S(1)}, u32[]{:S(2)}, u32[]{:S(2)}) %collective-permute-start.24) | collective-permute-done | bytes 262176 | tf_op jit(solution)/shard_map/kv_gather_vx1/ppermute | solution.py:817
  123.0 3.2 attend.1
  127.3 4.2 collective-permute-done.19.refs_11_.refs_13_
  132.7 5.1 %collective-permute-start.34 = (bf16[112,3456]{1,0:T(8,128)(2,1)S(1)}, bf16[112,3456]{1,0:T(8,128)(2,1)S(1)}, u32[]{:S(2)}, u32[]{:S(2)}) collective-permute-start(bf16[112,3456]{1,0:T(8,128)(2,1)S(1)} %collective-permute-done.19.refs_11_.refs_13_), channel_id=1, source_target_pairs={{2,0},{4,2},{6,4},{0,6},{3,1},{5,3},{7,5},{1,7},{10,8},{12,10},{14... | collective-permute-start | bytes 2322440 | tf_op jit(solution)/shard_map/unit_gather_z1/ppermute | solution.py:817
  137.8 10.4 %collective-permute-done.28.refs_12_.refs_14_ = bf16[112,3456]{1,0:T(8,128)(2,1)S(1)} collective-permute-done((bf16[112,3456]{1,0:T(8,128)(2,1)}, bf16[112,3456]{1,0:T(8,128)(2,1)S(1)}, u32[]{:S(2)}, u32[]{:S(2)}) %collective-permute-start.28) | collective-permute-done | bytes 774176 | tf_op jit(solution)/shard_map/unit_gather_z1/ppermute | solution.py:817
  151.0 12.0 %collective-permute-done.34.refs_13_.refs_15_ = bf16[112,3456]{1,0:T(8,128)(2,1)S(1)} collective-permute-done((bf16[112,3456]{1,0:T(8,128)(2,1)S(1)}, bf16[112,3456]{1,0:T(8,128)(2,1)S(1)}, u32[]{:S(2)}, u32[]{:S(2)}) %collective-permute-start.34) | collective-permute-done | bytes 774176 | tf_op jit(solution)/shard_map/unit_gather_z1/ppermute | solution.py:817
  166.7 23.8 %ffn_forward.1 = (bf16[2048,896]{1,0:T(8,128)(2,1)}, bf16[2048,896]{1,0:T(8,128)(2,1)}, bf16[2048,896]{1,0:T(8,128)(2,1)}, bf16[256,1152]{1,0:T(8,128)(2,1)S(1)}...) custom-call(bf16[256,1152]{1,0:T(8,128)(2,1)S(1)} %get-tuple-element, ...), custom_call_target="tpu_custom_call" | custom-call | flops 12683575296 | tf_op jit(solution)/shard_map/ffn_forward/pallas_call | solution.py:560
  195.4 7.4 %collective-permute-done.42 = bf16[128,1152]{1,0:T(8,128)(2,1)S(1)} collective-permute-done((bf16[128,1152]{1,0:T(8,128)(2,1)S(1)}, bf16[128,1152]{1,0:T(8,128)(2,1)S(1)}, u32[]{:S(2)}, u32[]{:S(2)}) %collective-permute-start.42) | collective-permute-done | bytes 294944 | tf_op jit(solution)/shard_map/ffn_out_sum_x-1/ppermute | solution.py:817
  205.1 12.4 %collective-permute-done.43.refs_2_ = bf16[256,1152]{1,0:T(8,128)(2,1)S(1)} collective-permute-done((bf16[256,1152]{1,0:T(8,128)(2,1)S(1)}, bf16[256,1152]{1,0:T(8,128)(2,1)S(1)}, u32[]{:S(2)}, u32[]{:S(2)}) %collective-permute-start.43) | collective-permute-done | bytes 589856 | tf_op jit(solution)/shard_map/ffn_out_sum_y-1/ppermute | solution.py:817
  221.5 11.9 %collective-permute-done.47.refs_4_ = bf16[256,1152]{1,0:T(8,128)(2,1)S(1)} collective-permute-done((bf16[256,1152]{1,0:T(8,128)(2,1)S(1)}, bf16[256,1152]{1,0:T(8,128)(2,1)S(1)}, u32[]{:S(2)}, u32[]{:S(2)}) %collective-permute-start.47) | collective-permute-done | bytes 589856 | tf_op jit(solution)/shard_map/d_out_gather_x1/ppermute | solution.py:817
  237.0 3.2 collective-permute-done.49
  245.6 6.1 %unit_grads.3 = (bf16[224,1152]{1,0:T(8,128)(2,1)S(1)}, bf16[224,1152]{1,0:T(8,128)(2,1)S(1)}, bf16[224,1152]{1,0:T(8,128)(2,1)S(1)}, bf16[224,1152]{1,0:T(8,128)(2,1)S(1)}) custom-call(bf16[2048,896]{1,0:T(8,128)(2,1)S(1)} %copy-done.34, bf16[256,1152]{1,0:T(8,128)(2,1)S(1)} %get-tuple-element.266.refs_0_, ...), custom_call_target="tpu_custom_call" | custom-call | flops 4227858432 | tf_op jit(solution)/shard_map/unit_grads/pallas_call | solution.py:637
  252.6 23.2 %ffn_backward.1 = (bf16[2048,1792]{1,0:T(8,128)(2,1)}, bf16[256,1152]{1,0:T(8,128)(2,1)S(1)}, bf16[256,1152]{1,0:T(8,128)(2,1)}, bf16[256,1152]{1,0:T(8,128)(2,1...) custom-call(bf16[256,1152]{1,0:T(8,128)(2,1)S(1)} %get-tuple-element, ...), custom_call_target="tpu_custom_call" | custom-call | flops 12683575296 | tf_op jit(solution)/shard_map/ffn_backward/pallas_call | solution.py:560
  286.7 6.5 %unit_grads.4 = (bf16[224,1152]{1,0:T(8,128)(2,1)S(1)}, bf16[224,1152]{1,0:T(8,128)(2,1)S(1)}, bf16[224,1152]{1,0:T(8,128)(2,1)S(1)}, bf16[224,1152]{1,0:T(8,128)(2,1)S(1)}) custom-call(bf16[2048,1792]{1,0:T(8,128)(2,1)S(1)} %copy-done.33, bf16[256,1152]{1,0:T(8,128)(2,1)S(1)} %copy-done.23, bf16[256,1152]{1,0:T(8,128)(2,1)S(1)} %copy-done.29, ...), custom_call_target="tpu_custom_call" | custom-call | flops 4227858432 | tf_op jit(solution)/shard_map/unit_grads/pallas_call | solution.py:637
  298.1 6.3 %unit_grads.5 = (bf16[224,1152]{1,0:T(8,128)(2,1)S(1)}, bf16[224,1152]{1,0:T(8,128)(2,1)S(1)}, bf16[224,1152]{1,0:T(8,128)(2,1)S(1)}, bf16[224,1152]{1,0:T(8,128)(2,1)S(1)}) custom-call(bf16[2048,1792]{1,0:T(8,128)(2,1)S(1)} %copy-done.33, bf16[256,1152]{1,0:T(8,128)(2,1)S(1)} %copy-done.23, bf16[256,1152]{1,0:T(8,128)(2,1)S(1)} %copy-done.29, ...), custom_call_target="tpu_custom_call" | custom-call | flops 4227858432 | tf_op jit(solution)/shard_map/unit_grads/pallas_call | solution.py:637
  311.4 10.3 %attend_back.1 = (f32[256,1024]{1,0:T(8,128)S(1)}, bf16[256,1152]{1,0:T(8,128)(2,1)S(1)}, f32[256,1152]{1,0:T(8,128)S(1)}, f32[1,1152]{1,0:T(1,128)S(1)}, f32[1,...) custom-call(s32[2,8]{1,0:T(2,128)S(1)} %pad_add_fusion.info_ref, ...), custom_call_target="tpu_custom_call" | custom-call | tf_op jit(solution)/shard_map/attend_back/pallas_call | solution.py:418
  321.8 8.7 %collective-permute-done.63 = bf16[224,1152]{1,0:T(8,128)(2,1)S(1)} collective-permute-done((bf16[224,1152]{1,0:T(8,128)(2,1)S(1)}, bf16[224,1152]{1,0:T(8,128)(2,1)S(1)}, u32[]{:S(2)}, u32[]{:S(2)}) %collective-permute-start.63) | collective-permute-done | bytes 516128 | tf_op jit(solution)/shard_map/down_grad_sum_z-1/ppermute | solution.py:817
  336.1 3.7 collective-permute-done.68
  340.4 3.3 collective-permute-start.70
  345.9 5.1 %collective-permute-done.66 = bf16[256,512]{1,0:T(8,128)(2,1)S(1)} collective-permute-done((bf16[256,512]{1,0:T(8,128)(2,1)S(1)}, bf16[256,512]{1,0:T(8,128)(2,1)S(1)}, u32[]{:S(2)}, u32[]{:S(2)}) %collective-permute-start.66) | collective-permute-done | bytes 262176 | tf_op jit(solution)/shard_map/kv_sum_vx-1/ppermute | solution.py:817
  351.0 3.2 collective-permute-done.67
  356.9 10.2 %query_side.1 = (f32[23056,128]{1,0:T(8,128)}, f32[256,1152]{1,0:T(8,128)}, f32[1,256]{1,0:T(1,128)}) custom-call(f32[256,1024]{1,0:T(8,128)} %copy-done.7, f32[256,1280]{1,0:T(8,128)} %get-tuple-element.329.raw_ref.refs_3_, f32[256,128]{1,0:T(8,128)} %get-tuple-element.425.refs_9_.cos_ref.refs_4_, f32[256,128]{1,0:T(8,128)} %get-tuple-element.424.refs_10_.sin_ref.refs_5_, ...), custom_call_target="tpu_custom_call" | custom-call | tf_op jit(solution)/shard_map/query_side/pallas_call | solution.py:90
  371.8 12.4 %last_part.1 = (bf16[256,1152]{1,0:T(8,128)(2,1)}, bf16[4,736,128]{2,1,0:T(8,128)(2,1)}, bf16[4,736,128]{2,1,0:T(8,128)(2,1)}, bf16[4,736,128]{2,1,0:T(8,128)(2,...) custom-call(s32[32]{0:T(128)} %fusion.11.order_ref, ...), custom_call_target="tpu_custom_call" | custom-call | tf_op jit(solution)/shard_map/last_part/pallas_call | solution.py:90
  387.0 5.3 %collective-permute-done.76 = bf16[224,1152]{1,0:T(8,128)(2,1)S(1)} collective-permute-done((bf16[224,1152]{1,0:T(8,128)(2,1)S(1)}, bf16[224,1152]{1,0:T(8,128)(2,1)S(1)}, u32[]{:S(2)}, u32[]{:S(2)}) %collective-permute-start.76) | collective-permute-done | bytes 516128 | tf_op jit(solution)/shard_map/up_grad_sum_z-1/ppermute | solution.py:817
  395.8 4.5 %collective-permute-done.81 = bf16[1472,128]{1,0:T(8,128)(2,1)S(1)} collective-permute-done((bf16[1472,128]{1,0:T(8,128)(2,1)S(1)}, bf16[1472,128]{1,0:T(8,128)(2,1)S(1)}, u32[]{:S(2)}, u32[]{:S(2)}) %collective-permute-start.81) | collective-permute-done | bytes 376864 | tf_op jit(solution)/shard_map/attn_grad_sum_x-1/ppermute | solution.py:817
  402.0 3.1 collective-permute-done.78
  407.0 11.3 %collective-permute-done.82 = bf16[2944,128]{1,0:T(8,128)(2,1)S(1)} collective-permute-done((bf16[2944,128]{1,0:T(8,128)(2,1)S(1)}, bf16[2944,128]{1,0:T(8,128)(2,1)S(1)}, u32[]{:S(2)}, u32[]{:S(2)}) %collective-permute-start.82) | collective-permute-done | bytes 753696 | tf_op jit(solution)/shard_map/attn_grad_sum_y-1/ppermute | solution.py:817
  419.2 3.3 collective-permute-start.87
  425.3 3.7 collective-permute-start.88
  432.1 8.9 %collective-permute-done.90 = bf16[216,864]{1,0:T(8,128)(2,1)S(1)} collective-permute-done((bf16[216,864]{1,0:T(8,128)(2,1)S(1)}, bf16[216,864]{1,0:T(8,128)(2,1)S(1)}, u32[]{:S(2)}, u32[]{:S(2)}) %collective-permute-start.90) | collective-permute-done | bytes 373280 | tf_op jit(solution)/shard_map/grad_exchange_uyc2/ppermute | solution.py:817
  441.9 5.5 %multiply_subtract_fusion = (f32[864,864]{1,0:T(8,128)}, f32[864,864]{1,0:T(8,128)}, f32[864,864]{1,0:T(8,128)}, f32[864,864]{1,0:T(8,128)}) fusion(f32[864,864]{1,0:T(8,128)S(1)} %copy-done.35, f32[864,864]{1,0:T(8,128)S(1)} %copy-done.38, f32[864,864]{1,0:T(8,128)S(1)} %copy-done.39, bf16[4,216,864]{2,1,0:T(8,128)(2,1)S(1)} %bitcast_dynamic-update-slice_fusion), kind=kLoop, calls=%fused_computation.3 | loop fusion | flops 11197440 | bytes 22394880 | tf_op jit(solution)/shard_map/sub | solution.py:65
  (438 shorter events, 118.4 us)
Async XLA Ops:
  9.3 16.1 %collective-permute-start.4 = (bf16[216,864]{1,0:T(8,128)(2,1)}, bf16[216,864]{1,0:T(8,128)(2,1)S(1)}, u32[]{:S(2)}, u32[]{:S(2)}) collective-permute-start(bf16[216,864]{1,0:T(8,128)(2,1)} %get-tuple-element.199), channel_id=1, source_target_pairs={{8,0},{16,8},{24,16},{0,24},{9,1},{17,9},{25,17},{1,25},{10,2},{18... | collective-permute-start | bytes 1119752 | tf_op jit(solution)/shard_map/unit_exchange_uyc1/ppermute | solution.py:817
  10.0 19.1 %collective-permute-start.5 = (bf16[216,864]{1,0:T(8,128)(2,1)}, bf16[216,864]{1,0:T(8,128)(2,1)S(1)}, u32[]{:S(2)}, u32[]{:S(2)}) collective-permute-start(bf16[216,864]{1,0:T(8,128)(2,1)} %get-tuple-element.200), channel_id=1, source_target_pairs={{16,0},{24,8},{0,16},{8,24},{17,1},{25,9},{1,17},{9,25},{18,2},{26... | collective-permute-start | bytes 1119752 | tf_op jit(solution)/shard_map/unit_exchange_uyc2/ppermute | solution.py:817
  10.8 18.3 %collective-permute-start.6 = (bf16[216,864]{1,0:T(8,128)(2,1)S(1)}, bf16[216,864]{1,0:T(8,128)(2,1)S(1)}, u32[]{:S(2)}, u32[]{:S(2)}) collective-permute-start(bf16[216,864]{1,0:T(8,128)(2,1)S(1)} %get-tuple-element.201), channel_id=1, source_target_pairs={{24,0},{0,8},{8,16},{16,24},{25,1},{1,9},{9,17},{17,25},{26,2},{2,... | collective-permute-start | bytes 1119752 | tf_op jit(solution)/shard_map/unit_exchange_uyc3/ppermute | solution.py:817
  32.2 17.6 %collective-permute-start.10 = (bf16[2944,128]{1,0:T(8,128)(2,1)S(1)}, bf16[2944,128]{1,0:T(8,128)(2,1)S(1)}, u32[]{:S(2)}, u32[]{:S(2)}) collective-permute-start(bf16[2944,128]{1,0:T(8,128)(2,1)S(1)} %pad_maximum_fusion.1), channel_id=1, source_target_pairs={{1,0},{0,1},{3,2},{2,3},{5,4},{4,5},{7,6},{6,7},{9,8},{8,9},{11,10... | collective-permute-start | bytes 2261000 | tf_op jit(solution)/shard_map/attn_gather_x1/ppermute | solution.py:817
  33.8 17.8 %collective-permute-start.8 = (bf16[2944,128]{1,0:T(8,128)(2,1)S(1)}, bf16[2944,128]{1,0:T(8,128)(2,1)S(1)}, u32[]{:S(2)}, u32[]{:S(2)}) collective-permute-start(bf16[2944,128]{1,0:T(8,128)(2,1)S(1)} %pad_maximum_fusion.1), channel_id=1, source_target_pairs={{16,0},{0,16},{17,1},{1,17},{18,2},{2,18},{19,3},{3,19},{20,4},{4,... | collective-permute-start | bytes 2261000 | tf_op jit(solution)/shard_map/attn_gather_y1/ppermute | solution.py:817
  35.0 35.4 %collective-permute-start.15 = (bf16[224,3456]{1,0:T(8,128)(2,1)}, bf16[224,3456]{1,0:T(8,128)(2,1)}, u32[]{:S(2)}, u32[]{:S(2)}) collective-permute-start(bf16[224,3456]{1,0:T(8,128)(2,1)} %pad.4.refs_8_.refs_10_), channel_id=1, source_target_pairs={{2,0},{4,2},{6,4},{0,6},{3,1},{5,3},{7,5},{1,7},{10,8},{12,10},{14... | collective-permute-start | bytes 4644872 | tf_op jit(solution)/shard_map/unit_gather_z1/ppermute | solution.py:817
  72.1 30.3 %collective-permute-start.18 = (bf16[112,3456]{1,0:T(8,128)(2,1)S(1)}, bf16[112,3456]{1,0:T(8,128)(2,1)}, u32[]{:S(2)}, u32[]{:S(2)}) collective-permute-start(bf16[112,3456]{1,0:T(8,128)(2,1)S(1)} %get-tuple-element.398), channel_id=1, source_target_pairs={{2,0},{4,2},{6,4},{0,6},{3,1},{5,3},{7,5},{1,7},{10,8},{12,10},{14... | collective-permute-start | bytes 2322440 | tf_op jit(solution)/shard_map/unit_gather_z1/ppermute | solution.py:817
  86.5 16.0 %collective-permute-start.17 = (bf16[256,512]{1,0:T(8,128)(2,1)}, bf16[256,512]{1,0:T(8,128)(2,1)S(1)}, u32[]{:S(2)}, u32[]{:S(2)}) collective-permute-start(bf16[256,512]{1,0:T(8,128)(2,1)} %get-tuple-element.221), channel_id=1, source_target_pairs={{6,0},{0,2},{2,4},{4,6},{7,1},{1,3},{3,5},{5,7},{14,8},{8,10},{10,... | collective-permute-start | bytes 786440 | tf_op jit(solution)/shard_map/kv_gather_z-1/ppermute | solution.py:817
  102.5 15.0 %collective-permute-start.21 = (bf16[256,512]{1,0:T(8,128)(2,1)S(1)}, bf16[256,512]{1,0:T(8,128)(2,1)S(1)}, u32[]{:S(2)}, u32[]{:S(2)}) collective-permute-start(bf16[256,512]{1,0:T(8,128)(2,1)S(1)} %collective-permute-done.16), channel_id=1, source_target_pairs={{1,0},{0,1},{3,2},{2,3},{5,4},{4,5},{7,6},{6,7},{9,8},{8,9},{11,10... | collective-permute-start | bytes 786440 | tf_op jit(solution)/shard_map/kv_gather_vx1/ppermute | solution.py:817
  103.1 19.9 %collective-permute-start.25 = (bf16[256,512]{1,0:T(8,128)(2,1)S(1)}, bf16[256,512]{1,0:T(8,128)(2,1)S(1)}, u32[]{:S(2)}, u32[]{:S(2)}) collective-permute-start(bf16[256,512]{1,0:T(8,128)(2,1)S(1)} %collective-permute-done.17), channel_id=1, source_target_pairs={{1,0},{0,1},{3,2},{2,3},{5,4},{4,5},{7,6},{6,7},{9,8},{8,9},{11,10... | collective-permute-start | bytes 786440 | tf_op jit(solution)/shard_map/kv_gather_vx1/ppermute | solution.py:817
  108.3 23.3 %collective-permute-start.19 = (bf16[112,3456]{1,0:T(8,128)(2,1)S(1)}, bf16[112,3456]{1,0:T(8,128)(2,1)S(1)}, u32[]{:S(2)}, u32[]{:S(2)}) collective-permute-start(bf16[112,3456]{1,0:T(8,128)(2,1)S(1)} %get-tuple-element.222), channel_id=1, source_target_pairs={{2,0},{4,2},{6,4},{0,6},{3,1},{5,3},{7,5},{1,7},{10,8},{12,10},{14... | collective-permute-start | bytes 2322440 | tf_op jit(solution)/shard_map/unit_gather_z1/ppermute | solution.py:817
  117.1 31.2 %collective-permute-start.28 = (bf16[112,3456]{1,0:T(8,128)(2,1)}, bf16[112,3456]{1,0:T(8,128)(2,1)S(1)}, u32[]{:S(2)}, u32[]{:S(2)}) collective-permute-start(bf16[112,3456]{1,0:T(8,128)(2,1)} %collective-permute-done.18.refs_10_.refs_12_), channel_id=1, source_target_pairs={{2,0},{4,2},{6,4},{0,6},{3,1},{5,3},{7,5},{1,7},{10,8},{12,10},{14... | collective-permute-start | bytes 2322440 | tf_op jit(solution)/shard_map/unit_gather_z1/ppermute | solution.py:817
  131.5 16.7 %collective-permute-start.26 = (bf16[256,1152]{1,0:T(8,128)(2,1)S(1)}, bf16[256,1152]{1,0:T(8,128)(2,1)S(1)}, u32[]{:S(2)}, u32[]{:S(2)}) collective-permute-start(bf16[256,1152]{1,0:T(8,128)(2,1)S(1)} %get-tuple-element.242.refs_0_), channel_id=1, source_target_pairs={{16,0},{0,16},{17,1},{1,17},{18,2},{2,18},{19,3},{3,19},{20,4},{4,... | collective-permute-start | bytes 1769480 | tf_op jit(solution)/shard_map/ffn_in_gather_y1/ppermute | solution.py:817
  132.2 16.1 %collective-permute-start.27 = (bf16[256,1152]{1,0:T(8,128)(2,1)S(1)}, bf16[256,1152]{1,0:T(8,128)(2,1)S(1)}, u32[]{:S(2)}, u32[]{:S(2)}) collective-permute-start(bf16[256,1152]{1,0:T(8,128)(2,1)S(1)} %get-tuple-element.242.refs_0_), channel_id=1, source_target_pairs={{1,0},{0,1},{3,2},{2,3},{5,4},{4,5},{7,6},{6,7},{9,8},{8,9},{11,10... | collective-permute-start | bytes 1769480 | tf_op jit(solution)/shard_map/ffn_in_gather_x1/ppermute | solution.py:817
  132.7 30.3 %collective-permute-start.34 = (bf16[112,3456]{1,0:T(8,128)(2,1)S(1)}, bf16[112,3456]{1,0:T(8,128)(2,1)S(1)}, u32[]{:S(2)}, u32[]{:S(2)}) collective-permute-start(bf16[112,3456]{1,0:T(8,128)(2,1)S(1)} %collective-permute-done.19.refs_11_.refs_13_), channel_id=1, source_target_pairs={{2,0},{4,2},{6,4},{0,6},{3,1},{5,3},{7,5},{1,7},{10,8},{12,10},{14... | collective-permute-start | bytes 2322440 | tf_op jit(solution)/shard_map/unit_gather_z1/ppermute | solution.py:817
  149.2 13.9 %collective-permute-start.32 = (bf16[128,1152]{1,0:T(8,128)(2,1)S(1)}, bf16[128,1152]{1,0:T(8,128)(2,1)S(1)}, u32[]{:S(2)}, u32[]{:S(2)}) collective-permute-start(bf16[128,1152]{1,0:T(8,128)(2,1)S(1)} %slice.209), channel_id=1, source_target_pairs={{16,0},{0,16},{17,1},{1,17},{18,2},{2,18},{19,3},{3,19},{20,4},{4,... | collective-permute-start | bytes 884744 | tf_op jit(solution)/shard_map/ffn_in_gather_y1/ppermute | solution.py:817
  149.9 13.2 %collective-permute-start.33 = (bf16[128,1152]{1,0:T(8,128)(2,1)S(1)}, bf16[128,1152]{1,0:T(8,128)(2,1)S(1)}, u32[]{:S(2)}, u32[]{:S(2)}) collective-permute-start(bf16[128,1152]{1,0:T(8,128)(2,1)S(1)} %slice.210), channel_id=1, source_target_pairs={{1,0},{0,1},{3,2},{2,3},{5,4},{4,5},{7,6},{6,7},{9,8},{8,9},{11,10... | collective-permute-start | bytes 884744 | tf_op jit(solution)/shard_map/ffn_in_gather_x1/ppermute | solution.py:817
  150.5 14.6 %collective-permute-start.30 = (bf16[256,1152]{1,0:T(8,128)(2,1)S(1)}, bf16[256,1152]{1,0:T(8,128)(2,1)S(1)}, u32[]{:S(2)}, u32[]{:S(2)}) collective-permute-start(bf16[256,1152]{1,0:T(8,128)(2,1)S(1)} %collective-permute-done.26.refs_2_), channel_id=1, source_target_pairs={{8,0},{0,8},{9,1},{1,9},{10,2},{2,10},{11,3},{3,11},{12,4},{4,12},... | collective-permute-start | bytes 1769480 | tf_op jit(solution)/shard_map/ffn_in_gather_c1/ppermute | solution.py:817
  150.5 14.6 %collective-permute-start.31 = (bf16[256,1152]{1,0:T(8,128)(2,1)S(1)}, bf16[256,1152]{1,0:T(8,128)(2,1)S(1)}, u32[]{:S(2)}, u32[]{:S(2)}) collective-permute-start(bf16[256,1152]{1,0:T(8,128)(2,1)S(1)} %collective-permute-done.27.refs_4_), channel_id=1, source_target_pairs={{8,0},{0,8},{9,1},{1,9},{10,2},{2,10},{11,3},{3,11},{12,4},{4,12},... | collective-permute-start | bytes 1769480 | tf_op jit(solution)/shard_map/ffn_in_gather_c1/ppermute | solution.py:817
  202.9 14.6 %collective-permute-start.43 = (bf16[256,1152]{1,0:T(8,128)(2,1)S(1)}, bf16[256,1152]{1,0:T(8,128)(2,1)S(1)}, u32[]{:S(2)}, u32[]{:S(2)}) collective-permute-start(bf16[256,1152]{1,0:T(8,128)(2,1)S(1)} %pad_maximum_fusion.5), channel_id=1, source_target_pairs={{16,0},{0,16},{17,1},{1,17},{18,2},{2,18},{19,3},{3,19},{20,4},{4,... | collective-permute-start | bytes 1769480 | tf_op jit(solution)/shard_map/ffn_out_sum_y-1/ppermute | solution.py:817
  203.8 14.6 %collective-permute-start.40 = (bf16[256,1152]{1,0:T(8,128)(2,1)S(1)}, bf16[256,1152]{1,0:T(8,128)(2,1)S(1)}, u32[]{:S(2)}, u32[]{:S(2)}) collective-permute-start(bf16[256,1152]{1,0:T(8,128)(2,1)S(1)} %pad_maximum_fusion.4), channel_id=1, source_target_pairs={{1,0},{0,1},{3,2},{2,3},{5,4},{4,5},{7,6},{6,7},{9,8},{8,9},{11,10... | collective-permute-start | bytes 1769480 | tf_op jit(solution)/shard_map/ffn_out_sum_x-1/ppermute | solution.py:817
  219.8 13.6 %collective-permute-start.47 = (bf16[256,1152]{1,0:T(8,128)(2,1)S(1)}, bf16[256,1152]{1,0:T(8,128)(2,1)S(1)}, u32[]{:S(2)}, u32[]{:S(2)}) collective-permute-start(bf16[256,1152]{1,0:T(8,128)(2,1)S(1)} %get-tuple-element.266.refs_0_), channel_id=1, source_target_pairs={{1,0},{0,1},{3,2},{2,3},{5,4},{4,5},{7,6},{6,7},{9,8},{8,9},{11,10... | collective-permute-start | bytes 1769480 | tf_op jit(solution)/shard_map/d_out_gather_x1/ppermute | solution.py:817
  220.7 13.7 %collective-permute-start.45 = (bf16[256,1152]{1,0:T(8,128)(2,1)S(1)}, bf16[256,1152]{1,0:T(8,128)(2,1)S(1)}, u32[]{:S(2)}, u32[]{:S(2)}) collective-permute-start(bf16[256,1152]{1,0:T(8,128)(2,1)S(1)} %get-tuple-element.266.refs_0_), channel_id=1, source_target_pairs={{16,0},{0,16},{17,1},{1,17},{18,2},{2,18},{19,3},{3,19},{20,4},{4,... | collective-permute-start | bytes 1769480 | tf_op jit(solution)/shard_map/d_out_gather_y1/ppermute | solution.py:817
  251.8 24.7 %collective-permute-start.52 = (bf16[224,1152]{1,0:T(8,128)(2,1)S(1)}, bf16[224,1152]{1,0:T(8,128)(2,1)S(1)}, u32[]{:S(2)}, u32[]{:S(2)}) collective-permute-start(bf16[224,1152]{1,0:T(8,128)(2,1)S(1)} %get-tuple-element.270), channel_id=1, source_target_pairs={{6,0},{0,2},{2,4},{4,6},{7,1},{1,3},{3,5},{5,7},{14,8},{8,10},{10,... | collective-permute-start | bytes 1548296 | tf_op jit(solution)/shard_map/down_grad_sum_z-1/ppermute | solution.py:817
  276.4 32.1 %collective-permute-start.55 = (bf16[256,1152]{1,0:T(8,128)(2,1)}, bf16[256,1152]{1,0:T(8,128)(2,1)S(1)}, u32[]{:S(2)}, u32[]{:S(2)}) collective-permute-start(bf16[256,1152]{1,0:T(8,128)(2,1)} %get-tuple-element.277), channel_id=1, source_target_pairs={{8,0},{0,8},{9,1},{1,9},{10,2},{2,10},{11,3},{3,11},{12,4},{4,12},... | collective-permute-start | bytes 1769480 | tf_op jit(solution)/shard_map/d_in_sum_c1/ppermute | solution.py:817
  277.0 19.2 %collective-permute-start.56 = (bf16[224,1152]{1,0:T(8,128)(2,1)S(1)}, bf16[224,1152]{1,0:T(8,128)(2,1)S(1)}, u32[]{:S(2)}, u32[]{:S(2)}) collective-permute-start(bf16[224,1152]{1,0:T(8,128)(2,1)S(1)} %add_convert_fusion.16), channel_id=1, source_target_pairs={{6,0},{0,2},{2,4},{4,6},{7,1},{1,3},{3,5},{5,7},{14,8},{8,10},{10,... | collective-permute-start | bytes 1548296 | tf_op jit(solution)/shard_map/down_grad_sum_z-1/ppermute | solution.py:817
  280.6 14.5 %collective-permute-start.60 = (bf16[128,1152]{1,0:T(8,128)(2,1)S(1)}, bf16[128,1152]{1,0:T(8,128)(2,1)S(1)}, u32[]{:S(2)}, u32[]{:S(2)}) collective-permute-start(bf16[128,1152]{1,0:T(8,128)(2,1)S(1)} %get-tuple-element.416), channel_id=1, source_target_pairs={{1,0},{0,1},{3,2},{2,3},{5,4},{4,5},{7,6},{6,7},{9,8},{8,9},{11,10... | collective-permute-start | bytes 884744 | tf_op jit(solution)/shard_map/d_in_sum_x-1/ppermute | solution.py:817
  293.2 18.2 %collective-permute-start.54 = (bf16[224,1152]{1,0:T(8,128)(2,1)S(1)}, bf16[224,1152]{1,0:T(8,128)(2,1)}, u32[]{:S(2)}, u32[]{:S(2)}) collective-permute-start(bf16[224,1152]{1,0:T(8,128)(2,1)S(1)} %get-tuple-element.275), channel_id=1, source_target_pairs={{6,0},{0,2},{2,4},{4,6},{7,1},{1,3},{3,5},{5,7},{14,8},{8,10},{10,... | collective-permute-start | bytes 1548296 | tf_op jit(solution)/shard_map/gate_grad_sum_z-1/ppermute | solution.py:817
  296.2 14.6 %collective-permute-start.61 = (bf16[256,1152]{1,0:T(8,128)(2,1)}, bf16[256,1152]{1,0:T(8,128)(2,1)S(1)}, u32[]{:S(2)}, u32[]{:S(2)}) collective-permute-start(bf16[256,1152]{1,0:T(8,128)(2,1)} %pad_maximum_fusion.6), channel_id=1, source_target_pairs={{1,0},{0,1},{3,2},{2,3},{5,4},{4,5},{7,6},{6,7},{9,8},{8,9},{11,10... | collective-permute-start | bytes 1769480 | tf_op jit(solution)/shard_map/d_in_sum_x-1/ppermute | solution.py:817
  297.0 14.4 %collective-permute-start.62 = (bf16[256,1152]{1,0:T(8,128)(2,1)S(1)}, bf16[256,1152]{1,0:T(8,128)(2,1)S(1)}, u32[]{:S(2)}, u32[]{:S(2)}) collective-permute-start(bf16[256,1152]{1,0:T(8,128)(2,1)S(1)} %pad_maximum_fusion.7), channel_id=1, source_target_pairs={{16,0},{0,16},{17,1},{1,17},{18,2},{2,18},{19,3},{3,19},{20,4},{4,... | collective-permute-start | bytes 1769480 | tf_op jit(solution)/shard_map/d_in_sum_y-1/ppermute | solution.py:817
  304.4 17.4 %collective-permute-start.64 = (bf16[224,1152]{1,0:T(8,128)(2,1)S(1)}, bf16[224,1152]{1,0:T(8,128)(2,1)S(1)}, u32[]{:S(2)}, u32[]{:S(2)}) collective-permute-start(bf16[224,1152]{1,0:T(8,128)(2,1)S(1)} %get-tuple-element.301), channel_id=1, source_target_pairs={{6,0},{0,2},{2,4},{4,6},{7,1},{1,3},{3,5},{5,7},{14,8},{8,10},{10,... | collective-permute-start | bytes 1548296 | tf_op jit(solution)/shard_map/up_grad_sum_z-1/ppermute | solution.py:817
  308.5 22.0 %collective-permute-start.63 = (bf16[224,1152]{1,0:T(8,128)(2,1)S(1)}, bf16[224,1152]{1,0:T(8,128)(2,1)S(1)}, u32[]{:S(2)}, u32[]{:S(2)}) collective-permute-start(bf16[224,1152]{1,0:T(8,128)(2,1)S(1)} %add_convert_fusion.15), channel_id=1, source_target_pairs={{6,0},{0,2},{2,4},{4,6},{7,1},{1,3},{3,5},{5,7},{14,8},{8,10},{10,... | collective-permute-start | bytes 1548296 | tf_op jit(solution)/shard_map/down_grad_sum_z-1/ppermute | solution.py:817
  331.1 14.2 %collective-permute-start.65 = (bf16[256,512]{1,0:T(8,128)(2,1)S(1)}, bf16[256,512]{1,0:T(8,128)(2,1)S(1)}, u32[]{:S(2)}, u32[]{:S(2)}) collective-permute-start(bf16[256,512]{1,0:T(8,128)(2,1)S(1)} %get-tuple-element.319), channel_id=1, source_target_pairs={{1,0},{0,1},{3,2},{2,3},{5,4},{4,5},{7,6},{6,7},{9,8},{8,9},{11,10... | collective-permute-start | bytes 786440 | tf_op jit(solution)/shard_map/kv_sum_vx-1/ppermute | solution.py:817
  332.5 18.5 %collective-permute-start.66 = (bf16[256,512]{1,0:T(8,128)(2,1)S(1)}, bf16[256,512]{1,0:T(8,128)(2,1)S(1)}, u32[]{:S(2)}, u32[]{:S(2)}) collective-permute-start(bf16[256,512]{1,0:T(8,128)(2,1)S(1)} %get-tuple-element.321), channel_id=1, source_target_pairs={{1,0},{0,1},{3,2},{2,3},{5,4},{4,5},{7,6},{6,7},{9,8},{8,9},{11,10... | collective-permute-start | bytes 786440 | tf_op jit(solution)/shard_map/kv_sum_vx-1/ppermute | solution.py:817
  333.2 21.0 %collective-permute-start.67 = (bf16[256,512]{1,0:T(8,128)(2,1)S(1)}, bf16[256,512]{1,0:T(8,128)(2,1)S(1)}, u32[]{:S(2)}, u32[]{:S(2)}) collective-permute-start(bf16[256,512]{1,0:T(8,128)(2,1)S(1)} %get-tuple-element.323), channel_id=1, source_target_pairs={{1,0},{0,1},{3,2},{2,3},{5,4},{4,5},{7,6},{6,7},{9,8},{8,9},{11,10... | collective-permute-start | bytes 786440 | tf_op jit(solution)/shard_map/kv_sum_vx-1/ppermute | solution.py:817
  339.8 14.4 %collective-permute-start.69 = (bf16[128,512]{1,0:T(8,128)(2,1)S(1)}, bf16[128,512]{1,0:T(8,128)(2,1)S(1)}, u32[]{:S(2)}, u32[]{:S(2)}) collective-permute-start(bf16[128,512]{1,0:T(8,128)(2,1)S(1)} %get-tuple-element.423), channel_id=1, source_target_pairs={{6,0},{0,2},{2,4},{4,6},{7,1},{1,3},{3,5},{5,7},{14,8},{8,10},{10,... | collective-permute-start | bytes 393224 | tf_op jit(solution)/shard_map/kv_sum_z-1/ppermute | solution.py:817
  340.4 13.7 %collective-permute-start.70 = (bf16[128,512]{1,0:T(8,128)(2,1)S(1)}, bf16[128,512]{1,0:T(8,128)(2,1)S(1)}, u32[]{:S(2)}, u32[]{:S(2)}) collective-permute-start(bf16[128,512]{1,0:T(8,128)(2,1)S(1)} %get-tuple-element.422), channel_id=1, source_target_pairs={{2,0},{4,2},{6,4},{0,6},{3,1},{5,3},{7,5},{1,7},{10,8},{12,10},{14... | collective-permute-start | bytes 393224 | tf_op jit(solution)/shard_map/kv_sum_z1/ppermute | solution.py:817
  345.4 22.5 %collective-permute-start.73 = (bf16[224,1152]{1,0:T(8,128)(2,1)S(1)}, bf16[224,1152]{1,0:T(8,128)(2,1)S(1)}, u32[]{:S(2)}, u32[]{:S(2)}) collective-permute-start(bf16[224,1152]{1,0:T(8,128)(2,1)S(1)} %add_convert_fusion.14), channel_id=1, source_target_pairs={{6,0},{0,2},{2,4},{4,6},{7,1},{1,3},{3,5},{5,7},{14,8},{8,10},{10,... | collective-permute-start | bytes 1548296 | tf_op jit(solution)/shard_map/gate_grad_sum_z-1/ppermute | solution.py:817
  354.4 16.6 %collective-permute-start.72 = (bf16[256,512]{1,0:T(8,128)(2,1)S(1)}, bf16[256,512]{1,0:T(8,128)(2,1)S(1)}, u32[]{:S(2)}, u32[]{:S(2)}) collective-permute-start(bf16[256,512]{1,0:T(8,128)(2,1)S(1)} %pad_maximum_fusion.11), channel_id=1, source_target_pairs={{2,0},{4,2},{6,4},{0,6},{3,1},{5,3},{7,5},{1,7},{10,8},{12,10},{14... | collective-permute-start | bytes 786440 | tf_op jit(solution)/shard_map/kv_sum_z1/ppermute | solution.py:817
  356.9 14.1 %collective-permute-start.71 = (bf16[256,512]{1,0:T(8,128)(2,1)S(1)}, bf16[256,512]{1,0:T(8,128)(2,1)S(1)}, u32[]{:S(2)}, u32[]{:S(2)}) collective-permute-start(bf16[256,512]{1,0:T(8,128)(2,1)S(1)} %pad_maximum_fusion.10), channel_id=1, source_target_pairs={{6,0},{0,2},{2,4},{4,6},{7,1},{1,3},{3,5},{5,7},{14,8},{8,10},{10,... | collective-permute-start | bytes 786440 | tf_op jit(solution)/shard_map/kv_sum_z-1/ppermute | solution.py:817
  368.0 16.9 %collective-permute-start.83 = (bf16[224,1152]{1,0:T(8,128)(2,1)S(1)}, bf16[224,1152]{1,0:T(8,128)(2,1)S(1)}, u32[]{:S(2)}, u32[]{:S(2)}) collective-permute-start(bf16[224,1152]{1,0:T(8,128)(2,1)S(1)} %add_convert_fusion.12), channel_id=1, source_target_pairs={{6,0},{0,2},{2,4},{4,6},{7,1},{1,3},{3,5},{5,7},{14,8},{8,10},{10,... | collective-permute-start | bytes 1548296 | tf_op jit(solution)/shard_map/gate_grad_sum_z-1/ppermute | solution.py:817
  368.7 23.6 %collective-permute-start.76 = (bf16[224,1152]{1,0:T(8,128)(2,1)S(1)}, bf16[224,1152]{1,0:T(8,128)(2,1)S(1)}, u32[]{:S(2)}, u32[]{:S(2)}) collective-permute-start(bf16[224,1152]{1,0:T(8,128)(2,1)S(1)} %add_convert_fusion.13), channel_id=1, source_target_pairs={{6,0},{0,2},{2,4},{4,6},{7,1},{1,3},{3,5},{5,7},{14,8},{8,10},{10,... | collective-permute-start | bytes 1548296 | tf_op jit(solution)/shard_map/up_grad_sum_z-1/ppermute | solution.py:817
  400.5 17.8 %collective-permute-start.82 = (bf16[2944,128]{1,0:T(8,128)(2,1)S(1)}, bf16[2944,128]{1,0:T(8,128)(2,1)S(1)}, u32[]{:S(2)}, u32[]{:S(2)}) collective-permute-start(bf16[2944,128]{1,0:T(8,128)(2,1)S(1)} %pad_maximum_fusion.3), channel_id=1, source_target_pairs={{16,0},{0,16},{17,1},{1,17},{18,2},{2,18},{19,3},{3,19},{20,4},{4,... | collective-permute-start | bytes 2261000 | tf_op jit(solution)/shard_map/attn_grad_sum_y-1/ppermute | solution.py:817
  405.2 13.1 %collective-permute-start.79 = (bf16[2944,128]{1,0:T(8,128)(2,1)S(1)}, bf16[2944,128]{1,0:T(8,128)(2,1)S(1)}, u32[]{:S(2)}, u32[]{:S(2)}) collective-permute-start(bf16[2944,128]{1,0:T(8,128)(2,1)S(1)} %pad_maximum_fusion.2), channel_id=1, source_target_pairs={{1,0},{0,1},{3,2},{2,3},{5,4},{4,5},{7,6},{6,7},{9,8},{8,9},{11,10... | collective-permute-start | bytes 2261000 | tf_op jit(solution)/shard_map/attn_grad_sum_x-1/ppermute | solution.py:817
  422.9 18.0 %collective-permute-start.90 = (bf16[216,864]{1,0:T(8,128)(2,1)S(1)}, bf16[216,864]{1,0:T(8,128)(2,1)S(1)}, u32[]{:S(2)}, u32[]{:S(2)}) collective-permute-start(bf16[216,864]{1,0:T(8,128)(2,1)S(1)} %get-tuple-element.395), channel_id=1, source_target_pairs={{16,0},{24,8},{0,16},{8,24},{17,1},{25,9},{1,17},{9,25},{18,2},{26... | collective-permute-start | bytes 1119752 | tf_op jit(solution)/shard_map/grad_exchange_uyc2/ppermute | solution.py:817
  423.7 18.1 %collective-permute-start.91 = (bf16[216,864]{1,0:T(8,128)(2,1)S(1)}, bf16[216,864]{1,0:T(8,128)(2,1)S(1)}, u32[]{:S(2)}, u32[]{:S(2)}) collective-permute-start(bf16[216,864]{1,0:T(8,128)(2,1)S(1)} %get-tuple-element.394), channel_id=1, source_target_pairs={{24,0},{0,8},{8,16},{16,24},{25,1},{1,9},{9,17},{17,25},{26,2},{2,... | collective-permute-start | bytes 1119752 | tf_op jit(solution)/shard_map/grad_exchange_uyc3/ppermute | solution.py:817
  425.3 22.1 %collective-permute-start.88 = (bf16[736,128]{1,0:T(8,128)(2,1)S(1)}, bf16[736,128]{1,0:T(8,128)(2,1)S(1)}, u32[]{:S(2)}, u32[]{:S(2)}) collective-permute-start(bf16[736,128]{1,0:T(8,128)(2,1)S(1)} %pad_maximum_fusion.15), channel_id=1, source_target_pairs={{2,0},{4,2},{6,4},{0,6},{3,1},{5,3},{7,5},{1,7},{10,8},{12,10},{14... | collective-permute-start | bytes 565256 | tf_op jit(solution)/shard_map/attn_grad_sum_z1/ppermute | solution.py:817
  429.1 18.3 %collective-permute-start.86 = (bf16[736,128]{1,0:T(8,128)(2,1)S(1)}, bf16[736,128]{1,0:T(8,128)(2,1)S(1)}, u32[]{:S(2)}, u32[]{:S(2)}) collective-permute-start(bf16[736,128]{1,0:T(8,128)(2,1)S(1)} %pad_maximum_fusion.14), channel_id=1, source_target_pairs={{6,0},{0,2},{2,4},{4,6},{7,1},{1,3},{3,5},{5,7},{14,8},{8,10},{10,... | collective-permute-start | bytes 565256 | tf_op jit(solution)/shard_map/attn_grad_sum_z-1/ppermute | solution.py:817
  (125 other events, 1568.0 us)

commit v7 on v6

--- a/solution.py
+++ b/solution.py
@@ -330,7 +330,7 @@
             jax.ShapeDtypeStruct((rows, D), f32),
             jax.ShapeDtypeStruct((rows, D), bf16),
         ),
-        compiler_params=pltpu.CompilerParams(vmem_limit_bytes=44 * 1024 * 1024),
+        compiler_params=pltpu.CompilerParams(vmem_limit_bytes=48 * 1024 * 1024),
         cost_estimate=pl.CostEstimate(
             flops=8 * 4 * blocks * rows * rows * H * HD, bytes_accessed=0, transcendentals=0
         ),
@@ -450,7 +450,7 @@
             jax.ShapeDtypeStruct((1, D), f32),
             *[jax.ShapeDtypeStruct((rows, 2 * HD), bf16)] * blocks,
         ),
-        compiler_params=pltpu.CompilerParams(vmem_limit_bytes=44 * 1024 * 1024),
+        compiler_params=pltpu.CompilerParams(vmem_limit_bytes=48 * 1024 * 1024),
         cost_estimate=pl.CostEstimate(flops=0, bytes_accessed=0, transcendentals=0),
         name="attend_back",
     )(
@@ -721,11 +721,13 @@
     wide = H * HD
     each = flat.devices // groups
 
+    straight = flat.lines % 16 == 0
+
     def body(order_ref, lines_ref, *refs):
         kv_refs = refs[:terms]
         (
             raw_ref, cos_ref, sin_ref, gk_ref, a_ref, w_ref, tok_ref, gpre_ref, dmid_ref, da_ref,
-            dgq, dgpost, dgfpre, dgfpost, in_ref, *outs, held, grad, gains, blocks, sems,
+            dgq, dgpost, dgfpre, dgfpost, in_ref, *outs, held, grad, gains, blocks, windows, sems,
         ) = refs[terms:]
         q_copy = pltpu.make_async_copy(
             lines_ref.at[: flat.q_lines], held.at[: flat.q_lines], sems.at[0]
@@ -763,18 +765,22 @@
             ]
         o_copy.wait()
         for i in range(flat.devices):
-            at = i * flat.lines
-            blocks[i, : flat.gain_at, :] = held[at : at + flat.gain_at, :].astype(bf16)
             at = flat.gain_line(i)
-            blocks[i, flat.gain_at :, :] = gains[at : at + 16, :].astype(bf16)
-        copies = [
-            pltpu.make_async_copy(
-                blocks.at[order_ref[k]], outs[k // each].at[k % each], sems.at[2 + k]
-            )
-            for k in range(flat.devices)
-        ]
-        for copy in copies:
-            copy.start()
+            windows[i] = gains[at : at + 16, :].astype(bf16)
+            if not straight:
+                at = i * flat.lines
+                blocks[i, : flat.gain_at, :] = held[at : at + flat.gain_at, :].astype(bf16)
+        copies = []
+        for k in range(flat.devices):
+            device = order_ref[k]
+            if straight:
+                at = pl.multiple_of(device * flat.lines, 8)
+                blocks[k, : flat.gain_at, :] = held[pl.ds(at, flat.gain_at), :].astype(bf16)
+            source = blocks.at[k if straight else device]
+            for part, low, high in ((source.at[: flat.gain_at], 0, flat.gain_at), (windows.at[device], flat.gain_at, flat.rows)):
+                target = outs[k // each].at[k % each, low:high]
+                copies.append(pltpu.make_async_copy(part, target, sems.at[2 + len(copies)]))
+                copies[-1].start()
         for copy in copies:
             copy.wait()
 
@@ -789,8 +795,9 @@
             pltpu.VMEM(lines.shape, f32),
             pltpu.VMEM((D, 2 * HD), f32),
             pltpu.VMEM((-(-(flat.gain_lines + 16) // 8) * 8, LANES), f32),
-            pltpu.VMEM((flat.devices, flat.rows, LANES), bf16),
-            pltpu.SemaphoreType.DMA((2 + flat.devices,)),
+            pltpu.VMEM((flat.devices, flat.gain_at, LANES), bf16),
+            pltpu.VMEM((flat.devices, 16, LANES), bf16),
+            pltpu.SemaphoreType.DMA((2 + 2 * flat.devices,)),
         ],
         "v" + "h" * groups,
     )

time: 457 us -> 455 us (level)
  Pallas kernels: 118 us -> 125 us
  waiting for transfers between devices: 187 us -> 180 us
    ppermute x92, waiting for transfers between devices: 187 us -> 180 us  [fro(): return lax.ppermute(value, axis, [((i + offset) % n, i) for i in range(n)])]
    unnamed x167 -> x161, local copies, waits for them, and re-layouts: 11.4 us -> 11.7 us
  transfers between devices with their start and end apart: 92 -> 92, of which waited for: 44 -> 46; matrix products, arithmetic and copies ran while one was open for 5% -> 4% of each run, Pallas kernels for 19% -> 21%
where the time goes in v7:
time: 455 us; the launch traced here: 448 us
  waiting for transfers between devices  180 us (40%)
  Pallas kernels  125 us (27%)
  starting transfers between devices  102 us (22%)
  local copies, waits for them, and re-layouts  21.2 us (5%)
  other arithmetic  17.8 us (4%)
    ppermute x92, waiting for transfers between devices, fro(): return lax.ppermute(value, axis, [((i + offset) % n, i) for i in range(n)])  180 us
    ppermute x92, starting transfers between devices, fro(): return lax.ppermute(value, axis, [((i + offset) % n, i) for i in range(n)])  102 us
    pallas_call x2, Pallas kernels, ffn_call(): pl.pallas_call(kernel, grid=(chunks,), in_specs=[anywhere] * count + [chu...  47 us
    pallas_call x5, Pallas kernels, run(): pl.pallas_call(body, out_shape=tuple((jax.ShapeDtypeStruct(s, d) for s, d...  38.6 us
    pallas_call x3, Pallas kernels, unit_grads(): pl.pallas_call(body, grid=(1,), in_specs=[pl.BlockSpec((tokens, both), la...  19.7 us
    pallas_call x1, Pallas kernels, attend_back(): pl.pallas_call(body, grid_spec=pltpu.PrefetchScalarGridSpec(num_scalar_pr...  11.9 us
    unnamed x161, local copies, waits for them, and re-layouts  11.7 us
  transfers between devices with their start and end apart: 92, of which 46 were waited for; matrix products, arithmetic and copies ran while one was open for 4% of the time, Pallas kernels for 21%

profile of v7, /device:TPU:0, one launch (start us, length us, event | category | flops | bytes accessed | tf_op | source)
XLA Modules:
  0.0 448.2 jit_solution(17415496624417098150)
XLA Ops:
  4.3 5.0 %collective-permute-start = (bf16[736,128]{1,0:T(8,128)(2,1)S(1)}, bf16[736,128]{1,0:T(8,128)(2,1)S(1)}, u32[]{:S(2)}, u32[]{:S(2)}) collective-permute-start(bf16[736,128]{1,0:T(8,128)(2,1)S(1)} %pad_maximum_fusion.12), channel_id=1, source_target_pairs={{2,0},{4,2},{6,4},{0,6},{3,1},{5,3},{7,5},{1,7},{10,8},{12,10},{14... | collective-permute-start | bytes 565256 | tf_op jit(solution)/shard_map/attn_gather_z1/ppermute | solution.py:824
  11.1 3.4 collective-permute-done
  14.5 4.3 collective-permute-start.1
  21.1 4.3 collective-permute-done.3
  25.4 3.7 collective-permute-done.5
  35.0 3.5 collective-permute-start.15
  38.5 11.3 %collective-permute-done.10 = bf16[2944,128]{1,0:T(8,128)(2,1)S(1)} collective-permute-done((bf16[2944,128]{1,0:T(8,128)(2,1)S(1)}, bf16[2944,128]{1,0:T(8,128)(2,1)S(1)}, u32[]{:S(2)}, u32[]{:S(2)}) %collective-permute-start.10) | collective-permute-done | bytes 753696 | tf_op jit(solution)/shard_map/attn_gather_x1/ppermute | solution.py:824
  54.1 5.0 %collective-permute-done.12 = bf16[1472,128]{1,0:T(8,128)(2,1)S(1)} collective-permute-done((bf16[1472,128]{1,0:T(8,128)(2,1)S(1)}, bf16[1472,128]{1,0:T(8,128)(2,1)S(1)}, u32[]{:S(2)}, u32[]{:S(2)}) %collective-permute-start.12) | collective-permute-done | bytes 376864 | tf_op jit(solution)/shard_map/attn_gather_y1/ppermute | solution.py:824
  63.7 6.7 %collective-permute-done.15.refs_9_.refs_11_ = bf16[224,3456]{1,0:T(8,128)(2,1)} collective-permute-done((bf16[224,3456]{1,0:T(8,128)(2,1)}, bf16[224,3456]{1,0:T(8,128)(2,1)}, u32[]{:S(2)}, u32[]{:S(2)}) %collective-permute-start.15) | collective-permute-done | bytes 1548320 | tf_op jit(solution)/shard_map/unit_gather_z1/ppermute | solution.py:824
  72.1 4.3 collective-permute-start.18
  76.5 8.9 %first_part.1 = (bf16[1152,1536]{1,0:T(8,128)(2,1)}, f32[1,1152]{1,0:T(1,128)}, f32[1,256]{1,0:T(1,128)}, f32[1,256]{1,0:T(1,128)}, f32[1,1152]{1,0:T(1,128)}, /...) custom-call(s32[32]{0:T(128)} %fusion.11.order_ref, ...), custom_call_target="tpu_custom_call" | custom-call | flops 7247757312 | tf_op jit(solution)/shard_map/first_part/pallas_call | solution.py:90
  89.5 5.9 %spread_out.1.w_ref.refs_6_ = bf16[1024,1152]{1,0:T(8,128)(2,1)} custom-call(s32[32]{0:T(128)} %fusion.11.order_ref, bf16[4,736,128]{2,1,0:T(8,128)(2,1)} %bitcast.118, bf16[4,736,128]{2,1,0:T(8,128)(2,1)} %bitcast.126, bf16[4,736,128]{2,1,0:T(8,128)(2,1)} %bitcast.122, bf16[4,736,128]{2,1,0:T(8,128)(2,1)} %bitcast.128, bf16[4,736,128]{2,1,0:T(8,128)(2,1)} %bitcast.120, ...), custom_call_target="tpu_custom_call" | custom-call | tf_op jit(solution)/shard_map/spread_out/pallas_call | solution.py:90
  95.4 3.7 collective-permute-done.16
  99.1 3.4 collective-permute-done.17
  104.6 3.5 collective-permute-start.22
  108.3 3.9 collective-permute-start.19
  112.1 4.3 collective-permute-done.23
  117.6 5.3 %collective-permute-done.24 = bf16[256,512]{1,0:T(8,128)(2,1)S(1)} collective-permute-done((bf16[256,512]{1,0:T(8,128)(2,1)S(1)}, bf16[256,512]{1,0:T(8,128)(2,1)S(1)}, u32[]{:S(2)}, u32[]{:S(2)}) %collective-permute-start.24) | collective-permute-done | bytes 262176 | tf_op jit(solution)/shard_map/kv_gather_vx1/ppermute | solution.py:824
  124.3 7.7 %attend.1 = (bf16[256,1024]{1,0:T(8,128)(2,1)S(1)}, f32[8,256]{1,0:T(8,128)S(1)}, f32[256,1152]{1,0:T(8,128)S(1)}, f32[256,1152]{1,0:T(8,128)S(1)}, bf16[256,1152]{1,0:T(8,128)(2,1)S(1)}) custom-call(s32[2,8]{1,0:T(2,128)S(1)} %pad_add_fusion.info_ref, bf16[256,1024]{1,0:T(8,128)(2,1)S(1)} %copy-done.7, bf16[8,256,512]{2,1,0:T(8,128)(2,1)} %copy-done.35, ...), custom_call_target="tpu_custom_call" | custom-call | flops 17179869184 | tf_op jit(solution)/shard_map/attend/pallas_call | solution.py:298
  135.2 5.6 %collective-permute-start.34 = (bf16[112,3456]{1,0:T(8,128)(2,1)S(1)}, bf16[112,3456]{1,0:T(8,128)(2,1)S(1)}, u32[]{:S(2)}, u32[]{:S(2)}) collective-permute-start(bf16[112,3456]{1,0:T(8,128)(2,1)S(1)} %collective-permute-done.19.refs_11_.refs_13_), channel_id=1, source_target_pairs={{2,0},{4,2},{6,4},{0,6},{3,1},{5,3},{7,5},{1,7},{10,8},{12,10},{14... | collective-permute-start | bytes 2322440 | tf_op jit(solution)/shard_map/unit_gather_z1/ppermute | solution.py:824
  140.9 7.4 %collective-permute-done.28.refs_12_.refs_14_ = bf16[112,3456]{1,0:T(8,128)(2,1)S(1)} collective-permute-done((bf16[112,3456]{1,0:T(8,128)(2,1)}, bf16[112,3456]{1,0:T(8,128)(2,1)S(1)}, u32[]{:S(2)}, u32[]{:S(2)}) %collective-permute-start.28) | collective-permute-done | bytes 774176 | tf_op jit(solution)/shard_map/unit_gather_z1/ppermute | solution.py:824
  150.1 12.9 %collective-permute-done.34.refs_13_.refs_15_ = bf16[112,3456]{1,0:T(8,128)(2,1)S(1)} collective-permute-done((bf16[112,3456]{1,0:T(8,128)(2,1)S(1)}, bf16[112,3456]{1,0:T(8,128)(2,1)S(1)}, u32[]{:S(2)}, u32[]{:S(2)}) %collective-permute-start.34) | collective-permute-done | bytes 774176 | tf_op jit(solution)/shard_map/unit_gather_z1/ppermute | solution.py:824
  166.8 23.8 %ffn_forward.1 = (bf16[2048,896]{1,0:T(8,128)(2,1)}, bf16[2048,896]{1,0:T(8,128)(2,1)}, bf16[2048,896]{1,0:T(8,128)(2,1)}, bf16[256,1152]{1,0:T(8,128)(2,1)S(1)}...) custom-call(bf16[256,1152]{1,0:T(8,128)(2,1)S(1)} %get-tuple-element, ...), custom_call_target="tpu_custom_call" | custom-call | flops 12683575296 | tf_op jit(solution)/shard_map/ffn_forward/pallas_call | solution.py:560
  194.6 7.4 %collective-permute-done.42 = bf16[128,1152]{1,0:T(8,128)(2,1)S(1)} collective-permute-done((bf16[128,1152]{1,0:T(8,128)(2,1)S(1)}, bf16[128,1152]{1,0:T(8,128)(2,1)S(1)}, u32[]{:S(2)}, u32[]{:S(2)}) %collective-permute-start.42) | collective-permute-done | bytes 294944 | tf_op jit(solution)/shard_map/ffn_out_sum_x-1/ppermute | solution.py:824
  204.3 12.4 %collective-permute-done.43.refs_2_ = bf16[256,1152]{1,0:T(8,128)(2,1)S(1)} collective-permute-done((bf16[256,1152]{1,0:T(8,128)(2,1)S(1)}, bf16[256,1152]{1,0:T(8,128)(2,1)S(1)}, u32[]{:S(2)}, u32[]{:S(2)}) %collective-permute-start.43) | collective-permute-done | bytes 589856 | tf_op jit(solution)/shard_map/ffn_out_sum_y-1/ppermute | solution.py:824
  220.7 12.0 %collective-permute-done.47.refs_4_ = bf16[256,1152]{1,0:T(8,128)(2,1)S(1)} collective-permute-done((bf16[256,1152]{1,0:T(8,128)(2,1)S(1)}, bf16[256,1152]{1,0:T(8,128)(2,1)S(1)}, u32[]{:S(2)}, u32[]{:S(2)}) %collective-permute-start.47) | collective-permute-done | bytes 589856 | tf_op jit(solution)/shard_map/d_out_gather_x1/ppermute | solution.py:824
  236.3 3.2 collective-permute-done.49
  244.9 6.1 %unit_grads.3 = (bf16[224,1152]{1,0:T(8,128)(2,1)S(1)}, bf16[224,1152]{1,0:T(8,128)(2,1)S(1)}, bf16[224,1152]{1,0:T(8,128)(2,1)S(1)}, bf16[224,1152]{1,0:T(8,128)(2,1)S(1)}) custom-call(bf16[2048,896]{1,0:T(8,128)(2,1)S(1)} %copy-done.27, bf16[256,1152]{1,0:T(8,128)(2,1)S(1)} %get-tuple-element.266.refs_0_, ...), custom_call_target="tpu_custom_call" | custom-call | flops 4227858432 | tf_op jit(solution)/shard_map/unit_grads/pallas_call | solution.py:637
  251.8 23.2 %ffn_backward.1 = (bf16[2048,1792]{1,0:T(8,128)(2,1)}, bf16[256,1152]{1,0:T(8,128)(2,1)S(1)}, bf16[256,1152]{1,0:T(8,128)(2,1)}, bf16[256,1152]{1,0:T(8,128)(2,1...) custom-call(bf16[256,1152]{1,0:T(8,128)(2,1)S(1)} %get-tuple-element, ...), custom_call_target="tpu_custom_call" | custom-call | flops 12683575296 | tf_op jit(solution)/shard_map/ffn_backward/pallas_call | solution.py:560
  282.8 3.1 copy-done.26
  285.9 6.5 %unit_grads.4 = (bf16[224,1152]{1,0:T(8,128)(2,1)S(1)}, bf16[224,1152]{1,0:T(8,128)(2,1)S(1)}, bf16[224,1152]{1,0:T(8,128)(2,1)S(1)}, bf16[224,1152]{1,0:T(8,128)(2,1)S(1)}) custom-call(bf16[2048,1792]{1,0:T(8,128)(2,1)S(1)} %copy-done.26, bf16[256,1152]{1,0:T(8,128)(2,1)S(1)} %get-tuple-element.242.refs_0_, bf16[256,1152]{1,0:T(8,128)(2,1)S(1)} %copy-done.22, ...), custom_call_target="tpu_custom_call" | custom-call | flops 4227858432 | tf_op jit(solution)/shard_map/unit_grads/pallas_call | solution.py:637
  296.5 7.1 %unit_grads.5 = (bf16[224,1152]{1,0:T(8,128)(2,1)S(1)}, bf16[224,1152]{1,0:T(8,128)(2,1)S(1)}, bf16[224,1152]{1,0:T(8,128)(2,1)S(1)}, bf16[224,1152]{1,0:T(8,128)(2,1)}) custom-call(bf16[2048,1792]{1,0:T(8,128)(2,1)S(1)} %copy-done.26, bf16[256,1152]{1,0:T(8,128)(2,1)S(1)} %get-tuple-element.242.refs_0_, bf16[256,1152]{1,0:T(8,128)(2,1)S(1)} %copy-done.22, ...), custom_call_target="tpu_custom_call" | custom-call | flops 4227858432 | tf_op jit(solution)/shard_map/unit_grads/pallas_call | solution.py:637
  303.6 2.9 collective-permute-start.64
  310.5 11.9 %attend_back.1 = (f32[256,1024]{1,0:T(8,128)}, bf16[256,1152]{1,0:T(8,128)(2,1)S(1)}, f32[256,1152]{1,0:T(8,128)}, f32[1,1152]{1,0:T(1,128)S(1)}, f32[1,1152]{1,...) custom-call(s32[2,8]{1,0:T(2,128)S(1)} %pad_add_fusion.info_ref, ...), custom_call_target="tpu_custom_call" | custom-call | tf_op jit(solution)/shard_map/attend_back/pallas_call | solution.py:418
  322.5 7.1 %collective-permute-done.63 = bf16[224,1152]{1,0:T(8,128)(2,1)S(1)} collective-permute-done((bf16[224,1152]{1,0:T(8,128)(2,1)S(1)}, bf16[224,1152]{1,0:T(8,128)(2,1)S(1)}, u32[]{:S(2)}, u32[]{:S(2)}) %collective-permute-start.63) | collective-permute-done | bytes 516128 | tf_op jit(solution)/shard_map/down_grad_sum_z-1/ppermute | solution.py:824
  334.0 4.9 %collective-permute-done.68 = bf16[256,512]{1,0:T(8,128)(2,1)S(1)} collective-permute-done((bf16[256,512]{1,0:T(8,128)(2,1)S(1)}, bf16[256,512]{1,0:T(8,128)(2,1)S(1)}, u32[]{:S(2)}, u32[]{:S(2)}) %collective-permute-start.68) | collective-permute-done | bytes 262176 | tf_op jit(solution)/shard_map/kv_sum_vx-1/ppermute | solution.py:824
  339.8 3.0 collective-permute-start.70
  345.3 4.8 %collective-permute-done.66 = bf16[256,512]{1,0:T(8,128)(2,1)S(1)} collective-permute-done((bf16[256,512]{1,0:T(8,128)(2,1)S(1)}, bf16[256,512]{1,0:T(8,128)(2,1)S(1)}, u32[]{:S(2)}, u32[]{:S(2)}) %collective-permute-start.66) | collective-permute-done | bytes 262176 | tf_op jit(solution)/shard_map/kv_sum_vx-1/ppermute | solution.py:824
  350.1 3.0 collective-permute-done.67
  356.0 10.2 %query_side.1 = (f32[23056,128]{1,0:T(8,128)}, f32[256,1152]{1,0:T(8,128)}, f32[1,256]{1,0:T(1,128)}) custom-call(f32[256,1024]{1,0:T(8,128)} %get-tuple-element.328.dq_ref, f32[256,1280]{1,0:T(8,128)} %get-tuple-element.329.raw_ref.refs_3_, f32[256,128]{1,0:T(8,128)} %get-tuple-element.425.refs_9_.cos_ref.refs_4_, ...), custom_call_target="tpu_custom_call" | custom-call | tf_op jit(solution)/shard_map/query_side/pallas_call | solution.py:90
  370.9 12.2 %last_part.1 = (bf16[256,1152]{1,0:T(8,128)(2,1)}, bf16[4,736,128]{2,1,0:T(8,128)(2,1)}, bf16[4,736,128]{2,1,0:T(8,128)(2,1)}, bf16[4,736,128]{2,1,0:T(8,128)(2,...) custom-call(s32[32]{0:T(128)} %fusion.11.order_ref, ...), custom_call_target="tpu_custom_call" | custom-call | tf_op jit(solution)/shard_map/last_part/pallas_call | solution.py:90
  385.9 5.5 %collective-permute-done.76 = bf16[224,1152]{1,0:T(8,128)(2,1)S(1)} collective-permute-done((bf16[224,1152]{1,0:T(8,128)(2,1)S(1)}, bf16[224,1152]{1,0:T(8,128)(2,1)S(1)}, u32[]{:S(2)}, u32[]{:S(2)}) %collective-permute-start.76) | collective-permute-done | bytes 516128 | tf_op jit(solution)/shard_map/up_grad_sum_z-1/ppermute | solution.py:824
  394.4 4.9 %collective-permute-done.81 = bf16[1472,128]{1,0:T(8,128)(2,1)S(1)} collective-permute-done((bf16[1472,128]{1,0:T(8,128)(2,1)S(1)}, bf16[1472,128]{1,0:T(8,128)(2,1)S(1)}, u32[]{:S(2)}, u32[]{:S(2)}) %collective-permute-start.81) | collective-permute-done | bytes 376864 | tf_op jit(solution)/shard_map/attn_grad_sum_x-1/ppermute | solution.py:824
  405.9 10.7 %collective-permute-done.82 = bf16[2944,128]{1,0:T(8,128)(2,1)S(1)} collective-permute-done((bf16[2944,128]{1,0:T(8,128)(2,1)S(1)}, bf16[2944,128]{1,0:T(8,128)(2,1)S(1)}, u32[]{:S(2)}, u32[]{:S(2)}) %collective-permute-start.82) | collective-permute-done | bytes 753696 | tf_op jit(solution)/shard_map/attn_grad_sum_y-1/ppermute | solution.py:824
  424.3 3.1 collective-permute-start.88
  427.5 2.7 collective-permute-done.89
  430.2 9.6 %collective-permute-done.90 = bf16[216,864]{1,0:T(8,128)(2,1)S(1)} collective-permute-done((bf16[216,864]{1,0:T(8,128)(2,1)S(1)}, bf16[216,864]{1,0:T(8,128)(2,1)S(1)}, u32[]{:S(2)}, u32[]{:S(2)}) %collective-permute-start.90) | collective-permute-done | bytes 373280 | tf_op jit(solution)/shard_map/grad_exchange_uyc2/ppermute | solution.py:824
  440.5 5.5 %multiply_subtract_fusion = (f32[864,864]{1,0:T(8,128)}, f32[864,864]{1,0:T(8,128)}, f32[864,864]{1,0:T(8,128)}, f32[864,864]{1,0:T(8,128)}) fusion(f32[864,864]{1,0:T(8,128)S(1)} %copy-done.28, f32[864,864]{1,0:T(8,128)S(1)} %copy-done.31, f32[864,864]{1,0:T(8,128)S(1)} %copy-done.32, bf16[4,216,864]{2,1,0:T(8,128)(2,1)S(1)} %bitcast_dynamic-update-slice_fusion), kind=kLoop, calls=%fused_computation.3 | loop fusion | flops 11197440 | bytes 22394880 | tf_op jit(solution)/shard_map/sub | solution.py:65
  (432 shorter events, 114.5 us)
Async XLA Ops:
  9.3 16.1 %collective-permute-start.4 = (bf16[216,864]{1,0:T(8,128)(2,1)}, bf16[216,864]{1,0:T(8,128)(2,1)S(1)}, u32[]{:S(2)}, u32[]{:S(2)}) collective-permute-start(bf16[216,864]{1,0:T(8,128)(2,1)} %get-tuple-element.199), channel_id=1, source_target_pairs={{8,0},{16,8},{24,16},{0,24},{9,1},{17,9},{25,17},{1,25},{10,2},{18... | collective-permute-start | bytes 1119752 | tf_op jit(solution)/shard_map/unit_exchange_uyc1/ppermute | solution.py:824
  10.0 19.1 %collective-permute-start.5 = (bf16[216,864]{1,0:T(8,128)(2,1)}, bf16[216,864]{1,0:T(8,128)(2,1)S(1)}, u32[]{:S(2)}, u32[]{:S(2)}) collective-permute-start(bf16[216,864]{1,0:T(8,128)(2,1)} %get-tuple-element.200), channel_id=1, source_target_pairs={{16,0},{24,8},{0,16},{8,24},{17,1},{25,9},{1,17},{9,25},{18,2},{26... | collective-permute-start | bytes 1119752 | tf_op jit(solution)/shard_map/unit_exchange_uyc2/ppermute | solution.py:824
  10.8 18.3 %collective-permute-start.6 = (bf16[216,864]{1,0:T(8,128)(2,1)S(1)}, bf16[216,864]{1,0:T(8,128)(2,1)S(1)}, u32[]{:S(2)}, u32[]{:S(2)}) collective-permute-start(bf16[216,864]{1,0:T(8,128)(2,1)S(1)} %get-tuple-element.201), channel_id=1, source_target_pairs={{24,0},{0,8},{8,16},{16,24},{25,1},{1,9},{9,17},{17,25},{26,2},{2,... | collective-permute-start | bytes 1119752 | tf_op jit(solution)/shard_map/unit_exchange_uyc3/ppermute | solution.py:824
  32.2 17.6 %collective-permute-start.10 = (bf16[2944,128]{1,0:T(8,128)(2,1)S(1)}, bf16[2944,128]{1,0:T(8,128)(2,1)S(1)}, u32[]{:S(2)}, u32[]{:S(2)}) collective-permute-start(bf16[2944,128]{1,0:T(8,128)(2,1)S(1)} %pad_maximum_fusion.1), channel_id=1, source_target_pairs={{1,0},{0,1},{3,2},{2,3},{5,4},{4,5},{7,6},{6,7},{9,8},{8,9},{11,10... | collective-permute-start | bytes 2261000 | tf_op jit(solution)/shard_map/attn_gather_x1/ppermute | solution.py:824
  33.8 17.7 %collective-permute-start.8 = (bf16[2944,128]{1,0:T(8,128)(2,1)S(1)}, bf16[2944,128]{1,0:T(8,128)(2,1)S(1)}, u32[]{:S(2)}, u32[]{:S(2)}) collective-permute-start(bf16[2944,128]{1,0:T(8,128)(2,1)S(1)} %pad_maximum_fusion.1), channel_id=1, source_target_pairs={{16,0},{0,16},{17,1},{1,17},{18,2},{2,18},{19,3},{3,19},{20,4},{4,... | collective-permute-start | bytes 2261000 | tf_op jit(solution)/shard_map/attn_gather_y1/ppermute | solution.py:824
  35.0 35.4 %collective-permute-start.15 = (bf16[224,3456]{1,0:T(8,128)(2,1)}, bf16[224,3456]{1,0:T(8,128)(2,1)}, u32[]{:S(2)}, u32[]{:S(2)}) collective-permute-start(bf16[224,3456]{1,0:T(8,128)(2,1)} %pad.4.refs_8_.refs_10_), channel_id=1, source_target_pairs={{2,0},{4,2},{6,4},{0,6},{3,1},{5,3},{7,5},{1,7},{10,8},{12,10},{14... | collective-permute-start | bytes 4644872 | tf_op jit(solution)/shard_map/unit_gather_z1/ppermute | solution.py:824
  72.1 30.3 %collective-permute-start.18 = (bf16[112,3456]{1,0:T(8,128)(2,1)S(1)}, bf16[112,3456]{1,0:T(8,128)(2,1)}, u32[]{:S(2)}, u32[]{:S(2)}) collective-permute-start(bf16[112,3456]{1,0:T(8,128)(2,1)S(1)} %get-tuple-element.398), channel_id=1, source_target_pairs={{2,0},{4,2},{6,4},{0,6},{3,1},{5,3},{7,5},{1,7},{10,8},{12,10},{14... | collective-permute-start | bytes 2322440 | tf_op jit(solution)/shard_map/unit_gather_z1/ppermute | solution.py:824
  86.5 16.0 %collective-permute-start.17 = (bf16[256,512]{1,0:T(8,128)(2,1)}, bf16[256,512]{1,0:T(8,128)(2,1)S(1)}, u32[]{:S(2)}, u32[]{:S(2)}) collective-permute-start(bf16[256,512]{1,0:T(8,128)(2,1)} %get-tuple-element.221), channel_id=1, source_target_pairs={{6,0},{0,2},{2,4},{4,6},{7,1},{1,3},{3,5},{5,7},{14,8},{8,10},{10,... | collective-permute-start | bytes 786440 | tf_op jit(solution)/shard_map/kv_gather_z-1/ppermute | solution.py:824
  102.5 15.0 %collective-permute-start.21 = (bf16[256,512]{1,0:T(8,128)(2,1)S(1)}, bf16[256,512]{1,0:T(8,128)(2,1)S(1)}, u32[]{:S(2)}, u32[]{:S(2)}) collective-permute-start(bf16[256,512]{1,0:T(8,128)(2,1)S(1)} %collective-permute-done.16), channel_id=1, source_target_pairs={{1,0},{0,1},{3,2},{2,3},{5,4},{4,5},{7,6},{6,7},{9,8},{8,9},{11,10... | collective-permute-start | bytes 786440 | tf_op jit(solution)/shard_map/kv_gather_vx1/ppermute | solution.py:824
  103.1 19.9 %collective-permute-start.25 = (bf16[256,512]{1,0:T(8,128)(2,1)S(1)}, bf16[256,512]{1,0:T(8,128)(2,1)S(1)}, u32[]{:S(2)}, u32[]{:S(2)}) collective-permute-start(bf16[256,512]{1,0:T(8,128)(2,1)S(1)} %collective-permute-done.17), channel_id=1, source_target_pairs={{1,0},{0,1},{3,2},{2,3},{5,4},{4,5},{7,6},{6,7},{9,8},{8,9},{11,10... | collective-permute-start | bytes 786440 | tf_op jit(solution)/shard_map/kv_gather_vx1/ppermute | solution.py:824
  108.3 24.8 %collective-permute-start.19 = (bf16[112,3456]{1,0:T(8,128)(2,1)S(1)}, bf16[112,3456]{1,0:T(8,128)(2,1)S(1)}, u32[]{:S(2)}, u32[]{:S(2)}) collective-permute-start(bf16[112,3456]{1,0:T(8,128)(2,1)S(1)} %get-tuple-element.222), channel_id=1, source_target_pairs={{2,0},{4,2},{6,4},{0,6},{3,1},{5,3},{7,5},{1,7},{10,8},{12,10},{14... | collective-permute-start | bytes 2322440 | tf_op jit(solution)/shard_map/unit_gather_z1/ppermute | solution.py:824
  117.1 31.2 %collective-permute-start.28 = (bf16[112,3456]{1,0:T(8,128)(2,1)}, bf16[112,3456]{1,0:T(8,128)(2,1)S(1)}, u32[]{:S(2)}, u32[]{:S(2)}) collective-permute-start(bf16[112,3456]{1,0:T(8,128)(2,1)} %collective-permute-done.18.refs_10_.refs_12_), channel_id=1, source_target_pairs={{2,0},{4,2},{6,4},{0,6},{3,1},{5,3},{7,5},{1,7},{10,8},{12,10},{14... | collective-permute-start | bytes 2322440 | tf_op jit(solution)/shard_map/unit_gather_z1/ppermute | solution.py:824
  133.1 15.2 %collective-permute-start.26 = (bf16[256,1152]{1,0:T(8,128)(2,1)S(1)}, bf16[256,1152]{1,0:T(8,128)(2,1)S(1)}, u32[]{:S(2)}, u32[]{:S(2)}) collective-permute-start(bf16[256,1152]{1,0:T(8,128)(2,1)S(1)} %get-tuple-element.242.refs_0_), channel_id=1, source_target_pairs={{16,0},{0,16},{17,1},{1,17},{18,2},{2,18},{19,3},{3,19},{20,4},{4,... | collective-permute-start | bytes 1769480 | tf_op jit(solution)/shard_map/ffn_in_gather_y1/ppermute | solution.py:824
  133.8 14.5 %collective-permute-start.27 = (bf16[256,1152]{1,0:T(8,128)(2,1)S(1)}, bf16[256,1152]{1,0:T(8,128)(2,1)S(1)}, u32[]{:S(2)}, u32[]{:S(2)}) collective-permute-start(bf16[256,1152]{1,0:T(8,128)(2,1)S(1)} %get-tuple-element.242.refs_0_), channel_id=1, source_target_pairs={{1,0},{0,1},{3,2},{2,3},{5,4},{4,5},{7,6},{6,7},{9,8},{8,9},{11,10... | collective-permute-start | bytes 1769480 | tf_op jit(solution)/shard_map/ffn_in_gather_x1/ppermute | solution.py:824
  135.2 27.8 %collective-permute-start.34 = (bf16[112,3456]{1,0:T(8,128)(2,1)S(1)}, bf16[112,3456]{1,0:T(8,128)(2,1)S(1)}, u32[]{:S(2)}, u32[]{:S(2)}) collective-permute-start(bf16[112,3456]{1,0:T(8,128)(2,1)S(1)} %collective-permute-done.19.refs_11_.refs_13_), channel_id=1, source_target_pairs={{2,0},{4,2},{6,4},{0,6},{3,1},{5,3},{7,5},{1,7},{10,8},{12,10},{14... | collective-permute-start | bytes 2322440 | tf_op jit(solution)/shard_map/unit_gather_z1/ppermute | solution.py:824
  148.3 14.8 %collective-permute-start.32 = (bf16[128,1152]{1,0:T(8,128)(2,1)S(1)}, bf16[128,1152]{1,0:T(8,128)(2,1)S(1)}, u32[]{:S(2)}, u32[]{:S(2)}) collective-permute-start(bf16[128,1152]{1,0:T(8,128)(2,1)S(1)} %slice.209), channel_id=1, source_target_pairs={{16,0},{0,16},{17,1},{1,17},{18,2},{2,18},{19,3},{3,19},{20,4},{4,... | collective-permute-start | bytes 884744 | tf_op jit(solution)/shard_map/ffn_in_gather_y1/ppermute | solution.py:824
  149.0 14.1 %collective-permute-start.33 = (bf16[128,1152]{1,0:T(8,128)(2,1)S(1)}, bf16[128,1152]{1,0:T(8,128)(2,1)S(1)}, u32[]{:S(2)}, u32[]{:S(2)}) collective-permute-start(bf16[128,1152]{1,0:T(8,128)(2,1)S(1)} %slice.210), channel_id=1, source_target_pairs={{1,0},{0,1},{3,2},{2,3},{5,4},{4,5},{7,6},{6,7},{9,8},{8,9},{11,10... | collective-permute-start | bytes 884744 | tf_op jit(solution)/shard_map/ffn_in_gather_x1/ppermute | solution.py:824
  149.6 15.5 %collective-permute-start.30 = (bf16[256,1152]{1,0:T(8,128)(2,1)S(1)}, bf16[256,1152]{1,0:T(8,128)(2,1)S(1)}, u32[]{:S(2)}, u32[]{:S(2)}) collective-permute-start(bf16[256,1152]{1,0:T(8,128)(2,1)S(1)} %collective-permute-done.26.refs_2_), channel_id=1, source_target_pairs={{8,0},{0,8},{9,1},{1,9},{10,2},{2,10},{11,3},{3,11},{12,4},{4,12},... | collective-permute-start | bytes 1769480 | tf_op jit(solution)/shard_map/ffn_in_gather_c1/ppermute | solution.py:824
  149.6 15.5 %collective-permute-start.31 = (bf16[256,1152]{1,0:T(8,128)(2,1)S(1)}, bf16[256,1152]{1,0:T(8,128)(2,1)S(1)}, u32[]{:S(2)}, u32[]{:S(2)}) collective-permute-start(bf16[256,1152]{1,0:T(8,128)(2,1)S(1)} %collective-permute-done.27.refs_4_), channel_id=1, source_target_pairs={{8,0},{0,8},{9,1},{1,9},{10,2},{2,10},{11,3},{3,11},{12,4},{4,12},... | collective-permute-start | bytes 1769480 | tf_op jit(solution)/shard_map/ffn_in_gather_c1/ppermute | solution.py:824
  202.1 14.6 %collective-permute-start.43 = (bf16[256,1152]{1,0:T(8,128)(2,1)S(1)}, bf16[256,1152]{1,0:T(8,128)(2,1)S(1)}, u32[]{:S(2)}, u32[]{:S(2)}) collective-permute-start(bf16[256,1152]{1,0:T(8,128)(2,1)S(1)} %pad_maximum_fusion.5), channel_id=1, source_target_pairs={{16,0},{0,16},{17,1},{1,17},{18,2},{2,18},{19,3},{3,19},{20,4},{4,... | collective-permute-start | bytes 1769480 | tf_op jit(solution)/shard_map/ffn_out_sum_y-1/ppermute | solution.py:824
  203.0 14.6 %collective-permute-start.40 = (bf16[256,1152]{1,0:T(8,128)(2,1)S(1)}, bf16[256,1152]{1,0:T(8,128)(2,1)S(1)}, u32[]{:S(2)}, u32[]{:S(2)}) collective-permute-start(bf16[256,1152]{1,0:T(8,128)(2,1)S(1)} %pad_maximum_fusion.4), channel_id=1, source_target_pairs={{1,0},{0,1},{3,2},{2,3},{5,4},{4,5},{7,6},{6,7},{9,8},{8,9},{11,10... | collective-permute-start | bytes 1769480 | tf_op jit(solution)/shard_map/ffn_out_sum_x-1/ppermute | solution.py:824
  219.1 13.6 %collective-permute-start.47 = (bf16[256,1152]{1,0:T(8,128)(2,1)S(1)}, bf16[256,1152]{1,0:T(8,128)(2,1)S(1)}, u32[]{:S(2)}, u32[]{:S(2)}) collective-permute-start(bf16[256,1152]{1,0:T(8,128)(2,1)S(1)} %get-tuple-element.266.refs_0_), channel_id=1, source_target_pairs={{1,0},{0,1},{3,2},{2,3},{5,4},{4,5},{7,6},{6,7},{9,8},{8,9},{11,10... | collective-permute-start | bytes 1769480 | tf_op jit(solution)/shard_map/d_out_gather_x1/ppermute | solution.py:824
  219.9 13.7 %collective-permute-start.45 = (bf16[256,1152]{1,0:T(8,128)(2,1)S(1)}, bf16[256,1152]{1,0:T(8,128)(2,1)S(1)}, u32[]{:S(2)}, u32[]{:S(2)}) collective-permute-start(bf16[256,1152]{1,0:T(8,128)(2,1)S(1)} %get-tuple-element.266.refs_0_), channel_id=1, source_target_pairs={{16,0},{0,16},{17,1},{1,17},{18,2},{2,18},{19,3},{3,19},{20,4},{4,... | collective-permute-start | bytes 1769480 | tf_op jit(solution)/shard_map/d_out_gather_y1/ppermute | solution.py:824
  251.1 24.7 %collective-permute-start.52 = (bf16[224,1152]{1,0:T(8,128)(2,1)S(1)}, bf16[224,1152]{1,0:T(8,128)(2,1)S(1)}, u32[]{:S(2)}, u32[]{:S(2)}) collective-permute-start(bf16[224,1152]{1,0:T(8,128)(2,1)S(1)} %get-tuple-element.270), channel_id=1, source_target_pairs={{6,0},{0,2},{2,4},{4,6},{7,1},{1,3},{3,5},{5,7},{14,8},{8,10},{10,... | collective-permute-start | bytes 1548296 | tf_op jit(solution)/shard_map/down_grad_sum_z-1/ppermute | solution.py:824
  275.6 31.0 %collective-permute-start.55 = (bf16[256,1152]{1,0:T(8,128)(2,1)}, bf16[256,1152]{1,0:T(8,128)(2,1)S(1)}, u32[]{:S(2)}, u32[]{:S(2)}) collective-permute-start(bf16[256,1152]{1,0:T(8,128)(2,1)} %get-tuple-element.277), channel_id=1, source_target_pairs={{8,0},{0,8},{9,1},{1,9},{10,2},{2,10},{11,3},{3,11},{12,4},{4,12},... | collective-permute-start | bytes 1769480 | tf_op jit(solution)/shard_map/d_in_sum_c1/ppermute | solution.py:824
  276.3 18.2 %collective-permute-start.56 = (bf16[224,1152]{1,0:T(8,128)(2,1)S(1)}, bf16[224,1152]{1,0:T(8,128)(2,1)S(1)}, u32[]{:S(2)}, u32[]{:S(2)}) collective-permute-start(bf16[224,1152]{1,0:T(8,128)(2,1)S(1)} %add_convert_fusion.16), channel_id=1, source_target_pairs={{6,0},{0,2},{2,4},{4,6},{7,1},{1,3},{3,5},{5,7},{14,8},{8,10},{10,... | collective-permute-start | bytes 1548296 | tf_op jit(solution)/shard_map/down_grad_sum_z-1/ppermute | solution.py:824
  279.9 14.3 %collective-permute-start.60 = (bf16[128,1152]{1,0:T(8,128)(2,1)S(1)}, bf16[128,1152]{1,0:T(8,128)(2,1)S(1)}, u32[]{:S(2)}, u32[]{:S(2)}) collective-permute-start(bf16[128,1152]{1,0:T(8,128)(2,1)S(1)} %get-tuple-element.416), channel_id=1, source_target_pairs={{1,0},{0,1},{3,2},{2,3},{5,4},{4,5},{7,6},{6,7},{9,8},{8,9},{11,10... | collective-permute-start | bytes 884744 | tf_op jit(solution)/shard_map/d_in_sum_x-1/ppermute | solution.py:824
  292.4 17.3 %collective-permute-start.54 = (bf16[224,1152]{1,0:T(8,128)(2,1)S(1)}, bf16[224,1152]{1,0:T(8,128)(2,1)S(1)}, u32[]{:S(2)}, u32[]{:S(2)}) collective-permute-start(bf16[224,1152]{1,0:T(8,128)(2,1)S(1)} %get-tuple-element.275), channel_id=1, source_target_pairs={{6,0},{0,2},{2,4},{4,6},{7,1},{1,3},{3,5},{5,7},{14,8},{8,10},{10,... | collective-permute-start | bytes 1548296 | tf_op jit(solution)/shard_map/gate_grad_sum_z-1/ppermute | solution.py:824
  294.5 14.5 %collective-permute-start.61 = (bf16[256,1152]{1,0:T(8,128)(2,1)S(1)}, bf16[256,1152]{1,0:T(8,128)(2,1)S(1)}, u32[]{:S(2)}, u32[]{:S(2)}) collective-permute-start(bf16[256,1152]{1,0:T(8,128)(2,1)S(1)} %pad_maximum_fusion.6), channel_id=1, source_target_pairs={{1,0},{0,1},{3,2},{2,3},{5,4},{4,5},{7,6},{6,7},{9,8},{8,9},{11,10... | collective-permute-start | bytes 1769480 | tf_op jit(solution)/shard_map/d_in_sum_x-1/ppermute | solution.py:824
  295.3 14.4 %collective-permute-start.62 = (bf16[256,1152]{1,0:T(8,128)(2,1)S(1)}, bf16[256,1152]{1,0:T(8,128)(2,1)S(1)}, u32[]{:S(2)}, u32[]{:S(2)}) collective-permute-start(bf16[256,1152]{1,0:T(8,128)(2,1)S(1)} %pad_maximum_fusion.7), channel_id=1, source_target_pairs={{16,0},{0,16},{17,1},{1,17},{18,2},{2,18},{19,3},{3,19},{20,4},{4,... | collective-permute-start | bytes 1769480 | tf_op jit(solution)/shard_map/d_in_sum_y-1/ppermute | solution.py:824
  303.6 18.9 %collective-permute-start.64 = (bf16[224,1152]{1,0:T(8,128)(2,1)}, bf16[224,1152]{1,0:T(8,128)(2,1)S(1)}, u32[]{:S(2)}, u32[]{:S(2)}) collective-permute-start(bf16[224,1152]{1,0:T(8,128)(2,1)} %get-tuple-element.301), channel_id=1, source_target_pairs={{6,0},{0,2},{2,4},{4,6},{7,1},{1,3},{3,5},{5,7},{14,8},{8,10},{10,... | collective-permute-start | bytes 1548296 | tf_op jit(solution)/shard_map/up_grad_sum_z-1/ppermute | solution.py:824
  306.6 23.0 %collective-permute-start.63 = (bf16[224,1152]{1,0:T(8,128)(2,1)S(1)}, bf16[224,1152]{1,0:T(8,128)(2,1)S(1)}, u32[]{:S(2)}, u32[]{:S(2)}) collective-permute-start(bf16[224,1152]{1,0:T(8,128)(2,1)S(1)} %add_convert_fusion.15), channel_id=1, source_target_pairs={{6,0},{0,2},{2,4},{4,6},{7,1},{1,3},{3,5},{5,7},{14,8},{8,10},{10,... | collective-permute-start | bytes 1548296 | tf_op jit(solution)/shard_map/down_grad_sum_z-1/ppermute | solution.py:824
  330.2 14.2 %collective-permute-start.65 = (bf16[256,512]{1,0:T(8,128)(2,1)S(1)}, bf16[256,512]{1,0:T(8,128)(2,1)S(1)}, u32[]{:S(2)}, u32[]{:S(2)}) collective-permute-start(bf16[256,512]{1,0:T(8,128)(2,1)S(1)} %get-tuple-element.319), channel_id=1, source_target_pairs={{1,0},{0,1},{3,2},{2,3},{5,4},{4,5},{7,6},{6,7},{9,8},{8,9},{11,10... | collective-permute-start | bytes 786440 | tf_op jit(solution)/shard_map/kv_sum_vx-1/ppermute | solution.py:824
  331.6 18.5 %collective-permute-start.66 = (bf16[256,512]{1,0:T(8,128)(2,1)S(1)}, bf16[256,512]{1,0:T(8,128)(2,1)S(1)}, u32[]{:S(2)}, u32[]{:S(2)}) collective-permute-start(bf16[256,512]{1,0:T(8,128)(2,1)S(1)} %get-tuple-element.321), channel_id=1, source_target_pairs={{1,0},{0,1},{3,2},{2,3},{5,4},{4,5},{7,6},{6,7},{9,8},{8,9},{11,10... | collective-permute-start | bytes 786440 | tf_op jit(solution)/shard_map/kv_sum_vx-1/ppermute | solution.py:824
  332.3 20.8 %collective-permute-start.67 = (bf16[256,512]{1,0:T(8,128)(2,1)S(1)}, bf16[256,512]{1,0:T(8,128)(2,1)S(1)}, u32[]{:S(2)}, u32[]{:S(2)}) collective-permute-start(bf16[256,512]{1,0:T(8,128)(2,1)S(1)} %get-tuple-element.323), channel_id=1, source_target_pairs={{1,0},{0,1},{3,2},{2,3},{5,4},{4,5},{7,6},{6,7},{9,8},{8,9},{11,10... | collective-permute-start | bytes 786440 | tf_op jit(solution)/shard_map/kv_sum_vx-1/ppermute | solution.py:824
  339.0 14.1 %collective-permute-start.69 = (bf16[128,512]{1,0:T(8,128)(2,1)S(1)}, bf16[128,512]{1,0:T(8,128)(2,1)S(1)}, u32[]{:S(2)}, u32[]{:S(2)}) collective-permute-start(bf16[128,512]{1,0:T(8,128)(2,1)S(1)} %get-tuple-element.423), channel_id=1, source_target_pairs={{6,0},{0,2},{2,4},{4,6},{7,1},{1,3},{3,5},{5,7},{14,8},{8,10},{10,... | collective-permute-start | bytes 393224 | tf_op jit(solution)/shard_map/kv_sum_z-1/ppermute | solution.py:824
  344.5 22.5 %collective-permute-start.73 = (bf16[224,1152]{1,0:T(8,128)(2,1)S(1)}, bf16[224,1152]{1,0:T(8,128)(2,1)S(1)}, u32[]{:S(2)}, u32[]{:S(2)}) collective-permute-start(bf16[224,1152]{1,0:T(8,128)(2,1)S(1)} %add_convert_fusion.14), channel_id=1, source_target_pairs={{6,0},{0,2},{2,4},{4,6},{7,1},{1,3},{3,5},{5,7},{14,8},{8,10},{10,... | collective-permute-start | bytes 1548296 | tf_op jit(solution)/shard_map/gate_grad_sum_z-1/ppermute | solution.py:824
  353.2 16.9 %collective-permute-start.72 = (bf16[256,512]{1,0:T(8,128)(2,1)S(1)}, bf16[256,512]{1,0:T(8,128)(2,1)S(1)}, u32[]{:S(2)}, u32[]{:S(2)}) collective-permute-start(bf16[256,512]{1,0:T(8,128)(2,1)S(1)} %pad_maximum_fusion.11), channel_id=1, source_target_pairs={{2,0},{4,2},{6,4},{0,6},{3,1},{5,3},{7,5},{1,7},{10,8},{12,10},{14... | collective-permute-start | bytes 786440 | tf_op jit(solution)/shard_map/kv_sum_z1/ppermute | solution.py:824
  356.0 14.1 %collective-permute-start.71 = (bf16[256,512]{1,0:T(8,128)(2,1)S(1)}, bf16[256,512]{1,0:T(8,128)(2,1)S(1)}, u32[]{:S(2)}, u32[]{:S(2)}) collective-permute-start(bf16[256,512]{1,0:T(8,128)(2,1)S(1)} %pad_maximum_fusion.10), channel_id=1, source_target_pairs={{6,0},{0,2},{2,4},{4,6},{7,1},{1,3},{3,5},{5,7},{14,8},{8,10},{10,... | collective-permute-start | bytes 786440 | tf_op jit(solution)/shard_map/kv_sum_z-1/ppermute | solution.py:824
  367.1 16.7 %collective-permute-start.83 = (bf16[224,1152]{1,0:T(8,128)(2,1)S(1)}, bf16[224,1152]{1,0:T(8,128)(2,1)S(1)}, u32[]{:S(2)}, u32[]{:S(2)}) collective-permute-start(bf16[224,1152]{1,0:T(8,128)(2,1)S(1)} %add_convert_fusion.12), channel_id=1, source_target_pairs={{6,0},{0,2},{2,4},{4,6},{7,1},{1,3},{3,5},{5,7},{14,8},{8,10},{10,... | collective-permute-start | bytes 1548296 | tf_op jit(solution)/shard_map/gate_grad_sum_z-1/ppermute | solution.py:824
  367.8 23.5 %collective-permute-start.76 = (bf16[224,1152]{1,0:T(8,128)(2,1)S(1)}, bf16[224,1152]{1,0:T(8,128)(2,1)S(1)}, u32[]{:S(2)}, u32[]{:S(2)}) collective-permute-start(bf16[224,1152]{1,0:T(8,128)(2,1)S(1)} %add_convert_fusion.13), channel_id=1, source_target_pairs={{6,0},{0,2},{2,4},{4,6},{7,1},{1,3},{3,5},{5,7},{14,8},{8,10},{10,... | collective-permute-start | bytes 1548296 | tf_op jit(solution)/shard_map/up_grad_sum_z-1/ppermute | solution.py:824
  391.5 13.5 %collective-permute-start.84 = (bf16[224,1152]{1,0:T(8,128)(2,1)S(1)}, bf16[224,1152]{1,0:T(8,128)(2,1)S(1)}, u32[]{:S(2)}, u32[]{:S(2)}) collective-permute-start(bf16[224,1152]{1,0:T(8,128)(2,1)S(1)} %add_convert_fusion.10), channel_id=1, source_target_pairs={{6,0},{0,2},{2,4},{4,6},{7,1},{1,3},{3,5},{5,7},{14,8},{8,10},{10,... | collective-permute-start | bytes 1548296 | tf_op jit(solution)/shard_map/up_grad_sum_z-1/ppermute | solution.py:824
  399.5 17.1 %collective-permute-start.82 = (bf16[2944,128]{1,0:T(8,128)(2,1)S(1)}, bf16[2944,128]{1,0:T(8,128)(2,1)S(1)}, u32[]{:S(2)}, u32[]{:S(2)}) collective-permute-start(bf16[2944,128]{1,0:T(8,128)(2,1)S(1)} %pad_maximum_fusion.3), channel_id=1, source_target_pairs={{16,0},{0,16},{17,1},{1,17},{18,2},{2,18},{19,3},{3,19},{20,4},{4,... | collective-permute-start | bytes 2261000 | tf_op jit(solution)/shard_map/attn_grad_sum_y-1/ppermute | solution.py:824
  403.0 13.6 %collective-permute-start.79 = (bf16[2944,128]{1,0:T(8,128)(2,1)S(1)}, bf16[2944,128]{1,0:T(8,128)(2,1)S(1)}, u32[]{:S(2)}, u32[]{:S(2)}) collective-permute-start(bf16[2944,128]{1,0:T(8,128)(2,1)S(1)} %pad_maximum_fusion.2), channel_id=1, source_target_pairs={{1,0},{0,1},{3,2},{2,3},{5,4},{4,5},{7,6},{6,7},{9,8},{8,9},{11,10... | collective-permute-start | bytes 2261000 | tf_op jit(solution)/shard_map/attn_grad_sum_x-1/ppermute | solution.py:824
  421.3 18.5 %collective-permute-start.90 = (bf16[216,864]{1,0:T(8,128)(2,1)S(1)}, bf16[216,864]{1,0:T(8,128)(2,1)S(1)}, u32[]{:S(2)}, u32[]{:S(2)}) collective-permute-start(bf16[216,864]{1,0:T(8,128)(2,1)S(1)} %get-tuple-element.395), channel_id=1, source_target_pairs={{16,0},{24,8},{0,16},{8,24},{17,1},{25,9},{1,17},{9,25},{18,2},{26... | collective-permute-start | bytes 1119752 | tf_op jit(solution)/shard_map/grad_exchange_uyc2/ppermute | solution.py:824
  422.3 18.1 %collective-permute-start.91 = (bf16[216,864]{1,0:T(8,128)(2,1)S(1)}, bf16[216,864]{1,0:T(8,128)(2,1)S(1)}, u32[]{:S(2)}, u32[]{:S(2)}) collective-permute-start(bf16[216,864]{1,0:T(8,128)(2,1)S(1)} %get-tuple-element.394), channel_id=1, source_target_pairs={{24,0},{0,8},{8,16},{16,24},{25,1},{1,9},{9,17},{17,25},{26,2},{2,... | collective-permute-start | bytes 1119752 | tf_op jit(solution)/shard_map/grad_exchange_uyc3/ppermute | solution.py:824
  424.3 21.7 %collective-permute-start.88 = (bf16[736,128]{1,0:T(8,128)(2,1)S(1)}, bf16[736,128]{1,0:T(8,128)(2,1)S(1)}, u32[]{:S(2)}, u32[]{:S(2)}) collective-permute-start(bf16[736,128]{1,0:T(8,128)(2,1)S(1)} %pad_maximum_fusion.15), channel_id=1, source_target_pairs={{2,0},{4,2},{6,4},{0,6},{3,1},{5,3},{7,5},{1,7},{10,8},{12,10},{14... | collective-permute-start | bytes 565256 | tf_op jit(solution)/shard_map/attn_grad_sum_z1/ppermute | solution.py:824
  427.4 18.6 %collective-permute-start.86 = (bf16[736,128]{1,0:T(8,128)(2,1)S(1)}, bf16[736,128]{1,0:T(8,128)(2,1)S(1)}, u32[]{:S(2)}, u32[]{:S(2)}) collective-permute-start(bf16[736,128]{1,0:T(8,128)(2,1)S(1)} %pad_maximum_fusion.14), channel_id=1, source_target_pairs={{6,0},{0,2},{2,4},{4,6},{7,1},{1,3},{3,5},{5,7},{14,8},{8,10},{10,... | collective-permute-start | bytes 565256 | tf_op jit(solution)/shard_map/attn_grad_sum_z-1/ppermute | solution.py:824
  (122 other events, 1438.1 us)
